TPU v7x, 32 devices: a whole 2x2x4 slice. The times are simulated.
32 devices in a mesh: dp: 16 (over z, y, x), mp: 2 (over core).
Axes of the slice: x: 2, y: 2, z: 4, core: 2. Of those that a mesh axis runs over, the one named last changes fastest.
Arguments:
- layer_input: bfloat16 [32, 512, 768], P('dp'), may hold values from -6 to 6
- segments: int32 [32, 512], P('dp'), may hold values from 0 to 15, never falling along the last dimension, each value on 1 to 256 neighbouring positions
- modality: int32 [32, 16], P('dp'), may hold values from 0 to 2, as said below
- ln_gain: float32 [2, 768], replicated, may hold values from 0.1 to 1.9
- ln_bias: float32 [2, 768], replicated, may hold values from -3 to 3
- w_qkv: bfloat16 [3, 768, 768], P(None, 'dp', 'mp'), may hold values from -0.21875 to 0.21875
- qv_bias: float32 [2, 768], replicated, may hold values from -3 to 3
- w_out: bfloat16 [768, 768], P('dp', 'mp'), may hold values from -0.875 to 0.875
- out_bias: float32 [768], replicated, may hold values from -3 to 3
- w_up: bfloat16 [3, 768, 3072], P(None, 'dp', 'mp'), may hold values from -0.21875 to 0.21875
- up_bias: float32 [3, 3072], replicated, may hold values from -3 to 3
- w_down: bfloat16 [3, 768, 3072], P(None, 'dp', 'mp'), may hold values from -0.21875 to 0.21875
- down_bias: float32 [3, 768], replicated, may hold values from -3 to 3
- cotangent: bfloat16 [32, 512, 768], P('dp'), may hold values from -6 to 6
Outputs:
- layer_output: bfloat16 [32, 512, 768], P('dp')
- grad_input: float32 [32, 512, 768], P('dp')
- grad_ln_gain: float32 [2, 768], replicated
- grad_ln_bias: float32 [2, 768], replicated
- grad_w_qkv: float32 [3, 768, 768], P(None, 'dp', 'mp')
- grad_qv_bias: float32 [2, 768], replicated
- grad_w_out: float32 [768, 768], P('dp', 'mp')
- grad_out_bias: float32 [768], replicated
- grad_w_up: float32 [3, 768, 3072], P(None, 'dp', 'mp')
- grad_up_bias: float32 [3, 3072], replicated
- grad_w_down: float32 [3, 768, 3072], P(None, 'dp', 'mp')
- grad_down_bias: float32 [3, 768], replicated
Inputs may be any that keep to these rules, and one draw needn't show every extreme that they name: `segments`: within a row the document ids never fall; each document holds at most 256 tokens and one holds exactly that many. `modality`: every token of a document goes to the document's one expert (vision, language or vision-language); most documents are language, and any document may be of any kind.
All inputs are finite; a program needn't handle non-finite values.
Results may differ from a plain program's by a relative error of at most 0.015.
Values may be sent and summed in bfloat16 or wider, within the bound.
No kernel may reach another device: no remote copies, remote signals or barrier semaphores. Data moves between devices by JAX's collectives and lax.ppermute only.
A program may use at most 256 MiB of HBM per device.

v0:
```python
import jax
import jax.numpy as jnp
from jax import lax
from jax.sharding import PartitionSpec as P

HD = 64


EPS = 1e-05


def layer_norm(v, gain, shift):
    mean = jnp.mean(v, axis=-1, keepdims=True)
    cent = v - mean
    var = jnp.mean(cent * cent, axis=-1, keepdims=True)
    return cent * lax.rsqrt(var + EPS) * gain + shift


def exact_gelu(v):
    return jax.nn.gelu(v, approximate=False)


def row_probs(query, keys, seg_row, scale):
    scores = jnp.einsum("qhc,khc->hqk", query, keys, preferred_element_type=jnp.float32) * scale
    same = seg_row[:, None] == seg_row[None, :]
    scores = jnp.where(same[None], scores, jnp.float32(-1e30))
    top = jnp.max(scores, axis=-1, keepdims=True)
    expo = jnp.exp(scores - top)
    return expo / jnp.sum(expo, axis=-1, keepdims=True)


def body(
    layer_input,
    segments,
    modality,
    ln_gain,
    ln_bias,
    w_qkv,
    qv_bias,
    w_out,
    out_bias,
    w_up,
    up_bias,
    w_down,
    down_bias,
    cotangent,
):
    bf16 = jnp.bfloat16
    f32 = jnp.float32
    highest = lax.Precision.HIGHEST
    part = lax.axis_index("mp")
    parts = lax.axis_size("mp")
    row_count, seq_len, width = layer_input.shape
    tokens = row_count * seq_len
    local_cols = w_qkv.shape[-1]
    hidden_loc = w_up.shape[-1]
    heads_loc = local_cols // HD
    scale = HD ** (-0.5)
    expert_count = w_up.shape[0]
    qkv_full, out_full, up_full, down_full = (
        lax.all_gather(w_qkv, "dp", axis=1, tiled=True),
        lax.all_gather(w_out, "dp", axis=0, tiled=True),
        lax.all_gather(w_up, "dp", axis=1, tiled=True),
        lax.all_gather(w_down, "dp", axis=1, tiled=True),
    )
    col_start = part * local_cols
    q_bias = lax.dynamic_slice_in_dim(qv_bias[0], col_start, local_cols)
    v_bias = lax.dynamic_slice_in_dim(qv_bias[1], col_start, local_cols)
    hid_start = part * hidden_loc
    up_b = lax.dynamic_slice_in_dim(up_bias, hid_start, hidden_loc, 1)
    xf = layer_input.reshape(tokens, width).astype(f32)
    h1, ln1_pull = jax.vjp(layer_norm, xf, ln_gain[0], ln_bias[0])
    a1 = h1.astype(bf16)
    proj = jnp.einsum("td,jde->jte", a1, qkv_full, preferred_element_type=f32)
    query = (proj[0] + q_bias).astype(bf16).reshape(row_count, seq_len, heads_loc, HD)
    keys = proj[1].astype(bf16).reshape(row_count, seq_len, heads_loc, HD)
    values = (proj[2] + v_bias).astype(bf16).reshape(row_count, seq_len, heads_loc, HD)

    def attend_row(item):
        q_row, k_row, v_row, s_row = item
        probs = row_probs(q_row, k_row, s_row, scale)
        mixed = jnp.einsum("hqk,khc->qhc", probs.astype(bf16), v_row, preferred_element_type=f32)
        return mixed.astype(bf16)

    attended = lax.map(attend_row, (query, keys, values, segments)).reshape(tokens, local_cols)
    att_part = jnp.einsum("ti,oi->to", attended, out_full, preferred_element_type=f32)
    branch = lax.psum(att_part.astype(jnp.bfloat16), "mp").astype(jnp.float32)
    x2 = xf + branch + out_bias
    h2, ln2_pull = jax.vjp(layer_norm, x2, ln_gain[1], ln_bias[1])
    a2 = h2.astype(bf16)
    doc_ids = jnp.arange(modality.shape[1], dtype=jnp.int32)
    doc_match = segments[:, :, None] == doc_ids[None, None, :]
    mods = jnp.sum(jnp.where(doc_match, modality[:, None, :], jnp.int32(0)), axis=-1).reshape(
        tokens
    )
    onehot_int = (mods[:, None] == jnp.arange(expert_count, dtype=jnp.int32)[None, :]).astype(
        jnp.int32
    )
    onehot = onehot_int.astype(f32)
    actives = []
    pulls = []
    down_part = jnp.zeros((tokens, width), f32)
    for expert in range(expert_count):
        upper = jnp.dot(a2, up_full[expert], preferred_element_type=f32) + up_b[expert]
        gelu_out, gelu_pull = jax.vjp(exact_gelu, upper)
        active = (gelu_out.astype(bf16).astype(f32) * onehot[:, expert : expert + 1]).astype(bf16)
        actives.append(active)
        pulls.append(gelu_pull)
        down_part = down_part + jnp.einsum(
            "tf,of->to", active, down_full[expert], preferred_element_type=f32
        )
    down_sum = lax.psum(down_part.astype(jnp.bfloat16), "mp").astype(jnp.float32)
    down_sum = down_sum + jnp.dot(onehot, down_bias, precision=highest)
    layer_output = (x2 + down_sum).astype(bf16)
    grad_y = cotangent.reshape(tokens, width)
    grad_yf = grad_y.astype(f32)
    g_down_bias = jnp.dot(onehot.T, grad_yf, precision=highest) / parts
    g_up_loc = []
    g_down_loc = []
    g_upb_loc = []
    da2_part = jnp.zeros((tokens, width), f32)
    for expert in range(expert_count):
        d_active = (
            jnp.dot(grad_y, down_full[expert], preferred_element_type=f32)
            * onehot[:, expert : expert + 1]
        )
        d_upper = pulls[expert](d_active)[0].astype(bf16)
        g_down_loc.append(
            jnp.einsum("to,tf->of", grad_y, actives[expert], preferred_element_type=f32)
        )
        g_up_loc.append(jnp.einsum("td,tf->df", a2, d_upper, preferred_element_type=f32))
        g_upb_loc.append(jnp.sum(d_upper.astype(f32), axis=0))
        da2_part = da2_part + jnp.einsum(
            "tf,df->td", d_upper, up_full[expert], preferred_element_type=f32
        )
    g_up_all = jnp.stack(g_up_loc)
    g_down_all = jnp.stack(g_down_loc)
    g_upb_all = jnp.stack(g_upb_loc)
    da2 = lax.psum(da2_part, "mp")
    dx2_norm, g_gain1, g_lnb1 = ln2_pull(da2)
    dx2 = grad_yf + dx2_norm
    dx2_low = dx2.astype(bf16)
    g_out_bias = jnp.sum(dx2, axis=0) / parts
    g_out_loc = jnp.einsum("to,ti->oi", dx2_low, attended, preferred_element_type=f32)
    d_att = jnp.dot(dx2_low, out_full, preferred_element_type=f32).astype(bf16)
    d_att = d_att.reshape(row_count, seq_len, heads_loc, HD)

    def back_row(item):
        q_row, k_row, v_row, s_row, do_row = item
        probs = row_probs(q_row, k_row, s_row, scale)
        d_val = jnp.einsum("hqk,qhc->khc", probs.astype(bf16), do_row, preferred_element_type=f32)
        d_prob = jnp.einsum("qhc,khc->hqk", do_row, v_row, preferred_element_type=f32)
        d_score = probs * (d_prob - jnp.sum(probs * d_prob, axis=-1, keepdims=True))
        d_score = d_score.astype(bf16)
        d_query = jnp.einsum("hqk,khc->qhc", d_score, k_row, preferred_element_type=f32) * scale
        d_key = jnp.einsum("hqk,qhc->khc", d_score, q_row, preferred_element_type=f32) * scale
        return (d_query.astype(bf16), d_key.astype(bf16), d_val.astype(bf16))

    d_query, d_key, d_val = lax.map(back_row, (query, keys, values, segments, d_att))
    d_proj = jnp.stack(
        [
            d_query.reshape(tokens, local_cols),
            d_key.reshape(tokens, local_cols),
            d_val.reshape(tokens, local_cols),
        ]
    )
    g_qkv_loc = jnp.einsum("td,jte->jde", a1, d_proj, preferred_element_type=f32)
    bias_sums = jnp.sum(d_proj.astype(f32), axis=1)
    da1_part = jnp.einsum("jte,jde->td", d_proj, qkv_full, preferred_element_type=f32)
    da1 = lax.psum(da1_part.astype(jnp.bfloat16), "mp").astype(jnp.float32)
    dx_norm, g_gain0, g_lnb0 = ln1_pull(da1)
    grad_input = dx2 + dx_norm
    g_qkv_mine, g_out_mine, g_up_mine, g_down_mine = (
        lax.psum_scatter(g_qkv_loc, "dp", scatter_dimension=1, tiled=True),
        lax.psum_scatter(g_out_loc, "dp", scatter_dimension=0, tiled=True),
        lax.psum_scatter(g_up_all, "dp", scatter_dimension=1, tiled=True),
        lax.psum_scatter(g_down_all, "dp", scatter_dimension=1, tiled=True),
    )
    zero_index = jnp.int32(0)
    g_qv_full = lax.dynamic_update_slice(
        jnp.zeros((2, width), f32), jnp.stack([bias_sums[0], bias_sums[2]]), (zero_index, col_start)
    )
    g_upb_full = lax.dynamic_update_slice(
        jnp.zeros((expert_count, up_bias.shape[1]), f32), g_upb_all, (zero_index, hid_start)
    )
    g_gain = jnp.stack([g_gain0, g_gain1]) / parts
    g_lnb = jnp.stack([g_lnb0, g_lnb1]) / parts
    g_gain, g_lnb, g_qvb, g_outb, g_upb, g_downb = lax.psum(
        (g_gain, g_lnb, g_qv_full, g_out_bias, g_upb_full, g_down_bias), ("dp", "mp")
    )
    return (
        layer_output.reshape(row_count, seq_len, width),
        grad_input.reshape(row_count, seq_len, width),
        g_gain,
        g_lnb,
        g_qkv_mine,
        g_qvb,
        g_out_mine,
        g_outb,
        g_up_mine,
        g_upb,
        g_down_mine,
        g_downb,
    )


def solution(mesh):
    in_specs = (
        P("dp", None, None),
        P("dp", None),
        P("dp", None),
        P(),
        P(),
        P(None, "dp", "mp"),
        P(),
        P("dp", "mp"),
        P(),
        P(None, "dp", "mp"),
        P(),
        P(None, "dp", "mp"),
        P(),
        P("dp", None, None),
    )
    out_specs = (
        P("dp", None, None),
        P("dp", None, None),
        P(),
        P(),
        P(None, "dp", "mp"),
        P(),
        P("dp", "mp"),
        P(),
        P(None, "dp", "mp"),
        P(),
        P(None, "dp", "mp"),
        P(),
    )
    return jax.shard_map(body, mesh=mesh, in_specs=in_specs, out_specs=out_specs, check_vma=False)
```

profile of v0, /device:TPU:0, one launch (start us, length us, event | category | flops | bytes accessed | tf_op | source)
XLA Modules:
  0.0 1683.3 jit_solution(15060890203883411942)
XLA Ops:
  14.9 49.6 %all_gather.13 = bf16[768,384]{1,0:T(8,128)(2,1)} all-gather(bf16[48,384]{1,0:T(8,128)(2,1)} %param.25), channel_id=1, replica_groups=mesh['dp'=16,'mp'=2] {'dp'}, dimensions={0}, use_global_device_ids=true | all-gather | bytes 626688 | tf_op jit(solution)/shard_map/all_gather | solution.py:62
  66.5 6.8 all-gather.4.cloned.1.call-done
  91.5 20.0 %while.24 = (s32[]{:T(128)}, bf16[2,512,6,64]{1,3,2,0:T(8,128)(2,1)S(1)}, bf16[2,512,6,64]{1,3,2,0:T(8,128)(2,1)}, s32[2,512]{1,0:T(2,128)S(1)}, bf16[2,512,6,64...) while((s32[]{:T(128)}, bf16[2,512,6,64]{1,3,2,0:T(8,128)(2,1)S(1)}, ...), condition=%wide.region_5.6_spmd, body=%wide.region_2.5_spmd.sunk | while | flops 412549632 | bytes 17862764 | solution.py:85
  118.0 16.8 %all-reduce.11.cloned.1.call-done = bf16[1024,768]{1,0:T(8,128)(2,1)} async-done(((bf16[1024,768]{1,0:T(8,128)(2,1)}), bf16[1024,768]{1,0:T(8,128)(2,1)}) %all-reduce.11.cloned.1.call-update) | async-done | bytes 1572880 | tf_op jit(solution)/shard_map/psum | solution.py:87
  140.9 99.6 %all-gather.6.cloned.1.call-done = bf16[3,768,1536]{2,1,0:T(8,128)(2,1)} async-done(((bf16[3,48,1536]{2,1,0:T(8,128)(2,1)}), bf16[3,768,1536]{2,1,0:T(8,128)(2,1)}) %all-gather.6.cloned.1.call-update) | async-done | bytes 7077904 | tf_op jit(solution)/shard_map/all_gather | solution.py:63
  240.5 19.6 %multiply_convert_fusion.3 = (bf16[1024,1536]{1,0:T(8,128)(2,1)}, f32[1024,1536]{1,0:T(8,128)}, f32[1024,1536]{1,0:T(8,128)}) fusion(f32[1024]{0:T(1024)S(1)} %bitcast.340, f32[1536]{0:T(1024)S(1)} %get-tuple-element.214, bf16[1024,768]{1,0:T(8,128)(2,1)S(1)} %add_convert_fusion.5, bf16[3,768,1536]{2,1,0:T(8,128)(2,1)} %all-gather.6.cloned.1.call-done), kind=kOutput, calls=%fused_computation.113 | convolution fusion | flops 2524446720 | bytes 19671040 | tf_op jit(solution)/shard_map/dot_general | solution.py:104
  260.1 82.8 %all-gather.8.cloned.1.call-done = bf16[3,768,1536]{2,1,0:T(8,128)(2,1)} async-done(((bf16[3,48,1536]{2,1,0:T(8,128)(2,1)}), bf16[3,768,1536]{2,1,0:T(8,128)(2,1)}) %all-gather.8.cloned.1.call-update) | async-done | bytes 7077904 | tf_op jit(solution)/shard_map/all_gather | solution.py:64
  342.9 9.1 convert_reduce_fusion.1
  354.7 17.4 %multiply_convert_fusion.5 = (bf16[1024,1536]{1,0:T(8,128)(2,1)}, f32[1024,1536]{1,0:T(8,128)S(1)}, f32[1024,1536]{1,0:T(8,128)}) fusion(f32[1024]{0:T(1024)S(1)} %bitcast.338, f32[1536]{0:T(1024)S(1)} %get-tuple-element.215, bf16[1024,768]{1,0:T(8,128)(2,1)S(1)} %add_convert_fusion.5, bf16[3,768,1536]{2,1,0:T(8,128)(2,1)S(1)} %copy-done.68), kind=kOutput, calls=%fused_computation.127 | convolution fusion | flops 2524446720 | bytes 19673088 | tf_op jit(solution)/shard_map/dot_general | solution.py:104
  372.1 7.6 convert_reduce_fusion.2
  382.3 18.0 %multiply_convert_fusion.1 = (bf16[1024,1536]{1,0:T(8,128)(2,1)}, f32[1024,1536]{1,0:T(8,128)}, f32[1024,1536]{1,0:T(8,128)}) fusion(f32[1024]{0:T(1024)S(1)} %bitcast.336, f32[1536]{0:T(1024)S(1)} %get-tuple-element.213, bf16[1024,768]{1,0:T(8,128)(2,1)S(1)} %add_convert_fusion.5, bf16[3,768,1536]{2,1,0:T(8,128)(2,1)S(1)} %copy-done.68), kind=kOutput, calls=%fused_computation.99 | convolution fusion | flops 2524446720 | bytes 19673088 | tf_op jit(solution)/shard_map/dot_general | solution.py:104
  400.3 8.3 convert_reduce_fusion
  429.8 6.5 all-reduce.13.cloned.1.call-done
  450.0 36.0 %while.25 = (s32[]{:T(128)}, bf16[2,512,6,64]{1,3,2,0:T(8,128)(2,1)S(1)}, bf16[2,512,6,64]{1,3,2,0:T(8,128)(2,1)S(1)}, bf16[2,512,6,64]{1,3,2,0:T(8,128)(2,1)S(1...) while((s32[]{:T(128)}, ...), condition=%wide.region_18.19_spmd, body=%wide.region_14.18_spmd.sunk | while | flops 1028322816 | bytes 80047264 | solution.py:159
  497.7 6.9 convolution_bitcast_fusion
  513.6 12.0 pad_maximum_fusion.1
  525.5 20.7 %copy.117 = f32[3,768,1536]{2,0,1:T(4,128)} copy(f32[3,768,1536]{1,2,0:T(8,128)} %pad_maximum_fusion.1) | data formatting | bytes 28311552 | tf_op jit(solution)/shard_map/stack | solution.py:137
  551.8 6.3 copy.116
  573.0 6.8 convolution_bitcast_fusion.5
  587.9 11.9 pad_maximum_fusion
  610.0 571.6 %all-reduce.17.cloned.1.call-done = (f32[3,768,384]{2,0,1:T(4,128)}, f32[3,768,1536]{2,0,1:T(4,128)}) async-done(((f32[3,768,384]{2,0,1:T(4,128)}, f32[3,768,1536]{2,0,1:T(4,128)}), (f32[3,768,384]{2,0,1:T(4,128)}, f32[3,768,1536]{2,0,1:T(4,128)})) %all-reduce.17.cloned.1.call-update) | async-done | bytes 17694736
  1185.9 123.6 %reduce-scatter.3.cloned.1.call-done = f32[48,384]{1,0:T(8,128)} async-done(((f32[768,384]{1,0:T(8,128)}), f32[48,384]{1,0:T(8,128)}) %reduce-scatter.3.cloned.1.call-update) | async-done | bytes 73744 | tf_op jit(solution)/shard_map/reduce_scatter | solution.py:175
  1309.6 129.8 %all-reduce.15.cloned.1.call-done = (f32[2,768]{1,0:T(2,128)}, f32[2,768]{1,0:T(2,128)}, f32[2,768]{1,0:T(2,128)}, f32[768]{0:T(1024)}, f32[3,3072]{1,0:T(4,128)}, /*index=5*/f32[3,768]{1,0:T(4,128)}) async-done(((f32[2,768]{1,0:T(2,128)}, f32[2,768]{1,0:T(2,128)}, f32[2,768]{1,0:T(2,128)}, f32[768]{0:T(1024)}, f32[3,3072]{1,0:T(4,128)}, /*index=5*/f32[3,768]{1,0:T(4,128)}), (f32[2,768]{1,0:T(2,128)}, ...) | async-done | bytes 67600 | tf_op jit(solution)/shard_map/psum | solution.py:188
  1439.3 228.8 %reduce-scatter.5.cloned.1.call-done = f32[3,48,1536]{2,1,0:T(8,128)} async-done(((f32[3,768,1536]{2,1,0:T(8,128)}), f32[3,48,1536]{2,1,0:T(8,128)}) %reduce-scatter.5.cloned.1.call-update) | async-done | bytes 884752 | tf_op jit(solution)/shard_map/reduce_scatter | solution.py:176
  (316 shorter events, 206.0 us)
Async XLA Ops:
  7.2 594.5 %copy-start = (f32[3,768]{1,0:T(4,128)S(1)}, f32[3,768]{1,0:T(4,128)}, u32[]{:S(2)}) copy-start(f32[3,768]{1,0:T(4,128)} %param.30) | copy-start | bytes 27652
  7.2 66.2 %all-gather.4.cloned.1.call-start = ((), (), s32[]{:S(2)}) async-start(), calls=%async_computation.2 | async-start | bytes 1880064 | tf_op jit(solution)/shard_map/all_gather | solution.py:61
  7.9 126.9 %all-reduce.11.cloned.1.call-start = ((), (), s32[]{:S(2)}) async-start(), calls=%async_computation.3 | async-start | bytes 3145728 | tf_op jit(solution)/shard_map/psum | solution.py:87
  13.2 63.9 %copy-start.50 = (f32[1024]{0:T(1024)}, f32[1024]{0:T(1024)S(1)}, u32[]{:S(2)}) copy-start(f32[1024]{0:T(1024)S(1)} %rsqrt.20) | copy-start | bytes 12292
  13.2 63.9 %copy-start.44 = (f32[1,4,2,128]{3,1,2,0:T(4,128)}, f32[1,4,2,128]{3,1,2,0:T(4,128)S(1)}, u32[]{:S(2)}) copy-start(f32[1,4,2,128]{3,1,2,0:T(4,128)S(1)} %copy.125) | copy-start | bytes 12292
  14.1 50.4 %copy-start.46 = (f32[768]{0:T(1024)}, f32[768]{0:T(1024)S(1)}, u32[]{:S(2)}) copy-start(f32[768]{0:T(1024)S(1)} %get-tuple-element.216) | copy-start | bytes 9220
  14.1 125.9 %copy-start.48 = (f32[768]{0:T(1024)}, f32[768]{0:T(1024)S(1)}, u32[]{:S(2)}) copy-start(f32[768]{0:T(1024)S(1)} %get-tuple-element.217) | copy-start | bytes 9220
  91.5 21.9 %copy-start.30 = (bf16[768,384]{1,0:T(8,128)(2,1)S(1)}, bf16[768,384]{1,0:T(8,128)(2,1)}, u32[]{:S(2)}) copy-start(bf16[768,384]{1,0:T(8,128)(2,1)} %all_gather.13) | copy-start | bytes 1769476
  111.5 23.4 %copy-start.1 = (bf16[2,512,768]{2,1,0:T(8,128)(2,1)S(1)}, bf16[2,512,768]{2,1,0:T(8,128)(2,1)}, u32[]{:S(2)}) copy-start(bf16[2,512,768]{2,1,0:T(8,128)(2,1)} %param.18) | copy-start | bytes 4718596
  111.5 23.4 %copy-start.36 = (f32[768]{0:T(1024)S(1)}, f32[768]{0:T(1024)}, u32[]{:S(2)}) copy-start(f32[768]{0:T(1024)} %param.26) | copy-start | bytes 9220
  115.6 124.9 %all-gather.6.cloned.1.call-start = ((), (), s32[]{:S(2)}) async-start(), calls=%async_computation.4 | async-start | bytes 7520256 | tf_op jit(solution)/shard_map/all_gather | solution.py:63
  116.3 226.6 %all-gather.8.cloned.1.call-start = ((), (), s32[]{:S(2)}) async-start(), calls=%async_computation.5 | async-start | bytes 7520256 | tf_op jit(solution)/shard_map/all_gather | solution.py:64
  116.9 319.4 %all-reduce.13.cloned.1.call-start = ((), (), s32[]{:S(2)}) async-start(), calls=%async_computation.6 | async-start | bytes 6291456 | tf_op jit(solution)/shard_map/psum | solution.py:139
  117.0 143.1 %copy-start.52 = (s32[1,4,2,128]{3,1,2,0:T(4,128)}, s32[1,4,2,128]{3,1,2,0:T(4,128)S(1)}, u32[]{:S(2)}) copy-start(s32[1,4,2,128]{3,1,2,0:T(4,128)S(1)} %copy.128) | copy-start | bytes 12292
  140.9 241.4 %copy-start.12 = (bf16[1024,768]{1,0:T(8,128)(2,1)}, bf16[1024,768]{1,0:T(8,128)(2,1)S(1)}, u32[]{:S(2)}) copy-start(bf16[1024,768]{1,0:T(8,128)(2,1)S(1)} %add_convert_fusion.5) | copy-start | bytes 4718596
  240.5 102.4 %copy-start.15 = (bf16[2,512,768]{2,1,0:T(8,128)(2,1)S(1)}, bf16[2,512,768]{2,1,0:T(8,128)(2,1)}, u32[]{:S(2)}) copy-start(bf16[2,512,768]{2,1,0:T(8,128)(2,1)} %param.31) | copy-start | bytes 4718596
  352.0 20.0 %slice-start = ((s8[7077888]{0:T(1024)(128)(4,1)}), s8[4194304]{0:T(1024)(128)(4,1)S(1)}, s32[]{:S(2)}) async-start(s8[7077888]{0:T(1024)(128)(4,1)} %bitcast.342), calls=%async_computation.12 | async-start | bytes 8388608
  414.7 166.1 %all-reduce.19.cloned.1.call-start = ((), (), s32[]{:S(2)}) async-start(), calls=%async_computation.11 | async-start | bytes 6291456 | tf_op jit(solution)/shard_map/psum | solution.py:112
  487.8 58.4 %copy-start.20 = (bf16[1,1024,384]{2,1,0:T(8,128)(2,1)}, bf16[1,1024,384]{2,1,0:T(8,128)(2,1)S(1)}, u32[]{:S(2)}) copy-start(bf16[1,1024,384]{2,1,0:T(8,128)(2,1)S(1)} %copy.112) | copy-start | bytes 2359300
  497.6 683.9 %all-reduce.17.cloned.1.call-start = ((), (), s32[]{:S(2)}) async-start(), calls=%async_computation.10 | async-start | bytes 47185920
  525.5 20.7 %copy-start.22 = (bf16[1,1024,384]{2,1,0:T(8,128)(2,1)S(1)}, bf16[1,1024,384]{2,1,0:T(8,128)(2,1)}, u32[]{:S(2)}) copy-start(bf16[1,1024,384]{2,1,0:T(8,128)(2,1)} %copy.113) | copy-start | bytes 2359300
  558.1 751.5 %reduce-scatter.3.cloned.1.call-start = ((), (), s32[]{:S(2)}) async-start(), calls=%async_computation.7 | async-start | bytes 1253376 | tf_op jit(solution)/shard_map/reduce_scatter | solution.py:175
  572.9 866.4 %all-reduce.15.cloned.1.call-start = ((), (), s32[]{:S(2)}) async-start(), calls=%async_computation.9 | async-start | bytes 167936 | tf_op jit(solution)/shard_map/psum | solution.py:188
  587.8 1080.3 %reduce-scatter.5.cloned.1.call-start = ((), (), s32[]{:S(2)}) async-start(), calls=%async_computation.8 | async-start | bytes 15040512 | tf_op jit(solution)/shard_map/reduce_scatter | solution.py:176
  (66 other events, 382.0 us)
Sparse Core Ops, SparseCore 0:
  10.7 62.6 all-gather.3
  115.7 19.1 all-reduce.10
  137.9 102.5 all-gather.5
  243.4 99.4 all-gather.7
  414.8 21.3 all-reduce.12
  497.7 24.4 all-reduce.18
  558.2 623.2 all-reduce.16
  1186.9 122.6 reduce-scatter.2
  1317.1 122.1 all-reduce.14
  1445.5 222.5 reduce-scatter.4
where the time goes:
time: 1690 us; the launch traced here: 1680 us
  waiting for transfers between devices  1270 us (75%)
  matrix products  214 us (13%)
  local copies, waits for them, and re-layouts  72.8 us (4%)
  other arithmetic  60.8 us (4%)
  blocking collectives  49.6 us (3%)
    unnamed x11, waiting for transfers between devices  574 us
    reduce_scatter x1, waiting for transfers between devices, body(): lax.psum_scatter(g_up_all, 'dp', scatter_dimension=1, tiled=True)  229 us
    psum x1, waiting for transfers between devices, body(): lax.psum((g_gain, g_lnb, g_qv_full, g_out_bias, g_upb_full, g_down_bias),...  130 us
    reduce_scatter x1, waiting for transfers between devices, body(): lax.psum_scatter(g_out_loc, 'dp', scatter_dimension=0, tiled=True)  124 us
    all_gather x1, waiting for transfers between devices, body(): lax.all_gather(w_up, 'dp', axis=1, tiled=True)  99.6 us
    all_gather x1, waiting for transfers between devices, body(): lax.all_gather(w_down, 'dp', axis=1, tiled=True)  82.8 us
    dot_general x3, matrix products, body(): jnp.dot(a2, up_full[expert], preferred_element_type=f32) + up_b[expert]  55 us
    all_gather x1, blocking collectives, body(): lax.all_gather(w_out, 'dp', axis=0, tiled=True)  49.6 us
  transfers between devices with their start and end apart: 10, of which 9 were waited for; matrix products, arithmetic and copies ran while one was open for 10% of the time, Pallas kernels for 0%

commit v1 on v0

v1 whole, which is shorter than its diff:
```python
import functools
import math

import jax
import jax.numpy as jnp
from jax import lax
from jax.experimental import pallas as pl
from jax.experimental.pallas import tpu as pltpu
from jax.sharding import PartitionSpec as P

HD = 64
EPS = 1e-05
TILE = 256
CHUNKS = 2
VMEM = 58 * 1024 * 1024
LOG2E = math.log2(math.e)
f32 = jnp.float32
bf16 = jnp.bfloat16
ANY = pl.BlockSpec(memory_space=pl.ANY)


def full_spec(shape):
    zeros = (0,) * len(shape)
    return pl.BlockSpec(shape, lambda *_: zeros)


def nt_dot(a, b):
    return lax.dot_general(a, b, (((1,), (1,)), ((), ())), preferred_element_type=f32)


def nn_dot(a, b):
    return lax.dot_general(a, b, (((1,), (0,)), ((), ())), preferred_element_type=f32)


def params(grid_rank):
    return pltpu.CompilerParams(
        dimension_semantics=("arbitrary",) * grid_rank, vmem_limit_bytes=VMEM
    )


def cost(flops, nbytes, trans=0):
    return pl.CostEstimate(flops=int(flops), bytes_accessed=int(nbytes), transcendentals=int(trans))


def place(c_ref, kind, outer, inner, rz):
    ry, rx = (outer, inner) if kind == "a" else (inner, outer)
    return (c_ref[0] ^ rz) * 4 + (c_ref[1] ^ ry) * 2 + (c_ref[2] ^ rx)


def load_pieces(c_ref, jobs, sems):
    copies = []
    for kind, pair, view, target in jobs:
        for outer in range(2):
            for inner in range(2):
                for rz in range(4):
                    rows = place(c_ref, kind, outer, inner, rz)
                    copies.append(
                        pltpu.make_async_copy(
                            view(pair[outer], inner, rz), target(rows), sems.at[len(copies)]
                        )
                    )
    for c in copies:
        c.start()
    return copies


def gelu_parts(u):
    mag = jnp.abs(u)
    t = 1.0 / (1.0 + (0.3275911 * math.sqrt(0.5)) * mag)
    poly = t * (
        0.254829592
        + t * (-0.284496736 + t * (1.421413741 + t * (-1.453152027 + t * 1.061405429)))
    )
    gauss = jnp.exp(-0.5 * u * u)
    half = 0.5 * poly * gauss
    cdf = jnp.where(u >= 0, 1.0 - half, half)
    return u * cdf, cdf + u * gauss * (1.0 / math.sqrt(2.0 * math.pi))


def norm_parts(v):
    mean = jnp.mean(v, axis=-1, keepdims=True)
    cent = v - mean
    var = jnp.mean(cent * cent, axis=-1, keepdims=True)
    rstd = lax.rsqrt(var + EPS)
    return cent * rstd, rstd


def norm_back(d_out, xhat, rstd, gain):
    d_hat = d_out * gain
    m1 = jnp.mean(d_hat, axis=-1, keepdims=True)
    m2 = jnp.mean(d_hat * xhat, axis=-1, keepdims=True)
    return rstd * (d_hat - m1 - xhat * m2)


def attn_fwd_kernel(
    heads, piece, c_ref, x_ref, srow_ref, scol_ref, g_ref, b_ref, pb_ref, a0, a1_, b0, b1_,
    att_ref, qkv_ref, kt_ref, o_ref, ot_ref, lse_ref,
    w_s, wo_s, bias_s, sems,
):
    cols = heads * HD
    pairs = cols // 128
    seq, width = x_ref.shape[1], x_ref.shape[2]

    def into(block, j):
        return w_s.at[pl.ds(pl.multiple_of(block * piece, 16), piece), pl.ds(j * cols, cols)]

    def into_out(block):
        return wo_s.at[pl.ds(pl.multiple_of(block * piece, 16), piece), :]

    @pl.when(pl.program_id(0) == 0)
    def _():
        jobs = [
            ("a", (a0, a1_), lambda r, i, z: r.at[i, z, 0], lambda k: into(k, 0)),
            ("a", (a0, a1_), lambda r, i, z: r.at[i, z, 1], lambda k: into(k, 1)),
            ("b", (b0, b1_), lambda r, i, z: r.at[i, z, 0], lambda k: into(k, 2)),
            ("b", (b0, b1_), lambda r, i, z: r.at[i, z, 1], into_out),
        ]
        for c in load_pieces(c_ref, jobs, sems):
            c.wait()

    xhat, _ = norm_parts(x_ref[0].astype(f32))
    a1 = (xhat * g_ref[...] + b_ref[...]).astype(bf16)
    proj = (nn_dot(a1, w_s[...]) + pb_ref[...]).astype(bf16)
    for j in range(3):
        for p in range(pairs):
            qkv_ref[0, j, p] = proj[:, j * cols + p * 128 : j * cols + (p + 1) * 128]
    for p in range(pairs):
        kt_ref[0, p] = proj[:, cols + p * 128 : cols + (p + 1) * 128].T
    bias_s[...] = jnp.where(scol_ref[0] == srow_ref[0], 0.0, -1e30)
    lane = lax.broadcasted_iota(jnp.int32, (1, 128), 1)
    scale2 = HD ** (-0.5) * LOG2E

    @pl.loop(0, pairs)
    def _(p):
        q_p = qkv_ref[0, 0, p]
        k_p = qkv_ref[0, 1, p]
        v_t = qkv_ref[0, 2, p].T
        for h in range(2):
            keep = (lane < HD) if h == 0 else (lane >= HD)
            q_h = jnp.where(keep, q_p, jnp.zeros_like(q_p))
            s_t = nt_dot(k_p, q_h) + bias_s[...]
            top = jnp.max(s_t, axis=0, keepdims=True)
            e_t = jnp.exp2((s_t - top) * scale2)
            total = jnp.sum(e_t, axis=0, keepdims=True)
            p_t = (e_t * (1.0 / total)).astype(bf16)
            o_t = nn_dot(v_t[h * HD : (h + 1) * HD], p_t)
            ot_ref[0, p, h * HD : (h + 1) * HD] = o_t.astype(bf16)
            lse_ref[0, p, pl.ds(h, 1), :] = top * scale2 + jnp.log2(total)

    for p in range(pairs):
        o_ref[0, :, p * 128 : (p + 1) * 128] = ot_ref[0, p].T
    att_ref[0] = nt_dot(o_ref[0], wo_s[...]).astype(bf16)


def attn_fwd(coords, x, seg_row, seg_col, gain, bias, proj_bias, pa, pb):
    rows, seq, width = x.shape
    cols = proj_bias.shape[-1] // 3
    heads = cols // HD
    pairs = cols // 128
    piece = pa[0].shape[-2]
    row3 = lambda r, *_: (r, 0, 0)
    row4 = lambda r, *_: (r, 0, 0, 0)
    row5 = lambda r, *_: (r, 0, 0, 0, 0)
    outs = [
        ((rows, seq, width), bf16, (1, seq, width), row3),
        ((rows, 3, pairs, seq, 128), bf16, (1, 3, pairs, seq, 128), row5),
        ((rows, pairs, 128, seq), bf16, (1, pairs, 128, seq), row4),
        ((rows, seq, cols), bf16, (1, seq, cols), row3),
        ((rows, pairs, 128, seq), bf16, (1, pairs, 128, seq), row4),
        ((rows, pairs, 2, seq), f32, (1, pairs, 2, seq), row4),
    ]
    return pl.pallas_call(
        functools.partial(attn_fwd_kernel, heads, piece),
        out_shape=[jax.ShapeDtypeStruct(s, d) for s, d, _, _ in outs],
        grid_spec=pltpu.PrefetchScalarGridSpec(
            num_scalar_prefetch=1,
            grid=(rows,),
            in_specs=[
                pl.BlockSpec((1, seq, width), row3),
                pl.BlockSpec((1, 1, seq), row3),
                pl.BlockSpec((1, seq, 1), row3),
                full_spec((1, width)),
                full_spec((1, width)),
                full_spec((1, 3 * cols)),
                ANY, ANY, ANY, ANY,
            ],
            out_specs=[pl.BlockSpec(b, m) for _, _, b, m in outs],
            scratch_shapes=[
                pltpu.VMEM((width, 3 * cols), bf16),
                pltpu.VMEM((width, cols), bf16),
                pltpu.VMEM((seq, seq), f32),
                pltpu.SemaphoreType.DMA((64,)),
            ],
        ),
        compiler_params=params(1),
        cost_estimate=cost(2e10, 1e7, 3e6),
        name="attn_fwd",
    )(coords, x, seg_row, seg_col, gain, bias, proj_bias, *pa, *pb)


def attn_bwd_kernel(
    heads, piece, c_ref, own_ref, recv_ref, x2_ref, dy_ref, x_ref, srow_ref, scol_ref,
    ln_ref, qkv_ref, kt_ref, o_ref, ot_ref, lse_ref, a0, a1_, b0, b1_,
    da1_ref, dx2_ref, ga0_ref, ga1_ref, gb0_ref, gb1_ref, sums_ref, bsum_ref,
    w_s, wo_s, bias_s, dp_s, gw_s, go_s, sems,
):
    cols = heads * HD
    pairs = cols // 128
    step = pl.program_id(0)

    def into(block, j):
        return w_s.at[pl.ds(pl.multiple_of(block * piece, 16), piece), pl.ds(j * cols, cols)]

    def into_out(block):
        return wo_s.at[pl.ds(pl.multiple_of(block * piece, 16), piece), :]

    @pl.when(step == 0)
    def _():
        jobs = [
            ("a", (a0, a1_), lambda r, i, z: r.at[i, z, 0], lambda k: into(k, 0)),
            ("a", (a0, a1_), lambda r, i, z: r.at[i, z, 1], lambda k: into(k, 1)),
            ("b", (b0, b1_), lambda r, i, z: r.at[i, z, 0], lambda k: into(k, 2)),
            ("b", (b0, b1_), lambda r, i, z: r.at[i, z, 1], into_out),
        ]
        for c in load_pieces(c_ref, jobs, sems):
            c.wait()
        gw_s[...] = jnp.zeros_like(gw_s)
        go_s[...] = jnp.zeros_like(go_s)
        sums_ref[...] = jnp.zeros_like(sums_ref)
        bsum_ref[...] = jnp.zeros_like(bsum_ref)

    da2 = own_ref[0].astype(f32) + recv_ref[0].astype(f32)
    xhat2, rstd2 = norm_parts(x2_ref[0])
    dx2 = dy_ref[0].astype(f32) + norm_back(da2, xhat2, rstd2, ln_ref[2:3])
    dx2_ref[0] = dx2
    sums_ref[0:1] += jnp.sum(da2 * xhat2, axis=0, keepdims=True)
    sums_ref[1:2] += jnp.sum(da2, axis=0, keepdims=True)
    sums_ref[2:3] += jnp.sum(dx2, axis=0, keepdims=True)
    dxr = dx2.astype(bf16)
    do = nn_dot(dxr, wo_s[...]).astype(bf16)
    go_s[...] += nn_dot(dxr.T, o_ref[0])
    bias_s[...] = jnp.where(scol_ref[0] == srow_ref[0], 0.0, -1e30)
    lane = lax.broadcasted_iota(jnp.int32, (1, 128), 1)
    scale = HD ** (-0.5)
    scale2 = scale * LOG2E

    for p in range(pairs):
        q_p = qkv_ref[0, 0, p]
        k_p = qkv_ref[0, 1, p]
        v_p = qkv_ref[0, 2, p]
        do_p = do[:, p * 128 : (p + 1) * 128]
        prod = do_p.T.astype(f32) * ot_ref[0, p].astype(f32)
        dv = None
        for h in range(2):
            keep = (lane < HD) if h == 0 else (lane >= HD)
            q_h = jnp.where(keep, q_p, jnp.zeros_like(q_p))
            do_h = jnp.where(keep, do_p, jnp.zeros_like(do_p))
            row = jnp.sum(prod[h * HD : (h + 1) * HD], axis=0, keepdims=True)
            s_t = nt_dot(k_p, q_h)
            p_t = jnp.exp2(s_t * scale2 + (bias_s[...] - lse_ref[0, p, h : h + 1, :]))
            d_t = nt_dot(v_p, do_h)
            ds_t = (p_t * (d_t - row)).astype(bf16)
            dv_h = nn_dot(p_t.astype(bf16), do_h)
            dk_h = nn_dot(ds_t, q_h)
            dq_h = nn_dot(kt_ref[0, p, h * HD : (h + 1) * HD], ds_t)
            dv, dk, dq = (dv_h, dk_h, [dq_h]) if dv is None else (dv + dv_h, dk + dk_h, dq + [dq_h])
        dq = (jnp.concatenate(dq, axis=0) * scale).astype(bf16).T
        dp_s[:, p * 128 : (p + 1) * 128] = dq
        dp_s[:, cols + p * 128 : cols + (p + 1) * 128] = (dk * scale).astype(bf16)
        dp_s[:, 2 * cols + p * 128 : 2 * cols + (p + 1) * 128] = dv.astype(bf16)

    dproj = dp_s[...]
    da1_ref[0] = nt_dot(dproj, w_s[...]).astype(bf16)
    bsum_ref[...] += jnp.sum(dproj.astype(f32), axis=0, keepdims=True)
    xhat1, _ = norm_parts(x_ref[0].astype(f32))
    a1 = (xhat1 * ln_ref[0:1] + ln_ref[1:2]).astype(bf16)
    gw_s[...] += nn_dot(a1.T, dproj)

    @pl.when(step == pl.num_programs(0) - 1)
    def _():
        for outer in range(2):
            for inner in range(2):
                for rz in range(4):
                    ra = pl.ds(pl.multiple_of(place(c_ref, "a", outer, inner, rz) * piece, 16), piece)
                    rb = pl.ds(pl.multiple_of(place(c_ref, "b", outer, inner, rz) * piece, 16), piece)
                    ga, gb = ((ga0_ref, gb0_ref), (ga1_ref, gb1_ref))[outer]
                    ga[inner, rz, 0] = gw_s[ra, :cols].astype(bf16)
                    ga[inner, rz, 1] = gw_s[ra, cols : 2 * cols].astype(bf16)
                    gb[inner, rz, 0] = gw_s[rb, 2 * cols :].astype(bf16)
                    gb[inner, rz, 1] = go_s[rb, :].astype(bf16)


def attn_bwd(coords, own, recv, x2, dy, x, seg_row, seg_col, ln, saved, pa, pb):
    rows, seq, width = x.shape
    qkv, kt, o, ot, lse = saved
    cols = o.shape[-1]
    heads = cols // HD
    pairs = cols // 128
    piece = pa[0].shape[-2]
    row3 = lambda r, *_: (r, 0, 0)
    row4 = lambda r, *_: (r, 0, 0, 0)
    row5 = lambda r, *_: (r, 0, 0, 0, 0)
    tok = pl.BlockSpec((1, seq, width), row3)
    gshape = pa[0].shape
    return pl.pallas_call(
        functools.partial(attn_bwd_kernel, heads, piece),
        out_shape=[
            jax.ShapeDtypeStruct((rows, seq, width), bf16),
            jax.ShapeDtypeStruct((rows, seq, width), f32),
            *[jax.ShapeDtypeStruct(gshape, bf16)] * 4,
            jax.ShapeDtypeStruct((8, width), f32),
            jax.ShapeDtypeStruct((1, 3 * cols), f32),
        ],
        grid_spec=pltpu.PrefetchScalarGridSpec(
            num_scalar_prefetch=1,
            grid=(rows,),
            in_specs=[
                tok, tok, tok, tok, tok,
                pl.BlockSpec((1, 1, seq), row3),
                pl.BlockSpec((1, seq, 1), row3),
                full_spec((4, width)),
                pl.BlockSpec((1, 3, pairs, seq, 128), row5),
                pl.BlockSpec((1, pairs, 128, seq), row4),
                pl.BlockSpec((1, seq, cols), row3),
                pl.BlockSpec((1, pairs, 128, seq), row4),
                pl.BlockSpec((1, pairs, 2, seq), row4),
                ANY, ANY, ANY, ANY,
            ],
            out_specs=[
                tok, tok,
                *[full_spec(gshape)] * 4,
                full_spec((8, width)),
                full_spec((1, 3 * cols)),
            ],
            scratch_shapes=[
                pltpu.VMEM((width, 3 * cols), bf16),
                pltpu.VMEM((width, cols), bf16),
                pltpu.VMEM((seq, seq), f32),
                pltpu.VMEM((seq, 3 * cols), bf16),
                pltpu.VMEM((width, 3 * cols), f32),
                pltpu.VMEM((width, cols), f32),
                pltpu.SemaphoreType.DMA((64,)),
            ],
        ),
        compiler_params=params(1),
        cost_estimate=cost(4e10, 2e7, 3e6),
        name="attn_bwd",
    )(coords, own, recv, x2, dy, x, seg_row, seg_col, ln, qkv, kt, o, ot, lse, *pa, *pb)


def sort_kernel(pos_row, pos_col, v_ref, vs_ref, vst_ref, vt_s):
    _sort_tile(pos_row, pos_col, v_ref, vs_ref, vst_ref, vt_s)


def _sort_tile(pos_row, pos_col, v_ref, vs_ref, vst_ref, vt_s):
    i = pl.program_id(0)
    tokens = v_ref.shape[0]

    @pl.when(i == 0)
    def _():
        vt_s[...] = v_ref[...].T

    slot_c = lax.broadcasted_iota(jnp.int32, (TILE, tokens), 0) + i * TILE
    pick = (slot_c == pos_row[...]).astype(f32).astype(bf16)
    vs_ref[...] = nn_dot(pick, v_ref[...]).astype(bf16)
    slot_r = lax.broadcasted_iota(jnp.int32, (tokens, TILE), 1) + i * TILE
    pick_t = (slot_r == pos_col[...]).astype(f32).astype(bf16)
    vst_ref[...] = nn_dot(vt_s[...], pick_t).astype(bf16)


def sort_tokens(pos_row, pos_col, v, tiles):
    tokens, width = v.shape
    return pl.pallas_call(
        sort_kernel,
        out_shape=[
            jax.ShapeDtypeStruct((tiles * TILE, width), bf16),
            jax.ShapeDtypeStruct((width, tiles * TILE), bf16),
        ],
        grid=(tiles,),
        in_specs=[full_spec((1, tokens)), full_spec((tokens, 1)), full_spec((tokens, width))],
        out_specs=[
            pl.BlockSpec((TILE, width), lambda i: (i, 0)),
            pl.BlockSpec((width, TILE), lambda i: (0, i)),
        ],
        scratch_shapes=[pltpu.VMEM((width, tokens), bf16)],
        compiler_params=params(1),
        cost_estimate=cost(4 * tiles * TILE * tokens * width, 1e7),
        name="sort_tokens",
    )(pos_row, pos_col, v)


def mid_kernel(pos_row, pos_col, x_ref, own_ref, recv_ref, vec_ref, x2_ref, vs_ref, vst_ref, a2_s, vt_s):
    @pl.when(pl.program_id(0) == 0)
    def _():
        tokens = x_ref.shape[0]
        block = math.gcd(tokens, 256)
        for start in range(0, tokens, block):
            rows = slice(start, start + block)
            x2 = (
                x_ref[rows].astype(f32)
                + (own_ref[rows].astype(f32) + recv_ref[rows].astype(f32))
                + vec_ref[0:1]
            )
            x2_ref[rows] = x2
            xhat, _ = norm_parts(x2)
            a2_s[rows] = (xhat * vec_ref[1:2] + vec_ref[2:3]).astype(bf16)

    _sort_tile(pos_row, pos_col, a2_s, vs_ref, vst_ref, vt_s)


def mid(pos_row, pos_col, x, own, recv, vec, tiles):
    tokens, width = x.shape
    whole = full_spec((tokens, width))
    return pl.pallas_call(
        mid_kernel,
        out_shape=[
            jax.ShapeDtypeStruct((tokens, width), f32),
            jax.ShapeDtypeStruct((tiles * TILE, width), bf16),
            jax.ShapeDtypeStruct((width, tiles * TILE), bf16),
        ],
        grid=(tiles,),
        in_specs=[
            full_spec((1, tokens)), full_spec((tokens, 1)), whole, whole, whole, full_spec((4, width)),
        ],
        out_specs=[
            whole,
            pl.BlockSpec((TILE, width), lambda i: (i, 0)),
            pl.BlockSpec((width, TILE), lambda i: (0, i)),
        ],
        scratch_shapes=[pltpu.VMEM((tokens, width), bf16), pltpu.VMEM((width, tokens), bf16)],
        compiler_params=params(1),
        cost_estimate=cost(4 * tiles * TILE * tokens * width, 2e7),
        name="norm_sort",
    )(pos_row, pos_col, x, own, recv, vec)


def unsort_kernel(pos_col, vs_ref, out_ref):
    slots = vs_ref.shape[0]
    slot_r = lax.broadcasted_iota(jnp.int32, (TILE, slots), 1)
    pick = (slot_r == pos_col[...]).astype(f32).astype(bf16)
    out_ref[...] = nn_dot(pick, vs_ref[...]).astype(bf16)


def unsort_tokens(pos_col, vs):
    slots, width = vs.shape
    tokens = pos_col.shape[0]
    return pl.pallas_call(
        unsort_kernel,
        out_shape=jax.ShapeDtypeStruct((tokens, width), bf16),
        grid=(tokens // TILE,),
        in_specs=[pl.BlockSpec((TILE, 1), lambda i: (i, 0)), full_spec((slots, width))],
        out_specs=pl.BlockSpec((TILE, width), lambda i: (i, 0)),
        compiler_params=params(1),
        cost_estimate=cost(2 * slots * tokens * width, 1e7),
        name="unsort_tokens",
    )(pos_col, vs)


def ffn_kernel(first, last, piece, c_ref, te_ref, n_ref, *refs):
    xs_ref, xst_ref, dys_ref, dyst_ref, ub_ref, a0, a1_, b0, b1_, *rest = refs
    if not first:
        zin_ref, din_ref, *rest = rest
    (z_ref, da_ref, ga0_ref, ga1_ref, gb0_ref, gb1_ref, gub_ref,
     wu_s, wd_s, gu_s, gd_s, sems) = rest
    experts = wu_s.shape[0]
    i = pl.program_id(0)

    @pl.when(i == 0)
    def _():
        jobs = [
            ("a", (a0, a1_), lambda r, k, z: r.at[k, z],
             lambda k: wu_s.at[:, pl.ds(pl.multiple_of(k * piece, 16), piece), :]),
            ("b", (b0, b1_), lambda r, k, z: r.at[k, z],
             lambda k: wd_s.at[:, pl.ds(pl.multiple_of(k * piece, 16), piece), :]),
        ]
        copies = load_pieces(c_ref, jobs, sems)
        gu_s[...] = jnp.zeros_like(gu_s)
        gd_s[...] = jnp.zeros_like(gd_s)
        gub_ref[...] = jnp.zeros_like(gub_ref)
        for c in copies:
            c.wait()

    @pl.when(i < n_ref[0])
    def _():
        e = te_ref[i]
        dy = dys_ref[...]
        u = nn_dot(xs_ref[...], wu_s[e]) + ub_ref[e]
        act, slope = gelu_parts(u)
        act = act.astype(bf16)
        du = nn_dot(dy, wd_s[e]) * slope
        du = du.astype(bf16)
        z = nt_dot(act, wd_s[e])
        da = nt_dot(du, wu_s[e])
        if not first:
            z = z + zin_ref[...]
            da = da + din_ref[...]
        z_ref[...] = z.astype(z_ref.dtype)
        da_ref[...] = da.astype(da_ref.dtype)
        gd_s[e] += nn_dot(dyst_ref[...], act)
        gu_s[e] += nn_dot(xst_ref[...], du)
        gub_ref[e] += jnp.sum(du.astype(f32), axis=0, keepdims=True)

    @pl.when(i >= n_ref[0])
    def _():
        z_ref[...] = jnp.zeros_like(z_ref)
        da_ref[...] = jnp.zeros_like(da_ref)

    @pl.when(i == pl.num_programs(0) - 1)
    def _():
        for outer in range(2):
            for inner in range(2):
                for rz in range(4):
                    ra = pl.ds(pl.multiple_of(place(c_ref, "a", outer, inner, rz) * piece, 16), piece)
                    rb = pl.ds(pl.multiple_of(place(c_ref, "b", outer, inner, rz) * piece, 16), piece)
                    ga, gb = ((ga0_ref, gb0_ref), (ga1_ref, gb1_ref))[outer]
                    for e in range(experts):
                        ga[inner, rz, e] = gu_s[e, ra, :].astype(bf16)
                        gb[inner, rz, e] = gd_s[e, rb, :].astype(bf16)


def ffn(first, last, coords, tile_expert, used, xs, xst, dys, dyst, up_b, pa, pb, carry):
    slots, width = xs.shape
    tiles = slots // TILE
    gshape = pa[0].shape
    experts, piece, hid = gshape[2:]
    tile = pl.BlockSpec((TILE, width), lambda i, *_: (i, 0))
    tile_t = pl.BlockSpec((width, TILE), lambda i, *_: (0, i))
    kept = bf16 if last else f32
    return pl.pallas_call(
        functools.partial(ffn_kernel, first, last, piece),
        out_shape=[
            jax.ShapeDtypeStruct((slots, width), kept),
            jax.ShapeDtypeStruct((slots, width), kept),
            *[jax.ShapeDtypeStruct(gshape, bf16)] * 4,
            jax.ShapeDtypeStruct((experts, 1, hid), f32),
        ],
        grid_spec=pltpu.PrefetchScalarGridSpec(
            num_scalar_prefetch=3,
            grid=(tiles,),
            in_specs=[
                tile, tile_t, tile, tile_t, full_spec((experts, 1, hid)), ANY, ANY, ANY, ANY,
                *([] if first else [tile, tile]),
            ],
            out_specs=[tile, tile, *[full_spec(gshape)] * 4, full_spec((experts, 1, hid))],
            scratch_shapes=[
                pltpu.VMEM((experts, width, hid), bf16),
                pltpu.VMEM((experts, width, hid), bf16),
                pltpu.VMEM((experts, width, hid), f32),
                pltpu.VMEM((experts, width, hid), f32),
                pltpu.SemaphoreType.DMA((32,)),
            ],
        ),
        compiler_params=params(1),
        cost_estimate=cost(12 * slots * width * hid * 1.5, 4e7, 2 * slots * hid),
        name="ffn",
    )(coords, tile_expert, used, xs, xst, dys, dyst, up_b, *pa, *pb, *carry)


def input_grad_kernel(own_ref, recv_ref, x_ref, dx2_ref, gain_ref, out_ref, sums_ref):
    @pl.when(pl.program_id(0) == 0)
    def _():
        sums_ref[...] = jnp.zeros_like(sums_ref)

    da1 = own_ref[...].astype(f32) + recv_ref[...].astype(f32)
    xhat, rstd = norm_parts(x_ref[...].astype(f32))
    out_ref[...] = dx2_ref[...] + norm_back(da1, xhat, rstd, gain_ref[...])
    sums_ref[0:1] += jnp.sum(da1 * xhat, axis=0, keepdims=True)
    sums_ref[1:2] += jnp.sum(da1, axis=0, keepdims=True)


def input_grad(own, recv, x, dx2, gain):
    tokens, width = x.shape
    tile = pl.BlockSpec((TILE, width), lambda i: (i, 0))
    return pl.pallas_call(
        input_grad_kernel,
        out_shape=[
            jax.ShapeDtypeStruct((tokens, width), f32),
            jax.ShapeDtypeStruct((8, width), f32),
        ],
        grid=(tokens // TILE,),
        in_specs=[tile, tile, tile, tile, full_spec((1, width))],
        out_specs=[tile, full_spec((8, width))],
        compiler_params=params(1),
        cost_estimate=cost(2e7, 1.3e7),
        name="input_grad",
    )(own, recv, x, dx2, gain)


def flip(x, mask, size):
    return lax.ppermute(x, "dp", [(i, i ^ mask) for i in range(size)])


def swap(x, parts):
    if parts == 2:
        return lax.ppermute(x, "mp", [(0, 1), (1, 0)])
    return (lax.psum(x.astype(f32), "mp") - x.astype(f32)).astype(x.dtype)


def gather_staged(a, b, size):
    both = jnp.stack([a, b])
    blocks = [both] + [flip(both, 4 * rz, size) for rz in (1, 2, 3)]
    a0 = jnp.stack([v[0] for v in blocks])
    b0 = jnp.stack([v[1] for v in blocks])
    a0 = jnp.stack([a0, flip(a0, 1, size)])
    b0 = jnp.stack([b0, flip(b0, 2, size)])
    return (a0, flip(a0, 2, size)), (b0, flip(b0, 1, size))


def scatter_staged(ga, gb, size):
    ra = ga[0].astype(f32) + flip(ga[1], 2, size).astype(f32)
    rb = gb[0].astype(f32) + flip(gb[1], 1, size).astype(f32)
    sa = ra[0] + flip(ra[1].astype(bf16), 1, size).astype(f32)
    sb = rb[0] + flip(rb[1].astype(bf16), 2, size).astype(f32)
    own = jnp.stack([sa[0], sb[0]])
    for rz in (1, 2, 3):
        sent = jnp.stack([sa[rz].astype(bf16), sb[rz].astype(bf16)])
        own = own + flip(sent, 4 * rz, size).astype(f32)
    return own[0], own[1]


def gather_plain(w):
    full = lax.all_gather(w, "dp", axis=1, tiled=True)
    n, rows, cols = full.shape
    return full.reshape(n, 16, rows // 16, cols).swapaxes(0, 1)


def gather_pieces(a, b, size, staged):
    if staged:
        return gather_staged(a, b, size)
    blocks = [gather_plain(v) for v in (a, b)]
    blocks = [v.reshape((4, 2, 2) + v.shape[1:]) for v in blocks]
    fa = jnp.moveaxis(blocks[0], 0, 2)
    fb = jnp.swapaxes(jnp.moveaxis(blocks[1], 0, 2), 0, 1)
    return (fa[0], fa[1]), (fb[0], fb[1])


def scatter_pieces(ga, gb, size, staged):
    if staged:
        return scatter_staged(ga, gb, size)
    fa = jnp.moveaxis(jnp.stack(ga), 2, 0)
    fb = jnp.moveaxis(jnp.swapaxes(jnp.stack(gb), 0, 1), 2, 0)
    outs = []
    for v in (fa, fb):
        v = v.reshape((16,) + v.shape[3:]).swapaxes(0, 1)
        v = v.reshape(v.shape[0], -1, v.shape[-1]).astype(f32)
        outs.append(lax.psum_scatter(v, "dp", scatter_dimension=1, tiled=True))
    return outs


def sum_small(v, size, parts):
    if size & (size - 1) or parts != 2:
        return lax.psum(v, ("dp", "mp"))
    v = v + swap(v, parts)
    mask = 1
    while mask < size:
        v = v + flip(v, mask, size)
        mask *= 2
    return v


def body(
    layer_input, segments, modality, ln_gain, ln_bias, w_qkv, qv_bias, w_out, out_bias,
    w_up, up_bias, w_down, down_bias, cotangent,
):
    part = lax.axis_index("mp")
    parts = lax.axis_size("mp")
    size = lax.axis_size("dp")
    me = lax.axis_index("dp")
    rows, seq, width = layer_input.shape
    tokens = rows * seq
    cols = w_qkv.shape[-1]
    hid = w_up.shape[-1]
    experts = w_up.shape[0]
    staged = size == 16
    if staged:
        coords = jnp.stack([me // 4, (me // 2) % 2, me % 2]).astype(jnp.int32)
    else:
        coords = jnp.zeros((3,), jnp.int32)

    pa, pb = gather_pieces(w_qkv[:2], jnp.stack([w_qkv[2], w_out]), size, staged)
    hc = hid // CHUNKS
    chunks = [
        gather_pieces(w_up[:, :, c * hc : (c + 1) * hc], w_down[:, :, c * hc : (c + 1) * hc], size, staged)
        for c in range(CHUNKS)
    ]

    doc_ids = jnp.arange(modality.shape[1], dtype=jnp.int32)
    match = segments[:, :, None] == doc_ids
    mods = jnp.sum(jnp.where(match, modality[:, None, :], 0), axis=-1).reshape(tokens)
    hot_i = (mods[:, None] == jnp.arange(experts, dtype=jnp.int32)).astype(jnp.int32)
    hot = hot_i.astype(bf16)
    ids = jnp.arange(tokens, dtype=jnp.int32)
    lower = (ids[:, None] > ids[None, :]).astype(bf16)
    before = jnp.dot(lower, hot, preferred_element_type=f32).astype(jnp.int32)
    counts = jnp.sum(hot_i, axis=0)
    need = (counts + TILE - 1) // TILE
    kinds = jnp.arange(experts, dtype=jnp.int32)
    ends = jnp.sum(jnp.where(kinds[:, None] >= kinds[None, :], need[None, :], 0), axis=1)
    begins = ends - need
    pos = jnp.sum(hot_i * (before + begins[None, :] * TILE), axis=1)
    pos_row, pos_col = pos.reshape(1, tokens), pos.reshape(tokens, 1)
    tiles = (tokens + experts * (TILE - 1)) // TILE
    tile_ids = jnp.arange(tiles, dtype=jnp.int32)
    tile_expert = jnp.minimum(
        jnp.sum((tile_ids[:, None] >= ends[None, :]).astype(jnp.int32), axis=1), experts - 1
    )
    used = ends[-1:].astype(jnp.int32)

    dy = cotangent.reshape(tokens, width)
    dys, dyst = sort_tokens(pos_row, pos_col, dy, tiles)
    g_down_bias = lax.dot_general(hot, dy, (((0,), (0,)), ((), ())), preferred_element_type=f32)

    col_start = part * cols
    q_b = lax.dynamic_slice_in_dim(qv_bias[0], col_start, cols)
    v_b = lax.dynamic_slice_in_dim(qv_bias[1], col_start, cols)
    proj_bias = jnp.concatenate([q_b, jnp.zeros_like(q_b), v_b]).reshape(1, 3 * cols)
    seg_row, seg_col = segments.reshape(rows, 1, seq), segments.reshape(rows, seq, 1)
    att, *saved = attn_fwd(
        coords, layer_input, seg_row, seg_col, ln_gain[0:1], ln_bias[0:1], proj_bias, pa, pb
    )
    att = att.reshape(tokens, width)
    vec = jnp.concatenate([out_bias[None], ln_gain[1:2], ln_bias[1:2], out_bias[None]])
    x_tok = layer_input.reshape(tokens, width)
    x2, xs, xst = mid(pos_row, pos_col, x_tok, att, swap(att, parts), vec, tiles)

    up_b = lax.dynamic_slice_in_dim(up_bias, part * hid, hid, 1)
    carry = ()
    g_ffn = []
    g_upb = []
    for c in range(CHUNKS):
        ca, cb = chunks[c]
        ub = up_b[:, None, c * hc : (c + 1) * hc]
        zs, das, ga0, ga1, gb0, gb1, gub = ffn(
            c == 0, c == CHUNKS - 1, coords, tile_expert, used, xs, xst, dys, dyst, ub, ca, cb, carry
        )
        carry = (zs, das)
        g_ffn.append(scatter_pieces((ga0, ga1), (gb0, gb1), size, staged))
        g_upb.append(gub[:, 0])
    g_up = jnp.concatenate([g[0] for g in g_ffn], axis=-1)
    g_down = jnp.concatenate([g[1] for g in g_ffn], axis=-1)
    g_upb = jnp.concatenate(g_upb, axis=-1)
    da2 = unsort_tokens(pos_col, das)
    da2_other = swap(da2, parts)

    shape3 = (rows, seq, width)
    ln = jnp.concatenate([ln_gain[0:1], ln_bias[0:1], ln_gain[1:2], ln_bias[1:2]])
    da1, dx2, ga0, ga1, gb0, gb1, sums2, bsum = attn_bwd(
        coords, da2.reshape(shape3), da2_other.reshape(shape3), x2.reshape(shape3), cotangent,
        layer_input, seg_row, seg_col, ln, saved, pa, pb,
    )
    g_qk, g_vo = scatter_pieces((ga0, ga1), (gb0, gb1), size, staged)
    da1 = da1.reshape(tokens, width)
    grad_input, sums1 = input_grad(
        da1, swap(da1, parts), x_tok, dx2.reshape(tokens, width), ln_gain[0:1]
    )

    z = unsort_tokens(pos_col, zs)
    z_sum = z.astype(f32) + swap(z, parts).astype(f32)
    bias_of = jnp.zeros((tokens, width), f32)
    for e in range(experts):
        bias_of = jnp.where(mods[:, None] == e, down_bias[e][None], bias_of)
    layer_output = (x2 + (z_sum + bias_of)).astype(bf16)

    bsum = bsum.reshape(3, cols)
    g_qv = lax.dynamic_update_slice(
        jnp.zeros((2, width), f32), jnp.stack([bsum[0], bsum[2]]), (jnp.int32(0), col_start)
    )
    g_upb_full = lax.dynamic_update_slice(
        jnp.zeros((experts, up_bias.shape[1]), f32), g_upb, (jnp.int32(0), part * hid)
    )
    once = jnp.concatenate([sums1[0:2], sums2[0:3], g_down_bias]) / parts
    small = jnp.concatenate([once, g_qv, g_upb_full.reshape(-1, width)])
    small = sum_small(small, size, parts)
    g_gain = jnp.stack([small[0], small[2]])
    g_lnb = jnp.stack([small[1], small[3]])
    return (
        layer_output.reshape(shape3),
        grad_input.reshape(shape3),
        g_gain,
        g_lnb,
        jnp.concatenate([g_qk, g_vo[:1]]),
        small[5 + experts : 7 + experts],
        g_vo[1],
        small[4],
        g_up,
        small[7 + experts :].reshape(experts, up_bias.shape[1]),
        g_down,
        small[5 : 5 + experts],
    )


def solution(mesh):
    tok = P("dp", None, None)
    rep = P()
    wide = P(None, "dp", "mp")
    in_specs = (
        tok, P("dp", None), P("dp", None), rep, rep, wide, rep, P("dp", "mp"), rep, wide, rep,
        wide, rep, tok,
    )
    out_specs = (
        tok, tok, rep, rep, wide, rep, P("dp", "mp"), rep, wide, rep, wide, rep,
    )
    return jax.shard_map(body, mesh=mesh, in_specs=in_specs, out_specs=out_specs, check_vma=False)
```

time: 1690 us -> 501 us (0.30)
  waiting for transfers between devices: 1270 us -> 236 us
  matrix products: 214 us -> 0.79 us
  Pallas kernels: 0 us -> 137 us
  starting transfers between devices: 0.81 us -> 74.9 us
  local copies, waits for them, and re-layouts: 72.8 us -> 16.6 us
  blocking collectives: 49.6 us -> 0 us
  other arithmetic: 60.8 us -> 30.9 us
    unnamed x11 -> x0, waiting for transfers between devices: 574 us -> none
    reduce_scatter x2 -> x0, waiting for transfers between devices: 352 us -> none  [the longest x1 229 us: body(): lax.psum_scatter(g_up_all, 'dp', scatter_dimension=1, tiled=True)]
    ppermute x0 -> x51, waiting for transfers between devices: none -> 236 us  [the longest x46 236 us: flip(): return lax.ppermute(x, 'dp', [(i, i ^ mask) for i in range(size)])]
    all_gather x3 -> x0, waiting for transfers between devices: 189 us -> none  [the longest x1 99.6 us: body(): lax.all_gather(w_up, 'dp', axis=1, tiled=True)]
    dot_general x36 -> x2, matrix products: 189 us -> 0.79 us  [the longest x1 0.48 us: body(): before = jnp.dot(lower, hot, preferred_element_type=f32).astype(jnp.int32)]
    psum x4 -> x0, waiting for transfers between devices: 153 us -> none  [the longest x1 130 us: body(): lax.psum((g_gain, g_lnb, g_qv_full, g_out_bias, g_upb_full, g_down_bias),...]
    pallas_call x0 -> x9, Pallas kernels: none -> 137 us  [the longest x2 51.7 us: ffn(): pl.pallas_call(functools.partial(ffn_kernel, first, last, piece), out_sha...]
    ppermute x0 -> x51, starting transfers between devices: none -> 74.9 us  [the longest x46 74.7 us: flip(): return lax.ppermute(x, 'dp', [(i, i ^ mask) for i in range(size)])]
  transfers between devices with their start and end apart: 10 -> 51, of which waited for: 9 -> 19; matrix products, arithmetic and copies ran while one was open for 10% -> 8% of each run, Pallas kernels for 0% -> 21%
where the time goes in v1:
time: 501 us; the launch traced here: 498 us
  waiting for transfers between devices  236 us (47%)
  Pallas kernels  137 us (27%)
  starting transfers between devices  74.9 us (15%)
  other arithmetic  30.9 us (6%)
  local copies, waits for them, and re-layouts  16.6 us (3%)
    ppermute x46, waiting for transfers between devices, flip(): return lax.ppermute(x, 'dp', [(i, i ^ mask) for i in range(size)])  236 us
    ppermute x46, starting transfers between devices, flip(): return lax.ppermute(x, 'dp', [(i, i ^ mask) for i in range(size)])  74.7 us
    pallas_call x2, Pallas kernels, ffn(): pl.pallas_call(functools.partial(ffn_kernel, first, last, piece), out_sha...  51.7 us
    pallas_call x1, Pallas kernels, attn_bwd(): pl.pallas_call(functools.partial(attn_bwd_kernel, heads, piece), out_shap...  27.7 us
    pallas_call x1, Pallas kernels, attn_fwd(): pl.pallas_call(functools.partial(attn_fwd_kernel, heads, piece), out_shap...  17.6 us
    pallas_call x2, Pallas kernels, unsort_tokens(): pl.pallas_call(unsort_kernel, out_shape=jax.ShapeDtypeStruct((tokens, wid...  12.7 us
    pallas_call x1, Pallas kernels, mid(): pl.pallas_call(mid_kernel, out_shape=[jax.ShapeDtypeStruct((tokens, width...  11.6 us
  transfers between devices with their start and end apart: 51, of which 19 were waited for; matrix products, arithmetic and copies ran while one was open for 8% of the time, Pallas kernels for 21%

profile of v1, /device:TPU:0, one launch (start us, length us, event | category | flops | bytes accessed | tf_op | source)
XLA Modules:
  0.0 497.8 jit_solution(14141348451489594568)
XLA Ops:
  21.7 11.1 %collective-permute-done.15 = bf16[2,3,48,768]{3,2,1,0:T(8,128)(2,1)S(1)} collective-permute-done((bf16[2,3,48,768]{3,2,1,0:T(8,128)(2,1)S(1)}, bf16[2,3,48,768]{3,2,1,0:T(8,128)(2,1)S(1)}, u32[]{:S(2)}, u32[]{:S(2)}) %collective-permute-start.15) | collective-permute-done | bytes 442400 | tf_op jit(solution)/shard_map/ppermute | solution.py:590
  34.9 16.3 %collective-permute-done.16 = bf16[2,3,48,768]{3,2,1,0:T(8,128)(2,1)S(1)} collective-permute-done((bf16[2,3,48,768]{3,2,1,0:T(8,128)(2,1)S(1)}, bf16[2,3,48,768]{3,2,1,0:T(8,128)(2,1)S(1)}, u32[]{:S(2)}, u32[]{:S(2)}) %collective-permute-start.16) | collective-permute-done | bytes 442400 | tf_op jit(solution)/shard_map/ppermute | solution.py:590
  59.6 29.5 %collective-permute-done.9 = bf16[2,3,48,768]{3,2,1,0:T(8,128)(2,1)S(1)} collective-permute-done((bf16[2,3,48,768]{3,2,1,0:T(8,128)(2,1)S(1)}, bf16[2,3,48,768]{3,2,1,0:T(8,128)(2,1)S(1)}, u32[]{:S(2)}, u32[]{:S(2)}) %collective-permute-start.9) | collective-permute-done | bytes 442400 | tf_op jit(solution)/shard_map/ppermute | solution.py:590
  91.6 17.6 %attn_fwd.1 = (bf16[2,512,768]{2,1,0:T(8,128)(2,1)}, bf16[2,3,3,512,128]{4,3,2,1,0:T(8,128)(2,1)}, bf16[2,3,128,512]{3,2,1,0:T(8,128)(2,1)}, bf16[2,512,384]{2,1...) custom-call(s32[3]{0:T(128)} %pad_add_fusion.c_ref, bf16[2,512,768]{2,1,0:T(8,128)(2,1)} %x_ref.3, ...), custom_call_target="tpu_custom_call" | custom-call | flops 20000000000 | bytes 10000000 | tf_op jit(solution)/shard_map/attn_fwd/pallas_call | solution.py:172
  121.7 9.0 %sort_tokens.1 = (bf16[1536,768]{1,0:T(8,128)(2,1)}, bf16[768,1536]{1,0:T(8,128)(2,1)}) custom-call(s32[1,1024]{1,0:T(1,128)} %bitcast.138, s32[1024,1]{1,0:T(8,128)} %copy.35.pos_col, bf16[1024,768]{1,0:T(8,128)(2,1)} %bitcast.117), custom_call_target="tpu_custom_call" | custom-call | flops 4831838208 | bytes 10000000 | tf_op jit(solution)/shard_map/sort_tokens/pallas_call | solution.py:373
  130.7 41.8 %collective-permute-done.11 = bf16[4,3,48,768]{3,2,1,0:T(8,128)(2,1)S(1)} collective-permute-done((bf16[4,3,48,768]{3,2,1,0:T(8,128)(2,1)}, bf16[4,3,48,768]{3,2,1,0:T(8,128)(2,1)S(1)}, u32[]{:S(2)}, u32[]{:S(2)}) %collective-permute-start.11) | collective-permute-done | bytes 884768 | tf_op jit(solution)/shard_map/ppermute | solution.py:590
  177.2 11.6 %norm_sort.1 = (f32[1024,768]{1,0:T(8,128)}, bf16[1536,768]{1,0:T(8,128)(2,1)}, bf16[768,1536]{1,0:T(8,128)(2,1)}) custom-call(s32[1,1024]{1,0:T(1,128)} %bitcast.139, s32[1024,1]{1,0:T(8,128)} %copy.35.pos_col, bf16[1024,768]{1,0:T(8,128)(2,1)} %bitcast.119, bf16[1024,768]{1,0:T(8,128)(2,1)} %bitcast.142, ...), custom_call_target="tpu_custom_call" | custom-call | flops 4831838208 | bytes 20000000 | tf_op jit(solution)/shard_map/norm_sort/pallas_call | solution.py:414
  188.7 25.5 %ffn.2 = (f32[1536,768]{1,0:T(8,128)}, f32[1536,768]{1,0:T(8,128)}, bf16[2,4,3,48,768]{4,3,2,1,0:T(8,128)(2,1)}, bf16[2,4,3,48,768]{4,3,2,1,0:T(8,128)(2,1)}, bf...) custom-call(s32[3]{0:T(128)} %pad_add_fusion.c_ref, ...), custom_call_target="tpu_custom_call" | custom-call | flops 16307453952 | bytes 40000000 | tf_op jit(solution)/shard_map/ffn/pallas_call | solution.py:529
  215.5 26.2 %ffn.3 = (bf16[1536,768]{1,0:T(8,128)(2,1)}, bf16[1536,768]{1,0:T(8,128)(2,1)}, bf16[2,4,3,48,768]{4,3,2,1,0:T(8,128)(2,1)}, bf16[2,4,3,48,768]{4,3,2,1,0:T(8,12...) custom-call(s32[3]{0:T(128)} %pad_add_fusion.c_ref, ...), custom_call_target="tpu_custom_call" | custom-call | flops 16307453952 | bytes 40000000 | tf_op jit(solution)/shard_map/ffn/pallas_call | solution.py:529
  241.8 6.4 %unsort_tokens.3 = bf16[1024,768]{1,0:T(8,128)(2,1)} custom-call(s32[1024,1]{1,0:T(8,128)} %copy.35.pos_col, bf16[1536,768]{1,0:T(8,128)(2,1)} %get-tuple-element.56.vs_ref), custom_call_target="tpu_custom_call" | custom-call | flops 2415919104 | bytes 10000000 | tf_op jit(solution)/shard_map/unsort_tokens/pallas_call | solution.py:447
  252.7 6.3 %unsort_tokens.2 = bf16[1024,768]{1,0:T(8,128)(2,1)} custom-call(s32[1024,1]{1,0:T(8,128)} %copy.35.pos_col, bf16[1536,768]{1,0:T(8,128)(2,1)} %get-tuple-element.55.vs_ref), custom_call_target="tpu_custom_call" | custom-call | flops 2415919104 | bytes 10000000 | tf_op jit(solution)/shard_map/unsort_tokens/pallas_call | solution.py:447
  259.0 27.7 %attn_bwd.1 = (bf16[2,512,768]{2,1,0:T(8,128)(2,1)}, f32[2,512,768]{2,1,0:T(8,128)}, bf16[2,4,2,48,384]{4,3,2,1,0:T(8,128)(2,1)}, bf16[2,4,2,48,384]{4,3,2,1,0:T...) custom-call(s32[3]{0:T(128)} %pad_add_fusion.c_ref, ...), custom_call_target="tpu_custom_call" | custom-call | flops 40000000000 | bytes 20000000 | tf_op jit(solution)/shard_map/attn_bwd/pallas_call | solution.py:305
  287.7 5.3 %add_convert_fusion = bf16[1024,768]{1,0:T(8,128)(2,1)} fusion(f32[1024,768]{1,0:T(8,128)S(1)} %copy-done, bf16[1024,768]{1,0:T(8,128)(2,1)} %collective-permute-done.22, bf16[1024,768]{1,0:T(8,128)(2,1)} %unsort_tokens.2, f32[768]{0:T(1024)S(1)} %get-tuple-element.83, f32[768]{0:T(1024)S(1)} %get-tuple-element.84, f32[768]{0:T(1024)S(1)} %get-tuple-element.82, ...), kind=kLoop, calls=%fused_computation.6 | loop fusion | flops 7077888 | bytes 7876608 | tf_op jit(solution)/shard_map/convert_element_type | solution.py:762
  300.9 27.3 %collective-permute-done.44 = bf16[2,4,3,48,768]{4,3,2,1,0:T(8,128)(2,1)} collective-permute-done((bf16[2,4,3,48,768]{4,3,2,1,0:T(8,128)(2,1)}, bf16[2,4,3,48,768]{4,3,2,1,0:T(8,128)(2,1)}, u32[]{:S(2)}, u32[]{:S(2)}) %collective-permute-start.44) | collective-permute-done | bytes 1769504 | tf_op jit(solution)/shard_map/ppermute | solution.py:590
  332.5 7.9 %collective-permute-done.30 = bf16[2,4,2,48,384]{4,3,2,1,0:T(8,128)(2,1)S(1)} collective-permute-done((bf16[2,4,2,48,384]{4,3,2,1,0:T(8,128)(2,1)}, bf16[2,4,2,48,384]{4,3,2,1,0:T(8,128)(2,1)S(1)}, u32[]{:S(2)}, u32[]{:S(2)}) %collective-permute-start.30) | collective-permute-done | bytes 589856 | tf_op jit(solution)/shard_map/ppermute | solution.py:590
  343.1 22.8 %collective-permute-done.31 = bf16[4,2,48,384]{3,2,1,0:T(8,128)(2,1)S(1)} collective-permute-done((bf16[4,2,48,384]{3,2,1,0:T(8,128)(2,1)S(1)}, bf16[4,2,48,384]{3,2,1,0:T(8,128)(2,1)S(1)}, u32[]{:S(2)}, u32[]{:S(2)}) %collective-permute-start.31) | collective-permute-done | bytes 294944 | tf_op jit(solution)/shard_map/ppermute | solution.py:590
  366.1 8.1 %collective-permute-start.34 = (bf16[2,2,48,384]{3,2,1,0:T(8,128)(2,1)S(1)}, bf16[2,2,48,384]{3,2,1,0:T(8,128)(2,1)S(1)}, u32[]{:S(2)}, u32[]{:S(2)}) collective-permute-start(bf16[2,2,48,384]{3,2,1,0:T(8,128)(2,1)S(1)} %pad_maximum_fusion.24), channel_id=1, source_target_pairs={{0,8},{2,10},{4,12},{6,14},{8,0},{10,2},{12,4},{14,6},{16,24},{18,... | collective-permute-start | bytes 442376 | tf_op jit(solution)/shard_map/ppermute | solution.py:590
  380.1 8.0 %collective-permute-done.35 = bf16[2,2,48,384]{3,2,1,0:T(8,128)(2,1)S(1)} collective-permute-done((bf16[2,2,48,384]{3,2,1,0:T(8,128)(2,1)S(1)}, bf16[2,2,48,384]{3,2,1,0:T(8,128)(2,1)S(1)}, u32[]{:S(2)}, u32[]{:S(2)}) %collective-permute-start.35) | collective-permute-done | bytes 147488 | tf_op jit(solution)/shard_map/ppermute | solution.py:590
  391.8 10.2 %collective-permute-done.40 = bf16[4,3,48,768]{3,2,1,0:T(8,128)(2,1)S(1)} collective-permute-done((bf16[4,3,48,768]{3,2,1,0:T(8,128)(2,1)S(1)}, bf16[4,3,48,768]{3,2,1,0:T(8,128)(2,1)S(1)}, u32[]{:S(2)}, u32[]{:S(2)}) %collective-permute-start.40) | collective-permute-done | bytes 884768 | tf_op jit(solution)/shard_map/ppermute | solution.py:590
  410.1 6.9 %collective-permute-done.47 = bf16[4,3,48,768]{3,2,1,0:T(8,128)(2,1)S(1)} collective-permute-done((bf16[4,3,48,768]{3,2,1,0:T(8,128)(2,1)S(1)}, bf16[4,3,48,768]{3,2,1,0:T(8,128)(2,1)S(1)}, u32[]{:S(2)}, u32[]{:S(2)}) %collective-permute-start.47) | collective-permute-done | bytes 884768 | tf_op jit(solution)/shard_map/ppermute | solution.py:590
  421.8 15.5 %collective-permute-done.42 = bf16[2,3,48,768]{3,2,1,0:T(8,128)(2,1)S(1)} collective-permute-done((bf16[2,3,48,768]{3,2,1,0:T(8,128)(2,1)S(1)}, bf16[2,3,48,768]{3,2,1,0:T(8,128)(2,1)S(1)}, u32[]{:S(2)}, u32[]{:S(2)}) %collective-permute-start.42) | collective-permute-done | bytes 442400 | tf_op jit(solution)/shard_map/ppermute | solution.py:590
  440.0 6.4 %input_grad.1 = (f32[1024,768]{1,0:T(8,128)}, f32[8,768]{1,0:T(8,128)}) custom-call(bf16[1024,768]{1,0:T(8,128)(2,1)} %bitcast.121, bf16[1024,768]{1,0:T(8,128)(2,1)} %copy-done.9, bf16[1024,768]{1,0:T(8,128)(2,1)} %bitcast.120, f32[1024,768]{1,0:T(8,128)} %bitcast.115, f32[1,768]{1,0:T(1,128)} %copy-done.15), custom_call_target="tpu_custom_call" | custom-call | flops 20000000 | bytes 13000000 | tf_op jit(solution)/shard_map/input_grad/pallas_call | solution.py:574
  447.3 24.0 %collective-permute-done.49 = bf16[2,3,48,768]{3,2,1,0:T(8,128)(2,1)S(1)} collective-permute-done((bf16[2,3,48,768]{3,2,1,0:T(8,128)(2,1)S(1)}, bf16[2,3,48,768]{3,2,1,0:T(8,128)(2,1)S(1)}, u32[]{:S(2)}, u32[]{:S(2)}) %collective-permute-start.49) | collective-permute-done | bytes 442400 | tf_op jit(solution)/shard_map/ppermute | solution.py:590
  480.3 5.4 %collective-permute-start.28 = (f32[22,768]{1,0:T(8,128)S(1)}, f32[22,768]{1,0:T(8,128)S(1)}, u32[]{:S(2)}, u32[]{:S(2)}) collective-permute-start(f32[22,768]{1,0:T(8,128)S(1)} %add.145), channel_id=1, source_target_pairs={{0,8},{2,10},{4,12},{6,14},{8,0},{10,2},{12,4},{14,6},{16,24},{18,... | collective-permute-start | bytes 202760 | tf_op jit(solution)/shard_map/ppermute | solution.py:590
  (284 shorter events, 119.0 us)
Async XLA Ops:
  10.5 40.7 %collective-permute-start.16 = (bf16[2,3,48,768]{3,2,1,0:T(8,128)(2,1)S(1)}, bf16[2,3,48,768]{3,2,1,0:T(8,128)(2,1)S(1)}, u32[]{:S(2)}, u32[]{:S(2)}) collective-permute-start(bf16[2,3,48,768]{3,2,1,0:T(8,128)(2,1)S(1)} %pad_maximum_fusion.13), channel_id=1, source_target_pairs={{0,16},{2,18},{4,20},{6,22},{8,24},{10,26},{12,28},{14,30},{16,0},... | collective-permute-start | bytes 1327112 | tf_op jit(solution)/shard_map/ppermute | solution.py:590
  19.2 36.1 %collective-permute-start.17 = (bf16[2,3,48,768]{3,2,1,0:T(8,128)(2,1)S(1)}, bf16[2,3,48,768]{3,2,1,0:T(8,128)(2,1)S(1)}, u32[]{:S(2)}, u32[]{:S(2)}) collective-permute-start(bf16[2,3,48,768]{3,2,1,0:T(8,128)(2,1)S(1)} %pad_maximum_fusion.13), channel_id=1, source_target_pairs={{0,24},{2,26},{4,28},{6,30},{8,16},{10,18},{12,20},{14,22},{16,8},... | collective-permute-start | bytes 1327112 | tf_op jit(solution)/shard_map/ppermute | solution.py:590
  19.6 38.4 %collective-permute-start.8 = (bf16[2,3,48,768]{3,2,1,0:T(8,128)(2,1)S(1)}, bf16[2,3,48,768]{3,2,1,0:T(8,128)(2,1)S(1)}, u32[]{:S(2)}, u32[]{:S(2)}) collective-permute-start(bf16[2,3,48,768]{3,2,1,0:T(8,128)(2,1)S(1)} %pad_maximum_fusion.12), channel_id=1, source_target_pairs={{0,8},{2,10},{4,12},{6,14},{8,0},{10,2},{12,4},{14,6},{16,24},{18,... | collective-permute-start | bytes 1327112 | tf_op jit(solution)/shard_map/ppermute | solution.py:590
  32.9 56.3 %collective-permute-start.9 = (bf16[2,3,48,768]{3,2,1,0:T(8,128)(2,1)S(1)}, bf16[2,3,48,768]{3,2,1,0:T(8,128)(2,1)S(1)}, u32[]{:S(2)}, u32[]{:S(2)}) collective-permute-start(bf16[2,3,48,768]{3,2,1,0:T(8,128)(2,1)S(1)} %pad_maximum_fusion.12), channel_id=1, source_target_pairs={{0,16},{2,18},{4,20},{6,22},{8,24},{10,26},{12,28},{14,30},{16,0},... | collective-permute-start | bytes 1327112 | tf_op jit(solution)/shard_map/ppermute | solution.py:590
  51.2 39.5 %collective-permute-start.10 = (bf16[2,3,48,768]{3,2,1,0:T(8,128)(2,1)S(1)}, bf16[2,3,48,768]{3,2,1,0:T(8,128)(2,1)S(1)}, u32[]{:S(2)}, u32[]{:S(2)}) collective-permute-start(bf16[2,3,48,768]{3,2,1,0:T(8,128)(2,1)S(1)} %pad_maximum_fusion.12), channel_id=1, source_target_pairs={{0,24},{2,26},{4,28},{6,30},{8,16},{10,18},{12,20},{14,22},{16,8},... | collective-permute-start | bytes 1327112 | tf_op jit(solution)/shard_map/ppermute | solution.py:590
  53.6 37.1 %collective-permute-start.6 = (bf16[2,4,2,48,384]{4,3,2,1,0:T(8,128)(2,1)S(1)}, bf16[2,4,2,48,384]{4,3,2,1,0:T(8,128)(2,1)S(1)}, u32[]{:S(2)}, u32[]{:S(2)}) collective-permute-start(bf16[2,4,2,48,384]{4,3,2,1,0:T(8,128)(2,1)S(1)} %pad_maximum_fusion.11.b0), channel_id=1, source_target_pairs={{0,2},{2,0},{4,6},{6,4},{8,10},{10,8},{12,14},{14,12},{16,18},{18,... | collective-permute-start | bytes 1769480 | tf_op jit(solution)/shard_map/ppermute | solution.py:590
  55.3 36.3 %collective-permute-start.4 = (bf16[2,4,2,48,384]{4,3,2,1,0:T(8,128)(2,1)S(1)}, bf16[2,4,2,48,384]{4,3,2,1,0:T(8,128)(2,1)}, u32[]{:S(2)}, u32[]{:S(2)}) collective-permute-start(bf16[2,4,2,48,384]{4,3,2,1,0:T(8,128)(2,1)S(1)} %pad_maximum_fusion.10.a0), channel_id=1, source_target_pairs={{0,4},{2,6},{4,0},{6,2},{8,12},{10,14},{12,8},{14,10},{16,20},{18,... | collective-permute-start | bytes 1769480 | tf_op jit(solution)/shard_map/ppermute | solution.py:590
  57.9 51.4 %collective-permute-start.18 = (bf16[4,3,48,768]{3,2,1,0:T(8,128)(2,1)}, bf16[4,3,48,768]{3,2,1,0:T(8,128)(2,1)S(1)}, u32[]{:S(2)}, u32[]{:S(2)}) collective-permute-start(bf16[4,3,48,768]{3,2,1,0:T(8,128)(2,1)} %get-tuple-element.116), channel_id=1, source_target_pairs={{0,2},{2,0},{4,6},{6,4},{8,10},{10,8},{12,14},{14,12},{16,18},{18,... | collective-permute-start | bytes 2654216 | tf_op jit(solution)/shard_map/ppermute | solution.py:590
  109.2 67.9 %collective-permute-start.7 = (bf16[1024,768]{1,0:T(8,128)(2,1)}, bf16[1024,768]{1,0:T(8,128)(2,1)}, u32[]{:S(2)}, u32[]{:S(2)}) collective-permute-start(bf16[1024,768]{1,0:T(8,128)(2,1)} %bitcast.141), channel_id=1, source_target_pairs={{0,1},{1,0},{2,3},{3,2},{4,5},{5,4},{6,7},{7,6},{8,9},{9,8},{10,11... | collective-permute-start | bytes 4718600 | tf_op jit(solution)/shard_map/ppermute | solution.py:595
  110.7 78.0 %collective-permute-start.19 = (bf16[2,4,3,48,768]{4,3,2,1,0:T(8,128)(2,1)}, bf16[2,4,3,48,768]{4,3,2,1,0:T(8,128)(2,1)}, u32[]{:S(2)}, u32[]{:S(2)}) collective-permute-start(bf16[2,4,3,48,768]{4,3,2,1,0:T(8,128)(2,1)} %pad_maximum_fusion.2.refs_5_), channel_id=1, source_target_pairs={{0,4},{2,6},{4,0},{6,2},{8,12},{10,14},{12,8},{14,10},{16,20},{18,... | collective-permute-start | bytes 5308424 | tf_op jit(solution)/shard_map/ppermute | solution.py:590
  112.6 76.1 %collective-permute-start.21 = (bf16[2,4,3,48,768]{4,3,2,1,0:T(8,128)(2,1)}, bf16[2,4,3,48,768]{4,3,2,1,0:T(8,128)(2,1)}, u32[]{:S(2)}, u32[]{:S(2)}) collective-permute-start(bf16[2,4,3,48,768]{4,3,2,1,0:T(8,128)(2,1)} %pad_maximum_fusion.3.refs_7_), channel_id=1, source_target_pairs={{0,2},{2,0},{4,6},{6,4},{8,10},{10,8},{12,14},{14,12},{16,18},{18,... | collective-permute-start | bytes 5308424 | tf_op jit(solution)/shard_map/ppermute | solution.py:590
  115.1 57.3 %collective-permute-start.11 = (bf16[4,3,48,768]{3,2,1,0:T(8,128)(2,1)}, bf16[4,3,48,768]{3,2,1,0:T(8,128)(2,1)S(1)}, u32[]{:S(2)}, u32[]{:S(2)}) collective-permute-start(bf16[4,3,48,768]{3,2,1,0:T(8,128)(2,1)} %get-tuple-element.120), channel_id=1, source_target_pairs={{0,2},{2,0},{4,6},{6,4},{8,10},{10,8},{12,14},{14,12},{16,18},{18,... | collective-permute-start | bytes 2654216 | tf_op jit(solution)/shard_map/ppermute | solution.py:590
  116.7 57.5 %collective-permute-start.13 = (bf16[4,3,48,768]{3,2,1,0:T(8,128)(2,1)}, bf16[4,3,48,768]{3,2,1,0:T(8,128)(2,1)}, u32[]{:S(2)}, u32[]{:S(2)}) collective-permute-start(bf16[4,3,48,768]{3,2,1,0:T(8,128)(2,1)} %get-tuple-element.118), channel_id=1, source_target_pairs={{0,4},{2,6},{4,0},{6,2},{8,12},{10,14},{12,8},{14,10},{16,20},{18,... | collective-permute-start | bytes 2654216 | tf_op jit(solution)/shard_map/ppermute | solution.py:590
  172.7 41.6 %collective-permute-start.12 = (bf16[2,4,3,48,768]{4,3,2,1,0:T(8,128)(2,1)S(1)}, bf16[2,4,3,48,768]{4,3,2,1,0:T(8,128)(2,1)S(1)}, u32[]{:S(2)}, u32[]{:S(2)}) collective-permute-start(bf16[2,4,3,48,768]{4,3,2,1,0:T(8,128)(2,1)S(1)} %pad_maximum_fusion.refs_5_), channel_id=1, source_target_pairs={{0,4},{2,6},{4,0},{6,2},{8,12},{10,14},{12,8},{14,10},{16,20},{18,... | collective-permute-start | bytes 5308424 | tf_op jit(solution)/shard_map/ppermute | solution.py:590
  175.6 39.8 %collective-permute-start.14 = (bf16[2,4,3,48,768]{4,3,2,1,0:T(8,128)(2,1)S(1)}, bf16[2,4,3,48,768]{4,3,2,1,0:T(8,128)(2,1)}, u32[]{:S(2)}, u32[]{:S(2)}) collective-permute-start(bf16[2,4,3,48,768]{4,3,2,1,0:T(8,128)(2,1)S(1)} %pad_maximum_fusion.1.refs_7_), channel_id=1, source_target_pairs={{0,2},{2,0},{4,6},{6,4},{8,10},{10,8},{12,14},{14,12},{16,18},{18,... | collective-permute-start | bytes 5308424 | tf_op jit(solution)/shard_map/ppermute | solution.py:590
  248.5 44.6 %collective-permute-start.37 = (bf16[2,4,3,48,768]{4,3,2,1,0:T(8,128)(2,1)}, bf16[2,4,3,48,768]{4,3,2,1,0:T(8,128)(2,1)}, u32[]{:S(2)}, u32[]{:S(2)}) collective-permute-start(bf16[2,4,3,48,768]{4,3,2,1,0:T(8,128)(2,1)} %get-tuple-element.75), channel_id=1, source_target_pairs={{0,4},{2,6},{4,0},{6,2},{8,12},{10,14},{12,8},{14,10},{16,20},{18,... | collective-permute-start | bytes 5308424 | tf_op jit(solution)/shard_map/ppermute | solution.py:590
  248.5 48.9 %collective-permute-start.39 = (bf16[2,4,3,48,768]{4,3,2,1,0:T(8,128)(2,1)}, bf16[2,4,3,48,768]{4,3,2,1,0:T(8,128)(2,1)}, u32[]{:S(2)}, u32[]{:S(2)}) collective-permute-start(bf16[2,4,3,48,768]{4,3,2,1,0:T(8,128)(2,1)} %get-tuple-element.77), channel_id=1, source_target_pairs={{0,2},{2,0},{4,6},{6,4},{8,10},{10,8},{12,14},{14,12},{16,18},{18,... | collective-permute-start | bytes 5308424 | tf_op jit(solution)/shard_map/ppermute | solution.py:590
  250.8 77.4 %collective-permute-start.44 = (bf16[2,4,3,48,768]{4,3,2,1,0:T(8,128)(2,1)}, bf16[2,4,3,48,768]{4,3,2,1,0:T(8,128)(2,1)}, u32[]{:S(2)}, u32[]{:S(2)}) collective-permute-start(bf16[2,4,3,48,768]{4,3,2,1,0:T(8,128)(2,1)} %get-tuple-element.79), channel_id=1, source_target_pairs={{0,4},{2,6},{4,0},{6,2},{8,12},{10,14},{12,8},{14,10},{16,20},{18,... | collective-permute-start | bytes 5308424 | tf_op jit(solution)/shard_map/ppermute | solution.py:590
  252.0 79.7 %collective-permute-start.46 = (bf16[2,4,3,48,768]{4,3,2,1,0:T(8,128)(2,1)}, bf16[2,4,3,48,768]{4,3,2,1,0:T(8,128)(2,1)S(1)}, u32[]{:S(2)}, u32[]{:S(2)}) collective-permute-start(bf16[2,4,3,48,768]{4,3,2,1,0:T(8,128)(2,1)} %get-tuple-element.81), channel_id=1, source_target_pairs={{0,2},{2,0},{4,6},{6,4},{8,10},{10,8},{12,14},{14,12},{16,18},{18,... | collective-permute-start | bytes 5308424 | tf_op jit(solution)/shard_map/ppermute | solution.py:590
  287.5 52.8 %collective-permute-start.30 = (bf16[2,4,2,48,384]{4,3,2,1,0:T(8,128)(2,1)}, bf16[2,4,2,48,384]{4,3,2,1,0:T(8,128)(2,1)S(1)}, u32[]{:S(2)}, u32[]{:S(2)}) collective-permute-start(bf16[2,4,2,48,384]{4,3,2,1,0:T(8,128)(2,1)} %get-tuple-element.71), channel_id=1, source_target_pairs={{0,4},{2,6},{4,0},{6,2},{8,12},{10,14},{12,8},{14,10},{16,20},{18,... | collective-permute-start | bytes 1769480 | tf_op jit(solution)/shard_map/ppermute | solution.py:590
  293.1 48.9 %collective-permute-start.32 = (bf16[2,4,2,48,384]{4,3,2,1,0:T(8,128)(2,1)S(1)}, bf16[2,4,2,48,384]{4,3,2,1,0:T(8,128)(2,1)S(1)}, u32[]{:S(2)}, u32[]{:S(2)}) collective-permute-start(bf16[2,4,2,48,384]{4,3,2,1,0:T(8,128)(2,1)S(1)} %copy-done.30), channel_id=1, source_target_pairs={{0,2},{2,0},{4,6},{6,4},{8,10},{10,8},{12,14},{14,12},{16,18},{18,... | collective-permute-start | bytes 1769480 | tf_op jit(solution)/shard_map/ppermute | solution.py:590
  297.5 141.3 %collective-permute-start.24 = (bf16[1024,768]{1,0:T(8,128)(2,1)S(1)}, bf16[1024,768]{1,0:T(8,128)(2,1)S(1)}, u32[]{:S(2)}, u32[]{:S(2)}) collective-permute-start(bf16[1024,768]{1,0:T(8,128)(2,1)S(1)} %bitcast.122), channel_id=1, source_target_pairs={{0,1},{1,0},{2,3},{3,2},{4,5},{5,4},{6,7},{7,6},{8,9},{9,8},{10,11... | collective-permute-start | bytes 4718600 | tf_op jit(solution)/shard_map/ppermute | solution.py:595
  328.2 63.3 %collective-permute-start.38 = (bf16[4,3,48,768]{3,2,1,0:T(8,128)(2,1)S(1)}, bf16[4,3,48,768]{3,2,1,0:T(8,128)(2,1)S(1)}, u32[]{:S(2)}, u32[]{:S(2)}) collective-permute-start(bf16[4,3,48,768]{3,2,1,0:T(8,128)(2,1)S(1)} %fusion.9), channel_id=1, source_target_pairs={{0,2},{2,0},{4,6},{6,4},{8,10},{10,8},{12,14},{14,12},{16,18},{18,... | collective-permute-start | bytes 2654216 | tf_op jit(solution)/shard_map/ppermute | solution.py:590
  418.9 52.3 %collective-permute-start.49 = (bf16[2,3,48,768]{3,2,1,0:T(8,128)(2,1)S(1)}, bf16[2,3,48,768]{3,2,1,0:T(8,128)(2,1)S(1)}, u32[]{:S(2)}, u32[]{:S(2)}) collective-permute-start(bf16[2,3,48,768]{3,2,1,0:T(8,128)(2,1)S(1)} %pad_maximum_fusion.18), channel_id=1, source_target_pairs={{0,16},{2,18},{4,20},{6,22},{8,24},{10,26},{12,28},{14,30},{16,0},... | collective-permute-start | bytes 1327112 | tf_op jit(solution)/shard_map/ppermute | solution.py:590
  (61 other events, 899.3 us)

commit v2 on v1

v2 whole, which is shorter than its diff:
```python
import functools
import math

import jax
import jax.numpy as jnp
from jax import lax
from jax.experimental import pallas as pl
from jax.experimental.pallas import tpu as pltpu
from jax.sharding import PartitionSpec as P

HD = 64
EPS = 1e-05
TILE = 256
CHUNKS = 3
SCALE = 1.0
CALLS = ((0,), (1, 2))
VMEM = 58 * 1024 * 1024
LOG2E = math.log2(math.e)
f32 = jnp.float32
bf16 = jnp.bfloat16
ANY = pl.BlockSpec(memory_space=pl.ANY)


def full_spec(shape):
    zeros = (0,) * len(shape)
    return pl.BlockSpec(shape, lambda *_: zeros)


def nt_dot(a, b):
    return lax.dot_general(a, b, (((1,), (1,)), ((), ())), preferred_element_type=f32)


def nn_dot(a, b):
    return lax.dot_general(a, b, (((1,), (0,)), ((), ())), preferred_element_type=f32)


def tn_dot(a, b):
    return lax.dot_general(a, b, (((0,), (0,)), ((), ())), preferred_element_type=f32)


def params(grid_rank):
    return pltpu.CompilerParams(
        dimension_semantics=("arbitrary",) * grid_rank, vmem_limit_bytes=VMEM
    )


def cost(flops, nbytes, trans=0):
    return pl.CostEstimate(
        flops=int(flops * SCALE), bytes_accessed=int(nbytes * SCALE), transcendentals=int(trans * SCALE)
    )


def place(c_ref, kind, outer, inner, rz):
    ry, rx = (outer, inner) if kind == "a" else (inner, outer)
    return (c_ref[0] ^ rz) * 4 + (c_ref[1] ^ ry) * 2 + (c_ref[2] ^ rx)


def load_pieces(c_ref, jobs, sems):
    copies = []
    for kind, pair, view, target in jobs:
        for outer in range(2):
            for inner in range(2):
                for rz in range(4):
                    rows = place(c_ref, kind, outer, inner, rz)
                    copies.append(
                        pltpu.make_async_copy(
                            view(pair[outer], inner, rz), target(rows), sems.at[len(copies)]
                        )
                    )
    for c in copies:
        c.start()
    return copies


def gelu_parts(u):
    mag = jnp.abs(u)
    t = 1.0 / (1.0 + (0.3275911 * math.sqrt(0.5)) * mag)
    poly = t * (
        0.254829592
        + t * (-0.284496736 + t * (1.421413741 + t * (-1.453152027 + t * 1.061405429)))
    )
    gauss = jnp.exp(-0.5 * u * u)
    half = 0.5 * poly * gauss
    cdf = jnp.where(u >= 0, 1.0 - half, half)
    return u * cdf, cdf + u * gauss * (1.0 / math.sqrt(2.0 * math.pi))


def norm_parts(v):
    mean = jnp.mean(v, axis=-1, keepdims=True)
    cent = v - mean
    var = jnp.mean(cent * cent, axis=-1, keepdims=True)
    rstd = lax.rsqrt(var + EPS)
    return cent * rstd, rstd


def norm_back(d_out, xhat, rstd, gain):
    d_hat = d_out * gain
    m1 = jnp.mean(d_hat, axis=-1, keepdims=True)
    m2 = jnp.mean(d_hat * xhat, axis=-1, keepdims=True)
    return rstd * (d_hat - m1 - xhat * m2)


def attn_fwd_kernel(
    heads, piece, c_ref, x_ref, srow_ref, scol_ref, g_ref, b_ref, pb_ref, a0, a1_, b0, b1_,
    att_ref, qkv_ref, kt_ref, o_ref, ot_ref, lse_ref,
    w_s, wo_s, bias_s, sems,
):
    cols = heads * HD
    pairs = cols // 128
    seq, width = x_ref.shape[1], x_ref.shape[2]

    def into(block, j):
        return w_s.at[pl.ds(pl.multiple_of(block * piece, 16), piece), pl.ds(j * cols, cols)]

    def into_out(block):
        return wo_s.at[pl.ds(pl.multiple_of(block * piece, 16), piece), :]

    @pl.when(pl.program_id(0) == 0)
    def _():
        jobs = [
            ("a", (a0, a1_), lambda r, i, z: r.at[i, z, 0], lambda k: into(k, 0)),
            ("a", (a0, a1_), lambda r, i, z: r.at[i, z, 1], lambda k: into(k, 1)),
            ("b", (b0, b1_), lambda r, i, z: r.at[i, z, 0], lambda k: into(k, 2)),
            ("b", (b0, b1_), lambda r, i, z: r.at[i, z, 1], into_out),
        ]
        for c in load_pieces(c_ref, jobs, sems):
            c.wait()

    xhat, _ = norm_parts(x_ref[0].astype(f32))
    a1 = (xhat * g_ref[...] + b_ref[...]).astype(bf16)
    proj = (nn_dot(a1, w_s[...]) + pb_ref[...]).astype(bf16)
    for j in range(3):
        for p in range(pairs):
            qkv_ref[0, j, p] = proj[:, j * cols + p * 128 : j * cols + (p + 1) * 128]
    for p in range(pairs):
        kt_ref[0, p] = proj[:, cols + p * 128 : cols + (p + 1) * 128].T
    bias_s[...] = jnp.where(scol_ref[0] == srow_ref[0], 0.0, -1e30)
    lane = lax.broadcasted_iota(jnp.int32, (1, 128), 1)
    scale2 = HD ** (-0.5) * LOG2E

    @pl.loop(0, pairs)
    def _(p):
        q_p = qkv_ref[0, 0, p]
        k_p = qkv_ref[0, 1, p]
        v_t = qkv_ref[0, 2, p].T
        for h in range(2):
            keep = (lane < HD) if h == 0 else (lane >= HD)
            q_h = jnp.where(keep, q_p, jnp.zeros_like(q_p))
            s_t = nt_dot(k_p, q_h) + bias_s[...]
            top = jnp.max(s_t, axis=0, keepdims=True)
            e_t = jnp.exp2((s_t - top) * scale2)
            total = jnp.sum(e_t, axis=0, keepdims=True)
            p_t = (e_t * (1.0 / total)).astype(bf16)
            o_t = nn_dot(v_t[h * HD : (h + 1) * HD], p_t)
            ot_ref[0, p, h * HD : (h + 1) * HD] = o_t.astype(bf16)
            lse_ref[0, p, pl.ds(h, 1), :] = top * scale2 + jnp.log2(total)

    for p in range(pairs):
        o_ref[0, :, p * 128 : (p + 1) * 128] = ot_ref[0, p].T
    att_ref[0] = nt_dot(o_ref[0], wo_s[...]).astype(bf16)


def attn_fwd(coords, x, seg_row, seg_col, gain, bias, proj_bias, pa, pb):
    rows, seq, width = x.shape
    cols = proj_bias.shape[-1] // 3
    heads = cols // HD
    pairs = cols // 128
    piece = pa[0].shape[-2]
    row3 = lambda r, *_: (r, 0, 0)
    row4 = lambda r, *_: (r, 0, 0, 0)
    row5 = lambda r, *_: (r, 0, 0, 0, 0)
    outs = [
        ((rows, seq, width), bf16, (1, seq, width), row3),
        ((rows, 3, pairs, seq, 128), bf16, (1, 3, pairs, seq, 128), row5),
        ((rows, pairs, 128, seq), bf16, (1, pairs, 128, seq), row4),
        ((rows, seq, cols), bf16, (1, seq, cols), row3),
        ((rows, pairs, 128, seq), bf16, (1, pairs, 128, seq), row4),
        ((rows, pairs, 2, seq), f32, (1, pairs, 2, seq), row4),
    ]
    return pl.pallas_call(
        functools.partial(attn_fwd_kernel, heads, piece),
        out_shape=[jax.ShapeDtypeStruct(s, d) for s, d, _, _ in outs],
        grid_spec=pltpu.PrefetchScalarGridSpec(
            num_scalar_prefetch=1,
            grid=(rows,),
            in_specs=[
                pl.BlockSpec((1, seq, width), row3),
                pl.BlockSpec((1, 1, seq), row3),
                pl.BlockSpec((1, seq, 1), row3),
                full_spec((1, width)),
                full_spec((1, width)),
                full_spec((1, 3 * cols)),
                ANY, ANY, ANY, ANY,
            ],
            out_specs=[pl.BlockSpec(b, m) for _, _, b, m in outs],
            scratch_shapes=[
                pltpu.VMEM((width, 3 * cols), bf16),
                pltpu.VMEM((width, cols), bf16),
                pltpu.VMEM((seq, seq), f32),
                pltpu.SemaphoreType.DMA((64,)),
            ],
        ),
        compiler_params=params(1),
        cost_estimate=cost(2e10, 1e7, 3e6),
        name="attn_fwd",
    )(coords, x, seg_row, seg_col, gain, bias, proj_bias, *pa, *pb)


def attn_bwd_kernel(
    heads, piece, c_ref, dxr_ref, dxr2_ref, x_ref, srow_ref, scol_ref, ln_ref, qkv_ref, kt_ref, o_ref, ot_ref, lse_ref, a0, a1_, b0, b1_,
    da1_ref, ga0_ref, ga1_ref, gb0_ref, gb1_ref, bsum_ref,
    w_s, wo_s, bias_s, dp_s, gw_s, go_s, sems,
):
    cols = heads * HD
    pairs = cols // 128
    step = pl.program_id(0)

    def into(block, j):
        return w_s.at[pl.ds(pl.multiple_of(block * piece, 16), piece), pl.ds(j * cols, cols)]

    def into_out(block):
        return wo_s.at[pl.ds(pl.multiple_of(block * piece, 16), piece), :]

    @pl.when(step == 0)
    def _():
        jobs = [
            ("a", (a0, a1_), lambda r, i, z: r.at[i, z, 0], lambda k: into(k, 0)),
            ("a", (a0, a1_), lambda r, i, z: r.at[i, z, 1], lambda k: into(k, 1)),
            ("b", (b0, b1_), lambda r, i, z: r.at[i, z, 0], lambda k: into(k, 2)),
            ("b", (b0, b1_), lambda r, i, z: r.at[i, z, 1], into_out),
        ]
        for c in load_pieces(c_ref, jobs, sems):
            c.wait()
        gw_s[...] = jnp.zeros_like(gw_s)
        go_s[...] = jnp.zeros_like(go_s)
        bsum_ref[...] = jnp.zeros_like(bsum_ref)

    dxr = jnp.where(step == c_ref[3], dxr_ref[...], dxr2_ref[...])
    do = nn_dot(dxr, wo_s[...]).astype(bf16)
    go_s[...] += nn_dot(dxr.T, o_ref[0])
    bias_s[...] = jnp.where(scol_ref[0] == srow_ref[0], 0.0, -1e30)
    lane = lax.broadcasted_iota(jnp.int32, (1, 128), 1)
    scale = HD ** (-0.5)
    scale2 = scale * LOG2E

    for p in range(pairs):
        q_p = qkv_ref[0, 0, p]
        k_p = qkv_ref[0, 1, p]
        v_p = qkv_ref[0, 2, p]
        do_p = do[:, p * 128 : (p + 1) * 128]
        prod = do_p.T.astype(f32) * ot_ref[0, p].astype(f32)
        dv = None
        for h in range(2):
            keep = (lane < HD) if h == 0 else (lane >= HD)
            q_h = jnp.where(keep, q_p, jnp.zeros_like(q_p))
            do_h = jnp.where(keep, do_p, jnp.zeros_like(do_p))
            row = jnp.sum(prod[h * HD : (h + 1) * HD], axis=0, keepdims=True)
            s_t = nt_dot(k_p, q_h)
            p_t = jnp.exp2(s_t * scale2 + (bias_s[...] - lse_ref[0, p, h : h + 1, :]))
            d_t = nt_dot(v_p, do_h)
            ds_t = (p_t * (d_t - row)).astype(bf16)
            dv_h = nn_dot(p_t.astype(bf16), do_h)
            dk_h = nn_dot(ds_t, q_h)
            dq_h = nn_dot(kt_ref[0, p, h * HD : (h + 1) * HD], ds_t)
            dv, dk, dq = (dv_h, dk_h, [dq_h]) if dv is None else (dv + dv_h, dk + dk_h, dq + [dq_h])
        dq = (jnp.concatenate(dq, axis=0) * scale).astype(bf16).T
        dp_s[:, p * 128 : (p + 1) * 128] = dq
        dp_s[:, cols + p * 128 : cols + (p + 1) * 128] = (dk * scale).astype(bf16)
        dp_s[:, 2 * cols + p * 128 : 2 * cols + (p + 1) * 128] = dv.astype(bf16)

    dproj = dp_s[...]
    da1_ref[0] = nt_dot(dproj, w_s[...]).astype(bf16)
    bsum_ref[...] += jnp.sum(dproj.astype(f32), axis=0, keepdims=True)
    xhat1, _ = norm_parts(x_ref[0].astype(f32))
    a1 = (xhat1 * ln_ref[0:1] + ln_ref[1:2]).astype(bf16)
    gw_s[...] += nn_dot(a1.T, dproj)

    @pl.when(step == pl.num_programs(0) - 1)
    def _():
        for outer in range(2):
            for inner in range(2):
                for rz in range(4):
                    ra = pl.ds(pl.multiple_of(place(c_ref, "a", outer, inner, rz) * piece, 16), piece)
                    rb = pl.ds(pl.multiple_of(place(c_ref, "b", outer, inner, rz) * piece, 16), piece)
                    ga, gb = ((ga0_ref, gb0_ref), (ga1_ref, gb1_ref))[outer]
                    ga[inner, rz, 0] = gw_s[ra, :cols].astype(bf16)
                    ga[inner, rz, 1] = gw_s[ra, cols : 2 * cols].astype(bf16)
                    gb[inner, rz, 0] = gw_s[rb, 2 * cols :].astype(bf16)
                    gb[inner, rz, 1] = go_s[rb, :].astype(bf16)


def attn_bwd(coords, dxr, dxr2, x, seg_row, seg_col, ln, saved, pa, pb):
    rows, seq, width = x.shape
    qkv, kt, o, ot, lse = saved
    cols = o.shape[-1]
    heads = cols // HD
    pairs = cols // 128
    piece = pa[0].shape[-2]
    row3 = lambda r, *_: (r, 0, 0)
    row4 = lambda r, *_: (r, 0, 0, 0)
    row5 = lambda r, *_: (r, 0, 0, 0, 0)
    tok = pl.BlockSpec((1, seq, width), row3)
    gshape = pa[0].shape
    return pl.pallas_call(
        functools.partial(attn_bwd_kernel, heads, piece),
        out_shape=[
            jax.ShapeDtypeStruct((rows, seq, width), bf16),
            *[jax.ShapeDtypeStruct(gshape, bf16)] * 4,
            jax.ShapeDtypeStruct((1, 3 * cols), f32),
        ],
        grid_spec=pltpu.PrefetchScalarGridSpec(
            num_scalar_prefetch=1,
            grid=(rows,),
            in_specs=[
                full_spec((seq, width)), full_spec((seq, width)), tok,
                pl.BlockSpec((1, 1, seq), row3),
                pl.BlockSpec((1, seq, 1), row3),
                full_spec((2, width)),
                pl.BlockSpec((1, 3, pairs, seq, 128), row5),
                pl.BlockSpec((1, pairs, 128, seq), row4),
                pl.BlockSpec((1, seq, cols), row3),
                pl.BlockSpec((1, pairs, 128, seq), row4),
                pl.BlockSpec((1, pairs, 2, seq), row4),
                ANY, ANY, ANY, ANY,
            ],
            out_specs=[
                tok,
                *[full_spec(gshape)] * 4,
                full_spec((1, 3 * cols)),
            ],
            scratch_shapes=[
                pltpu.VMEM((width, 3 * cols), bf16),
                pltpu.VMEM((width, cols), bf16),
                pltpu.VMEM((seq, seq), f32),
                pltpu.VMEM((seq, 3 * cols), bf16),
                pltpu.VMEM((width, 3 * cols), f32),
                pltpu.VMEM((width, cols), f32),
                pltpu.SemaphoreType.DMA((64,)),
            ],
        ),
        compiler_params=params(1),
        cost_estimate=cost(4e10, 2e7, 3e6),
        name="attn_bwd",
    )(coords, dxr, dxr2, x, seg_row, seg_col, ln, qkv, kt, o, ot, lse, *pa, *pb)


def sort_kernel(sources, *refs):
    vs_ref = refs[-1]
    block = vs_ref.shape[0]
    total = None
    for k in range(sources):
        pos_row, v_ref = refs[2 * k], refs[2 * k + 1]
        slot = lax.broadcasted_iota(jnp.int32, (block, v_ref.shape[0]), 0)
        slot = slot + pl.program_id(0) * block
        pick = (slot == pos_row[...]).astype(f32).astype(bf16)
        part = nn_dot(pick, v_ref[...])
        total = part if total is None else total + part
    vs_ref[...] = total.astype(bf16)


def sort_tokens(sources, tiles, group, groups, into=None):
    width = sources[0][1].shape[1]
    tokens = sum(v.shape[0] for _, v in sources)
    slots = tiles * TILE
    steps = 2
    block = slots // steps
    flat = [x for pair in sources for x in pair]
    return pl.pallas_call(
        functools.partial(sort_kernel, len(sources)),
        out_shape=jax.ShapeDtypeStruct((groups * slots, width), bf16),
        grid=(steps,),
        in_specs=[*[full_spec(x.shape) for x in flat], *([] if into is None else [ANY])],
        out_specs=pl.BlockSpec((block, width), lambda i: (i + group * steps, 0)),
        input_output_aliases={} if into is None else {len(flat): 0},
        compiler_params=params(1),
        cost_estimate=cost(2 * slots * tokens * width, 1e7),
        name="sort_tokens",
    )(*flat, *([] if into is None else [into]))


def unsort_kernel(targets, *refs):
    vs = refs[targets][...]
    for k in range(targets):
        pos_row, out_ref = refs[k], refs[targets + 1 + k]
        slot = lax.broadcasted_iota(jnp.int32, (vs.shape[0], out_ref.shape[0]), 0)
        pick = (slot == pos_row[...]).astype(f32).astype(bf16)
        out_ref[...] = tn_dot(pick, vs).astype(bf16)


def unsort_tokens(places, vs, group, groups):
    width = vs.shape[1]
    slots = vs.shape[0] // groups
    tokens = sum(p.shape[1] for p in places)
    return pl.pallas_call(
        functools.partial(unsort_kernel, len(places)),
        out_shape=[jax.ShapeDtypeStruct((p.shape[1], width), bf16) for p in places],
        grid=(1,),
        in_specs=[
            *[full_spec(p.shape) for p in places],
            pl.BlockSpec((slots, width), lambda i: (group, 0)),
        ],
        out_specs=[full_spec((p.shape[1], width)) for p in places],
        compiler_params=params(1),
        cost_estimate=cost(2 * slots * tokens * width, 1e7),
        name="unsort_tokens",
    )(*places, vs)


def mid_kernel(x_ref, parts_ref, vec_ref, x2_ref, a2_ref):
    att = jnp.sum(parts_ref[...].astype(f32), axis=0)
    x2 = x_ref[...].astype(f32) + att + vec_ref[0:1]
    x2_ref[...] = x2
    xhat, _ = norm_parts(x2)
    a2_ref[...] = (xhat * vec_ref[1:2] + vec_ref[2:3]).astype(bf16)


def mid(x, partial, vec):
    tokens, width = x.shape
    tile = pl.BlockSpec((TILE, width), lambda i: (i, 0))
    return pl.pallas_call(
        mid_kernel,
        out_shape=[
            jax.ShapeDtypeStruct((tokens, width), f32),
            jax.ShapeDtypeStruct((tokens, width), bf16),
        ],
        grid=(tokens // TILE,),
        in_specs=[
            tile, pl.BlockSpec((partial.shape[0], TILE, width), lambda i: (0, i, 0)),
            full_spec((3, width)),
        ],
        out_specs=[tile, tile],
        compiler_params=params(1),
        cost_estimate=cost(1e7, 5e6),
        name="mid_norm",
    )(x, partial, vec)


def ffn_kernel(first, count, piece, groups, c_ref, te_ref, n_ref, *refs):
    xs_ref, dys_ref, ub_ref, *rest = refs
    if not first:
        zin_ref, din_ref, *rest = rest
    w_refs = [rest[2 * c : 2 * c + 2] for c in range(count)]
    rest = rest[2 * count :]
    z_ref, da_ref, *rest = rest
    g_refs = [rest[2 * c : 2 * c + 2] for c in range(count)]
    gub_ref, wu_s, wd_s, gu_s, gd_s, sems = rest[2 * count :]
    experts = wu_s.shape[0]
    hc = wu_s.shape[2] // count
    i = pl.program_id(0)
    spots = [(ry, rz, rx) for ry in range(2) for rz in range(4) for rx in range(2)]

    def rows_of(ry, rz, rx):
        block = (c_ref[0] ^ rz) * 4 + (c_ref[1] ^ ry) * 2 + (c_ref[2] ^ rx)
        return pl.ds(pl.multiple_of(block * piece, 16), piece)

    @pl.when(i == 0)
    def _():
        copies = []
        for c in range(count):
            for ry, rz, rx in spots:
                for k, w_s in ((0, wu_s), (1, wd_s)):
                    copies.append(
                        pltpu.make_async_copy(
                            w_refs[c][ry].at[rz, rx, k],
                            w_s.at[:, rows_of(ry, rz, rx), pl.ds(c * hc, hc)],
                            sems.at[len(copies)],
                        )
                    )
        for c in copies:
            c.start()
        gu_s[...] = jnp.zeros_like(gu_s)
        gd_s[...] = jnp.zeros_like(gd_s)
        gub_ref[...] = jnp.zeros_like(gub_ref)
        for c in copies:
            c.wait()

    per = pl.num_programs(0) // groups
    group = i // per
    live = i - group * per < n_ref[group]

    @pl.when(live)
    def _():
        e = te_ref[i]
        x = xs_ref[...]
        dy = dys_ref[...]
        u = nn_dot(x, wu_s[e]) + ub_ref[e]
        act, slope = gelu_parts(u)
        act = act.astype(bf16)
        du = (nn_dot(dy, wd_s[e]) * slope).astype(bf16)
        z = nt_dot(act, wd_s[e])
        da = nt_dot(du, wu_s[e])
        if not first:
            z = z + zin_ref[...].astype(f32)
            da = da + din_ref[...].astype(f32)
        z_ref[...] = z.astype(bf16)
        da_ref[...] = da.astype(bf16)
        gd_s[e] += tn_dot(dy, act)
        gu_s[e] += tn_dot(x, du)
        gub_ref[e] += jnp.sum(du.astype(f32), axis=0, keepdims=True)

    @pl.when(jnp.logical_not(live))
    def _():
        z_ref[...] = jnp.zeros_like(z_ref)
        da_ref[...] = jnp.zeros_like(da_ref)

    @pl.when(i == pl.num_programs(0) - 1)
    def _():
        for c in range(count):
            lanes = pl.ds(c * hc, hc)
            for ry, rz, rx in spots:
                rows = rows_of(ry, rz, rx)
                for e in range(experts):
                    g_refs[c][ry][rz, rx, 0, e] = gu_s[e, rows, lanes].astype(bf16)
                    g_refs[c][ry][rz, rx, 1, e] = gd_s[e, rows, lanes].astype(bf16)


def ffn(coords, tile_expert, used, xs, dys, up_b, weights, carry):
    slots, width = xs.shape
    tiles = slots // TILE
    groups = used.shape[0]
    first = not carry
    count = len(weights)
    gshape = weights[0][0].shape
    experts, piece, hc = gshape[3:]
    hid = hc * count
    tile = pl.BlockSpec((TILE, width), lambda i, *_: (i, 0))
    out = pl.pallas_call(
        functools.partial(ffn_kernel, first, count, piece, groups),
        out_shape=[
            jax.ShapeDtypeStruct((slots, width), bf16),
            jax.ShapeDtypeStruct((slots, width), bf16),
            *[jax.ShapeDtypeStruct(gshape, bf16)] * (2 * count),
            jax.ShapeDtypeStruct((experts, 1, hid), f32),
        ],
        grid_spec=pltpu.PrefetchScalarGridSpec(
            num_scalar_prefetch=3,
            grid=(tiles,),
            in_specs=[
                tile, tile, full_spec((experts, 1, hid)), *([] if first else [tile, tile]),
                *[ANY] * (2 * count),
            ],
            out_specs=[
                tile, tile, *[full_spec(gshape)] * (2 * count), full_spec((experts, 1, hid)),
            ],
            scratch_shapes=[
                pltpu.VMEM((experts, width, hid), bf16),
                pltpu.VMEM((experts, width, hid), bf16),
                pltpu.VMEM((experts, width, hid), f32),
                pltpu.VMEM((experts, width, hid), f32),
                pltpu.SemaphoreType.DMA((32 * count,)),
            ],
        ),
        compiler_params=params(1),
        cost_estimate=cost(12 * slots * width * hid * 1.5, 4e7, 2 * slots * hid),
        name="ffn",
    )(coords, tile_expert, used, xs, dys, up_b, *carry, *[w for pair in weights for w in pair])
    zs, das, *rest = out
    return zs, das, [rest[2 * c : 2 * c + 2] for c in range(count)], rest[2 * count]


def norm_grad_kernel(count, low, *refs):
    parts, (v_ref, add_ref, gain_ref, out_ref, *refs) = refs[:count], refs[count:]
    sums_ref = refs[-1]

    @pl.when(pl.program_id(0) == 0)
    def _():
        sums_ref[...] = jnp.zeros_like(sums_ref)

    grad = sum(
        jnp.sum(p[...].astype(f32), axis=0) if len(p.shape) == 3 else p[...].astype(f32) for p in parts
    )
    xhat, rstd = norm_parts(v_ref[...].astype(f32))
    out = add_ref[...].astype(f32) + norm_back(grad, xhat, rstd, gain_ref[...])
    out_ref[...] = out
    if low:
        refs[0][...] = out.astype(bf16)
    sums_ref[0:1] += jnp.sum(grad * xhat, axis=0, keepdims=True)
    sums_ref[1:2] += jnp.sum(grad, axis=0, keepdims=True)
    sums_ref[2:3] += jnp.sum(out, axis=0, keepdims=True)


def norm_grad(partial, v, add, gain, low):
    tokens, width = v.shape
    tile = pl.BlockSpec((TILE, width), lambda i: (i, 0))
    return pl.pallas_call(
        functools.partial(norm_grad_kernel, len(partial), low),
        out_shape=[
            jax.ShapeDtypeStruct((tokens, width), f32),
            *([jax.ShapeDtypeStruct((tokens, width), bf16)] if low else []),
            jax.ShapeDtypeStruct((8, width), f32),
        ],
        grid=(tokens // TILE,),
        in_specs=[
            *[
                pl.BlockSpec((p.shape[0], TILE, width), lambda i: (0, i, 0)) if p.ndim == 3 else tile
                for p in partial
            ],
            tile, tile, full_spec((1, width)),
        ],
        out_specs=[tile, *([tile] if low else []), full_spec((8, width))],
        compiler_params=params(1),
        cost_estimate=cost(2e7, 8e6),
        name="norm_grad",
    )(*partial, v, add, gain)


def whole(kernel, name, outs, *args, prefetch=()):
    return pl.pallas_call(
        kernel,
        out_shape=[jax.ShapeDtypeStruct(s, d) for s, d in outs],
        grid_spec=pltpu.PrefetchScalarGridSpec(
            num_scalar_prefetch=len(prefetch),
            grid=(1,),
            in_specs=[full_spec(x.shape) for x in args],
            out_specs=[full_spec(s) for s, _ in outs],
        ),
        compiler_params=params(1),
        cost_estimate=cost(1e6, 4e6),
        name=name,
    )(*prefetch, *args)


def sums_y_kernel(keep, got, own, *sends):
    add = lambda rz: keep[rz].astype(f32) + got[rz].astype(f32)
    own[...] = add(0)
    for rz, send in zip((1, 2, 3), sends):
        send[...] = add(rz).astype(bf16)


def sums_z_kernel(own, r1, r2, r3, mine, near):
    add = lambda k: own[k] + r1[k].astype(f32) + r2[k].astype(f32) + r3[k].astype(f32)
    mine[...] = add(0)
    near[...] = add(1).astype(bf16)


def two_sums_kernel(a_keep, a_got, b_keep, b_got, a_own, a_send, b_own, b_send):
    for keep, got, own, send in ((a_keep, a_got, a_own, a_send), (b_keep, b_got, b_own, b_send)):
        own[...] = keep[0].astype(f32) + got[0].astype(f32)
        send[...] = (keep[1].astype(f32) + got[1].astype(f32)).astype(bf16)


def four_sums_kernel(a_own, a_got, b_own, b_got, own, *sends):
    add = lambda rz: (a_own[rz] + a_got[rz].astype(f32), b_own[rz] + b_got[rz].astype(f32))
    own[0], own[1] = add(0)
    for rz, send in zip((1, 2, 3), sends):
        va, vb = add(rz)
        send[0] = va.astype(bf16)
        send[1] = vb.astype(bf16)


def qkv_grad_kernel(own, r1, r2, r3, g_qkv, g_out):
    add = lambda k, j: (
        own[k, j] + r1[k, j].astype(f32) + r2[k, j].astype(f32) + r3[k, j].astype(f32)
    )
    g_qkv[0] = add(0, 0)
    g_qkv[1] = add(0, 1)
    g_qkv[2] = add(1, 0)
    g_out[...] = add(1, 1)


def rows_kernel(c_ref, *refs):
    for k in range(2):
        mine, other, out = refs[2 * k], refs[2 * k + 1], refs[4 + k]
        out[c_ref[3]] = mine[...]
        out[1 - c_ref[3]] = other[...]


def expert_grad_kernel(c_ref, *refs):
    *mines, near, g_up, g_down = refs
    hc = mines[0].shape[-1]
    half = hc * len(mines)
    here = pl.multiple_of(c_ref[2] * half, 128)
    there = pl.multiple_of((1 - c_ref[2]) * half, 128)
    for k, out in ((0, g_up), (1, g_down)):
        for c, mine in enumerate(mines):
            out[:, :, pl.ds(here + c * hc, hc)] = mine[k]
        out[:, :, pl.ds(there, half)] = near[k].astype(f32)


def flip(x, mask, size):
    return lax.ppermute(x, "dp", [(i, i ^ mask) for i in range(size)])


def after(v, *deps):
    return lax.optimization_barrier((v, deps))[0]


def deal(v):
    return lax.all_to_all(v, "mp", 0, 0)


def swap(v):
    return lax.ppermute(v, "mp", [(0, 1), (1, 0)])


def share(v):
    return deal(jnp.broadcast_to(v, (lax.axis_size("mp"),) + v.shape))


def gather_staged(a, b, size):
    both = jnp.stack([a, b])
    blocks = [both] + [flip(both, 4 * rz, size) for rz in (1, 2, 3)]
    a0 = jnp.stack([v[0] for v in blocks])
    b0 = jnp.stack([v[1] for v in blocks])
    a0 = jnp.stack([a0, flip(a0, 1, size)])
    b0 = jnp.stack([b0, flip(b0, 2, size)])
    return (a0, flip(a0, 2, size)), (b0, flip(b0, 1, size))


def attn_sums_xy(ga, gb, size):
    shape = ga[0].shape[1:]
    a_own, a_send, b_own, b_send = whole(
        two_sums_kernel, "two_sums", [(shape, f32), (shape, bf16)] * 2,
        ga[0], flip(ga[1], 2, size), gb[0], flip(gb[1], 1, size),
    )
    shape = (2,) + shape[1:]
    own, *sends = whole(
        four_sums_kernel, "four_sums", [(shape, f32), *[(shape, bf16)] * 3],
        a_own, flip(a_send, 1, size), b_own, flip(b_send, 2, size),
    )
    return own, sends


def gather_plain(w):
    full = lax.all_gather(w, "dp", axis=1, tiled=True)
    n, rows, cols = full.shape
    return full.reshape(n, 16, rows // 16, cols).swapaxes(0, 1)


def gather_pieces(a, b, size, staged):
    if staged:
        return gather_staged(a, b, size)
    blocks = [gather_plain(v) for v in (a, b)]
    blocks = [v.reshape((4, 2, 2) + v.shape[1:]) for v in blocks]
    fa = jnp.moveaxis(blocks[0], 0, 2)
    fb = jnp.swapaxes(jnp.moveaxis(blocks[1], 0, 2), 0, 1)
    return (fa[0], fa[1]), (fb[0], fb[1])


def scatter_plain(ga, gb):
    fa = jnp.moveaxis(jnp.stack(ga), 2, 0)
    fb = jnp.moveaxis(jnp.swapaxes(jnp.stack(gb), 0, 1), 2, 0)
    outs = []
    for v in (fa, fb):
        v = v.reshape((16,) + v.shape[3:]).swapaxes(0, 1)
        v = v.reshape(v.shape[0], -1, v.shape[-1]).astype(f32)
        outs.append(lax.psum_scatter(v, "dp", scatter_dimension=1, tiled=True))
    return outs


def phase(pred, f):
    shapes = jax.eval_shape(f)
    return lax.cond(
        pred, f, lambda: jax.tree.map(lambda v: jnp.zeros(v.shape, v.dtype), shapes)
    )


def along_z(p, size):
    return jnp.stack([p] + [flip(p, 4 * rz, size) for rz in (1, 2, 3)])


def sums_y(pair, size):
    shape = pair[0].shape[1:]
    return whole(
        sums_y_kernel, "sums_y", [(shape, f32), *[(shape, bf16)] * 3],
        pair[0], flip(pair[1], 2, size),
    )


def sums_z(parts_y, size):
    own, *sends = parts_y
    got = [flip(v, 4 * rz, size) for rz, v in zip((1, 2, 3), sends)]
    shape = own.shape[1:]
    return whole(sums_z_kernel, "sums_z", [(shape, f32), (shape, bf16)], own, *got)


def expert_pieces_plain(w_up, w_down):
    hc = w_up.shape[-1] // CHUNKS
    blocks = jnp.stack([gather_plain(w_up), gather_plain(w_down)], axis=1)
    blocks = blocks.reshape((4, 2, 2) + blocks.shape[1:])
    return [
        tuple(blocks[:, ry, ..., c * hc : (c + 1) * hc] for ry in range(2)) for c in range(CHUNKS)
    ]


def expert_sums_plain(pair):
    v = jnp.stack(pair, axis=1)
    v = v.reshape((16,) + v.shape[3:])
    v = jnp.moveaxis(v, 0, 2)
    v = v.reshape(v.shape[:2] + (-1, v.shape[-1])).astype(f32)
    return lax.psum_scatter(v, "dp", scatter_dimension=2, tiled=True)


def sum_small(v, size):
    if size & (size - 1):
        return lax.psum(v, ("dp", "mp"))
    v = v + swap(v)
    mask = 1
    while mask < size:
        v = v + flip(v, mask, size)
        mask *= 2
    return v


def token_plan(segments, modality, experts):
    tokens = segments.size
    doc_ids = jnp.arange(modality.shape[1], dtype=jnp.int32)
    match = segments[:, :, None] == doc_ids
    mods = jnp.sum(jnp.where(match, modality[:, None, :], 0), axis=-1).reshape(tokens)
    kinds = jnp.arange(experts, dtype=jnp.int32)
    hot = (mods[:, None] == kinds).astype(jnp.int32)
    ids = jnp.arange(tokens, dtype=jnp.int32)
    lower = (ids[:, None] > ids[None, :]).astype(bf16)
    before = jnp.dot(lower, hot.astype(bf16), preferred_element_type=f32).astype(jnp.int32)
    need = (jnp.sum(hot, axis=0) + TILE - 1) // TILE
    ends = jnp.sum(jnp.where(kinds[:, None] >= kinds[None, :], need[None, :], 0), axis=1)
    pos = jnp.sum(hot * (before + (ends - need)[None, :] * TILE), axis=1)
    tiles = (tokens + experts * (TILE - 1)) // TILE
    tile_ids = jnp.arange(tiles, dtype=jnp.int32)
    tile_expert = jnp.minimum(
        jnp.sum((tile_ids[:, None] >= ends[None, :]).astype(jnp.int32), axis=1), experts - 1
    )
    return mods, pos, tile_expert, ends[-1:]


def body(
    layer_input, segments, modality, ln_gain, ln_bias, w_qkv, qv_bias, w_out, out_bias,
    w_up, up_bias, w_down, down_bias, cotangent,
):
    part = lax.axis_index("mp")
    parts = lax.axis_size("mp")
    size = lax.axis_size("dp")
    me = lax.axis_index("dp")
    rows, seq, width = layer_input.shape
    tokens = rows * seq
    cols = w_qkv.shape[-1]
    hid = w_up.shape[-1]
    experts = w_up.shape[0]
    shape3 = (rows, seq, width)
    tiles = (tokens + experts * (TILE - 1)) // TILE
    staged = size == 16

    mine_rows = rows // parts
    mine_tokens = tokens // parts
    by_core = (parts, mine_tokens, width)
    dy = cotangent.reshape(tokens, width)
    rows_here = lambda v: lax.dynamic_slice_in_dim(v, part * mine_rows, mine_rows, 0)
    x_mine = rows_here(layer_input).reshape(mine_tokens, width)
    dy_mine = rows_here(cotangent).reshape(mine_tokens, width)
    col_start = part * cols
    q_b = lax.dynamic_slice_in_dim(qv_bias[0], col_start, cols)
    v_b = lax.dynamic_slice_in_dim(qv_bias[1], col_start, cols)
    proj_bias = jnp.concatenate([q_b, jnp.zeros_like(q_b), v_b]).reshape(1, 3 * cols)
    seg_row, seg_col = segments.reshape(rows, 1, seq), segments.reshape(rows, seq, 1)
    vec = jnp.concatenate([out_bias[None], ln_gain[1:2], ln_bias[1:2]])
    ln1 = jnp.concatenate([ln_gain[0:1], ln_bias[0:1]])
    w_ab = w_qkv[:2], jnp.stack([w_qkv[2], w_out])

    def fwd(coords, pa, pb):
        att, *saved = attn_fwd(
            coords, layer_input, seg_row, seg_col, ln_gain[0:1], ln_bias[0:1], proj_bias, pa, pb
        )
        return (saved, *mid(x_mine, deal(att.reshape(by_core)), vec))

    def bwd(coords, dxr, saved, pa, pb):
        return attn_bwd(coords, *dxr, layer_input, seg_row, seg_col, ln1, saved, pa, pb)

    def halves(v):
        take = lambda k: lax.dynamic_slice_in_dim(v, k * mine_tokens, mine_tokens, 0)
        return take(part).reshape(1, mine_tokens), take(1 - part).reshape(1, mine_tokens)

    def finish(x2, z_sum, mods):
        kinds = lax.dynamic_slice_in_dim(mods, part * mine_tokens, mine_tokens, 0)[:, None]
        bias_of = jnp.zeros((mine_tokens, width), f32)
        for e in range(experts):
            bias_of = jnp.where(kinds == e, down_bias[e][None], bias_of)
        return (x2 + (z_sum + bias_of)).astype(bf16)

    if staged:
        x_bit = me % 2
        coords = jnp.stack([me // 4, (me // 2) % 2, x_bit, part]).astype(jnp.int32)
        pred = me < size
        half = hid // 2
        hid_start = part * hid + x_bit * half
        hc = half // CHUNKS
        up_b = lax.dynamic_slice_in_dim(up_bias, hid_start, half, 1)

        def call_experts(k, xs, dys, weights, carry):
            call = CALLS[k]
            ub = up_b[:, None, call[0] * hc : (call[-1] + 1) * hc]
            return ffn(
                coords, tile_expert, used, xs, dys, ub, [weights[c] for c in call], carry
            )

        def begin():
            w = jnp.stack([w_up, w_down])
            keep = lax.dynamic_slice_in_dim(w, x_bit * half, half, 3)
            near = flip(lax.dynamic_slice_in_dim(w, (1 - x_bit) * half, half, 3), 1, size)
            pieces = [
                jnp.stack([keep[..., c * hc : (c + 1) * hc], near[..., c * hc : (c + 1) * hc]])
                for c in range(CHUNKS)
            ]
            pa, pb = gather_pieces(*w_ab, size, True)
            mods, pos, tile_expert, used = token_plan(segments, modality, experts)
            plan = flip(jnp.concatenate([pos, tile_expert, used]), 1, size)
            dys = sort_tokens([(pos.reshape(1, tokens), dy)], tiles, 0, 2)
            hot = (mods[:, None] == jnp.arange(experts, dtype=jnp.int32)).astype(bf16)
            return (
                pieces, pa, pb, mods, pos, tile_expert, used, plan,
                dys, tn_dot(hot, dy), along_z(pieces[0], size),
            )

        (pieces, pa, pb, mods, pos, tile_expert, used, plan, dys, g_down_bias,
         z0) = phase(pred, begin)
        pos_here = halves(pos)
        pos_near = halves(plan)
        tile_expert = jnp.concatenate([tile_expert, plan[tokens : tokens + tiles]])
        used = jnp.concatenate([used, plan[tokens + tiles :]])

        saved, x2, a2, y0, z1, dy_near = phase(
            pred,
            lambda: (
                *fwd(coords, pa, pb), flip(z0, 2, size), along_z(pieces[1], size),
                flip(dy_mine, 1, size),
            ),
        )

        def exchange():
            near = flip(a2, 1, size)
            y1 = flip(z1, 2, size)
            z2 = along_z(pieces[2], size)
            pos_row = pos.reshape(1, tokens)
            near_row = plan[:tokens].reshape(1, tokens)
            both = share(dy_near).reshape(tokens, width)
            d = sort_tokens([(near_row, both)], tiles, 1, 2, dys)
            xs = sort_tokens([(pos_row, share(a2).reshape(tokens, width))], tiles, 0, 2)
            near = share(after(near, d, xs)).reshape(tokens, width)
            return sort_tokens([(near_row, near)], tiles, 1, 2, xs), d, y1, z2

        xs, dys, y1, z2 = phase(pred, exchange)
        weights = [(z0, y0), (z1, y1)]
        (zs, das, grads, gub0), y2 = phase(
            pred, lambda: (call_experts(0, xs, dys, weights, ()), flip(z2, 2, size))
        )
        weights.append((z2, y2))
        def second():
            v0 = sums_y(grads[0], size)
            zs, das, more, gub = call_experts(1, xs, dys, weights, (zs0, das0))
            mine, other = unsort_tokens(pos_near, das, 1, 2)
            near = (mine.astype(f32) + swap(other).astype(f32)).astype(bf16)
            return zs, das, more, gub, near, v0

        zs0, das0 = zs, das
        zs, das, more, gub1, da_near, v0 = phase(pred, second)
        grads = grads + more
        g_upb = jnp.concatenate([gub0, gub1], axis=-1)[:, 0]
        pos_row = pos.reshape(1, tokens)
        near_row = plan[:tokens].reshape(1, tokens)

        def dealt(place, vs, group):
            return deal(unsort_tokens([place], vs, group, 2)[0].reshape(by_core))

        def back():
            near = flip(da_near, 1, size)
            g0 = sums_z(v0, size)
            v1 = sums_y(grads[1], size)
            own = dealt(pos_row, das, 0)
            z_near = jnp.sum(dealt(near_row, zs, 1).astype(f32), axis=0).astype(bf16)
            near = after(near, g0, v1, z_near)
            dx2, dxr, sums2 = norm_grad((own, near), x2, dy_mine, ln_gain[1:2], True)
            return dx2, (dxr, swap(dxr)), sums2, z_near, g0, v1

        dx2, dxr, sums2, z_near, g0, v1 = phase(pred, back)
        (da1, ga0, ga1, gb0, gb1, bsum), z_near, g1, v2 = phase(
            pred,
            lambda: (
                bwd(coords, dxr, saved, pa, pb), flip(z_near, 1, size), sums_z(v1, size),
                sums_y(grads[2], size),
            ),
        )

        def sum_up():
            own, sends = attn_sums_xy((ga0, ga1), (gb0, gb1), size)
            g2 = sums_z(v2, size)
            grad, sums1 = norm_grad((deal(da1.reshape(by_core)),), x_mine, dx2, ln_gain[0:1], False)
            z_own = dealt(pos_row, zs, 0)
            out = finish(x2, jnp.sum(z_own.astype(f32), axis=0) + z_near.astype(f32), mods)
            return own, sends, g2, grad, sums1, out

        own, sends, g2, grad, sums1, out = phase(pred, sum_up)
        got = [flip(v, 4 * rz, size) for rz, v in zip((1, 2, 3), sends)]
        near = flip(jnp.concatenate([v[1] for v in (g0, g1, g2)], axis=-1), 1, size)
        g_qkv, g_out = whole(
            qkv_grad_kernel, "qkv_grad", [(w_qkv.shape, f32), (w_out.shape, f32)], own, *got
        )
        g_up, g_down = whole(
            expert_grad_kernel, "expert_grad", [(w_up.shape, f32)] * 2,
            g0[0], g1[0], g2[0], near, prefetch=(coords,),
        )
        layer_output, grad_input = whole(
            rows_kernel, "rows", [((parts,) + v.shape, v.dtype) for v in (out, grad)],
            out, swap(out), grad, swap(grad), prefetch=(coords,),
        )
    else:
        coords = jnp.stack([0, 0, 0, part]).astype(jnp.int32)
        hid_start = part * hid
        hc = hid // CHUNKS
        up_b = lax.dynamic_slice_in_dim(up_bias, hid_start, hid, 1)
        pa, pb = gather_pieces(*w_ab, size, False)
        weights = expert_pieces_plain(w_up, w_down)
        mods, pos, tile_expert, used = token_plan(segments, modality, experts)
        pos_row = pos.reshape(1, tokens)
        hot = (mods[:, None] == jnp.arange(experts, dtype=jnp.int32)).astype(bf16)
        g_down_bias = tn_dot(hot, dy)
        dys = sort_tokens([(pos_row, dy)], tiles, 0, 1)
        saved, x2, a2 = fwd(coords, pa, pb)
        xs = sort_tokens([(pos_row, share(a2).reshape(tokens, width))], tiles, 0, 1)
        carry = ()
        grads = []
        g_upb = []
        for call in CALLS:
            ub = up_b[:, None, call[0] * hc : (call[-1] + 1) * hc]
            zs, das, pairs, gub = ffn(
                coords, tile_expert, used, xs, dys, ub, [weights[c] for c in call], carry
            )
            carry = (zs, das)
            g_upb.append(gub[:, 0])
            grads += pairs
        g_upb = jnp.concatenate(g_upb, axis=-1)
        g_up, g_down = jnp.concatenate([expert_sums_plain(pair) for pair in grads], axis=-1)
        own = deal(unsort_tokens([pos_row], das, 0, 1)[0].reshape(by_core))
        dx2, dxr, sums2 = norm_grad((own[0], own[1]), x2, dy_mine, ln_gain[1:2], True)
        da1, ga0, ga1, gb0, gb1, bsum = bwd(coords, (dxr, swap(dxr)), saved, pa, pb)
        own = deal(da1.reshape(by_core))
        grad_mine, sums1 = norm_grad((own[0], own[1]), x_mine, dx2, ln_gain[0:1], False)
        g_qk, g_vo = scatter_plain((ga0, ga1), (gb0, gb1))
        g_qkv, g_out = jnp.concatenate([g_qk, g_vo[:1]]), g_vo[1]
        own = deal(unsort_tokens([pos_row], zs, 0, 1)[0].reshape(by_core))
        layer_output = share(finish(x2, jnp.sum(own.astype(f32), axis=0), mods))
        grad_input = share(grad_mine)

    bsum = bsum.reshape(3, cols)
    g_qv = lax.dynamic_update_slice(
        jnp.zeros((2, width), f32), jnp.stack([bsum[0], bsum[2]]), (jnp.int32(0), col_start)
    )
    g_upb_full = lax.dynamic_update_slice(
        jnp.zeros((experts, up_bias.shape[1]), f32), g_upb, (jnp.int32(0), hid_start)
    )
    small = jnp.concatenate([sums1[0:2], sums2[0:3], g_down_bias / parts, g_qv, g_upb_full.reshape(-1, width)])
    small = sum_small(small, size)
    g_gain = jnp.stack([small[0], small[2]])
    g_lnb = jnp.stack([small[1], small[3]])
    return (
        layer_output.reshape(shape3),
        grad_input.reshape(shape3),
        g_gain,
        g_lnb,
        g_qkv,
        small[5 + experts : 7 + experts],
        g_out,
        small[4],
        g_up,
        small[7 + experts :].reshape(experts, up_bias.shape[1]),
        g_down,
        small[5 : 5 + experts],
    )


def solution(mesh):
    tok = P("dp", None, None)
    rep = P()
    wide = P(None, "dp", "mp")
    in_specs = (
        tok, P("dp", None), P("dp", None), rep, rep, wide, rep, P("dp", "mp"), rep, wide, rep,
        wide, rep, tok,
    )
    out_specs = (
        tok, tok, rep, rep, wide, rep, P("dp", "mp"), rep, wide, rep, wide, rep,
    )
    return jax.shard_map(body, mesh=mesh, in_specs=in_specs, out_specs=out_specs, check_vma=False)
```

time: 501 us -> 415 us (0.83)
  waiting for transfers between devices: 236 us -> 55.1 us
  Pallas kernels: 137 us -> 170 us
  starting transfers between devices: 74.9 us -> 97.4 us
  local copies, waits for them, and re-layouts: 16.6 us -> 36.9 us
  blocking collectives: 0 us -> 19.8 us
  other arithmetic: 30.9 us -> 24.6 us
    ppermute x46 -> x49, waiting for transfers between devices: 236 us -> 49.8 us  [flip(): return lax.ppermute(x, 'dp', [(i, i ^ mask) for i in range(size)])]
    pallas_call x6 -> x23, Pallas kernels: 79.8 us -> 128 us  [the longest x2 50.4 us: ffn(): pl.pallas_call(functools.partial(ffn_kernel, first, count, piece, groups)...]
    all_to_all x0 -> x5, starting transfers between devices: none -> 32.7 us  [deal(): return lax.all_to_all(v, 'mp', 0, 0)]
    all_to_all x0 -> x3, blocking collectives: none -> 19.8 us  [deal(): return lax.all_to_all(v, 'mp', 0, 0)]
    ppermute x46 -> x49, starting transfers between devices: 74.7 us -> 63.6 us  [flip(): return lax.ppermute(x, 'dp', [(i, i ^ mask) for i in range(size)])]
    pallas_call x1, Pallas kernels: 11.6 us -> 2.69 us  [mid(): pl.pallas_call(mid_kernel, out_shape=[jax.ShapeDtypeStruct((tokens, width...]
    add x10 -> x1, other arithmetic: 7.51 us -> 0.01 us  [sum_small(): v = v + swap(v)]
    slice x18 -> x16, local copies, waits for them, and re-layouts: 3.36 us -> 10.3 us  [the longest x1 1.35 us: body(): used = jnp.concatenate([used, plan[tokens + tiles:]])]
  transfers between devices with their start and end apart: 51 -> 59, of which waited for: 19 -> 16; matrix products, arithmetic and copies ran while one was open for 8% -> 12% of each run, Pallas kernels for 21% -> 38%
where the time goes in v2:
time: 415 us; the launch traced here: 408 us
  Pallas kernels  170 us (41%)
  starting transfers between devices  97.4 us (23%)
  waiting for transfers between devices  55.1 us (13%)
  local copies, waits for them, and re-layouts  36.9 us (9%)
  other arithmetic  24.6 us (6%)
  blocking collectives  19.8 us (5%)
    ppermute x49, starting transfers between devices, flip(): return lax.ppermute(x, 'dp', [(i, i ^ mask) for i in range(size)])  63.6 us
    pallas_call x2, Pallas kernels, ffn(): pl.pallas_call(functools.partial(ffn_kernel, first, count, piece, groups)...  50.4 us
    ppermute x49, waiting for transfers between devices, flip(): return lax.ppermute(x, 'dp', [(i, i ^ mask) for i in range(size)])  49.8 us
    all_to_all x5, starting transfers between devices, deal(): return lax.all_to_all(v, 'mp', 0, 0)  32.7 us
    pallas_call x11, Pallas kernels, whole(): pl.pallas_call(kernel, out_shape=[jax.ShapeDtypeStruct(s, d) for s, d in...  29 us
    pallas_call x1, Pallas kernels, attn_bwd(): pl.pallas_call(functools.partial(attn_bwd_kernel, heads, piece), out_shap...  22.4 us
    pallas_call x4, Pallas kernels, unsort_tokens(): pl.pallas_call(functools.partial(unsort_kernel, len(places)), out_shape=[...  21.7 us
    all_to_all x3, blocking collectives, deal(): return lax.all_to_all(v, 'mp', 0, 0)  19.8 us
  transfers between devices with their start and end apart: 59, of which 16 were waited for; matrix products, arithmetic and copies ran while one was open for 12% of the time, Pallas kernels for 38%

profile of v2, /device:TPU:0, one launch (start us, length us, event | category | flops | bytes accessed | tf_op | source)
XLA Modules:
  0.0 407.7 jit_solution(6721961216840856292)
XLA Ops:
  3.5 58.6 %conditional.8 = (bf16[2,2,3,48,256]{4,3,2,1,0:T(8,128)(2,1)S(1)}, bf16[2,2,3,48,256]{4,3,2,1,0:T(8,128)(2,1)S(1)}, bf16[2,4,2,48,384]{4,3,2,1,0:T(8,128)(2,1)S(...) conditional(s32[]{:T(128)} %convert_element_type.44, () %tuple.88, ...), branch_computations={%region_0.1_spmd, %region_1.7_spmd} | conditional | flops 2433591552 | bytes 50332352 | solution.py:753
  47.4 12.9 %collective-permute-done.41 = bf16[2,2,3,48,256]{4,3,2,1,0:T(8,128)(2,1)S(1)} collective-permute-done((bf16[2,2,3,48,256]{4,3,2,1,0:T(8,128)(2,1)S(1)}, bf16[2,2,3,48,256]{4,3,2,1,0:T(8,128)(2,1)S(1)}, u32[]{:S(2)}, u32[]{:S(2)}) %collective-permute-start.41) | collective-permute-done | bytes 294944 | tf_op jit(solution)/shard_map/cond/branch_1_fun/ppermute | solution.py:681
  67.3 41.1 %conditional.9 = (bf16[2,3,3,512,128]{4,3,2,1,0:T(8,128)(2,1)}, bf16[2,3,128,512]{3,2,1,0:T(8,128)(2,1)}, bf16[2,512,384]{2,1,0:T(8,128)(2,1)}, bf16[2,3,128,512...) conditional(s32[]{:T(128)} %convert_element_type.44, () %tuple.92, ...), branch_computations={%region_7.8_spmd, %region_8.9_spmd} | conditional | flops 20011769856 | bytes 31938264 | solution.py:753
  78.5 17.1 %attn_fwd.1 = (bf16[2,512,768]{2,1,0:T(8,128)(2,1)}, bf16[2,3,3,512,128]{4,3,2,1,0:T(8,128)(2,1)}, bf16[2,3,128,512]{3,2,1,0:T(8,128)(2,1)}, bf16[2,512,384]{2,1...) custom-call(s32[4]{0:T(128)S(1)} %get-tuple-element.262.c_ref, ...), custom_call_target="tpu_custom_call" | custom-call | flops 20000000000 | bytes 10000000 | tf_op jit(solution)/shard_map/cond/branch_1_fun/attn_fwd/pallas_call | solution.py:180
  95.6 7.8 %all_to_all.32.parts_ref = bf16[2,512,768]{2,1,0:T(8,128)(2,1)} all-to-all(bf16[2,512,768]{2,1,0:T(8,128)(2,1)} %get-tuple-element.279), channel_id=1, replica_groups=mesh['dp'=16,'mp'=2] {'mp'}, dimensions={0} | all-to-all | bytes 3145728 | tf_op jit(solution)/shard_map/cond/branch_1_fun/all_to_all | solution.py:689
  108.5 47.5 %conditional.10 = (bf16[3072,768]{1,0:T(8,128)(2,1)}, bf16[3072,768]{1,0:T(8,128)(2,1)}, bf16[4,2,2,3,48,256]{5,4,3,2,1,0:T(8,128)(2,1)}, bf16[4,2,2,3,48,256]{5,4,3,2,1,0:T(8,128)(2,1)}) conditional(s32[]{:T(128)} %convert_element_type.44, () %tuple.91, (s32[1031]{0:T(1024)}, bf16[512,768]{1,0:T(8,128)(2,1)}, bf16[512,768]{1,0:T(8,128)(2,1)}, ...), branch_computations={%region_9.10_spmd, %region_10.11_spmd} | conditional | flops 7249526784 | bytes 63038628 | solution.py:753
  116.4 5.8 %all_to_all.33 = bf16[2,512,768]{2,1,0:T(8,128)(2,1)} all-to-all(bf16[2,512,768]{2,1,0:T(8,128)(2,1)S(1)} %broadcast_in_dim.90), channel_id=1, replica_groups=mesh['dp'=16,'mp'=2] {'mp'}, dimensions={0} | all-to-all | bytes 3145728 | tf_op jit(solution)/shard_map/cond/branch_1_fun/all_to_all | solution.py:689
  129.3 5.2 %sort_tokens.6.refs_2_ = bf16[3072,768]{1,0:T(8,128)(2,1)} custom-call(s32[1,1024]{1,0:T(1,128)S(1)} %bitcast.92, bf16[1024,768]{1,0:T(8,128)(2,1)} %bitcast.69), custom_call_target="tpu_custom_call" | custom-call | flops 2415919104 | bytes 10000000 | tf_op jit(solution)/shard_map/cond/branch_1_fun/sort_tokens/pallas_call | solution.py:368
  135.8 5.3 %sort_tokens.5 = bf16[3072,768]{1,0:T(8,128)(2,1)} custom-call(s32[1,1024]{1,0:T(1,128)} %bitcast.88, bf16[1024,768]{1,0:T(8,128)(2,1)} %bitcast.25.refs_1_, bf16[3072,768]{1,0:T(8,128)(2,1)} %get-tuple-element.289.refs_2_), custom_call_target="tpu_custom_call", output_to_operand_aliasing={{}: (2, {})} | custom-call | flops 2415919104 | bytes 10000000 | tf_op jit(solution)/shard_map/cond/branch_1_fun/sort_tokens/pallas_call | solution.py:368
  144.7 6.1 %all_to_all.34 = bf16[2,512,768]{2,1,0:T(8,128)(2,1)} all-to-all(bf16[2,512,768]{2,1,0:T(8,128)(2,1)S(1)} %broadcast_in_dim.91), channel_id=1, replica_groups=mesh['dp'=16,'mp'=2] {'mp'}, dimensions={0} | all-to-all | bytes 3145728 | tf_op jit(solution)/shard_map/cond/branch_1_fun/all_to_all | solution.py:689
  157.4 28.4 %conditional.11 = (bf16[3072,768]{1,0:T(8,128)(2,1)}, bf16[3072,768]{1,0:T(8,128)(2,1)}, bf16[4,2,2,3,48,256]{5,4,3,2,1,0:T(8,128)(2,1)}, bf16[4,2,2,3,48,256]{5...) conditional(s32[]{:T(128)} %convert_element_type.44, () %tuple.95, ...), branch_computations={%region_11.12_spmd, %region_12.13_spmd} | conditional | flops 10871635968 | bytes 44730968 | solution.py:753
  158.6 20.8 %ffn.2 = (bf16[3072,768]{1,0:T(8,128)(2,1)}, bf16[3072,768]{1,0:T(8,128)(2,1)}, bf16[4,2,2,3,48,256]{5,4,3,2,1,0:T(8,128)(2,1)}, bf16[4,2,2,3,48,256]{5,4,3,2,1,0:T(8,128)(2,1)}, f32[3,1,256]{2,1,0:T(1,128)S(1)}) custom-call(s32[4]{0:T(128)S(1)} %get-tuple-element.294.c_ref, s32[12]{0:T(128)S(1)} %get-tuple-element.295.te_ref, ...), custom_call_target="tpu_custom_call" | custom-call | flops 10871635968 | bytes 40000000 | tf_op jit(solution)/shard_map/cond/branch_1_fun/ffn/pallas_call | solution.py:527
  179.4 6.4 %collective-permute-done = bf16[4,2,2,3,48,256]{5,4,3,2,1,0:T(8,128)(2,1)} collective-permute-done((bf16[4,2,2,3,48,256]{5,4,3,2,1,0:T(8,128)(2,1)}, bf16[4,2,2,3,48,256]{5,4,3,2,1,0:T(8,128)(2,1)}, u32[]{:S(2)}, u32[]{:S(2)}) %collective-permute-start) | collective-permute-done | bytes 1179680 | tf_op jit(solution)/shard_map/cond/branch_1_fun/ppermute | solution.py:681
  185.8 44.9 %conditional.12 = (bf16[3072,768]{1,0:T(8,128)(2,1)}, bf16[3072,768]{1,0:T(8,128)(2,1)}, bf16[4,2,2,3,48,256]{5,4,3,2,1,0:T(8,128)(2,1)}, bf16[4,2,2,3,48,256]{5...) conditional(s32[]{:T(128)} %convert_element_type.44, () %tuple.90, ...), branch_computations={%region_13.14_spmd, %region_14.15_spmd} | conditional | flops 24161763328 | bytes 64256668 | solution.py:753
  188.4 29.6 %ffn.3 = (bf16[3072,768]{1,0:T(8,128)(2,1)}, bf16[3072,768]{1,0:T(8,128)(2,1)}, bf16[4,2,2,3,48,256]{5,4,3,2,1,0:T(8,128)(2,1)}, bf16[4,2,2,3,48,256]{5,4,3,2,1,...) custom-call(s32[4]{0:T(128)S(1)} %get-tuple-element.308.c_ref, ...), custom_call_target="tpu_custom_call" | custom-call | flops 21743271936 | bytes 40000000 | tf_op jit(solution)/shard_map/cond/branch_1_fun/ffn/pallas_call | solution.py:527
  230.7 52.3 %conditional.13 = (f32[512,768]{1,0:T(8,128)}, bf16[512,768]{1,0:T(8,128)(2,1)}, bf16[512,768]{1,0:T(8,128)(2,1)}, bf16[512,768]{1,0:T(8,128)(2,1)}, f32[2,3,48,...) conditional(s32[]{:T(128)} %convert_element_type.44, () %tuple.87, ...), branch_computations={%region_15.16_spmd, %region_16.18_spmd} | conditional | flops 4854231040 | bytes 62378632 | solution.py:753
  238.3 5.5 %unsort_tokens.6 = bf16[1024,768]{1,0:T(8,128)(2,1)} custom-call(s32[1,1024]{1,0:T(1,128)} %bitcast.95, bf16[3072,768]{1,0:T(8,128)(2,1)} %get-tuple-element.353.refs_1_), custom_call_target="tpu_custom_call" | custom-call | flops 2415919104 | bytes 10000000 | tf_op jit(solution)/shard_map/cond/branch_1_fun/unsort_tokens/pallas_call | solution.py:394
  243.9 14.1 %all-to-all-start.1 = ((bf16[2,512,768]{2,1,0:T(8,128)(2,1)}), bf16[2,512,768]{2,1,0:T(8,128)(2,1)}, u32[]{:S(2)}, u32[]{:S(2)}) async-start(bf16[2,512,768]{2,1,0:T(8,128)(2,1)} %bitcast.70), calls=%async_computation.1 | async-start | bytes 3145728 | tf_op jit(solution)/shard_map/cond/branch_1_fun/all_to_all | solution.py:689
  258.5 5.5 %unsort_tokens.5 = bf16[1024,768]{1,0:T(8,128)(2,1)} custom-call(s32[1,1024]{1,0:T(1,128)} %get-tuple-element.337.refs_0_, bf16[3072,768]{1,0:T(8,128)(2,1)} %get-tuple-element.338.refs_1_), custom_call_target="tpu_custom_call" | custom-call | flops 2415919104 | bytes 10000000 | tf_op jit(solution)/shard_map/cond/branch_1_fun/unsort_tokens/pallas_call | solution.py:394
  283.0 35.0 %conditional.14 = (bf16[2,512,768]{2,1,0:T(8,128)(2,1)}, bf16[2,4,2,48,384]{4,3,2,1,0:T(8,128)(2,1)S(1)}, bf16[2,4,2,48,384]{4,3,2,1,0:T(8,128)(2,1)}, bf16[2,4,...) conditional(s32[]{:T(128)} %convert_element_type.44, () %tuple.86, ...), branch_computations={%region_18.19_spmd, %region_19.20_spmd} | conditional | flops 40001998848 | bytes 40591436 | solution.py:753
  290.6 22.4 %attn_bwd.1 = (bf16[2,512,768]{2,1,0:T(8,128)(2,1)}, bf16[2,4,2,48,384]{4,3,2,1,0:T(8,128)(2,1)S(1)}, bf16[2,4,2,48,384]{4,3,2,1,0:T(8,128)(2,1)}, bf16[2,4,2,48...) custom-call(s32[4]{0:T(128)S(1)} %get-tuple-element.361.c_ref, ...), custom_call_target="tpu_custom_call" | custom-call | flops 40000000000 | bytes 20000000 | tf_op jit(solution)/shard_map/cond/branch_1_fun/attn_bwd/pallas_call | solution.py:304
  318.0 44.9 %conditional.15 = (f32[2,2,48,384]{3,2,1,0:T(8,128)}, bf16[2,2,48,384]{3,2,1,0:T(8,128)(2,1)}, bf16[2,2,48,384]{3,2,1,0:T(8,128)(2,1)}, bf16[2,2,48,384]{3,2,1,0...) conditional(s32[]{:T(128)} %convert_element_type.44, () %tuple.85, ...), branch_computations={%region_20.21_spmd, %region_21.23_spmd} | conditional | flops 2443246080 | bytes 60329352 | solution.py:753
  330.0 5.5 %unsort_tokens.7 = bf16[1024,768]{1,0:T(8,128)(2,1)} custom-call(s32[1,1024]{1,0:T(1,128)} %get-tuple-element.420.refs_0_, bf16[3072,768]{1,0:T(8,128)(2,1)} %get-tuple-element.421.refs_1_), custom_call_target="tpu_custom_call" | custom-call | flops 2415919104 | bytes 10000000 | tf_op jit(solution)/shard_map/cond/branch_1_fun/unsort_tokens/pallas_call | solution.py:394
  384.4 5.3 %collective-permute-done.51.r2 = bf16[2,2,48,384]{3,2,1,0:T(8,128)(2,1)S(1)} collective-permute-done((bf16[2,2,48,384]{3,2,1,0:T(8,128)(2,1)}, bf16[2,2,48,384]{3,2,1,0:T(8,128)(2,1)S(1)}, u32[]{:S(2)}, u32[]{:S(2)}) %collective-permute-start.51) | collective-permute-done | bytes 147488 | tf_op jit(solution)/shard_map/ppermute | solution.py:681
  (296 shorter events, 230.0 us)
Async XLA Ops:
  31.4 30.2 %collective-permute-start.36 = (bf16[2,4,2,48,384]{4,3,2,1,0:T(8,128)(2,1)S(1)}, bf16[2,4,2,48,384]{4,3,2,1,0:T(8,128)(2,1)}, u32[]{:S(2)}, u32[]{:S(2)}) collective-permute-start(bf16[2,4,2,48,384]{4,3,2,1,0:T(8,128)(2,1)S(1)} %pad_maximum_fusion.1), channel_id=1, source_target_pairs={{0,4},{2,6},{4,0},{6,2},{8,12},{10,14},{12,8},{14,10},{16,20},{18,... | collective-permute-start | bytes 1769480 | tf_op jit(solution)/shard_map/cond/branch_1_fun/ppermute | solution.py:681
  67.3 38.8 %collective-permute-start.13 = (bf16[2,2,3,48,256]{4,3,2,1,0:T(8,128)(2,1)S(1)}, bf16[2,2,3,48,256]{4,3,2,1,0:T(8,128)(2,1)}, u32[]{:S(2)}, u32[]{:S(2)}) collective-permute-start(bf16[2,2,3,48,256]{4,3,2,1,0:T(8,128)(2,1)S(1)} %get-tuple-element.284), channel_id=1, source_target_pairs={{0,8},{2,10},{4,12},{6,14},{8,0},{10,2},{12,4},{14,6},{16,24},{18,... | collective-permute-start | bytes 884744 | tf_op jit(solution)/shard_map/cond/branch_1_fun/ppermute | solution.py:681
  71.1 35.0 %collective-permute-start.14 = (bf16[2,2,3,48,256]{4,3,2,1,0:T(8,128)(2,1)S(1)}, bf16[2,2,3,48,256]{4,3,2,1,0:T(8,128)(2,1)}, u32[]{:S(2)}, u32[]{:S(2)}) collective-permute-start(bf16[2,2,3,48,256]{4,3,2,1,0:T(8,128)(2,1)S(1)} %get-tuple-element.284), channel_id=1, source_target_pairs={{0,16},{2,18},{4,20},{6,22},{8,24},{10,26},{12,28},{14,30},{16,0},... | collective-permute-start | bytes 884744 | tf_op jit(solution)/shard_map/cond/branch_1_fun/ppermute | solution.py:681
  72.6 33.6 %collective-permute-start.15 = (bf16[2,2,3,48,256]{4,3,2,1,0:T(8,128)(2,1)S(1)}, bf16[2,2,3,48,256]{4,3,2,1,0:T(8,128)(2,1)}, u32[]{:S(2)}, u32[]{:S(2)}) collective-permute-start(bf16[2,2,3,48,256]{4,3,2,1,0:T(8,128)(2,1)S(1)} %get-tuple-element.284), channel_id=1, source_target_pairs={{0,24},{2,26},{4,28},{6,30},{8,16},{10,18},{12,20},{14,22},{16,8},... | collective-permute-start | bytes 884744 | tf_op jit(solution)/shard_map/cond/branch_1_fun/ppermute | solution.py:681
  73.9 34.5 %collective-permute-start.12 = (bf16[4,2,2,3,48,256]{5,4,3,2,1,0:T(8,128)(2,1)}, bf16[4,2,2,3,48,256]{5,4,3,2,1,0:T(8,128)(2,1)}, u32[]{:S(2)}, u32[]{:S(2)}) collective-permute-start(bf16[4,2,2,3,48,256]{5,4,3,2,1,0:T(8,128)(2,1)} %get-tuple-element.283), channel_id=1, source_target_pairs={{0,4},{2,6},{4,0},{6,2},{8,12},{10,14},{12,8},{14,10},{16,20},{18,... | collective-permute-start | bytes 3538952 | tf_op jit(solution)/shard_map/cond/branch_1_fun/ppermute | solution.py:681
  74.5 34.0 %collective-permute-start.16 = (bf16[512,768]{1,0:T(8,128)(2,1)S(1)}, bf16[512,768]{1,0:T(8,128)(2,1)}, u32[]{:S(2)}, u32[]{:S(2)}) collective-permute-start(bf16[512,768]{1,0:T(8,128)(2,1)S(1)} %get-tuple-element.285), channel_id=1, source_target_pairs={{0,2},{2,0},{4,6},{6,4},{8,10},{10,8},{12,14},{14,12},{16,18},{18,... | collective-permute-start | bytes 2359304 | tf_op jit(solution)/shard_map/cond/branch_1_fun/ppermute | solution.py:681
  108.5 47.5 %collective-permute-start.18 = (bf16[4,2,2,3,48,256]{5,4,3,2,1,0:T(8,128)(2,1)}, bf16[4,2,2,3,48,256]{5,4,3,2,1,0:T(8,128)(2,1)}, u32[]{:S(2)}, u32[]{:S(2)}) collective-permute-start(bf16[4,2,2,3,48,256]{5,4,3,2,1,0:T(8,128)(2,1)} %get-tuple-element.292), channel_id=1, source_target_pairs={{0,4},{2,6},{4,0},{6,2},{8,12},{10,14},{12,8},{14,10},{16,20},{18,... | collective-permute-start | bytes 3538952 | tf_op jit(solution)/shard_map/cond/branch_1_fun/ppermute | solution.py:681
  109.4 34.1 %collective-permute-start.17 = (bf16[512,768]{1,0:T(8,128)(2,1)}, bf16[512,768]{1,0:T(8,128)(2,1)}, u32[]{:S(2)}, u32[]{:S(2)}) collective-permute-start(bf16[512,768]{1,0:T(8,128)(2,1)} %get-tuple-element.287), channel_id=1, source_target_pairs={{0,2},{2,0},{4,6},{6,4},{8,10},{10,8},{12,14},{14,12},{16,18},{18,... | collective-permute-start | bytes 2359304 | tf_op jit(solution)/shard_map/cond/branch_1_fun/ppermute | solution.py:681
  110.8 30.3 %collective-permute-start.19 = (bf16[2,2,3,48,256]{4,3,2,1,0:T(8,128)(2,1)}, bf16[2,2,3,48,256]{4,3,2,1,0:T(8,128)(2,1)}, u32[]{:S(2)}, u32[]{:S(2)}) collective-permute-start(bf16[2,2,3,48,256]{4,3,2,1,0:T(8,128)(2,1)} %get-tuple-element.293), channel_id=1, source_target_pairs={{0,8},{2,10},{4,12},{6,14},{8,0},{10,2},{12,4},{14,6},{16,24},{18,... | collective-permute-start | bytes 884744 | tf_op jit(solution)/shard_map/cond/branch_1_fun/ppermute | solution.py:681
  111.5 29.6 %collective-permute-start.20 = (bf16[2,2,3,48,256]{4,3,2,1,0:T(8,128)(2,1)}, bf16[2,2,3,48,256]{4,3,2,1,0:T(8,128)(2,1)}, u32[]{:S(2)}, u32[]{:S(2)}) collective-permute-start(bf16[2,2,3,48,256]{4,3,2,1,0:T(8,128)(2,1)} %get-tuple-element.293), channel_id=1, source_target_pairs={{0,16},{2,18},{4,20},{6,22},{8,24},{10,26},{12,28},{14,30},{16,0},... | collective-permute-start | bytes 884744 | tf_op jit(solution)/shard_map/cond/branch_1_fun/ppermute | solution.py:681
  185.8 42.1 %collective-permute-start.30 = (bf16[4,2,2,3,48,256]{5,4,3,2,1,0:T(8,128)(2,1)}, bf16[4,2,2,3,48,256]{5,4,3,2,1,0:T(8,128)(2,1)}, u32[]{:S(2)}, u32[]{:S(2)}) collective-permute-start(bf16[4,2,2,3,48,256]{5,4,3,2,1,0:T(8,128)(2,1)} %get-tuple-element.332), channel_id=1, source_target_pairs={{0,4},{2,6},{4,0},{6,2},{8,12},{10,14},{12,8},{14,10},{16,20},{18,... | collective-permute-start | bytes 3538952 | tf_op jit(solution)/shard_map/cond/branch_1_fun/ppermute | solution.py:681
  230.7 42.9 %collective-permute-start.5 = (bf16[4,2,2,3,48,256]{5,4,3,2,1,0:T(8,128)(2,1)}, bf16[4,2,2,3,48,256]{5,4,3,2,1,0:T(8,128)(2,1)}, u32[]{:S(2)}, u32[]{:S(2)}) collective-permute-start(bf16[4,2,2,3,48,256]{5,4,3,2,1,0:T(8,128)(2,1)} %get-tuple-element.347), channel_id=1, source_target_pairs={{0,4},{2,6},{4,0},{6,2},{8,12},{10,14},{12,8},{14,10},{16,20},{18,... | collective-permute-start | bytes 3538952 | tf_op jit(solution)/shard_map/cond/branch_1_fun/ppermute | solution.py:681
  232.1 44.3 %collective-permute-start.1 = (bf16[512,768]{1,0:T(8,128)(2,1)}, bf16[512,768]{1,0:T(8,128)(2,1)}, u32[]{:S(2)}, u32[]{:S(2)}) collective-permute-start(bf16[512,768]{1,0:T(8,128)(2,1)} %get-tuple-element.339), channel_id=1, source_target_pairs={{0,2},{2,0},{4,6},{6,4},{8,10},{10,8},{12,14},{14,12},{16,18},{18,... | collective-permute-start | bytes 2359304 | tf_op jit(solution)/shard_map/cond/branch_1_fun/ppermute | solution.py:681
  232.7 38.8 %collective-permute-start.2 = (bf16[2,2,3,48,256]{4,3,2,1,0:T(8,128)(2,1)S(1)}, bf16[2,2,3,48,256]{4,3,2,1,0:T(8,128)(2,1)}, u32[]{:S(2)}, u32[]{:S(2)}) collective-permute-start(bf16[2,2,3,48,256]{4,3,2,1,0:T(8,128)(2,1)S(1)} %get-tuple-element.341), channel_id=1, source_target_pairs={{0,8},{2,10},{4,12},{6,14},{8,0},{10,2},{12,4},{14,6},{16,24},{18,... | collective-permute-start | bytes 884744 | tf_op jit(solution)/shard_map/cond/branch_1_fun/ppermute | solution.py:681
  232.7 38.8 %collective-permute-start.3 = (bf16[2,2,3,48,256]{4,3,2,1,0:T(8,128)(2,1)}, bf16[2,2,3,48,256]{4,3,2,1,0:T(8,128)(2,1)}, u32[]{:S(2)}, u32[]{:S(2)}) collective-permute-start(bf16[2,2,3,48,256]{4,3,2,1,0:T(8,128)(2,1)} %get-tuple-element.342), channel_id=1, source_target_pairs={{0,16},{2,18},{4,20},{6,22},{8,24},{10,26},{12,28},{14,30},{16,0},... | collective-permute-start | bytes 884744 | tf_op jit(solution)/shard_map/cond/branch_1_fun/ppermute | solution.py:681
  235.7 35.8 %collective-permute-start.4 = (bf16[2,2,3,48,256]{4,3,2,1,0:T(8,128)(2,1)}, bf16[2,2,3,48,256]{4,3,2,1,0:T(8,128)(2,1)}, u32[]{:S(2)}, u32[]{:S(2)}) collective-permute-start(bf16[2,2,3,48,256]{4,3,2,1,0:T(8,128)(2,1)} %get-tuple-element.343), channel_id=1, source_target_pairs={{0,24},{2,26},{4,28},{6,30},{8,16},{10,18},{12,20},{14,22},{16,8},... | collective-permute-start | bytes 884744 | tf_op jit(solution)/shard_map/cond/branch_1_fun/ppermute | solution.py:681
  283.0 32.2 %collective-permute-start.11 = (bf16[4,2,2,3,48,256]{5,4,3,2,1,0:T(8,128)(2,1)}, bf16[4,2,2,3,48,256]{5,4,3,2,1,0:T(8,128)(2,1)}, u32[]{:S(2)}, u32[]{:S(2)}) collective-permute-start(bf16[4,2,2,3,48,256]{5,4,3,2,1,0:T(8,128)(2,1)} %get-tuple-element.391), channel_id=1, source_target_pairs={{0,4},{2,6},{4,0},{6,2},{8,12},{10,14},{12,8},{14,10},{16,20},{18,... | collective-permute-start | bytes 3538952 | tf_op jit(solution)/shard_map/cond/branch_1_fun/ppermute | solution.py:681
  284.3 28.7 %collective-permute-start.10 = (bf16[2,2,3,48,256]{4,3,2,1,0:T(8,128)(2,1)}, bf16[2,2,3,48,256]{4,3,2,1,0:T(8,128)(2,1)S(1)}, u32[]{:S(2)}, u32[]{:S(2)}) collective-permute-start(bf16[2,2,3,48,256]{4,3,2,1,0:T(8,128)(2,1)} %get-tuple-element.387), channel_id=1, source_target_pairs={{0,24},{2,26},{4,28},{6,30},{8,16},{10,18},{12,20},{14,22},{16,8},... | collective-permute-start | bytes 884744 | tf_op jit(solution)/shard_map/cond/branch_1_fun/ppermute | solution.py:681
  288.7 29.3 %collective-permute-start.7 = (bf16[512,768]{1,0:T(8,128)(2,1)}, bf16[512,768]{1,0:T(8,128)(2,1)}, u32[]{:S(2)}, u32[]{:S(2)}) collective-permute-start(bf16[512,768]{1,0:T(8,128)(2,1)} %get-tuple-element.383), channel_id=1, source_target_pairs={{0,2},{2,0},{4,6},{6,4},{8,10},{10,8},{12,14},{14,12},{16,18},{18,... | collective-permute-start | bytes 2359304 | tf_op jit(solution)/shard_map/cond/branch_1_fun/ppermute | solution.py:681
  318.0 28.4 %collective-permute-start.22 = (bf16[2,4,2,48,384]{4,3,2,1,0:T(8,128)(2,1)}, bf16[2,4,2,48,384]{4,3,2,1,0:T(8,128)(2,1)}, u32[]{:S(2)}, u32[]{:S(2)}) collective-permute-start(bf16[2,4,2,48,384]{4,3,2,1,0:T(8,128)(2,1)} %get-tuple-element.397), channel_id=1, source_target_pairs={{0,4},{2,6},{4,0},{6,2},{8,12},{10,14},{12,8},{14,10},{16,20},{18,... | collective-permute-start | bytes 1769480 | tf_op jit(solution)/shard_map/cond/branch_1_fun/ppermute | solution.py:681
  325.0 28.6 %collective-permute-start.26 = (bf16[2,2,3,48,256]{4,3,2,1,0:T(8,128)(2,1)}, bf16[2,2,3,48,256]{4,3,2,1,0:T(8,128)(2,1)}, u32[]{:S(2)}, u32[]{:S(2)}) collective-permute-start(bf16[2,2,3,48,256]{4,3,2,1,0:T(8,128)(2,1)} %get-tuple-element.409), channel_id=1, source_target_pairs={{0,8},{2,10},{4,12},{6,14},{8,0},{10,2},{12,4},{14,6},{16,24},{18,... | collective-permute-start | bytes 884744 | tf_op jit(solution)/shard_map/cond/branch_1_fun/ppermute | solution.py:681
  325.1 28.5 %collective-permute-start.27 = (bf16[2,2,3,48,256]{4,3,2,1,0:T(8,128)(2,1)}, bf16[2,2,3,48,256]{4,3,2,1,0:T(8,128)(2,1)}, u32[]{:S(2)}, u32[]{:S(2)}) collective-permute-start(bf16[2,2,3,48,256]{4,3,2,1,0:T(8,128)(2,1)} %get-tuple-element.410), channel_id=1, source_target_pairs={{0,16},{2,18},{4,20},{6,22},{8,24},{10,26},{12,28},{14,30},{16,0},... | collective-permute-start | bytes 884744 | tf_op jit(solution)/shard_map/cond/branch_1_fun/ppermute | solution.py:681
  363.0 38.3 %collective-permute-start.44 = (f32[512,768]{1,0:T(8,128)}, f32[512,768]{1,0:T(8,128)S(1)}, u32[]{:S(2)}, u32[]{:S(2)}) collective-permute-start(f32[512,768]{1,0:T(8,128)} %get-tuple-element.586.refs_2_), channel_id=1, source_target_pairs={{0,1},{1,0},{2,3},{3,2},{4,5},{5,4},{6,7},{7,6},{8,9},{9,8},{10,11... | collective-permute-start | bytes 4718600 | tf_op jit(solution)/shard_map/ppermute | solution.py:693
  367.1 34.2 %collective-permute-start.43 = (bf16[512,768]{1,0:T(8,128)(2,1)S(1)}, bf16[512,768]{1,0:T(8,128)(2,1)}, u32[]{:S(2)}, u32[]{:S(2)}) collective-permute-start(bf16[512,768]{1,0:T(8,128)(2,1)S(1)} %get-tuple-element.585.refs_0_), channel_id=1, source_target_pairs={{0,1},{1,0},{2,3},{3,2},{4,5},{5,4},{6,7},{7,6},{8,9},{9,8},{10,11... | collective-permute-start | bytes 2359304 | tf_op jit(solution)/shard_map/ppermute | solution.py:693
  (70 other events, 1397.6 us)

commit v3 on v2

--- a/solution.py
+++ b/solution.py
@@ -101,8 +101,8 @@
 
 
 def attn_fwd_kernel(
-    heads, piece, c_ref, x_ref, srow_ref, scol_ref, g_ref, b_ref, pb_ref, a0, a1_, b0, b1_,
-    att_ref, qkv_ref, kt_ref, o_ref, ot_ref, lse_ref,
+    heads, piece, c_ref, x_ref, srow_ref, scol_ref, ln_ref, pb_ref, a0, a1_, b0, b1_,
+    att_ref, att_other_ref, qkv_ref, kt_ref, o_ref, ot_ref, lse_ref,
     w_s, wo_s, bias_s, sems,
 ):
     cols = heads * HD
@@ -127,7 +127,7 @@
             c.wait()
 
     xhat, _ = norm_parts(x_ref[0].astype(f32))
-    a1 = (xhat * g_ref[...] + b_ref[...]).astype(bf16)
+    a1 = (xhat * ln_ref[0:1] + ln_ref[1:2]).astype(bf16)
     proj = (nn_dot(a1, w_s[...]) + pb_ref[...]).astype(bf16)
     for j in range(3):
         for p in range(pairs):
@@ -157,10 +157,18 @@
 
     for p in range(pairs):
         o_ref[0, :, p * 128 : (p + 1) * 128] = ot_ref[0, p].T
-    att_ref[0] = nt_dot(o_ref[0], wo_s[...]).astype(bf16)
-
-
-def attn_fwd(coords, x, seg_row, seg_col, gain, bias, proj_bias, pa, pb):
+    att = nt_dot(o_ref[0], wo_s[...]).astype(bf16)
+
+    @pl.when(pl.program_id(0) == c_ref[3])
+    def _():
+        att_ref[...] = att
+
+    @pl.when(pl.program_id(0) != c_ref[3])
+    def _():
+        att_other_ref[...] = att
+
+
+def attn_fwd(coords, x, seg_row, seg_col, ln, proj_bias, pa, pb):
     rows, seq, width = x.shape
     cols = proj_bias.shape[-1] // 3
     heads = cols // HD
@@ -170,7 +178,8 @@
     row4 = lambda r, *_: (r, 0, 0, 0)
     row5 = lambda r, *_: (r, 0, 0, 0, 0)
     outs = [
-        ((rows, seq, width), bf16, (1, seq, width), row3),
+        ((seq, width), bf16, (seq, width), lambda *_: (0, 0)),
+        ((seq, width), bf16, (seq, width), lambda *_: (0, 0)),
         ((rows, 3, pairs, seq, 128), bf16, (1, 3, pairs, seq, 128), row5),
         ((rows, pairs, 128, seq), bf16, (1, pairs, 128, seq), row4),
         ((rows, seq, cols), bf16, (1, seq, cols), row3),
@@ -187,8 +196,7 @@
                 pl.BlockSpec((1, seq, width), row3),
                 pl.BlockSpec((1, 1, seq), row3),
                 pl.BlockSpec((1, seq, 1), row3),
-                full_spec((1, width)),
-                full_spec((1, width)),
+                full_spec((2, width)),
                 full_spec((1, 3 * cols)),
                 ANY, ANY, ANY, ANY,
             ],
@@ -203,12 +211,12 @@
         compiler_params=params(1),
         cost_estimate=cost(2e10, 1e7, 3e6),
         name="attn_fwd",
-    )(coords, x, seg_row, seg_col, gain, bias, proj_bias, *pa, *pb)
+    )(coords, x, seg_row, seg_col, ln, proj_bias, *pa, *pb)
 
 
 def attn_bwd_kernel(
     heads, piece, c_ref, dxr_ref, dxr2_ref, x_ref, srow_ref, scol_ref, ln_ref, qkv_ref, kt_ref, o_ref, ot_ref, lse_ref, a0, a1_, b0, b1_,
-    da1_ref, ga0_ref, ga1_ref, gb0_ref, gb1_ref, bsum_ref,
+    da1_ref, da1_other_ref, ga0_ref, ga1_ref, gb0_ref, gb1_ref, bsum_ref,
     w_s, wo_s, bias_s, dp_s, gw_s, go_s, sems,
 ):
     cols = heads * HD
@@ -269,7 +277,16 @@
         dp_s[:, 2 * cols + p * 128 : 2 * cols + (p + 1) * 128] = dv.astype(bf16)
 
     dproj = dp_s[...]
-    da1_ref[0] = nt_dot(dproj, w_s[...]).astype(bf16)
+    da1 = nt_dot(dproj, w_s[...]).astype(bf16)
+
+    @pl.when(step == c_ref[3])
+    def _():
+        da1_ref[...] = da1
+
+    @pl.when(step != c_ref[3])
+    def _():
+        da1_other_ref[...] = da1
+
     bsum_ref[...] += jnp.sum(dproj.astype(f32), axis=0, keepdims=True)
     xhat1, _ = norm_parts(x_ref[0].astype(f32))
     a1 = (xhat1 * ln_ref[0:1] + ln_ref[1:2]).astype(bf16)
@@ -304,7 +321,7 @@
     return pl.pallas_call(
         functools.partial(attn_bwd_kernel, heads, piece),
         out_shape=[
-            jax.ShapeDtypeStruct((rows, seq, width), bf16),
+            *[jax.ShapeDtypeStruct((seq, width), bf16)] * 2,
             *[jax.ShapeDtypeStruct(gshape, bf16)] * 4,
             jax.ShapeDtypeStruct((1, 3 * cols), f32),
         ],
@@ -324,7 +341,7 @@
                 ANY, ANY, ANY, ANY,
             ],
             out_specs=[
-                tok,
+                *[full_spec((seq, width))] * 2,
                 *[full_spec(gshape)] * 4,
                 full_spec((1, 3 * cols)),
             ],
@@ -406,15 +423,14 @@
     )(*places, vs)
 
 
-def mid_kernel(x_ref, parts_ref, vec_ref, x2_ref, a2_ref):
-    att = jnp.sum(parts_ref[...].astype(f32), axis=0)
-    x2 = x_ref[...].astype(f32) + att + vec_ref[0:1]
+def mid_kernel(x_ref, own_ref, got_ref, vec_ref, x2_ref, a2_ref):
+    x2 = x_ref[...].astype(f32) + (own_ref[...].astype(f32) + got_ref[...].astype(f32)) + vec_ref[0:1]
     x2_ref[...] = x2
     xhat, _ = norm_parts(x2)
     a2_ref[...] = (xhat * vec_ref[1:2] + vec_ref[2:3]).astype(bf16)
 
 
-def mid(x, partial, vec):
+def mid(x, own, got, vec):
     tokens, width = x.shape
     tile = pl.BlockSpec((TILE, width), lambda i: (i, 0))
     return pl.pallas_call(
@@ -424,15 +440,12 @@
             jax.ShapeDtypeStruct((tokens, width), bf16),
         ],
         grid=(tokens // TILE,),
-        in_specs=[
-            tile, pl.BlockSpec((partial.shape[0], TILE, width), lambda i: (0, i, 0)),
-            full_spec((3, width)),
-        ],
+        in_specs=[tile, tile, tile, full_spec((3, width))],
         out_specs=[tile, tile],
         compiler_params=params(1),
         cost_estimate=cost(1e7, 5e6),
         name="mid_norm",
-    )(x, partial, vec)
+    )(x, own, got, vec)
 
 
 def ffn_kernel(first, count, piece, groups, c_ref, te_ref, n_ref, *refs):
@@ -443,75 +456,109 @@
     rest = rest[2 * count :]
     z_ref, da_ref, *rest = rest
     g_refs = [rest[2 * c : 2 * c + 2] for c in range(count)]
-    gub_ref, wu_s, wd_s, gu_s, gd_s, sems = rest[2 * count :]
+    gub_ref, wu_s, wd_s, gu_s, gd_s, x_s, dy_s, z_s, da_s, sems, in_sems, out_sems = rest[2 * count :]
     experts = wu_s.shape[0]
     hc = wu_s.shape[2] // count
-    i = pl.program_id(0)
+    tiles = x_s.shape[0]
+    per = tiles // groups
     spots = [(ry, rz, rx) for ry in range(2) for rz in range(4) for rx in range(2)]
 
     def rows_of(ry, rz, rx):
-        block = (c_ref[0] ^ rz) * 4 + (c_ref[1] ^ ry) * 2 + (c_ref[2] ^ rx)
+        block = rz * 4 + (c_ref[1] ^ ry) * 2 + (c_ref[2] ^ rx)
         return pl.ds(pl.multiple_of(block * piece, 16), piece)
 
-    @pl.when(i == 0)
-    def _():
-        copies = []
-        for c in range(count):
-            for ry, rz, rx in spots:
-                for k, w_s in ((0, wu_s), (1, wd_s)):
-                    copies.append(
-                        pltpu.make_async_copy(
-                            w_refs[c][ry].at[rz, rx, k],
-                            w_s.at[:, rows_of(ry, rz, rx), pl.ds(c * hc, hc)],
-                            sems.at[len(copies)],
-                        )
+    def tile_of(ref, i):
+        return ref.at[pl.ds(pl.multiple_of(i * TILE, TILE), TILE), :]
+
+    def reads(i):
+        pairs = [(xs_ref, x_s), (dys_ref, dy_s)]
+        if not first:
+            pairs += [(zin_ref, z_s), (din_ref, da_s)]
+        return [
+            pltpu.make_async_copy(tile_of(src, i), dst.at[i], in_sems.at[k, i])
+            for k, (src, dst) in enumerate(pairs)
+        ]
+
+    def writes(i):
+        return [
+            pltpu.make_async_copy(src.at[i], tile_of(dst, i), out_sems.at[k, i])
+            for k, (src, dst) in enumerate([(z_s, z_ref), (da_s, da_ref)])
+        ]
+
+    copies = []
+    for c in range(count):
+        for ry, rz, rx in spots:
+            for k, w_s in ((0, wu_s), (1, wd_s)):
+                copies.append(
+                    pltpu.make_async_copy(
+                        w_refs[c][ry].at[rz, rx, k],
+                        w_s.at[:, rows_of(ry, rz, rx), pl.ds(c * hc, hc)],
+                        sems.at[len(copies)],
                     )
-        for c in copies:
+                )
+    for c in reads(0):
+        c.start()
+    for c in copies:
+        c.start()
+
+    @pl.loop(1, tiles)
+    def _(i):
+        for c in reads(i):
             c.start()
-        gu_s[...] = jnp.zeros_like(gu_s)
-        gd_s[...] = jnp.zeros_like(gd_s)
-        gub_ref[...] = jnp.zeros_like(gub_ref)
-        for c in copies:
+
+    gu_s[...] = jnp.zeros_like(gu_s)
+    gd_s[...] = jnp.zeros_like(gd_s)
+    gub_ref[...] = jnp.zeros_like(gub_ref)
+    for c in copies:
+        c.wait()
+
+    @pl.loop(0, tiles)
+    def _(i):
+        group = i // per
+        live = i - group * per < n_ref[group]
+        for c in reads(i):
             c.wait()
 
-    per = pl.num_programs(0) // groups
-    group = i // per
-    live = i - group * per < n_ref[group]
-
-    @pl.when(live)
-    def _():
-        e = te_ref[i]
-        x = xs_ref[...]
-        dy = dys_ref[...]
-        u = nn_dot(x, wu_s[e]) + ub_ref[e]
-        act, slope = gelu_parts(u)
-        act = act.astype(bf16)
-        du = (nn_dot(dy, wd_s[e]) * slope).astype(bf16)
-        z = nt_dot(act, wd_s[e])
-        da = nt_dot(du, wu_s[e])
-        if not first:
-            z = z + zin_ref[...].astype(f32)
-            da = da + din_ref[...].astype(f32)
-        z_ref[...] = z.astype(bf16)
-        da_ref[...] = da.astype(bf16)
-        gd_s[e] += tn_dot(dy, act)
-        gu_s[e] += tn_dot(x, du)
-        gub_ref[e] += jnp.sum(du.astype(f32), axis=0, keepdims=True)
-
-    @pl.when(jnp.logical_not(live))
-    def _():
-        z_ref[...] = jnp.zeros_like(z_ref)
-        da_ref[...] = jnp.zeros_like(da_ref)
-
-    @pl.when(i == pl.num_programs(0) - 1)
-    def _():
-        for c in range(count):
-            lanes = pl.ds(c * hc, hc)
-            for ry, rz, rx in spots:
-                rows = rows_of(ry, rz, rx)
-                for e in range(experts):
-                    g_refs[c][ry][rz, rx, 0, e] = gu_s[e, rows, lanes].astype(bf16)
-                    g_refs[c][ry][rz, rx, 1, e] = gd_s[e, rows, lanes].astype(bf16)
+        @pl.when(live)
+        def _():
+            e = te_ref[i]
+            x = x_s[i]
+            dy = dy_s[i]
+            u = nn_dot(x, wu_s[e]) + ub_ref[e]
+            act, slope = gelu_parts(u)
+            act = act.astype(bf16)
+            du = (nn_dot(dy, wd_s[e]) * slope).astype(bf16)
+            z = nt_dot(act, wd_s[e])
+            da = nt_dot(du, wu_s[e])
+            if not first:
+                z = z + z_s[i].astype(f32)
+                da = da + da_s[i].astype(f32)
+            z_s[i] = z.astype(bf16)
+            da_s[i] = da.astype(bf16)
+            gd_s[e] += tn_dot(dy, act)
+            gu_s[e] += tn_dot(x, du)
+            gub_ref[e] += jnp.sum(du.astype(f32), axis=0, keepdims=True)
+
+        @pl.when(jnp.logical_not(live))
+        def _():
+            z_s[i] = jnp.zeros(z_s.shape[1:], bf16)
+            da_s[i] = jnp.zeros(da_s.shape[1:], bf16)
+
+        for c in writes(i):
+            c.start()
+
+    for c in range(count):
+        lanes = pl.ds(c * hc, hc)
+        for ry, rz, rx in spots:
+            rows = rows_of(ry, rz, rx)
+            for e in range(experts):
+                g_refs[c][ry][rz, rx, 0, e] = gu_s[e, rows, lanes].astype(bf16)
+                g_refs[c][ry][rz, rx, 1, e] = gd_s[e, rows, lanes].astype(bf16)
+
+    @pl.loop(0, tiles)
+    def _(i):
+        for c in writes(i):
+            c.wait()
 
 
 def ffn(coords, tile_expert, used, xs, dys, up_b, weights, carry):
@@ -523,7 +570,6 @@
     gshape = weights[0][0].shape
     experts, piece, hc = gshape[3:]
     hid = hc * count
-    tile = pl.BlockSpec((TILE, width), lambda i, *_: (i, 0))
     out = pl.pallas_call(
         functools.partial(ffn_kernel, first, count, piece, groups),
         out_shape=[
@@ -534,20 +580,19 @@
         ],
         grid_spec=pltpu.PrefetchScalarGridSpec(
             num_scalar_prefetch=3,
-            grid=(tiles,),
+            grid=(1,),
             in_specs=[
-                tile, tile, full_spec((experts, 1, hid)), *([] if first else [tile, tile]),
+                ANY, ANY, full_spec((experts, 1, hid)), *([] if first else [ANY, ANY]),
                 *[ANY] * (2 * count),
             ],
-            out_specs=[
-                tile, tile, *[full_spec(gshape)] * (2 * count), full_spec((experts, 1, hid)),
-            ],
+            out_specs=[ANY, ANY, *[full_spec(gshape)] * (2 * count), full_spec((experts, 1, hid))],
             scratch_shapes=[
-                pltpu.VMEM((experts, width, hid), bf16),
-                pltpu.VMEM((experts, width, hid), bf16),
-                pltpu.VMEM((experts, width, hid), f32),
-                pltpu.VMEM((experts, width, hid), f32),
+                *[pltpu.VMEM((experts, width, hid), bf16)] * 2,
+                *[pltpu.VMEM((experts, width, hid), f32)] * 2,
+                *[pltpu.VMEM((tiles, TILE, width), bf16)] * 4,
                 pltpu.SemaphoreType.DMA((32 * count,)),
+                pltpu.SemaphoreType.DMA((2 if first else 4, tiles)),
+                pltpu.SemaphoreType.DMA((2, tiles)),
             ],
         ),
         compiler_params=params(1),
@@ -620,15 +665,16 @@
     )(*prefetch, *args)
 
 
-def sums_y_kernel(keep, got, own, *sends):
-    add = lambda rz: keep[rz].astype(f32) + got[rz].astype(f32)
-    own[...] = add(0)
-    for rz, send in zip((1, 2, 3), sends):
-        send[...] = add(rz).astype(bf16)
-
-
-def sums_z_kernel(own, r1, r2, r3, mine, near):
-    add = lambda k: own[k] + r1[k].astype(f32) + r2[k].astype(f32) + r3[k].astype(f32)
+def sums_y_kernel(c_ref, keep, got, own, send):
+    for k in range(4):
+        send[k] = (keep[k].astype(f32) + got[k].astype(f32)).astype(bf16)
+    here = c_ref[0]
+    own[...] = keep[here].astype(f32) + got[here].astype(f32)
+
+
+def sums_z_kernel(c_ref, own, got, mine, near):
+    others = [c_ref[0] ^ rz for rz in (1, 2, 3)]
+    add = lambda k: own[k] + sum(got[z, k].astype(f32) for z in others)
     mine[...] = add(0)
     near[...] = add(1).astype(bf16)
 
@@ -639,19 +685,19 @@
         send[...] = (keep[1].astype(f32) + got[1].astype(f32)).astype(bf16)
 
 
-def four_sums_kernel(a_own, a_got, b_own, b_got, own, *sends):
-    add = lambda rz: (a_own[rz] + a_got[rz].astype(f32), b_own[rz] + b_got[rz].astype(f32))
-    own[0], own[1] = add(0)
-    for rz, send in zip((1, 2, 3), sends):
-        va, vb = add(rz)
-        send[0] = va.astype(bf16)
-        send[1] = vb.astype(bf16)
-
-
-def qkv_grad_kernel(own, r1, r2, r3, g_qkv, g_out):
-    add = lambda k, j: (
-        own[k, j] + r1[k, j].astype(f32) + r2[k, j].astype(f32) + r3[k, j].astype(f32)
-    )
+def four_sums_kernel(c_ref, a_own, a_got, b_own, b_got, own, send):
+    for rz in range(4):
+        va = a_own[rz] + a_got[rz].astype(f32)
+        vb = b_own[rz] + b_got[rz].astype(f32)
+        if rz == 0:
+            own[0], own[1] = va, vb
+        send[c_ref[0] ^ rz, 0] = va.astype(bf16)
+        send[c_ref[0] ^ rz, 1] = vb.astype(bf16)
+
+
+def qkv_grad_kernel(c_ref, own, got, g_qkv, g_out):
+    others = [c_ref[0] ^ rz for rz in (1, 2, 3)]
+    add = lambda k, j: own[k, j] + sum(got[z, k, j].astype(f32) for z in others)
     g_qkv[0] = add(0, 0)
     g_qkv[1] = add(0, 1)
     g_qkv[2] = add(1, 0)
@@ -659,8 +705,9 @@
 
 
 def rows_kernel(c_ref, *refs):
-    for k in range(2):
-        mine, other, out = refs[2 * k], refs[2 * k + 1], refs[4 + k]
+    n = len(refs) // 3
+    for k in range(n):
+        mine, other, out = refs[2 * k], refs[2 * k + 1], refs[2 * n + k]
         out[c_ref[3]] = mine[...]
         out[1 - c_ref[3]] = other[...]
 
@@ -697,28 +744,32 @@
     return deal(jnp.broadcast_to(v, (lax.axis_size("mp"),) + v.shape))
 
 
-def gather_staged(a, b, size):
+def gather_z(a, b, size):
     both = jnp.stack([a, b])
     blocks = [both] + [flip(both, 4 * rz, size) for rz in (1, 2, 3)]
-    a0 = jnp.stack([v[0] for v in blocks])
-    b0 = jnp.stack([v[1] for v in blocks])
+    return jnp.stack([v[0] for v in blocks]), jnp.stack([v[1] for v in blocks])
+
+
+def gather_xy(a0, b0, size):
     a0 = jnp.stack([a0, flip(a0, 1, size)])
     b0 = jnp.stack([b0, flip(b0, 2, size)])
     return (a0, flip(a0, 2, size)), (b0, flip(b0, 1, size))
 
 
-def attn_sums_xy(ga, gb, size):
-    shape = ga[0].shape[1:]
-    a_own, a_send, b_own, b_send = whole(
+def attn_sums_1(keep, got, dep):
+    shape = keep[0].shape[1:]
+    return whole(
         two_sums_kernel, "two_sums", [(shape, f32), (shape, bf16)] * 2,
-        ga[0], flip(ga[1], 2, size), gb[0], flip(gb[1], 1, size),
-    )
-    shape = (2,) + shape[1:]
-    own, *sends = whole(
-        four_sums_kernel, "four_sums", [(shape, f32), *[(shape, bf16)] * 3],
-        a_own, flip(a_send, 1, size), b_own, flip(b_send, 2, size),
-    )
-    return own, sends
+        after(keep[0], dep), got[0], keep[1], got[1],
+    )
+
+
+def attn_sums_2(coords, own, got, dep):
+    shape = (2,) + own[0].shape[1:]
+    return whole(
+        four_sums_kernel, "four_sums", [(shape, f32), ((4,) + shape, bf16)],
+        own[0], got[0], own[1], got[1], prefetch=(after(coords, dep),),
+    )
 
 
 def gather_plain(w):
@@ -727,9 +778,7 @@
     return full.reshape(n, 16, rows // 16, cols).swapaxes(0, 1)
 
 
-def gather_pieces(a, b, size, staged):
-    if staged:
-        return gather_staged(a, b, size)
+def gather_pieces_plain(a, b):
     blocks = [gather_plain(v) for v in (a, b)]
     blocks = [v.reshape((4, 2, 2) + v.shape[1:]) for v in blocks]
     fa = jnp.moveaxis(blocks[0], 0, 2)
@@ -755,23 +804,30 @@
     )
 
 
-def along_z(p, size):
-    return jnp.stack([p] + [flip(p, 4 * rz, size) for rz in (1, 2, 3)])
-
-
-def sums_y(pair, size):
-    shape = pair[0].shape[1:]
+def deal_z(v):
+    groups = [[4 * z + k for z in range(4)] for k in range(4)]
+    return lax.all_to_all(v, "dp", 0, 0, axis_index_groups=groups, tiled=True)
+
+
+def along_z(p):
+    return deal_z(jnp.broadcast_to(p, (4,) + p.shape))
+
+
+def sums_y(coords, pair, size):
+    shape = pair[0].shape
     return whole(
-        sums_y_kernel, "sums_y", [(shape, f32), *[(shape, bf16)] * 3],
-        pair[0], flip(pair[1], 2, size),
-    )
-
-
-def sums_z(parts_y, size):
-    own, *sends = parts_y
-    got = [flip(v, 4 * rz, size) for rz, v in zip((1, 2, 3), sends)]
+        sums_y_kernel, "sums_y", [(shape[1:], f32), (shape, bf16)],
+        pair[0], flip(pair[1], 2, size), prefetch=(coords,),
+    )
+
+
+def sums_z(coords, parts_y):
+    own, send = parts_y
     shape = own.shape[1:]
-    return whole(sums_z_kernel, "sums_z", [(shape, f32), (shape, bf16)], own, *got)
+    return whole(
+        sums_z_kernel, "sums_z", [(shape, f32), (shape, bf16)], own, deal_z(send),
+        prefetch=(coords,),
+    )
 
 
 def expert_pieces_plain(w_up, w_down):
@@ -789,17 +845,6 @@
     v = jnp.moveaxis(v, 0, 2)
     v = v.reshape(v.shape[:2] + (-1, v.shape[-1])).astype(f32)
     return lax.psum_scatter(v, "dp", scatter_dimension=2, tiled=True)
-
-
-def sum_small(v, size):
-    if size & (size - 1):
-        return lax.psum(v, ("dp", "mp"))
-    v = v + swap(v)
-    mask = 1
-    while mask < size:
-        v = v + flip(v, mask, size)
-        mask *= 2
-    return v
 
 
 def token_plan(segments, modality, experts):
@@ -845,25 +890,30 @@
     by_core = (parts, mine_tokens, width)
     dy = cotangent.reshape(tokens, width)
     rows_here = lambda v: lax.dynamic_slice_in_dim(v, part * mine_rows, mine_rows, 0)
-    x_mine = rows_here(layer_input).reshape(mine_tokens, width)
-    dy_mine = rows_here(cotangent).reshape(mine_tokens, width)
     col_start = part * cols
-    q_b = lax.dynamic_slice_in_dim(qv_bias[0], col_start, cols)
-    v_b = lax.dynamic_slice_in_dim(qv_bias[1], col_start, cols)
-    proj_bias = jnp.concatenate([q_b, jnp.zeros_like(q_b), v_b]).reshape(1, 3 * cols)
-    seg_row, seg_col = segments.reshape(rows, 1, seq), segments.reshape(rows, seq, 1)
-    vec = jnp.concatenate([out_bias[None], ln_gain[1:2], ln_bias[1:2]])
-    ln1 = jnp.concatenate([ln_gain[0:1], ln_bias[0:1]])
-    w_ab = w_qkv[:2], jnp.stack([w_qkv[2], w_out])
+    seg_row = segments.reshape(rows, 1, seq)
+
+    def small_inputs():
+        q_b = lax.dynamic_slice_in_dim(qv_bias[0], col_start, cols)
+        v_b = lax.dynamic_slice_in_dim(qv_bias[1], col_start, cols)
+        return (
+            rows_here(layer_input).reshape(mine_tokens, width),
+            rows_here(cotangent).reshape(mine_tokens, width),
+            jnp.concatenate([q_b, jnp.zeros_like(q_b), v_b]).reshape(1, 3 * cols),
+            segments.reshape(rows, seq, 1),
+            jnp.concatenate([out_bias[None], ln_gain[1:2], ln_bias[1:2]]),
+            jnp.concatenate([ln_gain[0:1], ln_bias[0:1]]),
+        )
 
     def fwd(coords, pa, pb):
-        att, *saved = attn_fwd(
-            coords, layer_input, seg_row, seg_col, ln_gain[0:1], ln_bias[0:1], proj_bias, pa, pb
+        own, other, *saved = attn_fwd(coords, layer_input, seg_row, seg_col, ln1, proj_bias, pa, pb)
+        return (saved, *mid(x_mine, own, swap(other), vec))
+
+    def bwd(coords, dxr, dx2, saved, pa, pb):
+        own, other, *rest = attn_bwd(
+            coords, *dxr, layer_input, seg_row, seg_col, ln1, saved, pa, pb
         )
-        return (saved, *mid(x_mine, deal(att.reshape(by_core)), vec))
-
-    def bwd(coords, dxr, saved, pa, pb):
-        return attn_bwd(coords, *dxr, layer_input, seg_row, seg_col, ln1, saved, pa, pb)
+        return (*norm_grad((own, swap(other)), x_mine, dx2, ln_gain[0:1], False), *rest)
 
     def halves(v):
         take = lambda k: lax.dynamic_slice_in_dim(v, k * mine_tokens, mine_tokens, 0)
@@ -876,10 +926,23 @@
             bias_of = jnp.where(kinds == e, down_bias[e][None], bias_of)
         return (x2 + (z_sum + bias_of)).astype(bf16)
 
+    def small_rows(sums1, sums2, bsum, g_upb, g_down_bias):
+        sides = bsum.reshape(3, cols)
+        g_qv = lax.dynamic_update_slice(
+            jnp.zeros((2, width), f32), jnp.stack([sides[0], sides[2]]), (jnp.int32(0), col_start)
+        )
+        g_upb_full = lax.dynamic_update_slice(
+            jnp.zeros((experts, up_bias.shape[1]), f32), g_upb, (jnp.int32(0), hid_start)
+        )
+        return jnp.concatenate(
+            [sums1[0:2], sums2[0:3], g_down_bias / parts, g_qv, g_upb_full.reshape(-1, width)]
+        )
+
     if staged:
         x_bit = me % 2
         coords = jnp.stack([me // 4, (me // 2) % 2, x_bit, part]).astype(jnp.int32)
         pred = me < size
+        inner = part < parts
         half = hid // 2
         hid_start = part * hid + x_bit * half
         hc = half // CHUNKS
@@ -900,113 +963,152 @@
                 jnp.stack([keep[..., c * hc : (c + 1) * hc], near[..., c * hc : (c + 1) * hc]])
                 for c in range(CHUNKS)
             ]
-            pa, pb = gather_pieces(*w_ab, size, True)
+            ab = gather_z(w_qkv[:2], jnp.stack([w_qkv[2], w_out]), size)
             mods, pos, tile_expert, used = token_plan(segments, modality, experts)
             plan = flip(jnp.concatenate([pos, tile_expert, used]), 1, size)
-            dys = sort_tokens([(pos.reshape(1, tokens), dy)], tiles, 0, 2)
-            hot = (mods[:, None] == jnp.arange(experts, dtype=jnp.int32)).astype(bf16)
+            return pieces, ab, mods, pos, plan, tile_expert, used, small_inputs()
+
+        pieces, ab, mods, pos, plan, tile_expert, used, smalls = phase(pred, begin)
+        x_mine, dy_mine, proj_bias, seg_col, vec, ln1 = smalls
+
+        def weights_in():
+            def inside():
+                pos_row = pos.reshape(1, tokens)
+                dys = sort_tokens([(pos_row, dy)], tiles, 0, 2)
+                hot = (mods[:, None] == jnp.arange(experts, dtype=jnp.int32)).astype(bf16)
+                return (
+                    *gather_xy(*ab, size), halves(pos), halves(plan),
+                    jnp.concatenate([tile_expert, plan[tokens : tokens + tiles]]),
+                    jnp.concatenate([used, plan[tokens + tiles :]]), dys, tn_dot(hot, dy),
+                )
+
+            return along_z(pieces[0]), phase(inner, inside)
+
+        z0, (pa, pb, pos_here, pos_near, tile_expert, used, dys, g_down_bias) = phase(
+            pred, weights_in
+        )
+
+        def forward():
             return (
-                pieces, pa, pb, mods, pos, tile_expert, used, plan,
-                dys, tn_dot(hot, dy), along_z(pieces[0], size),
+                *phase(inner, lambda: fwd(coords, pa, pb)), flip(z0, 2, size),
+                along_z(pieces[1]), flip(dy_mine, 1, size),
             )
 
-        (pieces, pa, pb, mods, pos, tile_expert, used, plan, dys, g_down_bias,
-         z0) = phase(pred, begin)
-        pos_here = halves(pos)
-        pos_near = halves(plan)
-        tile_expert = jnp.concatenate([tile_expert, plan[tokens : tokens + tiles]])
-        used = jnp.concatenate([used, plan[tokens + tiles :]])
-
-        saved, x2, a2, y0, z1, dy_near = phase(
-            pred,
-            lambda: (
-                *fwd(coords, pa, pb), flip(z0, 2, size), along_z(pieces[1], size),
-                flip(dy_mine, 1, size),
-            ),
-        )
+        saved, x2, a2, y0, z1, dy_near = phase(pred, forward)
+
+        def sort(places, v, v2, group, into):
+            return sort_tokens(list(zip(places, (v, v2))), tiles, group, 2, into)
 
         def exchange():
             near = flip(a2, 1, size)
-            y1 = flip(z1, 2, size)
-            z2 = along_z(pieces[2], size)
-            pos_row = pos.reshape(1, tokens)
-            near_row = plan[:tokens].reshape(1, tokens)
-            both = share(dy_near).reshape(tokens, width)
-            d = sort_tokens([(near_row, both)], tiles, 1, 2, dys)
-            xs = sort_tokens([(pos_row, share(a2).reshape(tokens, width))], tiles, 0, 2)
-            near = share(after(near, d, xs)).reshape(tokens, width)
-            return sort_tokens([(near_row, near)], tiles, 1, 2, xs), d, y1, z2
+            d, xs = phase(
+                inner,
+                lambda: (
+                    sort(pos_near, dy_near, swap(dy_near), 1, dys),
+                    sort(pos_here, a2, swap(a2), 0, None),
+                ),
+            )
+            near = after(near, d, xs)
+            xs = phase(inner, lambda: sort(pos_near, near, swap(near), 1, xs))
+            return xs, d, flip(z1, 2, size), along_z(pieces[2])
 
         xs, dys, y1, z2 = phase(pred, exchange)
         weights = [(z0, y0), (z1, y1)]
-        (zs, das, grads, gub0), y2 = phase(
+        (zs0, das0, grads, gub0), y2 = phase(
             pred, lambda: (call_experts(0, xs, dys, weights, ()), flip(z2, 2, size))
         )
         weights.append((z2, y2))
+
+        def both_cores(places, vs, group):
+            mine, other = unsort_tokens(places, vs, group, 2)
+            return (mine.astype(f32) + swap(other).astype(f32)).astype(bf16)
+
         def second():
-            v0 = sums_y(grads[0], size)
-            zs, das, more, gub = call_experts(1, xs, dys, weights, (zs0, das0))
-            mine, other = unsort_tokens(pos_near, das, 1, 2)
-            near = (mine.astype(f32) + swap(other).astype(f32)).astype(bf16)
-            return zs, das, more, gub, near, v0
-
-        zs0, das0 = zs, das
-        zs, das, more, gub1, da_near, v0 = phase(pred, second)
+            def inside():
+                zs, das, more, gub = call_experts(1, xs, dys, weights, (zs0, das0))
+                return zs, das, more, gub, both_cores(pos_near, das, 1)
+
+            return phase(inner, inside), sums_y(coords, grads[0], size)
+
+        (zs, das, more, gub1, da_near), v0 = phase(pred, second)
         grads = grads + more
         g_upb = jnp.concatenate([gub0, gub1], axis=-1)[:, 0]
-        pos_row = pos.reshape(1, tokens)
-        near_row = plan[:tokens].reshape(1, tokens)
-
-        def dealt(place, vs, group):
-            return deal(unsort_tokens([place], vs, group, 2)[0].reshape(by_core))
 
         def back():
+            def inside():
+                mine, other = unsort_tokens(pos_here, das, 0, 2)
+                return mine, swap(other), both_cores(pos_near, zs, 1)
+
             near = flip(da_near, 1, size)
-            g0 = sums_z(v0, size)
-            v1 = sums_y(grads[1], size)
-            own = dealt(pos_row, das, 0)
-            z_near = jnp.sum(dealt(near_row, zs, 1).astype(f32), axis=0).astype(bf16)
-            near = after(near, g0, v1, z_near)
-            dx2, dxr, sums2 = norm_grad((own, near), x2, dy_mine, ln_gain[1:2], True)
-            return dx2, (dxr, swap(dxr)), sums2, z_near, g0, v1
+            mine, other, z_near = phase(inner, inside)
+            g0 = sums_z(coords, v0)
+            v1 = sums_y(coords, grads[1], size)
+
+            def to_x2():
+                dx2, dxr, sums2 = norm_grad((mine, other, near), x2, dy_mine, ln_gain[1:2], True)
+                return dx2, (dxr, swap(dxr)), sums2
+
+            return *phase(inner, to_x2), z_near, g0, v1
 
         dx2, dxr, sums2, z_near, g0, v1 = phase(pred, back)
-        (da1, ga0, ga1, gb0, gb1, bsum), z_near, g1, v2 = phase(
-            pred,
-            lambda: (
-                bwd(coords, dxr, saved, pa, pb), flip(z_near, 1, size), sums_z(v1, size),
-                sums_y(grads[2], size),
-            ),
-        )
-
+
+        def last():
+            return (
+                phase(inner, lambda: bwd(coords, dxr, dx2, saved, pa, pb)), flip(z_near, 1, size),
+                sums_z(coords, v1), sums_y(coords, grads[2], size),
+            )
+
+        (grad, sums1, ga0, ga1, gb0, gb1, bsum), z_near, g1, v2 = phase(pred, last)
         def sum_up():
-            own, sends = attn_sums_xy((ga0, ga1), (gb0, gb1), size)
-            g2 = sums_z(v2, size)
-            grad, sums1 = norm_grad((deal(da1.reshape(by_core)),), x_mine, dx2, ln_gain[0:1], False)
-            z_own = dealt(pos_row, zs, 0)
-            out = finish(x2, jnp.sum(z_own.astype(f32), axis=0) + z_near.astype(f32), mods)
-            return own, sends, g2, grad, sums1, out
-
-        own, sends, g2, grad, sums1, out = phase(pred, sum_up)
-        got = [flip(v, 4 * rz, size) for rz, v in zip((1, 2, 3), sends)]
+            def out_rows():
+                mine, other = unsort_tokens(pos_here, zs, 0, 2)
+                z_sum = mine.astype(f32) + swap(other).astype(f32) + z_near.astype(f32)
+                out = finish(x2, z_sum, mods)
+                return out, swap(out), swap(grad)
+
+            def small_start():
+                total = small_rows(sums1, sums2, bsum, g_upb, g_down_bias)
+                total = total + swap(total)
+                return total + flip(total, 1, size)
+
+            g2 = sums_z(coords, v2)
+            got_a, got_b = flip(ga1, 2, size), flip(gb1, 1, size)
+            outs = phase(inner, out_rows)
+            a_own, a_send, b_own, b_send = attn_sums_1((ga0, gb0), (got_a, got_b), outs)
+            got_a, got_b = flip(a_send, 1, size), flip(b_send, 2, size)
+            small = phase(inner, small_start)
+            return attn_sums_2(coords, (a_own, b_own), (got_a, got_b), small), g2, small, outs
+
+        (own, send), g2, small, (out, out_other, grad_other) = phase(pred, sum_up)
+
+        def inside():
+            total = small
+            for mask in (2, 4, 8):
+                total = total + flip(total, mask, size)
+            return total
+
+        got = deal_z(send)
         near = flip(jnp.concatenate([v[1] for v in (g0, g1, g2)], axis=-1), 1, size)
-        g_qkv, g_out = whole(
-            qkv_grad_kernel, "qkv_grad", [(w_qkv.shape, f32), (w_out.shape, f32)], own, *got
+        small = phase(inner, inside)
+        layer_output, grad_input = whole(
+            rows_kernel, "rows", [((parts,) + v.shape, v.dtype) for v in (out, grad)],
+            out, out_other, grad, grad_other, prefetch=(coords,),
         )
         g_up, g_down = whole(
             expert_grad_kernel, "expert_grad", [(w_up.shape, f32)] * 2,
             g0[0], g1[0], g2[0], near, prefetch=(coords,),
         )
-        layer_output, grad_input = whole(
-            rows_kernel, "rows", [((parts,) + v.shape, v.dtype) for v in (out, grad)],
-            out, swap(out), grad, swap(grad), prefetch=(coords,),
+        g_qkv, g_out = whole(
+            qkv_grad_kernel, "qkv_grad", [(w_qkv.shape, f32), (w_out.shape, f32)], own, got,
+            prefetch=(coords,),
         )
     else:
         coords = jnp.stack([0, 0, 0, part]).astype(jnp.int32)
+        x_mine, dy_mine, proj_bias, seg_col, vec, ln1 = small_inputs()
         hid_start = part * hid
         hc = hid // CHUNKS
         up_b = lax.dynamic_slice_in_dim(up_bias, hid_start, hid, 1)
-        pa, pb = gather_pieces(*w_ab, size, False)
+        pa, pb = gather_pieces_plain(w_qkv[:2], jnp.stack([w_qkv[2], w_out]))
         weights = expert_pieces_plain(w_up, w_down)
         mods, pos, tile_expert, used = token_plan(segments, modality, experts)
         pos_row = pos.reshape(1, tokens)
@@ -1030,24 +1132,16 @@
         g_up, g_down = jnp.concatenate([expert_sums_plain(pair) for pair in grads], axis=-1)
         own = deal(unsort_tokens([pos_row], das, 0, 1)[0].reshape(by_core))
         dx2, dxr, sums2 = norm_grad((own[0], own[1]), x2, dy_mine, ln_gain[1:2], True)
-        da1, ga0, ga1, gb0, gb1, bsum = bwd(coords, (dxr, swap(dxr)), saved, pa, pb)
-        own = deal(da1.reshape(by_core))
-        grad_mine, sums1 = norm_grad((own[0], own[1]), x_mine, dx2, ln_gain[0:1], False)
+        grad_mine, sums1, ga0, ga1, gb0, gb1, bsum = bwd(
+            coords, (dxr, swap(dxr)), dx2, saved, pa, pb
+        )
         g_qk, g_vo = scatter_plain((ga0, ga1), (gb0, gb1))
         g_qkv, g_out = jnp.concatenate([g_qk, g_vo[:1]]), g_vo[1]
         own = deal(unsort_tokens([pos_row], zs, 0, 1)[0].reshape(by_core))
         layer_output = share(finish(x2, jnp.sum(own.astype(f32), axis=0), mods))
         grad_input = share(grad_mine)
-
-    bsum = bsum.reshape(3, cols)
-    g_qv = lax.dynamic_update_slice(
-        jnp.zeros((2, width), f32), jnp.stack([bsum[0], bsum[2]]), (jnp.int32(0), col_start)
-    )
-    g_upb_full = lax.dynamic_update_slice(
-        jnp.zeros((experts, up_bias.shape[1]), f32), g_upb, (jnp.int32(0), hid_start)
-    )
-    small = jnp.concatenate([sums1[0:2], sums2[0:3], g_down_bias / parts, g_qv, g_upb_full.reshape(-1, width)])
-    small = sum_small(small, size)
+        small = lax.psum(small_rows(sums1, sums2, bsum, g_upb, g_down_bias), ("dp", "mp"))
+
     g_gain = jnp.stack([small[0], small[2]])
     g_lnb = jnp.stack([small[1], small[3]])
     return (

time: 415 us -> 391 us (0.942); the launches traced: 408 us -> 388 us
  blocking collectives: 19.8 us -> 0 us
  starting transfers between devices: 97.4 us -> 86.5 us
  Pallas kernels: 170 us -> 176 us
    ppermute x49 -> x28, starting transfers between devices: 63.6 us -> 37.7 us  [flip(): return lax.ppermute(x, 'dp', [(i, i ^ mask) for i in range(size)])]
    all_to_all x3 -> x0, blocking collectives: 19.8 us -> none  [deal(): return lax.all_to_all(v, 'mp', 0, 0)]
    ppermute x49 -> x28, waiting for transfers between devices: 49.8 us -> 32.9 us  [flip(): return lax.ppermute(x, 'dp', [(i, i ^ mask) for i in range(size)])]
    ppermute x5 -> x13, waiting for transfers between devices: 5.24 us -> 21.3 us  [swap(): return lax.ppermute(v, 'mp', [(0, 1), (1, 0)])]
    all_to_all x5 -> x7, starting transfers between devices: 32.7 us -> 46.8 us  [deal_z(): return lax.all_to_all(v, 'dp', 0, 0, axis_index_groups=groups, tiled=True)]
    cond x30 -> x60, local copies, waits for them, and re-layouts: 2.07 us -> 10.3 us
    reduce_sum x2 -> x0, other arithmetic: 4.64 us -> none  [the longest x1 2.82 us: back(): z_near = jnp.sum(dealt(near_row, zs, 1).astype(f32), axis=0).astype(bf16)]
    pallas_call x11, Pallas kernels: 29 us -> 33.6 us  [whole(): pl.pallas_call(kernel, out_shape=[jax.ShapeDtypeStruct(s, d) for s, d in...]
  transfers between devices with their start and end apart: 59 -> 48, of which waited for: 16 -> 23; matrix products, arithmetic and copies ran while one was open for 12% -> 12% of each run, Pallas kernels for 38% -> 43%
where the time goes in v3:
time: 391 us; the launch traced here: 388 us
  Pallas kernels  176 us (45%)
  starting transfers between devices  86.5 us (22%)
  waiting for transfers between devices  57.2 us (15%)
  local copies, waits for them, and re-layouts  40.9 us (10%)
  other arithmetic  23.2 us (6%)
    pallas_call x2, Pallas kernels, ffn(): pl.pallas_call(functools.partial(ffn_kernel, first, count, piece, groups)...  48.3 us
    all_to_all x7, starting transfers between devices, deal_z(): return lax.all_to_all(v, 'dp', 0, 0, axis_index_groups=groups, tiled=True)  46.8 us
    ppermute x28, starting transfers between devices, flip(): return lax.ppermute(x, 'dp', [(i, i ^ mask) for i in range(size)])  37.7 us
    pallas_call x11, Pallas kernels, whole(): pl.pallas_call(kernel, out_shape=[jax.ShapeDtypeStruct(s, d) for s, d in...  33.6 us
    ppermute x28, waiting for transfers between devices, flip(): return lax.ppermute(x, 'dp', [(i, i ^ mask) for i in range(size)])  32.9 us
    pallas_call x1, Pallas kernels, attn_bwd(): pl.pallas_call(functools.partial(attn_bwd_kernel, heads, piece), out_shap...  25.9 us
    ppermute x13, waiting for transfers between devices, swap(): return lax.ppermute(v, 'mp', [(0, 1), (1, 0)])  21.3 us
    pallas_call x4, Pallas kernels, unsort_tokens(): pl.pallas_call(functools.partial(unsort_kernel, len(places)), out_shape=[...  20.9 us
  transfers between devices with their start and end apart: 48, of which 23 were waited for; matrix products, arithmetic and copies ran while one was open for 12% of the time, Pallas kernels for 43%

profile of v3, /device:TPU:0, one launch (start us, length us, event | category | flops | bytes accessed | tf_op | source)
XLA Modules:
  0.0 388.1 jit_solution(10500950159742568744)
XLA Ops:
  2.0 23.6 %conditional.20 = (bf16[2,2,3,48,256]{4,3,2,1,0:T(8,128)(2,1)S(1)}, bf16[2,2,3,48,256]{4,3,2,1,0:T(8,128)(2,1)S(1)}, bf16[2,2,3,48,256]{4,3,2,1,0:T(8,128)(2,1)S...) conditional(s32[]{:T(128)} %convert_element_type.82, () %tuple.171, ...), branch_computations={%region_0.1_spmd, %region_1.7_spmd} | conditional | flops 10636736 | bytes 23106940 | solution.py:802
  26.4 34.3 %conditional.21 = (bf16[4,2,2,3,48,256]{5,4,3,2,1,0:T(8,128)(2,1)}, bf16[2,4,2,48,384]{4,3,2,1,0:T(8,128)(2,1)}, bf16[2,4,2,48,384]{4,3,2,1,0:T(8,128)(2,1)}, bf...) conditional(s32[]{:T(128)} %convert_element_type.82, () %tuple.170, ...), branch_computations={%region_7.8_spmd, %region_8.11_spmd} | conditional | flops 2421230592 | bytes 34704892 | solution.py:802
  33.5 25.0 %conditional = (bf16[2,4,2,48,384]{4,3,2,1,0:T(8,128)(2,1)}, bf16[2,4,2,48,384]{4,3,2,1,0:T(8,128)(2,1)}, bf16[2,4,2,48,384]{4,3,2,1,0:T(8,128)(2,1)}, bf16[2,4,...) conditional(s32[]{:T(128)} %convert_element_type.46, () %tuple.97, ...), branch_computations={%region_9.9_spmd, %region_10.10_spmd} | conditional | flops 2421230592 | bytes 21040338 | solution.py:802
  60.8 34.8 %conditional.22 = (bf16[2,3,3,512,128]{4,3,2,1,0:T(8,128)(2,1)}, bf16[2,3,128,512]{3,2,1,0:T(8,128)(2,1)}, bf16[2,512,384]{2,1,0:T(8,128)(2,1)}, bf16[2,3,128,51...) conditional(s32[]{:T(128)} %convert_element_type.82, () %tuple.176, ...), branch_computations={%region_11.12_spmd, %region_12.15_spmd} | conditional | flops 20010000384 | bytes 34177888 | solution.py:802
  70.3 25.3 %conditional.1 = (bf16[2,3,3,512,128]{4,3,2,1,0:T(8,128)(2,1)}, bf16[2,3,128,512]{3,2,1,0:T(8,128)(2,1)}, bf16[2,512,384]{2,1,0:T(8,128)(2,1)}, bf16[2,3,128,512...) conditional(s32[]{:T(128)} %convert_element_type.48, () %tuple.103, ...), branch_computations={%region_13.13_spmd, %region_14.14_spmd} | conditional | flops 20010000384 | bytes 21299772 | solution.py:802
  71.3 18.0 %attn_fwd.1 = (bf16[512,768]{1,0:T(8,128)(2,1)}, bf16[512,768]{1,0:T(8,128)(2,1)}, bf16[2,3,3,512,128]{4,3,2,1,0:T(8,128)(2,1)}, bf16[2,3,128,512]{3,2,1,0:T(8,1...) custom-call(s32[4]{0:T(128)S(1)} %get-tuple-element.533.c_ref, ...), custom_call_target="tpu_custom_call" | custom-call | flops 20000000000 | bytes 10000000 | tf_op jit(solution)/shard_map/cond/branch_1_fun/cond/branch_1_fun/attn_fwd/pallas_call | solution.py:189
  95.6 35.3 %conditional.23 = (bf16[3072,768]{1,0:T(8,128)(2,1)}, bf16[3072,768]{1,0:T(8,128)(2,1)}, bf16[4,2,2,3,48,256]{5,4,3,2,1,0:T(8,128)(2,1)}, bf16[4,2,2,3,48,256]{5,4,3,2,1,0:T(8,128)(2,1)}) conditional(s32[]{:T(128)} %convert_element_type.82, () %tuple.175, (pred[]{:T(512)}, bf16[512,768]{1,0:T(8,128)(2,1)}, bf16[512,768]{1,0:T(8,128)(2,1)}, ...), branch_computations={%region_15.16_spmd, %region_16.21_spmd} | conditional | flops 7247757312 | bytes 61752656 | solution.py:802
  104.0 14.8 %conditional.2 = (bf16[3072,768]{1,0:T(8,128)(2,1)}, bf16[3072,768]{1,0:T(8,128)(2,1)}) conditional(s32[]{:T(128)} %convert_element_type.49, () %tuple.110, (bf16[512,768]{1,0:T(8,128)(2,1)}, s32[1,512]{1,0:T(1,128)}, s32[1,512]{1,0:T(1,128)}, bf16[3072,768]{1,0:T(8,128)(2,1)}, bf16[512,768]{1,0:T(8,128)(2,1)}, /*index=5*/s32[1,512]{1,0:T(1,128)}, ...), branch_computations={%region_17.17_spmd, %region_18.18_spmd} | conditional | flops 4831838208 | bytes 32583064 | solution.py:802
  121.8 8.2 %conditional.3 = (bf16[3072,768]{1,0:T(8,128)(2,1)}) conditional(s32[]{:T(128)} %convert_element_type.49, () %tuple.109, (bf16[512,768]{1,0:T(8,128)(2,1)S(1)}, s32[1,512]{1,0:T(1,128)}, s32[1,512]{1,0:T(1,128)}, bf16[3072,768]{1,0:T(8,128)(2,1)}) %tuple.113), branch_computations={%region_19.19_spmd, %region_20.20_spmd} | conditional | flops 2415919104 | bytes 16291532 | solution.py:802
  130.9 27.5 %conditional.24 = (bf16[3072,768]{1,0:T(8,128)(2,1)}, bf16[3072,768]{1,0:T(8,128)(2,1)}, bf16[4,2,2,3,48,256]{5,4,3,2,1,0:T(8,128)(2,1)S(1)}, bf16[4,2,2,3,48,25...) conditional(s32[]{:T(128)} %convert_element_type.82, () %tuple.179, ...), branch_computations={%region_21.22_spmd, %region_22.23_spmd} | conditional | flops 10871635968 | bytes 44730968 | solution.py:802
  132.2 19.0 %ffn.2 = (bf16[3072,768]{1,0:T(8,128)(2,1)}, bf16[3072,768]{1,0:T(8,128)(2,1)}, bf16[4,2,2,3,48,256]{5,4,3,2,1,0:T(8,128)(2,1)S(1)}, bf16[4,2,2,3,48,256]{5,4,3,2,1,0:T(8,128)(2,1)}, f32[3,1,256]{2,1,0:T(1,128)S(1)}) custom-call(s32[4]{0:T(128)S(1)} %get-tuple-element.601.c_ref, s32[12]{0:T(128)} %get-tuple-element.602.te_ref, s32[2]{0:T(128)} %get-tuple-element.603.n_ref, ...), custom_call_target="tpu_custom_call" | custom-call | flops 10871635968 | bytes 40000000 | tf_op jit(solution)/shard_map/cond/branch_1_fun/ffn/pallas_call | solution.py:573
  158.4 44.8 %conditional.25 = (bf16[3072,768]{1,0:T(8,128)(2,1)}, bf16[3072,768]{1,0:T(8,128)(2,1)}, bf16[4,2,2,3,48,256]{5,4,3,2,1,0:T(8,128)(2,1)}, bf16[4,2,2,3,48,256]{5...) conditional(s32[]{:T(128)} %convert_element_type.82, () %tuple.174, ...), branch_computations={%region_23.24_spmd, %region_24.27_spmd} | conditional | flops 24161763328 | bytes 64248532 | solution.py:802
  159.9 39.9 %conditional.4 = (bf16[3072,768]{1,0:T(8,128)(2,1)}, bf16[3072,768]{1,0:T(8,128)(2,1)}, bf16[4,2,2,3,48,256]{5,4,3,2,1,0:T(8,128)(2,1)}, bf16[4,2,2,3,48,256]{5,...) conditional(s32[]{:T(128)} %convert_element_type.53, () %tuple.120, ...), branch_computations={%region_25.25_spmd, %region_26.26_spmd} | conditional | flops 24160763904 | bytes 55529704 | solution.py:802
  160.5 29.4 %ffn.3 = (bf16[3072,768]{1,0:T(8,128)(2,1)}, bf16[3072,768]{1,0:T(8,128)(2,1)}, bf16[4,2,2,3,48,256]{5,4,3,2,1,0:T(8,128)(2,1)}, bf16[4,2,2,3,48,256]{5,4,3,2,1,...) custom-call(s32[4]{0:T(128)S(1)} %get-tuple-element.615.c_ref, ...), custom_call_target="tpu_custom_call" | custom-call | flops 21743271936 | bytes 40000000 | tf_op jit(solution)/shard_map/cond/branch_1_fun/cond/branch_1_fun/ffn/pallas_call | solution.py:573
  203.9 52.2 %conditional.26 = (f32[512,768]{1,0:T(8,128)}, bf16[512,768]{1,0:T(8,128)(2,1)}, bf16[512,768]{1,0:T(8,128)(2,1)}, f32[8,768]{1,0:T(8,128)}, bf16[512,768]{1,0:T...) conditional(s32[]{:T(128)} %convert_element_type.82, () %tuple.183, ...), branch_computations={%region_27.28_spmd, %region_28.33_spmd} | conditional | flops 4855410688 | bytes 67070724 | solution.py:802
  203.9 16.6 %all-to-all-start.3 = ((bf16[4,2,2,3,48,256]{5,4,3,2,1,0:T(8,128)(2,1)}), bf16[4,2,2,3,48,256]{5,4,3,2,1,0:T(8,128)(2,1)S(1)}, u32[]{:S(2)}, u32[]{:S(2)}) async-start(bf16[4,2,2,3,48,256]{5,4,3,2,1,0:T(8,128)(2,1)} %get-tuple-element.704), calls=%async_computation.3 | async-start | bytes 2359296 | tf_op jit(solution)/shard_map/cond/branch_1_fun/all_to_all | solution.py:809
  221.7 13.2 %conditional.5 = (bf16[512,768]{1,0:T(8,128)(2,1)S(1)}, bf16[512,768]{1,0:T(8,128)(2,1)}, bf16[512,768]{1,0:T(8,128)(2,1)}) conditional(s32[]{:T(128)} %convert_element_type.73, () %tuple.129, (s32[1,512]{1,0:T(1,128)}, s32[1,512]{1,0:T(1,128)}, bf16[3072,768]{1,0:T(8,128)(2,1)}, s32[1,512]{1,0:T(1,128)}, s32[1,512]{1,0:T(1,128)}, ...), branch_computations={%region_29.29_spmd, %region_30.30_spmd} | conditional | flops 4833411072 | bytes 31796612 | solution.py:802
  256.1 47.9 %conditional.27 = (f32[512,768]{1,0:T(8,128)}, f32[8,768]{1,0:T(8,128)}, bf16[2,4,2,48,384]{4,3,2,1,0:T(8,128)(2,1)}, bf16[2,4,2,48,384]{4,3,2,1,0:T(8,128)(2,1)...) conditional(s32[]{:T(128)} %convert_element_type.82, () %tuple.182, ...), branch_computations={%region_33.34_spmd, %region_34.37_spmd} | conditional | flops 40021999616 | bytes 63146784 | solution.py:802
  262.2 34.1 %conditional.7 = (f32[512,768]{1,0:T(8,128)}, f32[8,768]{1,0:T(8,128)}, bf16[2,4,2,48,384]{4,3,2,1,0:T(8,128)(2,1)}, bf16[2,4,2,48,384]{4,3,2,1,0:T(8,128)(2,1)}...) conditional(s32[]{:T(128)} %convert_element_type.74, () %tuple.136, ...), branch_computations={%region_35.35_spmd, %region_36.36_spmd} | conditional | flops 40020000768 | bytes 34305916 | solution.py:802
  263.2 25.9 %attn_bwd.1 = (bf16[512,768]{1,0:T(8,128)(2,1)}, bf16[512,768]{1,0:T(8,128)(2,1)}, bf16[2,4,2,48,384]{4,3,2,1,0:T(8,128)(2,1)}, bf16[2,4,2,48,384]{4,3,2,1,0:T(8...) custom-call(s32[4]{0:T(128)S(1)} %get-tuple-element.711.c_ref, ...), custom_call_target="tpu_custom_call" | custom-call | flops 40000000000 | bytes 20000000 | tf_op jit(solution)/shard_map/cond/branch_1_fun/cond/branch_1_fun/attn_bwd/pallas_call | solution.py:321
  304.0 44.6 %conditional.28 = (f32[2,2,48,384]{3,2,1,0:T(8,128)S(1)}, bf16[4,2,2,48,384]{4,3,2,1,0:T(8,128)(2,1)}, f32[2,3,48,256]{3,2,1,0:T(8,128)S(1)}, bf16[2,3,48,256]{3...) conditional(s32[]{:T(128)} %convert_element_type.82, () %tuple.169, ...), branch_computations={%region_37.38_spmd, %region_38.43_spmd} | conditional | flops 2423282944 | bytes 58332356 | solution.py:802
  312.5 15.1 %conditional.8 = (bf16[512,768]{1,0:T(8,128)(2,1)}, bf16[512,768]{1,0:T(8,128)(2,1)}, f32[512,768]{1,0:T(8,128)}) conditional(s32[]{:T(128)} %convert_element_type.79, () %tuple.142, (s32[1,512]{1,0:T(1,128)}, s32[1,512]{1,0:T(1,128)}, bf16[3072,768]{1,0:T(8,128)(2,1)}, bf16[512,768]{1,0:T(8,128)(2,1)}, s32[]{:T(128)}, ...), branch_computations={%region_39.39_spmd, %region_40.40_spmd} | conditional | flops 2420246016 | bytes 27334466 | solution.py:802
  331.6 10.3 %conditional.9 = (f32[22,768]{1,0:T(8,128)}) conditional(s32[]{:T(128)} %convert_element_type.79, () %tuple.145, (f32[8,768]{1,0:T(8,128)}, f32[8,768]{1,0:T(8,128)}, f32[3,768]{1,0:T(4,128)}, f32[1,1152]{1,0:T(1,128)}, s32[]{:T(128)}, /*index=5*/s32[]{:T(128)}, f32[3,1,768]{2,1,0:T(1,128)S(1)}) %tuple.146), branch_computations={%region_41.41_spmd, %region_42.42_spmd} | conditional | flops 36870 | bytes 1302700 | solution.py:802
  355.7 17.0 %conditional.29 = (f32[22,768]{1,0:T(8,128)S(1)}) conditional(s32[]{:T(128)} %convert_element_type.83, () %tuple.187, f32[22,768]{1,0:T(8,128)} %get-tuple-element.1016), branch_computations={%region_43.44_spmd, %region_44.45_spmd} | conditional | flops 50688 | bytes 1419392 | solution.py:802
  (291 shorter events, 284.2 us)
Async XLA Ops:
  3.7 16.3 %collective-permute-start.32 = (bf16[2,2,48,384]{3,2,1,0:T(8,128)(2,1)S(1)}, bf16[2,2,48,384]{3,2,1,0:T(8,128)(2,1)}, u32[]{:S(2)}, u32[]{:S(2)}) collective-permute-start(bf16[2,2,48,384]{3,2,1,0:T(8,128)(2,1)S(1)} %pad_maximum_fusion.8), channel_id=1, source_target_pairs={{0,8},{2,10},{4,12},{6,14},{8,0},{10,2},{12,4},{14,6},{16,24},{18,... | collective-permute-start | bytes 442376 | tf_op jit(solution)/shard_map/cond/branch_1_fun/ppermute | solution.py:728
  6.8 14.2 %collective-permute-start.33 = (bf16[2,2,48,384]{3,2,1,0:T(8,128)(2,1)S(1)}, bf16[2,2,48,384]{3,2,1,0:T(8,128)(2,1)}, u32[]{:S(2)}, u32[]{:S(2)}) collective-permute-start(bf16[2,2,48,384]{3,2,1,0:T(8,128)(2,1)S(1)} %pad_maximum_fusion.8), channel_id=1, source_target_pairs={{0,16},{2,18},{4,20},{6,22},{8,24},{10,26},{12,28},{14,30},{16,0},... | collective-permute-start | bytes 442376 | tf_op jit(solution)/shard_map/cond/branch_1_fun/ppermute | solution.py:728
  9.4 12.6 %collective-permute-start.34 = (bf16[2,2,48,384]{3,2,1,0:T(8,128)(2,1)S(1)}, bf16[2,2,48,384]{3,2,1,0:T(8,128)(2,1)}, u32[]{:S(2)}, u32[]{:S(2)}) collective-permute-start(bf16[2,2,48,384]{3,2,1,0:T(8,128)(2,1)S(1)} %pad_maximum_fusion.8), channel_id=1, source_target_pairs={{0,24},{2,26},{4,28},{6,30},{8,16},{10,18},{12,20},{14,22},{16,8},... | collective-permute-start | bytes 442376 | tf_op jit(solution)/shard_map/cond/branch_1_fun/ppermute | solution.py:728
  28.3 32.4 %all-to-all-start.5 = ((bf16[4,2,2,3,48,256]{5,4,3,2,1,0:T(8,128)(2,1)}), bf16[4,2,2,3,48,256]{5,4,3,2,1,0:T(8,128)(2,1)}, u32[]{:S(2)}, u32[]{:S(2)}) async-start(bf16[4,2,2,3,48,256]{5,4,3,2,1,0:T(8,128)(2,1)} %broadcast_in_dim.87), calls=%async_computation.5 | async-start | bytes 2359296 | tf_op jit(solution)/shard_map/cond/branch_1_fun/all_to_all | solution.py:809
  43.0 13.1 %collective-permute-start.37 = (bf16[2,4,2,48,384]{4,3,2,1,0:T(8,128)(2,1)}, bf16[2,4,2,48,384]{4,3,2,1,0:T(8,128)(2,1)}, u32[]{:S(2)}, u32[]{:S(2)}) collective-permute-start(bf16[2,4,2,48,384]{4,3,2,1,0:T(8,128)(2,1)} %pad_maximum_fusion), channel_id=1, source_target_pairs={{0,4},{2,6},{4,0},{6,2},{8,12},{10,14},{12,8},{14,10},{16,20},{18,... | collective-permute-start | bytes 1769480 | tf_op jit(solution)/shard_map/cond/branch_1_fun/cond/branch_1_fun/ppermute | solution.py:728
  62.9 32.6 %all-to-all-start = ((bf16[4,2,2,3,48,256]{5,4,3,2,1,0:T(8,128)(2,1)}), bf16[4,2,2,3,48,256]{5,4,3,2,1,0:T(8,128)(2,1)}, u32[]{:S(2)}, u32[]{:S(2)}) async-start(bf16[4,2,2,3,48,256]{5,4,3,2,1,0:T(8,128)(2,1)} %broadcast_in_dim.88), calls=%async_computation | async-start | bytes 2359296 | tf_op jit(solution)/shard_map/cond/branch_1_fun/all_to_all | solution.py:809
  67.2 28.3 %collective-permute-start.1 = (bf16[4,2,2,3,48,256]{5,4,3,2,1,0:T(8,128)(2,1)}, bf16[4,2,2,3,48,256]{5,4,3,2,1,0:T(8,128)(2,1)}, u32[]{:S(2)}, u32[]{:S(2)}) collective-permute-start(bf16[4,2,2,3,48,256]{5,4,3,2,1,0:T(8,128)(2,1)} %get-tuple-element.574), channel_id=1, source_target_pairs={{0,4},{2,6},{4,0},{6,2},{8,12},{10,14},{12,8},{14,10},{16,20},{18,... | collective-permute-start | bytes 3538952 | tf_op jit(solution)/shard_map/cond/branch_1_fun/ppermute | solution.py:728
  68.8 26.8 %collective-permute-start.2 = (bf16[512,768]{1,0:T(8,128)(2,1)S(1)}, bf16[512,768]{1,0:T(8,128)(2,1)}, u32[]{:S(2)}, u32[]{:S(2)}) collective-permute-start(bf16[512,768]{1,0:T(8,128)(2,1)S(1)} %get-tuple-element.576), channel_id=1, source_target_pairs={{0,2},{2,0},{4,6},{6,4},{8,10},{10,8},{12,14},{14,12},{16,18},{18,... | collective-permute-start | bytes 2359304 | tf_op jit(solution)/shard_map/cond/branch_1_fun/ppermute | solution.py:728
  96.7 34.2 %all-to-all-start.1 = ((bf16[4,2,2,3,48,256]{5,4,3,2,1,0:T(8,128)(2,1)}), bf16[4,2,2,3,48,256]{5,4,3,2,1,0:T(8,128)(2,1)}, u32[]{:S(2)}, u32[]{:S(2)}) async-start(bf16[4,2,2,3,48,256]{5,4,3,2,1,0:T(8,128)(2,1)} %broadcast_in_dim.89), calls=%async_computation.1 | async-start | bytes 2359296 | tf_op jit(solution)/shard_map/cond/branch_1_fun/all_to_all | solution.py:809
  102.0 28.1 %collective-permute-start.7 = (bf16[4,2,2,3,48,256]{5,4,3,2,1,0:T(8,128)(2,1)}, bf16[4,2,2,3,48,256]{5,4,3,2,1,0:T(8,128)(2,1)}, u32[]{:S(2)}, u32[]{:S(2)}) collective-permute-start(bf16[4,2,2,3,48,256]{5,4,3,2,1,0:T(8,128)(2,1)} %get-tuple-element.599), channel_id=1, source_target_pairs={{0,4},{2,6},{4,0},{6,2},{8,12},{10,14},{12,8},{14,10},{16,20},{18,... | collective-permute-start | bytes 3538952 | tf_op jit(solution)/shard_map/cond/branch_1_fun/ppermute | solution.py:728
  102.5 19.2 %collective-permute-start.6 = (bf16[512,768]{1,0:T(8,128)(2,1)}, bf16[512,768]{1,0:T(8,128)(2,1)S(1)}, u32[]{:S(2)}, u32[]{:S(2)}) collective-permute-start(bf16[512,768]{1,0:T(8,128)(2,1)} %get-tuple-element.589), channel_id=1, source_target_pairs={{0,2},{2,0},{4,6},{6,4},{8,10},{10,8},{12,14},{14,12},{16,18},{18,... | collective-permute-start | bytes 2359304 | tf_op jit(solution)/shard_map/cond/branch_1_fun/ppermute | solution.py:728
  130.9 27.5 %collective-permute-start.8 = (bf16[4,2,2,3,48,256]{5,4,3,2,1,0:T(8,128)(2,1)}, bf16[4,2,2,3,48,256]{5,4,3,2,1,0:T(8,128)(2,1)}, u32[]{:S(2)}, u32[]{:S(2)}) collective-permute-start(bf16[4,2,2,3,48,256]{5,4,3,2,1,0:T(8,128)(2,1)} %get-tuple-element.614), channel_id=1, source_target_pairs={{0,4},{2,6},{4,0},{6,2},{8,12},{10,14},{12,8},{14,10},{16,20},{18,... | collective-permute-start | bytes 3538952 | tf_op jit(solution)/shard_map/cond/branch_1_fun/ppermute | solution.py:728
  158.4 41.5 %collective-permute-start.17 = (bf16[4,2,2,3,48,256]{5,4,3,2,1,0:T(8,128)(2,1)}, bf16[4,2,2,3,48,256]{5,4,3,2,1,0:T(8,128)(2,1)}, u32[]{:S(2)}, u32[]{:S(2)}) collective-permute-start(bf16[4,2,2,3,48,256]{5,4,3,2,1,0:T(8,128)(2,1)} %get-tuple-element.662), channel_id=1, source_target_pairs={{0,4},{2,6},{4,0},{6,2},{8,12},{10,14},{12,8},{14,10},{16,20},{18,... | collective-permute-start | bytes 3538952 | tf_op jit(solution)/shard_map/cond/branch_1_fun/ppermute | solution.py:728
  203.9 48.3 %all-to-all-start.3 = ((bf16[4,2,2,3,48,256]{5,4,3,2,1,0:T(8,128)(2,1)}), bf16[4,2,2,3,48,256]{5,4,3,2,1,0:T(8,128)(2,1)S(1)}, u32[]{:S(2)}, u32[]{:S(2)}) async-start(bf16[4,2,2,3,48,256]{5,4,3,2,1,0:T(8,128)(2,1)} %get-tuple-element.704), calls=%async_computation.3 | async-start | bytes 2359296 | tf_op jit(solution)/shard_map/cond/branch_1_fun/all_to_all | solution.py:809
  220.5 28.0 %collective-permute-start.21 = (bf16[4,2,2,3,48,256]{5,4,3,2,1,0:T(8,128)(2,1)}, bf16[4,2,2,3,48,256]{5,4,3,2,1,0:T(8,128)(2,1)}, u32[]{:S(2)}, u32[]{:S(2)}) collective-permute-start(bf16[4,2,2,3,48,256]{5,4,3,2,1,0:T(8,128)(2,1)} %get-tuple-element.708), channel_id=1, source_target_pairs={{0,4},{2,6},{4,0},{6,2},{8,12},{10,14},{12,8},{14,10},{16,20},{18,... | collective-permute-start | bytes 3538952 | tf_op jit(solution)/shard_map/cond/branch_1_fun/ppermute | solution.py:728
  221.0 19.3 %collective-permute-start.20 = (bf16[512,768]{1,0:T(8,128)(2,1)}, bf16[512,768]{1,0:T(8,128)(2,1)}, u32[]{:S(2)}, u32[]{:S(2)}) collective-permute-start(bf16[512,768]{1,0:T(8,128)(2,1)} %get-tuple-element.694), channel_id=1, source_target_pairs={{0,2},{2,0},{4,6},{6,4},{8,10},{10,8},{12,14},{14,12},{16,18},{18,... | collective-permute-start | bytes 2359304 | tf_op jit(solution)/shard_map/cond/branch_1_fun/ppermute | solution.py:728
  256.1 44.8 %all-to-all-start.2 = ((bf16[4,2,2,3,48,256]{5,4,3,2,1,0:T(8,128)(2,1)}), bf16[4,2,2,3,48,256]{5,4,3,2,1,0:T(8,128)(2,1)S(1)}, u32[]{:S(2)}, u32[]{:S(2)}) async-start(bf16[4,2,2,3,48,256]{5,4,3,2,1,0:T(8,128)(2,1)} %get-tuple-element.768), calls=%async_computation.2 | async-start | bytes 2359296 | tf_op jit(solution)/shard_map/cond/branch_1_fun/all_to_all | solution.py:809
  261.0 35.3 %collective-permute-start.12 = (bf16[4,2,2,3,48,256]{5,4,3,2,1,0:T(8,128)(2,1)}, bf16[4,2,2,3,48,256]{5,4,3,2,1,0:T(8,128)(2,1)S(1)}, u32[]{:S(2)}, u32[]{:S(2)}) collective-permute-start(bf16[4,2,2,3,48,256]{5,4,3,2,1,0:T(8,128)(2,1)} %get-tuple-element.772), channel_id=1, source_target_pairs={{0,4},{2,6},{4,0},{6,2},{8,12},{10,14},{12,8},{14,10},{16,20},{18,... | collective-permute-start | bytes 3538952 | tf_op jit(solution)/shard_map/cond/branch_1_fun/ppermute | solution.py:728
  261.5 42.5 %collective-permute-start.11 = (bf16[512,768]{1,0:T(8,128)(2,1)}, bf16[512,768]{1,0:T(8,128)(2,1)}, u32[]{:S(2)}, u32[]{:S(2)}) collective-permute-start(bf16[512,768]{1,0:T(8,128)(2,1)} %get-tuple-element.766), channel_id=1, source_target_pairs={{0,2},{2,0},{4,6},{6,4},{8,10},{10,8},{12,14},{14,12},{16,18},{18,... | collective-permute-start | bytes 2359304 | tf_op jit(solution)/shard_map/cond/branch_1_fun/ppermute | solution.py:728
  304.1 41.7 %all-to-all-start.4 = ((bf16[4,2,2,3,48,256]{5,4,3,2,1,0:T(8,128)(2,1)}), bf16[4,2,2,3,48,256]{5,4,3,2,1,0:T(8,128)(2,1)S(1)}, u32[]{:S(2)}, u32[]{:S(2)}) async-start(bf16[4,2,2,3,48,256]{5,4,3,2,1,0:T(8,128)(2,1)} %get-tuple-element.819), calls=%async_computation.4 | async-start | bytes 2359296 | tf_op jit(solution)/shard_map/cond/branch_1_fun/all_to_all | solution.py:809
  309.5 18.1 %collective-permute-start.27 = (bf16[2,4,2,48,384]{4,3,2,1,0:T(8,128)(2,1)}, bf16[2,4,2,48,384]{4,3,2,1,0:T(8,128)(2,1)}, u32[]{:S(2)}, u32[]{:S(2)}) collective-permute-start(bf16[2,4,2,48,384]{4,3,2,1,0:T(8,128)(2,1)} %get-tuple-element.809), channel_id=1, source_target_pairs={{0,4},{2,6},{4,0},{6,2},{8,12},{10,14},{12,8},{14,10},{16,20},{18,... | collective-permute-start | bytes 1769480 | tf_op jit(solution)/shard_map/cond/branch_1_fun/ppermute | solution.py:728
  311.0 16.6 %collective-permute-start.28 = (bf16[2,4,2,48,384]{4,3,2,1,0:T(8,128)(2,1)}, bf16[2,4,2,48,384]{4,3,2,1,0:T(8,128)(2,1)}, u32[]{:S(2)}, u32[]{:S(2)}) collective-permute-start(bf16[2,4,2,48,384]{4,3,2,1,0:T(8,128)(2,1)} %get-tuple-element.811), channel_id=1, source_target_pairs={{0,2},{2,0},{4,6},{6,4},{8,10},{10,8},{12,14},{14,12},{16,18},{18,... | collective-permute-start | bytes 1769480 | tf_op jit(solution)/shard_map/cond/branch_1_fun/ppermute | solution.py:728
  348.7 36.0 %all-to-all-start.6 = ((bf16[4,2,2,48,384]{4,3,2,1,0:T(8,128)(2,1)}), bf16[4,2,2,48,384]{4,3,2,1,0:T(8,128)(2,1)S(1)}, u32[]{:S(2)}, u32[]{:S(2)}) async-start(bf16[4,2,2,48,384]{4,3,2,1,0:T(8,128)(2,1)} %get-tuple-element.1018), calls=%async_computation.6 | async-start | bytes 1179648 | tf_op jit(solution)/shard_map/all_to_all | solution.py:809
  354.6 26.5 %collective-permute-start.40 = (bf16[2,3,48,768]{3,2,1,0:T(8,128)(2,1)}, bf16[2,3,48,768]{3,2,1,0:T(8,128)(2,1)S(1)}, u32[]{:S(2)}, u32[]{:S(2)}) collective-permute-start(bf16[2,3,48,768]{3,2,1,0:T(8,128)(2,1)} %pad_maximum_fusion.12), channel_id=1, source_target_pairs={{0,2},{2,0},{4,6},{6,4},{8,10},{10,8},{12,14},{14,12},{16,18},{18,... | collective-permute-start | bytes 1327112 | tf_op jit(solution)/shard_map/ppermute | solution.py:728
  (67 other events, 672.8 us)

commit v4 on v3

--- a/solution.py
+++ b/solution.py
@@ -13,7 +13,7 @@
 TILE = 256
 CHUNKS = 3
 SCALE = 1.0
-CALLS = ((0,), (1, 2))
+CALLS = ((0, 1), (2,))
 VMEM = 58 * 1024 * 1024
 LOG2E = math.log2(math.e)
 f32 = jnp.float32
@@ -55,7 +55,7 @@
     return (c_ref[0] ^ rz) * 4 + (c_ref[1] ^ ry) * 2 + (c_ref[2] ^ rx)
 
 
-def load_pieces(c_ref, jobs, sems):
+def piece_copies(c_ref, jobs, sems):
     copies = []
     for kind, pair, view, target in jobs:
         for outer in range(2):
@@ -67,8 +67,6 @@
                             view(pair[outer], inner, rz), target(rows), sems.at[len(copies)]
                         )
                     )
-    for c in copies:
-        c.start()
     return copies
 
 
@@ -100,10 +98,42 @@
     return rstd * (d_hat - m1 - xhat * m2)
 
 
+def two_heads(v):
+    lane = lax.broadcasted_iota(jnp.int32, v.shape, 1)
+    none = jnp.zeros_like(v)
+    return jnp.concatenate([jnp.where(lane < HD, v, none), jnp.where(lane >= HD, v, none)], axis=0)
+
+
+def fill_bias(srow_ref, bias_s):
+    seq = bias_s.shape[0]
+    column = jnp.broadcast_to(srow_ref[0], (128, seq)).T
+    for k in range(0, seq, 128):
+        bias_s[:, k : k + 128] = jnp.where(column == srow_ref[0, :, k : k + 128], 0.0, -1e30)
+
+
+def each_window(win_ref, row, blocks, f):
+    @pl.loop(0, blocks)
+    def _(j):
+        first = win_ref[(row * blocks + j) * 2]
+        n = win_ref[(row * blocks + j) * 2 + 1]
+        for size in range(1, blocks + 1):
+
+            @pl.when(n == size)
+            def _():
+                f(j, first, size)
+
+
+def key_windows(segments):
+    first, last = segments[:, ::128], segments[:, 127::128]
+    low = jnp.sum((last[:, None, :] < first[:, :, None]).astype(jnp.int32), axis=-1)
+    high = jnp.sum((first[:, None, :] <= last[:, :, None]).astype(jnp.int32), axis=-1)
+    return jnp.stack([low, high - low], axis=-1).reshape(-1)
+
+
 def attn_fwd_kernel(
-    heads, piece, c_ref, x_ref, srow_ref, scol_ref, ln_ref, pb_ref, a0, a1_, b0, b1_,
+    heads, piece, c_ref, win_ref, x_ref, srow_ref, ln_ref, pb_ref, a0, a1_, b0, b1_,
     att_ref, att_other_ref, qkv_ref, kt_ref, o_ref, ot_ref, lse_ref,
-    w_s, wo_s, bias_s, sems,
+    w_s, wo_s, bias_s, vt_s, a1_s, sems,
 ):
     cols = heads * HD
     pairs = cols // 128
@@ -115,45 +145,61 @@
     def into_out(block):
         return wo_s.at[pl.ds(pl.multiple_of(block * piece, 16), piece), :]
 
+    jobs = [
+        ("a", (a0, a1_), lambda r, i, z: r.at[i, z, 0], lambda k: into(k, 0)),
+        ("a", (a0, a1_), lambda r, i, z: r.at[i, z, 1], lambda k: into(k, 1)),
+        ("b", (b0, b1_), lambda r, i, z: r.at[i, z, 0], lambda k: into(k, 2)),
+        ("b", (b0, b1_), lambda r, i, z: r.at[i, z, 1], into_out),
+    ]
+    copies = piece_copies(c_ref, jobs, sems)
+
     @pl.when(pl.program_id(0) == 0)
     def _():
-        jobs = [
-            ("a", (a0, a1_), lambda r, i, z: r.at[i, z, 0], lambda k: into(k, 0)),
-            ("a", (a0, a1_), lambda r, i, z: r.at[i, z, 1], lambda k: into(k, 1)),
-            ("b", (b0, b1_), lambda r, i, z: r.at[i, z, 0], lambda k: into(k, 2)),
-            ("b", (b0, b1_), lambda r, i, z: r.at[i, z, 1], into_out),
-        ]
-        for c in load_pieces(c_ref, jobs, sems):
+        for c in copies:
+            c.start()
+
+    xhat, _ = norm_parts(x_ref[0].astype(f32))
+    a1_s[...] = (xhat * ln_ref[0:1] + ln_ref[1:2]).astype(bf16)
+    fill_bias(srow_ref, bias_s)
+
+    @pl.when(pl.program_id(0) == 0)
+    def _():
+        for c in copies:
             c.wait()
 
-    xhat, _ = norm_parts(x_ref[0].astype(f32))
-    a1 = (xhat * ln_ref[0:1] + ln_ref[1:2]).astype(bf16)
+    a1 = a1_s[...]
     proj = (nn_dot(a1, w_s[...]) + pb_ref[...]).astype(bf16)
     for j in range(3):
         for p in range(pairs):
             qkv_ref[0, j, p] = proj[:, j * cols + p * 128 : j * cols + (p + 1) * 128]
     for p in range(pairs):
         kt_ref[0, p] = proj[:, cols + p * 128 : cols + (p + 1) * 128].T
-    bias_s[...] = jnp.where(scol_ref[0] == srow_ref[0], 0.0, -1e30)
-    lane = lax.broadcasted_iota(jnp.int32, (1, 128), 1)
+        vt_s[p] = proj[:, 2 * cols + p * 128 : 2 * cols + (p + 1) * 128].T
     scale2 = HD ** (-0.5) * LOG2E
 
-    @pl.loop(0, pairs)
-    def _(p):
-        q_p = qkv_ref[0, 0, p]
-        k_p = qkv_ref[0, 1, p]
-        v_t = qkv_ref[0, 2, p].T
-        for h in range(2):
-            keep = (lane < HD) if h == 0 else (lane >= HD)
-            q_h = jnp.where(keep, q_p, jnp.zeros_like(q_p))
-            s_t = nt_dot(k_p, q_h) + bias_s[...]
-            top = jnp.max(s_t, axis=0, keepdims=True)
-            e_t = jnp.exp2((s_t - top) * scale2)
-            total = jnp.sum(e_t, axis=0, keepdims=True)
-            p_t = (e_t * (1.0 / total)).astype(bf16)
-            o_t = nn_dot(v_t[h * HD : (h + 1) * HD], p_t)
-            ot_ref[0, p, h * HD : (h + 1) * HD] = o_t.astype(bf16)
-            lse_ref[0, p, pl.ds(h, 1), :] = top * scale2 + jnp.log2(total)
+    def block(j, start, n):
+        keys = pl.ds(pl.multiple_of(start * 128, 128), n * 128)
+        mine = pl.ds(pl.multiple_of(j * 128, 128), 128)
+        bias = bias_s[keys, mine]
+        bias = jnp.concatenate([bias, bias], axis=1)
+        every = range(pairs)
+        s_t = [
+            nt_dot(qkv_ref[0, 1, p, keys, :], two_heads(qkv_ref[0, 0, p, mine, :])) + bias
+            for p in every
+        ]
+        top = [jnp.max(v, axis=0, keepdims=True) for v in s_t]
+        e_t = [jnp.exp2((v - m) * scale2) for v, m in zip(s_t, top)]
+        total = [jnp.sum(v, axis=0, keepdims=True) for v in e_t]
+        p_t = [(v * (1.0 / t)).astype(bf16) for v, t in zip(e_t, total)]
+        o_t = [nn_dot(vt_s[p, :, keys], p_t[p]).astype(bf16) for p in every]
+        for p in every:
+            ot_ref[0, p, :HD, mine] = o_t[p][:HD, :128]
+            ot_ref[0, p, HD:, mine] = o_t[p][HD:, 128:]
+            lse = top[p] * scale2 + jnp.log2(total[p])
+            lse_ref[0, p, 0:1, mine] = lse[:, :128]
+            lse_ref[0, p, 1:2, mine] = lse[:, 128:]
+
+    each_window(win_ref, pl.program_id(0), seq // 128, block)
 
     for p in range(pairs):
         o_ref[0, :, p * 128 : (p + 1) * 128] = ot_ref[0, p].T
@@ -168,7 +214,7 @@
         att_other_ref[...] = att
 
 
-def attn_fwd(coords, x, seg_row, seg_col, ln, proj_bias, pa, pb):
+def attn_fwd(coords, windows, x, seg_row, ln, proj_bias, pa, pb):
     rows, seq, width = x.shape
     cols = proj_bias.shape[-1] // 3
     heads = cols // HD
@@ -190,12 +236,11 @@
         functools.partial(attn_fwd_kernel, heads, piece),
         out_shape=[jax.ShapeDtypeStruct(s, d) for s, d, _, _ in outs],
         grid_spec=pltpu.PrefetchScalarGridSpec(
-            num_scalar_prefetch=1,
+            num_scalar_prefetch=2,
             grid=(rows,),
             in_specs=[
                 pl.BlockSpec((1, seq, width), row3),
                 pl.BlockSpec((1, 1, seq), row3),
-                pl.BlockSpec((1, seq, 1), row3),
                 full_spec((2, width)),
                 full_spec((1, 3 * cols)),
                 ANY, ANY, ANY, ANY,
@@ -205,22 +250,25 @@
                 pltpu.VMEM((width, 3 * cols), bf16),
                 pltpu.VMEM((width, cols), bf16),
                 pltpu.VMEM((seq, seq), f32),
+                pltpu.VMEM((pairs, 128, seq), bf16),
+                pltpu.VMEM((seq, width), bf16),
                 pltpu.SemaphoreType.DMA((64,)),
             ],
         ),
         compiler_params=params(1),
         cost_estimate=cost(2e10, 1e7, 3e6),
         name="attn_fwd",
-    )(coords, x, seg_row, seg_col, ln, proj_bias, *pa, *pb)
+    )(coords, windows, x, seg_row, ln, proj_bias, *pa, *pb)
 
 
 def attn_bwd_kernel(
-    heads, piece, c_ref, dxr_ref, dxr2_ref, x_ref, srow_ref, scol_ref, ln_ref, qkv_ref, kt_ref, o_ref, ot_ref, lse_ref, a0, a1_, b0, b1_,
+    heads, piece, c_ref, win_ref, dxr_ref, dxr2_ref, x_ref, srow_ref, ln_ref, qkv_ref, kt_ref, o_ref, ot_ref, lse_ref, a0, a1_, b0, b1_,
     da1_ref, da1_other_ref, ga0_ref, ga1_ref, gb0_ref, gb1_ref, bsum_ref,
-    w_s, wo_s, bias_s, dp_s, gw_s, go_s, sems,
+    w_s, wo_s, bias_s, dp_s, gw_s, go_s, do_s, row_s, dk_s, dv_s, dqt_s, a1t_s, sems,
 ):
     cols = heads * HD
     pairs = cols // 128
+    seq = x_ref.shape[1]
     step = pl.program_id(0)
 
     def into(block, j):
@@ -229,52 +277,71 @@
     def into_out(block):
         return wo_s.at[pl.ds(pl.multiple_of(block * piece, 16), piece), :]
 
+    jobs = [
+        ("a", (a0, a1_), lambda r, i, z: r.at[i, z, 0], lambda k: into(k, 0)),
+        ("a", (a0, a1_), lambda r, i, z: r.at[i, z, 1], lambda k: into(k, 1)),
+        ("b", (b0, b1_), lambda r, i, z: r.at[i, z, 0], lambda k: into(k, 2)),
+        ("b", (b0, b1_), lambda r, i, z: r.at[i, z, 1], into_out),
+    ]
+    copies = piece_copies(c_ref, jobs, sems)
+
     @pl.when(step == 0)
     def _():
-        jobs = [
-            ("a", (a0, a1_), lambda r, i, z: r.at[i, z, 0], lambda k: into(k, 0)),
-            ("a", (a0, a1_), lambda r, i, z: r.at[i, z, 1], lambda k: into(k, 1)),
-            ("b", (b0, b1_), lambda r, i, z: r.at[i, z, 0], lambda k: into(k, 2)),
-            ("b", (b0, b1_), lambda r, i, z: r.at[i, z, 1], into_out),
-        ]
-        for c in load_pieces(c_ref, jobs, sems):
-            c.wait()
+        for c in copies:
+            c.start()
         gw_s[...] = jnp.zeros_like(gw_s)
         go_s[...] = jnp.zeros_like(go_s)
         bsum_ref[...] = jnp.zeros_like(bsum_ref)
 
+    xhat1, _ = norm_parts(x_ref[0].astype(f32))
+    a1t_s[...] = (xhat1 * ln_ref[0:1] + ln_ref[1:2]).astype(bf16).T
+    fill_bias(srow_ref, bias_s)
+
+    @pl.when(step == 0)
+    def _():
+        for c in copies:
+            c.wait()
+
     dxr = jnp.where(step == c_ref[3], dxr_ref[...], dxr2_ref[...])
     do = nn_dot(dxr, wo_s[...]).astype(bf16)
     go_s[...] += nn_dot(dxr.T, o_ref[0])
-    bias_s[...] = jnp.where(scol_ref[0] == srow_ref[0], 0.0, -1e30)
-    lane = lax.broadcasted_iota(jnp.int32, (1, 128), 1)
     scale = HD ** (-0.5)
     scale2 = scale * LOG2E
-
+    do_s[...] = do
     for p in range(pairs):
-        q_p = qkv_ref[0, 0, p]
-        k_p = qkv_ref[0, 1, p]
-        v_p = qkv_ref[0, 2, p]
-        do_p = do[:, p * 128 : (p + 1) * 128]
-        prod = do_p.T.astype(f32) * ot_ref[0, p].astype(f32)
-        dv = None
+        prod = do[:, p * 128 : (p + 1) * 128].T.astype(f32) * ot_ref[0, p].astype(f32)
         for h in range(2):
-            keep = (lane < HD) if h == 0 else (lane >= HD)
-            q_h = jnp.where(keep, q_p, jnp.zeros_like(q_p))
-            do_h = jnp.where(keep, do_p, jnp.zeros_like(do_p))
-            row = jnp.sum(prod[h * HD : (h + 1) * HD], axis=0, keepdims=True)
-            s_t = nt_dot(k_p, q_h)
-            p_t = jnp.exp2(s_t * scale2 + (bias_s[...] - lse_ref[0, p, h : h + 1, :]))
-            d_t = nt_dot(v_p, do_h)
-            ds_t = (p_t * (d_t - row)).astype(bf16)
-            dv_h = nn_dot(p_t.astype(bf16), do_h)
-            dk_h = nn_dot(ds_t, q_h)
-            dq_h = nn_dot(kt_ref[0, p, h * HD : (h + 1) * HD], ds_t)
-            dv, dk, dq = (dv_h, dk_h, [dq_h]) if dv is None else (dv + dv_h, dk + dk_h, dq + [dq_h])
-        dq = (jnp.concatenate(dq, axis=0) * scale).astype(bf16).T
-        dp_s[:, p * 128 : (p + 1) * 128] = dq
-        dp_s[:, cols + p * 128 : cols + (p + 1) * 128] = (dk * scale).astype(bf16)
-        dp_s[:, 2 * cols + p * 128 : 2 * cols + (p + 1) * 128] = dv.astype(bf16)
+            row_s[p, h : h + 1] = jnp.sum(prod[h * HD : (h + 1) * HD], axis=0, keepdims=True)
+    dk_s[...] = jnp.zeros_like(dk_s)
+    dv_s[...] = jnp.zeros_like(dv_s)
+
+    def block(j, start, n):
+        keys = pl.ds(pl.multiple_of(start * 128, 128), n * 128)
+        mine = pl.ds(pl.multiple_of(j * 128, 128), 128)
+        pair = lambda ref: jnp.concatenate([ref[0:1, mine], ref[1:2, mine]], axis=1)
+        every = range(pairs)
+        bias = bias_s[keys, mine]
+        bias = jnp.concatenate([bias, bias], axis=1)
+        q_2 = [two_heads(qkv_ref[0, 0, p, mine, :]) for p in every]
+        do_2 = [two_heads(do_s[mine, p * 128 : (p + 1) * 128]) for p in every]
+        s_t = [nt_dot(qkv_ref[0, 1, p, keys, :], q_2[p]) * scale2 for p in every]
+        d_t = [nt_dot(qkv_ref[0, 2, p, keys, :], do_2[p]) - pair(row_s.at[p]) for p in every]
+        p_t = [jnp.exp2(s_t[p] + (bias - pair(lse_ref.at[0, p]))) for p in every]
+        for p in every:
+            dv_s[p, keys, :] += nn_dot(p_t[p].astype(bf16), do_2[p])
+        ds_t = [(p_t[p] * d_t[p]).astype(bf16) for p in every]
+        for p in every:
+            dk_s[p, keys, :] += nn_dot(ds_t[p], q_2[p])
+            dq_t = (nn_dot(kt_ref[0, p, :, keys], ds_t[p]) * scale).astype(bf16)
+            dqt_s[p, :HD, mine] = dq_t[:HD, :128]
+            dqt_s[p, HD:, mine] = dq_t[HD:, 128:]
+
+    each_window(win_ref, step, seq // 128, block)
+
+    for p in range(pairs):
+        dp_s[:, p * 128 : (p + 1) * 128] = dqt_s[p].T
+        dp_s[:, cols + p * 128 : cols + (p + 1) * 128] = (dk_s[p] * scale).astype(bf16)
+        dp_s[:, 2 * cols + p * 128 : 2 * cols + (p + 1) * 128] = dv_s[p].astype(bf16)
 
     dproj = dp_s[...]
     da1 = nt_dot(dproj, w_s[...]).astype(bf16)
@@ -288,9 +355,7 @@
         da1_other_ref[...] = da1
 
     bsum_ref[...] += jnp.sum(dproj.astype(f32), axis=0, keepdims=True)
-    xhat1, _ = norm_parts(x_ref[0].astype(f32))
-    a1 = (xhat1 * ln_ref[0:1] + ln_ref[1:2]).astype(bf16)
-    gw_s[...] += nn_dot(a1.T, dproj)
+    gw_s[...] += nn_dot(a1t_s[...], dproj)
 
     @pl.when(step == pl.num_programs(0) - 1)
     def _():
@@ -306,7 +371,7 @@
                     gb[inner, rz, 1] = go_s[rb, :].astype(bf16)
 
 
-def attn_bwd(coords, dxr, dxr2, x, seg_row, seg_col, ln, saved, pa, pb):
+def attn_bwd(coords, windows, dxr, dxr2, x, seg_row, ln, saved, pa, pb):
     rows, seq, width = x.shape
     qkv, kt, o, ot, lse = saved
     cols = o.shape[-1]
@@ -326,12 +391,11 @@
             jax.ShapeDtypeStruct((1, 3 * cols), f32),
         ],
         grid_spec=pltpu.PrefetchScalarGridSpec(
-            num_scalar_prefetch=1,
+            num_scalar_prefetch=2,
             grid=(rows,),
             in_specs=[
                 full_spec((seq, width)), full_spec((seq, width)), tok,
                 pl.BlockSpec((1, 1, seq), row3),
-                pl.BlockSpec((1, seq, 1), row3),
                 full_spec((2, width)),
                 pl.BlockSpec((1, 3, pairs, seq, 128), row5),
                 pl.BlockSpec((1, pairs, 128, seq), row4),
@@ -352,13 +416,19 @@
                 pltpu.VMEM((seq, 3 * cols), bf16),
                 pltpu.VMEM((width, 3 * cols), f32),
                 pltpu.VMEM((width, cols), f32),
+                pltpu.VMEM((seq, cols), bf16),
+                pltpu.VMEM((pairs, 2, seq), f32),
+                pltpu.VMEM((pairs, seq, 128), f32),
+                pltpu.VMEM((pairs, seq, 128), f32),
+                pltpu.VMEM((pairs, 128, seq), bf16),
+                pltpu.VMEM((width, seq), bf16),
                 pltpu.SemaphoreType.DMA((64,)),
             ],
         ),
         compiler_params=params(1),
         cost_estimate=cost(4e10, 2e7, 3e6),
         name="attn_bwd",
-    )(coords, dxr, dxr2, x, seg_row, seg_col, ln, qkv, kt, o, ot, lse, *pa, *pb)
+    )(coords, windows, dxr, dxr2, x, seg_row, ln, qkv, kt, o, ot, lse, *pa, *pb)
 
 
 def sort_kernel(sources, *refs):
@@ -448,7 +518,7 @@
     )(x, own, got, vec)
 
 
-def ffn_kernel(first, count, piece, groups, c_ref, te_ref, n_ref, *refs):
+def ffn_kernel(first, count, piece, groups, c_ref, plan0_ref, plan1_ref, *refs):
     xs_ref, dys_ref, ub_ref, *rest = refs
     if not first:
         zin_ref, din_ref, *rest = rest
@@ -515,13 +585,16 @@
     @pl.loop(0, tiles)
     def _(i):
         group = i // per
-        live = i - group * per < n_ref[group]
+        k = i - group * per
+        info = lambda at: jnp.where(group == 0, plan0_ref[at], plan1_ref[at])
+        tokens = plan0_ref.shape[0] - per - 1
+        live = k < info(tokens + per)
         for c in reads(i):
             c.wait()
 
         @pl.when(live)
         def _():
-            e = te_ref[i]
+            e = info(tokens + k)
             x = x_s[i]
             dy = dy_s[i]
             u = nn_dot(x, wu_s[e]) + ub_ref[e]
@@ -561,10 +634,10 @@
             c.wait()
 
 
-def ffn(coords, tile_expert, used, xs, dys, up_b, weights, carry):
+def ffn(coords, plans, xs, dys, up_b, weights, carry):
     slots, width = xs.shape
     tiles = slots // TILE
-    groups = used.shape[0]
+    groups = len(plans)
     first = not carry
     count = len(weights)
     gshape = weights[0][0].shape
@@ -598,7 +671,7 @@
         compiler_params=params(1),
         cost_estimate=cost(12 * slots * width * hid * 1.5, 4e7, 2 * slots * hid),
         name="ffn",
-    )(coords, tile_expert, used, xs, dys, up_b, *carry, *[w for pair in weights for w in pair])
+    )(coords, plans[0], plans[-1], xs, dys, up_b, *carry, *[w for pair in weights for w in pair])
     zs, das, *rest = out
     return zs, das, [rest[2 * c : 2 * c + 2] for c in range(count)], rest[2 * count]
 
@@ -750,8 +823,8 @@
     return jnp.stack([v[0] for v in blocks]), jnp.stack([v[1] for v in blocks])
 
 
-def gather_xy(a0, b0, size):
-    a0 = jnp.stack([a0, flip(a0, 1, size)])
+def gather_xy(a0, b0, dep, size):
+    a0 = jnp.stack([after(a0, dep), flip(a0, 1, size)])
     b0 = jnp.stack([b0, flip(b0, 2, size)])
     return (a0, flip(a0, 2, size)), (b0, flip(b0, 1, size))
 
@@ -809,8 +882,8 @@
     return lax.all_to_all(v, "dp", 0, 0, axis_index_groups=groups, tiled=True)
 
 
-def along_z(p):
-    return deal_z(jnp.broadcast_to(p, (4,) + p.shape))
+def four_times(p):
+    return jnp.broadcast_to(p, (4,) + p.shape)
 
 
 def sums_y(coords, pair, size):
@@ -823,10 +896,13 @@
 
 def sums_z(coords, parts_y):
     own, send = parts_y
+    return add_z(coords, own, deal_z(send))
+
+
+def add_z(coords, own, got):
     shape = own.shape[1:]
     return whole(
-        sums_z_kernel, "sums_z", [(shape, f32), (shape, bf16)], own, deal_z(send),
-        prefetch=(coords,),
+        sums_z_kernel, "sums_z", [(shape, f32), (shape, bf16)], own, got, prefetch=(coords,)
     )
 
 
@@ -865,7 +941,7 @@
     tile_expert = jnp.minimum(
         jnp.sum((tile_ids[:, None] >= ends[None, :]).astype(jnp.int32), axis=1), experts - 1
     )
-    return mods, pos, tile_expert, ends[-1:]
+    return mods, pos, jnp.concatenate([pos, tile_expert, ends[-1:]])
 
 
 def body(
@@ -891,7 +967,6 @@
     dy = cotangent.reshape(tokens, width)
     rows_here = lambda v: lax.dynamic_slice_in_dim(v, part * mine_rows, mine_rows, 0)
     col_start = part * cols
-    seg_row = segments.reshape(rows, 1, seq)
 
     def small_inputs():
         q_b = lax.dynamic_slice_in_dim(qv_bias[0], col_start, cols)
@@ -900,18 +975,19 @@
             rows_here(layer_input).reshape(mine_tokens, width),
             rows_here(cotangent).reshape(mine_tokens, width),
             jnp.concatenate([q_b, jnp.zeros_like(q_b), v_b]).reshape(1, 3 * cols),
-            segments.reshape(rows, seq, 1),
+            segments.reshape(rows, 1, seq),
+            key_windows(segments),
             jnp.concatenate([out_bias[None], ln_gain[1:2], ln_bias[1:2]]),
             jnp.concatenate([ln_gain[0:1], ln_bias[0:1]]),
         )
 
     def fwd(coords, pa, pb):
-        own, other, *saved = attn_fwd(coords, layer_input, seg_row, seg_col, ln1, proj_bias, pa, pb)
+        own, other, *saved = attn_fwd(coords, windows, layer_input, seg_row, ln1, proj_bias, pa, pb)
         return (saved, *mid(x_mine, own, swap(other), vec))
 
     def bwd(coords, dxr, dx2, saved, pa, pb):
         own, other, *rest = attn_bwd(
-            coords, *dxr, layer_input, seg_row, seg_col, ln1, saved, pa, pb
+            coords, windows, *dxr, layer_input, seg_row, ln1, saved, pa, pb
         )
         return (*norm_grad((own, swap(other)), x_mine, dx2, ln_gain[0:1], False), *rest)
 
@@ -952,46 +1028,46 @@
             call = CALLS[k]
             ub = up_b[:, None, call[0] * hc : (call[-1] + 1) * hc]
             return ffn(
-                coords, tile_expert, used, xs, dys, ub, [weights[c] for c in call], carry
+                coords, (plan_own, plan), xs, dys, ub, [weights[c] for c in call], carry
             )
 
         def begin():
             w = jnp.stack([w_up, w_down])
             keep = lax.dynamic_slice_in_dim(w, x_bit * half, half, 3)
-            near = flip(lax.dynamic_slice_in_dim(w, (1 - x_bit) * half, half, 3), 1, size)
+            send = lax.dynamic_slice_in_dim(w, (1 - x_bit) * half, half, 3)
+            near = flip(send, 1, size)
             pieces = [
                 jnp.stack([keep[..., c * hc : (c + 1) * hc], near[..., c * hc : (c + 1) * hc]])
                 for c in range(CHUNKS)
             ]
+            pieces[0] = four_times(pieces[0])
             ab = gather_z(w_qkv[:2], jnp.stack([w_qkv[2], w_out]), size)
-            mods, pos, tile_expert, used = token_plan(segments, modality, experts)
-            plan = flip(jnp.concatenate([pos, tile_expert, used]), 1, size)
-            return pieces, ab, mods, pos, plan, tile_expert, used, small_inputs()
-
-        pieces, ab, mods, pos, plan, tile_expert, used, smalls = phase(pred, begin)
-        x_mine, dy_mine, proj_bias, seg_col, vec, ln1 = smalls
+            mods, pos, plan_own = token_plan(segments, modality, experts)
+            return pieces, ab, mods, pos, plan_own, flip(plan_own, 1, size), small_inputs()
+
+        pieces, ab, mods, pos, plan_own, plan, smalls = phase(pred, begin)
+        x_mine, dy_mine, proj_bias, seg_row, windows, vec, ln1 = smalls
 
         def weights_in():
             def inside():
                 pos_row = pos.reshape(1, tokens)
                 dys = sort_tokens([(pos_row, dy)], tiles, 0, 2)
+                later = [four_times(v) for v in pieces[1:]]
                 hot = (mods[:, None] == jnp.arange(experts, dtype=jnp.int32)).astype(bf16)
                 return (
-                    *gather_xy(*ab, size), halves(pos), halves(plan),
-                    jnp.concatenate([tile_expert, plan[tokens : tokens + tiles]]),
-                    jnp.concatenate([used, plan[tokens + tiles :]]), dys, tn_dot(hot, dy),
+                    *gather_xy(*ab, later, size), halves(pos), halves(plan),
+                    dys, tn_dot(hot, dy),
+                    later,
                 )
 
-            return along_z(pieces[0]), phase(inner, inside)
-
-        z0, (pa, pb, pos_here, pos_near, tile_expert, used, dys, g_down_bias) = phase(
-            pred, weights_in
-        )
+            return deal_z(pieces[0]), phase(inner, inside)
+
+        z0, (pa, pb, pos_here, pos_near, dys, g_down_bias, later) = phase(pred, weights_in)
 
         def forward():
             return (
                 *phase(inner, lambda: fwd(coords, pa, pb)), flip(z0, 2, size),
-                along_z(pieces[1]), flip(dy_mine, 1, size),
+                deal_z(later[0]), flip(dy_mine, 1, size),
             )
 
         saved, x2, a2, y0, z1, dy_near = phase(pred, forward)
@@ -1010,7 +1086,7 @@
             )
             near = after(near, d, xs)
             xs = phase(inner, lambda: sort(pos_near, near, swap(near), 1, xs))
-            return xs, d, flip(z1, 2, size), along_z(pieces[2])
+            return xs, d, flip(z1, 2, size), deal_z(later[1])
 
         xs, dys, y1, z2 = phase(pred, exchange)
         weights = [(z0, y0), (z1, y1)]
@@ -1066,30 +1142,29 @@
                 out = finish(x2, z_sum, mods)
                 return out, swap(out), swap(grad)
 
+            rows_all = phase(inner, lambda: small_rows(sums1, sums2, bsum, g_upb, g_down_bias))
+
             def small_start():
-                total = small_rows(sums1, sums2, bsum, g_upb, g_down_bias)
-                total = total + swap(total)
+                total = rows_all + swap(rows_all)
                 return total + flip(total, 1, size)
 
-            g2 = sums_z(coords, v2)
+            got2 = deal_z(after(v2[1], rows_all))
             got_a, got_b = flip(ga1, 2, size), flip(gb1, 1, size)
             outs = phase(inner, out_rows)
             a_own, a_send, b_own, b_send = attn_sums_1((ga0, gb0), (got_a, got_b), outs)
             got_a, got_b = flip(a_send, 1, size), flip(b_send, 2, size)
             small = phase(inner, small_start)
-            return attn_sums_2(coords, (a_own, b_own), (got_a, got_b), small), g2, small, outs
-
-        (own, send), g2, small, (out, out_other, grad_other) = phase(pred, sum_up)
-
-        def inside():
-            total = small
-            for mask in (2, 4, 8):
-                total = total + flip(total, mask, size)
-            return total
+            return attn_sums_2(coords, (a_own, b_own), (got_a, got_b), small), got2, small, outs
+
+        (own, send), got2, small, (out, out_other, grad_other) = phase(pred, sum_up)
 
         got = deal_z(send)
+        g2 = add_z(coords, v2[0], got2)
         near = flip(jnp.concatenate([v[1] for v in (g0, g1, g2)], axis=-1), 1, size)
-        small = phase(inner, inside)
+        total = phase(inner, lambda: small + flip(small, 2, size))
+        rows_z = jnp.stack([total] + [flip(total, 4 * rz, size) for rz in (1, 2, 3)])
+        pick = lambda z: lax.dynamic_index_in_dim(rows_z, coords[0] ^ z, 0, False)
+        small = pick(0) + pick(1) + pick(2) + pick(3)
         layer_output, grad_input = whole(
             rows_kernel, "rows", [((parts,) + v.shape, v.dtype) for v in (out, grad)],
             out, out_other, grad, grad_other, prefetch=(coords,),
@@ -1104,13 +1179,13 @@
         )
     else:
         coords = jnp.stack([0, 0, 0, part]).astype(jnp.int32)
-        x_mine, dy_mine, proj_bias, seg_col, vec, ln1 = small_inputs()
+        x_mine, dy_mine, proj_bias, seg_row, windows, vec, ln1 = small_inputs()
         hid_start = part * hid
         hc = hid // CHUNKS
         up_b = lax.dynamic_slice_in_dim(up_bias, hid_start, hid, 1)
         pa, pb = gather_pieces_plain(w_qkv[:2], jnp.stack([w_qkv[2], w_out]))
         weights = expert_pieces_plain(w_up, w_down)
-        mods, pos, tile_expert, used = token_plan(segments, modality, experts)
+        mods, pos, plan_own = token_plan(segments, modality, experts)
         pos_row = pos.reshape(1, tokens)
         hot = (mods[:, None] == jnp.arange(experts, dtype=jnp.int32)).astype(bf16)
         g_down_bias = tn_dot(hot, dy)
@@ -1123,7 +1198,7 @@
         for call in CALLS:
             ub = up_b[:, None, call[0] * hc : (call[-1] + 1) * hc]
             zs, das, pairs, gub = ffn(
-                coords, tile_expert, used, xs, dys, ub, [weights[c] for c in call], carry
+                coords, (plan_own,), xs, dys, ub, [weights[c] for c in call], carry
             )
             carry = (zs, das)
             g_upb.append(gub[:, 0])

time: 391 us -> 374 us (0.957)
  waiting for transfers between devices: 57.2 us -> 46.1 us
    ppermute x28 -> x29, waiting for transfers between devices: 32.9 us -> 21.4 us  [flip(): return lax.ppermute(x, 'dp', [(i, i ^ mask) for i in range(size)])]
    cond x60 -> x61, local copies, waits for them, and re-layouts: 10.3 us -> 10.5 us
    ppermute x28 -> x29, starting transfers between devices: 37.7 us -> 37.8 us  [flip(): return lax.ppermute(x, 'dp', [(i, i ^ mask) for i in range(size)])]
  transfers between devices with their start and end apart: 48 -> 49, of which waited for: 23 -> 22; matrix products, arithmetic and copies ran while one was open for 12% -> 12% of each run, Pallas kernels for 43% -> 45%
where the time goes in v4:
time: 374 us; the launch traced here: 369 us
  Pallas kernels  175 us (47%)
  starting transfers between devices  84.5 us (23%)
  waiting for transfers between devices  46.1 us (12%)
  local copies, waits for them, and re-layouts  37.8 us (10%)
  other arithmetic  22.7 us (6%)
    pallas_call x2, Pallas kernels, ffn(): pl.pallas_call(functools.partial(ffn_kernel, first, count, piece, groups)...  48.3 us
    all_to_all x7, starting transfers between devices, deal_z(): return lax.all_to_all(v, 'dp', 0, 0, axis_index_groups=groups, tiled=True)  44.8 us
    ppermute x29, starting transfers between devices, flip(): return lax.ppermute(x, 'dp', [(i, i ^ mask) for i in range(size)])  37.8 us
    pallas_call x11, Pallas kernels, whole(): pl.pallas_call(kernel, out_shape=[jax.ShapeDtypeStruct(s, d) for s, d in...  34.1 us
    pallas_call x1, Pallas kernels, attn_bwd(): pl.pallas_call(functools.partial(attn_bwd_kernel, heads, piece), out_shap...  25.4 us
    ppermute x29, waiting for transfers between devices, flip(): return lax.ppermute(x, 'dp', [(i, i ^ mask) for i in range(size)])  21.4 us
    ppermute x13, waiting for transfers between devices, swap(): return lax.ppermute(v, 'mp', [(0, 1), (1, 0)])  21.3 us
    pallas_call x4, Pallas kernels, unsort_tokens(): pl.pallas_call(functools.partial(unsort_kernel, len(places)), out_shape=[...  20.9 us
  transfers between devices with their start and end apart: 49, of which 22 were waited for; matrix products, arithmetic and copies ran while one was open for 12% of the time, Pallas kernels for 45%

profile of v4, /device:TPU:0, one launch (start us, length us, event | category | flops | bytes accessed | tf_op | source)
XLA Modules:
  0.0 369.3 jit_solution(3269772712716345536)
XLA Ops:
  1.4 25.6 %conditional.21 = (bf16[4,2,2,3,48,256]{5,4,3,2,1,0:T(8,128)(2,1)}, bf16[2,2,3,48,256]{4,3,2,1,0:T(8,128)(2,1)S(1)}, bf16[2,2,3,48,256]{4,3,2,1,0:T(8,128)(2,1)}...) conditional(s32[]{:T(128)} %convert_element_type.89, () %tuple.183, ...), branch_computations={%region_0.1_spmd, %region_1.9_spmd} | conditional | flops 10636936 | bytes 24564060 | solution.py:875
  27.5 32.5 %conditional.22 = (bf16[4,2,2,3,48,256]{5,4,3,2,1,0:T(8,128)(2,1)}, bf16[2,4,2,48,384]{4,3,2,1,0:T(8,128)(2,1)}, bf16[2,4,2,48,384]{4,3,2,1,0:T(8,128)(2,1)}, bf...) conditional(s32[]{:T(128)} %convert_element_type.89, () %tuple.182, ...), branch_computations={%region_9.10_spmd, %region_10.13_spmd} | conditional | flops 2421230592 | bytes 33819932 | solution.py:875
  32.7 25.3 %conditional = (bf16[2,4,2,48,384]{4,3,2,1,0:T(8,128)(2,1)}, bf16[2,4,2,48,384]{4,3,2,1,0:T(8,128)(2,1)}, bf16[2,4,2,48,384]{4,3,2,1,0:T(8,128)(2,1)}, bf16[2,4,...) conditional(s32[]{:T(128)} %convert_element_type.53, () %tuple.106, ...), branch_computations={%region_11.11_spmd, %region_12.12_spmd} | conditional | flops 2421230592 | bytes 23989290 | solution.py:875
  60.0 32.5 %conditional.23 = (bf16[2,3,3,512,128]{4,3,2,1,0:T(8,128)(2,1)}, bf16[2,3,128,512]{3,2,1,0:T(8,128)(2,1)}, bf16[2,512,384]{2,1,0:T(8,128)(2,1)}, bf16[2,3,128,51...) conditional(s32[]{:T(128)} %convert_element_type.89, () %tuple.188, ...), branch_computations={%region_13.14_spmd, %region_14.17_spmd} | conditional | flops 20010000384 | bytes 38994812 | solution.py:875
  67.5 23.2 %conditional.1 = (bf16[2,3,3,512,128]{4,3,2,1,0:T(8,128)(2,1)}, bf16[2,3,128,512]{3,2,1,0:T(8,128)(2,1)}, bf16[2,512,384]{2,1,0:T(8,128)(2,1)}, bf16[2,3,128,512...) conditional(s32[]{:T(128)} %convert_element_type.54, () %tuple.112, ...), branch_computations={%region_15.15_spmd, %region_16.16_spmd} | conditional | flops 20010000384 | bytes 21299772 | solution.py:875
  68.1 16.3 %attn_fwd.1 = (bf16[512,768]{1,0:T(8,128)(2,1)}, bf16[512,768]{1,0:T(8,128)(2,1)}, bf16[2,3,3,512,128]{4,3,2,1,0:T(8,128)(2,1)}, bf16[2,3,128,512]{3,2,1,0:T(8,1...) custom-call(s32[4]{0:T(128)S(1)} %get-tuple-element.531.c_ref, ...), custom_call_target="tpu_custom_call" | custom-call | flops 20000000000 | bytes 10000000 | tf_op jit(solution)/shard_map/cond/branch_1_fun/cond/branch_1_fun/attn_fwd/pallas_call | solution.py:235
  92.5 32.7 %conditional.24 = (bf16[3072,768]{1,0:T(8,128)(2,1)}, bf16[3072,768]{1,0:T(8,128)(2,1)}, bf16[4,2,2,3,48,256]{5,4,3,2,1,0:T(8,128)(2,1)}, bf16[4,2,2,3,48,256]{5,4,3,2,1,0:T(8,128)(2,1)}) conditional(s32[]{:T(128)} %convert_element_type.89, () %tuple.187, (pred[]{:T(512)}, bf16[512,768]{1,0:T(8,128)(2,1)}, bf16[512,768]{1,0:T(8,128)(2,1)}, ...), branch_computations={%region_17.18_spmd, %region_18.23_spmd} | conditional | flops 7247757312 | bytes 60278096 | solution.py:875
  100.2 14.8 %conditional.2 = (bf16[3072,768]{1,0:T(8,128)(2,1)}, bf16[3072,768]{1,0:T(8,128)(2,1)}) conditional(s32[]{:T(128)} %convert_element_type.55, () %tuple.119, (bf16[512,768]{1,0:T(8,128)(2,1)}, s32[1,512]{1,0:T(1,128)}, s32[1,512]{1,0:T(1,128)}, bf16[3072,768]{1,0:T(8,128)(2,1)}, bf16[512,768]{1,0:T(8,128)(2,1)}, /*index=5*/s32[1,512]{1,0:T(1,128)}, ...), branch_computations={%region_19.19_spmd, %region_20.20_spmd} | conditional | flops 4831838208 | bytes 32583064 | solution.py:875
  117.1 8.2 %conditional.3 = (bf16[3072,768]{1,0:T(8,128)(2,1)}) conditional(s32[]{:T(128)} %convert_element_type.55, () %tuple.118, (bf16[512,768]{1,0:T(8,128)(2,1)S(1)}, s32[1,512]{1,0:T(1,128)}, s32[1,512]{1,0:T(1,128)}, bf16[3072,768]{1,0:T(8,128)(2,1)}) %tuple.122), branch_computations={%region_21.21_spmd, %region_22.22_spmd} | conditional | flops 2415919104 | bytes 16291532 | solution.py:875
  125.3 30.2 %conditional.25 = (bf16[3072,768]{1,0:T(8,128)(2,1)}, bf16[3072,768]{1,0:T(8,128)(2,1)}, bf16[4,2,2,3,48,256]{5,4,3,2,1,0:T(8,128)(2,1)S(1)}, bf16[4,2,2,3,48,25...) conditional(s32[]{:T(128)} %convert_element_type.89, () %tuple.191, ...), branch_computations={%region_23.24_spmd, %region_24.25_spmd} | conditional | flops 21743271936 | bytes 44743272 | solution.py:875
  127.4 28.2 %ffn.2 = (bf16[3072,768]{1,0:T(8,128)(2,1)}, bf16[3072,768]{1,0:T(8,128)(2,1)}, bf16[4,2,2,3,48,256]{5,4,3,2,1,0:T(8,128)(2,1)S(1)}, bf16[4,2,2,3,48,256]{5,4,3,...) custom-call(s32[4]{0:T(128)S(1)} %get-tuple-element.599.c_ref, ...), custom_call_target="tpu_custom_call" | custom-call | flops 21743271936 | bytes 40000000 | tf_op jit(solution)/shard_map/cond/branch_1_fun/ffn/pallas_call | solution.py:646
  155.6 34.6 %conditional.26 = (bf16[3072,768]{1,0:T(8,128)(2,1)}, bf16[3072,768]{1,0:T(8,128)(2,1)}, bf16[4,2,2,3,48,256]{5,4,3,2,1,0:T(8,128)(2,1)}, bf16[4,2,2,3,48,256]{5...) conditional(s32[]{:T(128)} %convert_element_type.89, () %tuple.186, ...), branch_computations={%region_25.26_spmd, %region_26.29_spmd} | conditional | flops 13290128384 | bytes 64236196 | solution.py:875
  156.3 30.6 %conditional.4 = (bf16[3072,768]{1,0:T(8,128)(2,1)}, bf16[3072,768]{1,0:T(8,128)(2,1)}, bf16[4,2,2,3,48,256]{5,4,3,2,1,0:T(8,128)(2,1)}, bf16[4,2,2,3,48,256]{5,...) conditional(s32[]{:T(128)} %convert_element_type.63, () %tuple.129, ...), branch_computations={%region_27.27_spmd, %region_28.28_spmd} | conditional | flops 13289127936 | bytes 55517400 | solution.py:875
  156.9 20.1 %ffn.3 = (bf16[3072,768]{1,0:T(8,128)(2,1)}, bf16[3072,768]{1,0:T(8,128)(2,1)}, bf16[4,2,2,3,48,256]{5,4,3,2,1,0:T(8,128)(2,1)}, bf16[4,2,2,3,48,256]{5,4,3,2,1,0:T(8,128)(2,1)}, f32[3,1,256]{2,1,0:T(1,128)}) custom-call(s32[4]{0:T(128)S(1)} %get-tuple-element.617.c_ref, s32[1031]{0:T(1024)} %get-tuple-element.618.plan0_ref, ...), custom_call_target="tpu_custom_call" | custom-call | flops 10871635968 | bytes 40000000 | tf_op jit(solution)/shard_map/cond/branch_1_fun/cond/branch_1_fun/ffn/pallas_call | solution.py:646
  190.9 50.5 %conditional.27 = (f32[512,768]{1,0:T(8,128)}, bf16[512,768]{1,0:T(8,128)(2,1)}, bf16[512,768]{1,0:T(8,128)(2,1)}, f32[8,768]{1,0:T(8,128)}, bf16[512,768]{1,0:T...) conditional(s32[]{:T(128)} %convert_element_type.89, () %tuple.195, ...), branch_computations={%region_29.30_spmd, %region_30.35_spmd} | conditional | flops 4855410688 | bytes 67070724 | solution.py:875
  190.9 15.3 %all-to-all-start.3 = ((bf16[4,2,2,3,48,256]{5,4,3,2,1,0:T(8,128)(2,1)}), bf16[4,2,2,3,48,256]{5,4,3,2,1,0:T(8,128)(2,1)S(1)}, u32[]{:S(2)}, u32[]{:S(2)}) async-start(bf16[4,2,2,3,48,256]{5,4,3,2,1,0:T(8,128)(2,1)} %get-tuple-element.698), calls=%async_computation.3 | async-start | bytes 2359296 | tf_op jit(solution)/shard_map/cond/branch_1_fun/all_to_all | solution.py:882
  208.7 13.3 %conditional.5 = (bf16[512,768]{1,0:T(8,128)(2,1)S(1)}, bf16[512,768]{1,0:T(8,128)(2,1)}, bf16[512,768]{1,0:T(8,128)(2,1)}) conditional(s32[]{:T(128)} %convert_element_type.80, () %tuple.138, (s32[1,512]{1,0:T(1,128)}, s32[1,512]{1,0:T(1,128)}, bf16[3072,768]{1,0:T(8,128)(2,1)}, s32[1,512]{1,0:T(1,128)}, s32[1,512]{1,0:T(1,128)}, ...), branch_computations={%region_31.31_spmd, %region_32.32_spmd} | conditional | flops 4833411072 | bytes 31796612 | solution.py:875
  226.9 7.2 %conditional.6 = (f32[512,768]{1,0:T(8,128)}, bf16[512,768]{1,0:T(8,128)(2,1)}, bf16[512,768]{1,0:T(8,128)(2,1)}, f32[8,768]{1,0:T(8,128)}) conditional(s32[]{:T(128)} %convert_element_type.80, () %tuple.137, (f32[2,768]{1,0:T(2,128)S(1)}, bf16[512,768]{1,0:T(8,128)(2,1)S(1)}, bf16[512,768]{1,0:T(8,128)(2,1)}, bf16[512,768]{1,0:T(8,128)(2,1)}, ...), branch_computations={%region_33.33_spmd, %region_34.34_spmd} | conditional | flops 20000000 | bytes 11151944 | solution.py:875
  241.4 48.6 %conditional.28 = (f32[512,768]{1,0:T(8,128)}, f32[8,768]{1,0:T(8,128)}, bf16[2,4,2,48,384]{4,3,2,1,0:T(8,128)(2,1)}, bf16[2,4,2,48,384]{4,3,2,1,0:T(8,128)(2,1)...) conditional(s32[]{:T(128)} %convert_element_type.89, () %tuple.194, ...), branch_computations={%region_35.36_spmd, %region_36.39_spmd} | conditional | flops 40021999616 | bytes 63146784 | solution.py:875
  249.1 33.2 %conditional.7 = (f32[512,768]{1,0:T(8,128)}, f32[8,768]{1,0:T(8,128)}, bf16[2,4,2,48,384]{4,3,2,1,0:T(8,128)(2,1)}, bf16[2,4,2,48,384]{4,3,2,1,0:T(8,128)(2,1)}...) conditional(s32[]{:T(128)} %convert_element_type.81, () %tuple.145, ...), branch_computations={%region_37.37_spmd, %region_38.38_spmd} | conditional | flops 40020000768 | bytes 34305916 | solution.py:875
  249.7 25.4 %attn_bwd.1 = (bf16[512,768]{1,0:T(8,128)(2,1)}, bf16[512,768]{1,0:T(8,128)(2,1)}, bf16[2,4,2,48,384]{4,3,2,1,0:T(8,128)(2,1)}, bf16[2,4,2,48,384]{4,3,2,1,0:T(8...) custom-call(s32[4]{0:T(128)S(1)} %get-tuple-element.705.c_ref, ...), custom_call_target="tpu_custom_call" | custom-call | flops 40000000000 | bytes 20000000 | tf_op jit(solution)/shard_map/cond/branch_1_fun/cond/branch_1_fun/attn_bwd/pallas_call | solution.py:386
  290.1 42.3 %conditional.29 = (f32[2,2,48,384]{3,2,1,0:T(8,128)S(1)}, bf16[4,2,2,48,384]{4,3,2,1,0:T(8,128)(2,1)}, bf16[4,2,2,3,48,256]{5,4,3,2,1,0:T(8,128)(2,1)}, bf16[512...) conditional(s32[]{:T(128)} %convert_element_type.89, () %tuple.181, ...), branch_computations={%region_39.40_spmd, %region_40.47_spmd} | conditional | flops 2422283008 | bytes 54332388 | solution.py:875
  296.8 15.1 %conditional.8 = (bf16[512,768]{1,0:T(8,128)(2,1)}, bf16[512,768]{1,0:T(8,128)(2,1)}, f32[512,768]{1,0:T(8,128)}) conditional(s32[]{:T(128)} %convert_element_type.86, () %tuple.151, (s32[1,512]{1,0:T(1,128)}, s32[1,512]{1,0:T(1,128)}, bf16[3072,768]{1,0:T(8,128)(2,1)}, bf16[512,768]{1,0:T(8,128)(2,1)}, s32[]{:T(128)}, ...), branch_computations={%region_41.41_spmd, %region_42.42_spmd} | conditional | flops 2420246016 | bytes 27334466 | solution.py:875
  332.3 7.0 %conditional.30 = (f32[22,768]{1,0:T(8,128)}, f32[1,22,768]{2,1,0:T(8,128)S(1)}) conditional(s32[]{:T(128)} %convert_element_type.90, () %tuple.199, f32[22,768]{1,0:T(8,128)} %get-tuple-element.1009), branch_computations={%region_47.48_spmd, %region_48.49_spmd} | conditional | flops 16896 | bytes 608312 | solution.py:875
  (291 shorter events, 272.2 us)
Async XLA Ops:
  3.1 16.3 %collective-permute-start.30 = (bf16[2,2,48,384]{3,2,1,0:T(8,128)(2,1)S(1)}, bf16[2,2,48,384]{3,2,1,0:T(8,128)(2,1)}, u32[]{:S(2)}, u32[]{:S(2)}) collective-permute-start(bf16[2,2,48,384]{3,2,1,0:T(8,128)(2,1)S(1)} %pad_maximum_fusion.8), channel_id=1, source_target_pairs={{0,8},{2,10},{4,12},{6,14},{8,0},{10,2},{12,4},{14,6},{16,24},{18,... | collective-permute-start | bytes 442376 | tf_op jit(solution)/shard_map/cond/branch_1_fun/ppermute | solution.py:801
  6.2 14.2 %collective-permute-start.31 = (bf16[2,2,48,384]{3,2,1,0:T(8,128)(2,1)S(1)}, bf16[2,2,48,384]{3,2,1,0:T(8,128)(2,1)}, u32[]{:S(2)}, u32[]{:S(2)}) collective-permute-start(bf16[2,2,48,384]{3,2,1,0:T(8,128)(2,1)S(1)} %pad_maximum_fusion.8), channel_id=1, source_target_pairs={{0,16},{2,18},{4,20},{6,22},{8,24},{10,26},{12,28},{14,30},{16,0},... | collective-permute-start | bytes 442376 | tf_op jit(solution)/shard_map/cond/branch_1_fun/ppermute | solution.py:801
  27.5 32.4 %all-to-all-start.5 = ((bf16[4,2,2,3,48,256]{5,4,3,2,1,0:T(8,128)(2,1)}), bf16[4,2,2,3,48,256]{5,4,3,2,1,0:T(8,128)(2,1)}, u32[]{:S(2)}, u32[]{:S(2)}) async-start(bf16[4,2,2,3,48,256]{5,4,3,2,1,0:T(8,128)(2,1)} %get-tuple-element.508), calls=%async_computation.5 | async-start | bytes 2359296 | tf_op jit(solution)/shard_map/cond/branch_1_fun/all_to_all | solution.py:882
  60.0 32.5 %all-to-all-start = ((bf16[4,2,2,3,48,256]{5,4,3,2,1,0:T(8,128)(2,1)}), bf16[4,2,2,3,48,256]{5,4,3,2,1,0:T(8,128)(2,1)}, u32[]{:S(2)}, u32[]{:S(2)}) async-start(bf16[4,2,2,3,48,256]{5,4,3,2,1,0:T(8,128)(2,1)} %get-tuple-element.573), calls=%async_computation | async-start | bytes 2359296 | tf_op jit(solution)/shard_map/cond/branch_1_fun/all_to_all | solution.py:882
  64.5 27.3 %collective-permute-start.1 = (bf16[4,2,2,3,48,256]{5,4,3,2,1,0:T(8,128)(2,1)}, bf16[4,2,2,3,48,256]{5,4,3,2,1,0:T(8,128)(2,1)}, u32[]{:S(2)}, u32[]{:S(2)}) collective-permute-start(bf16[4,2,2,3,48,256]{5,4,3,2,1,0:T(8,128)(2,1)} %get-tuple-element.572), channel_id=1, source_target_pairs={{0,4},{2,6},{4,0},{6,2},{8,12},{10,14},{12,8},{14,10},{16,20},{18,... | collective-permute-start | bytes 3538952 | tf_op jit(solution)/shard_map/cond/branch_1_fun/ppermute | solution.py:801
  66.0 24.7 %collective-permute-start.2 = (bf16[512,768]{1,0:T(8,128)(2,1)S(1)}, bf16[512,768]{1,0:T(8,128)(2,1)}, u32[]{:S(2)}, u32[]{:S(2)}) collective-permute-start(bf16[512,768]{1,0:T(8,128)(2,1)S(1)} %get-tuple-element.574), channel_id=1, source_target_pairs={{0,2},{2,0},{4,6},{6,4},{8,10},{10,8},{12,14},{14,12},{16,18},{18,... | collective-permute-start | bytes 2359304 | tf_op jit(solution)/shard_map/cond/branch_1_fun/ppermute | solution.py:801
  92.5 32.7 %all-to-all-start.1 = ((bf16[4,2,2,3,48,256]{5,4,3,2,1,0:T(8,128)(2,1)}), bf16[4,2,2,3,48,256]{5,4,3,2,1,0:T(8,128)(2,1)}, u32[]{:S(2)}, u32[]{:S(2)}) async-start(bf16[4,2,2,3,48,256]{5,4,3,2,1,0:T(8,128)(2,1)} %get-tuple-element.598), calls=%async_computation.1 | async-start | bytes 2359296 | tf_op jit(solution)/shard_map/cond/branch_1_fun/all_to_all | solution.py:882
  97.1 28.2 %collective-permute-start.7 = (bf16[4,2,2,3,48,256]{5,4,3,2,1,0:T(8,128)(2,1)}, bf16[4,2,2,3,48,256]{5,4,3,2,1,0:T(8,128)(2,1)}, u32[]{:S(2)}, u32[]{:S(2)}) collective-permute-start(bf16[4,2,2,3,48,256]{5,4,3,2,1,0:T(8,128)(2,1)} %get-tuple-element.597), channel_id=1, source_target_pairs={{0,4},{2,6},{4,0},{6,2},{8,12},{10,14},{12,8},{14,10},{16,20},{18,... | collective-permute-start | bytes 3538952 | tf_op jit(solution)/shard_map/cond/branch_1_fun/ppermute | solution.py:801
  98.7 18.4 %collective-permute-start.6 = (bf16[512,768]{1,0:T(8,128)(2,1)}, bf16[512,768]{1,0:T(8,128)(2,1)S(1)}, u32[]{:S(2)}, u32[]{:S(2)}) collective-permute-start(bf16[512,768]{1,0:T(8,128)(2,1)} %get-tuple-element.587), channel_id=1, source_target_pairs={{0,2},{2,0},{4,6},{6,4},{8,10},{10,8},{12,14},{14,12},{16,18},{18,... | collective-permute-start | bytes 2359304 | tf_op jit(solution)/shard_map/cond/branch_1_fun/ppermute | solution.py:801
  125.3 30.2 %collective-permute-start.8 = (bf16[4,2,2,3,48,256]{5,4,3,2,1,0:T(8,128)(2,1)}, bf16[4,2,2,3,48,256]{5,4,3,2,1,0:T(8,128)(2,1)}, u32[]{:S(2)}, u32[]{:S(2)}) collective-permute-start(bf16[4,2,2,3,48,256]{5,4,3,2,1,0:T(8,128)(2,1)} %get-tuple-element.616), channel_id=1, source_target_pairs={{0,4},{2,6},{4,0},{6,2},{8,12},{10,14},{12,8},{14,10},{16,20},{18,... | collective-permute-start | bytes 3538952 | tf_op jit(solution)/shard_map/cond/branch_1_fun/ppermute | solution.py:801
  155.6 31.3 %collective-permute-start.17 = (bf16[4,2,2,3,48,256]{5,4,3,2,1,0:T(8,128)(2,1)}, bf16[4,2,2,3,48,256]{5,4,3,2,1,0:T(8,128)(2,1)}, u32[]{:S(2)}, u32[]{:S(2)}) collective-permute-start(bf16[4,2,2,3,48,256]{5,4,3,2,1,0:T(8,128)(2,1)} %get-tuple-element.656), channel_id=1, source_target_pairs={{0,4},{2,6},{4,0},{6,2},{8,12},{10,14},{12,8},{14,10},{16,20},{18,... | collective-permute-start | bytes 3538952 | tf_op jit(solution)/shard_map/cond/branch_1_fun/ppermute | solution.py:801
  190.9 46.7 %all-to-all-start.3 = ((bf16[4,2,2,3,48,256]{5,4,3,2,1,0:T(8,128)(2,1)}), bf16[4,2,2,3,48,256]{5,4,3,2,1,0:T(8,128)(2,1)S(1)}, u32[]{:S(2)}, u32[]{:S(2)}) async-start(bf16[4,2,2,3,48,256]{5,4,3,2,1,0:T(8,128)(2,1)} %get-tuple-element.698), calls=%async_computation.3 | async-start | bytes 2359296 | tf_op jit(solution)/shard_map/cond/branch_1_fun/all_to_all | solution.py:882
  206.2 28.0 %collective-permute-start.21 = (bf16[4,2,2,3,48,256]{5,4,3,2,1,0:T(8,128)(2,1)}, bf16[4,2,2,3,48,256]{5,4,3,2,1,0:T(8,128)(2,1)}, u32[]{:S(2)}, u32[]{:S(2)}) collective-permute-start(bf16[4,2,2,3,48,256]{5,4,3,2,1,0:T(8,128)(2,1)} %get-tuple-element.702), channel_id=1, source_target_pairs={{0,4},{2,6},{4,0},{6,2},{8,12},{10,14},{12,8},{14,10},{16,20},{18,... | collective-permute-start | bytes 3538952 | tf_op jit(solution)/shard_map/cond/branch_1_fun/ppermute | solution.py:801
  207.3 19.6 %collective-permute-start.20 = (bf16[512,768]{1,0:T(8,128)(2,1)}, bf16[512,768]{1,0:T(8,128)(2,1)}, u32[]{:S(2)}, u32[]{:S(2)}) collective-permute-start(bf16[512,768]{1,0:T(8,128)(2,1)} %get-tuple-element.688), channel_id=1, source_target_pairs={{0,2},{2,0},{4,6},{6,4},{8,10},{10,8},{12,14},{14,12},{16,18},{18,... | collective-permute-start | bytes 2359304 | tf_op jit(solution)/shard_map/cond/branch_1_fun/ppermute | solution.py:801
  241.4 45.4 %all-to-all-start.2 = ((bf16[4,2,2,3,48,256]{5,4,3,2,1,0:T(8,128)(2,1)}), bf16[4,2,2,3,48,256]{5,4,3,2,1,0:T(8,128)(2,1)S(1)}, u32[]{:S(2)}, u32[]{:S(2)}) async-start(bf16[4,2,2,3,48,256]{5,4,3,2,1,0:T(8,128)(2,1)} %get-tuple-element.762), calls=%async_computation.2 | async-start | bytes 2359296 | tf_op jit(solution)/shard_map/cond/branch_1_fun/all_to_all | solution.py:882
  246.4 35.9 %collective-permute-start.12 = (bf16[4,2,2,3,48,256]{5,4,3,2,1,0:T(8,128)(2,1)}, bf16[4,2,2,3,48,256]{5,4,3,2,1,0:T(8,128)(2,1)S(1)}, u32[]{:S(2)}, u32[]{:S(2)}) collective-permute-start(bf16[4,2,2,3,48,256]{5,4,3,2,1,0:T(8,128)(2,1)} %get-tuple-element.766), channel_id=1, source_target_pairs={{0,4},{2,6},{4,0},{6,2},{8,12},{10,14},{12,8},{14,10},{16,20},{18,... | collective-permute-start | bytes 3538952 | tf_op jit(solution)/shard_map/cond/branch_1_fun/ppermute | solution.py:801
  247.6 42.4 %collective-permute-start.11 = (bf16[512,768]{1,0:T(8,128)(2,1)}, bf16[512,768]{1,0:T(8,128)(2,1)}, u32[]{:S(2)}, u32[]{:S(2)}) collective-permute-start(bf16[512,768]{1,0:T(8,128)(2,1)} %get-tuple-element.760), channel_id=1, source_target_pairs={{0,2},{2,0},{4,6},{6,4},{8,10},{10,8},{12,14},{14,12},{16,18},{18,... | collective-permute-start | bytes 2359304 | tf_op jit(solution)/shard_map/cond/branch_1_fun/ppermute | solution.py:801
  290.1 42.3 %all-to-all-start.4 = ((bf16[4,2,2,3,48,256]{5,4,3,2,1,0:T(8,128)(2,1)}), bf16[4,2,2,3,48,256]{5,4,3,2,1,0:T(8,128)(2,1)}, u32[]{:S(2)}, u32[]{:S(2)}) async-start(bf16[4,2,2,3,48,256]{5,4,3,2,1,0:T(8,128)(2,1)} %get-tuple-element.812), calls=%async_computation.4 | async-start | bytes 2359296 | tf_op jit(solution)/shard_map/cond/branch_1_fun/all_to_all | solution.py:882
  295.4 16.5 %collective-permute-start.25 = (bf16[2,4,2,48,384]{4,3,2,1,0:T(8,128)(2,1)}, bf16[2,4,2,48,384]{4,3,2,1,0:T(8,128)(2,1)S(1)}, u32[]{:S(2)}, u32[]{:S(2)}) collective-permute-start(bf16[2,4,2,48,384]{4,3,2,1,0:T(8,128)(2,1)} %get-tuple-element.803), channel_id=1, source_target_pairs={{0,4},{2,6},{4,0},{6,2},{8,12},{10,14},{12,8},{14,10},{16,20},{18,... | collective-permute-start | bytes 1769480 | tf_op jit(solution)/shard_map/cond/branch_1_fun/ppermute | solution.py:801
  296.3 15.7 %collective-permute-start.26 = (bf16[2,4,2,48,384]{4,3,2,1,0:T(8,128)(2,1)}, bf16[2,4,2,48,384]{4,3,2,1,0:T(8,128)(2,1)S(1)}, u32[]{:S(2)}, u32[]{:S(2)}) collective-permute-start(bf16[2,4,2,48,384]{4,3,2,1,0:T(8,128)(2,1)} %get-tuple-element.805), channel_id=1, source_target_pairs={{0,2},{2,0},{4,6},{6,4},{8,10},{10,8},{12,14},{14,12},{16,18},{18,... | collective-permute-start | bytes 1769480 | tf_op jit(solution)/shard_map/cond/branch_1_fun/ppermute | solution.py:801
  339.4 19.0 %collective-permute-start.38 = (f32[22,768]{1,0:T(8,128)}, f32[22,768]{1,0:T(8,128)S(1)}, u32[]{:S(2)}, u32[]{:S(2)}) collective-permute-start(f32[22,768]{1,0:T(8,128)} %get-tuple-element.1011), channel_id=1, source_target_pairs={{0,8},{2,10},{4,12},{6,14},{8,0},{10,2},{12,4},{14,6},{16,24},{18,... | collective-permute-start | bytes 202760 | tf_op jit(solution)/shard_map/ppermute | solution.py:801
  341.4 17.0 %collective-permute-start.39 = (f32[22,768]{1,0:T(8,128)}, f32[22,768]{1,0:T(8,128)S(1)}, u32[]{:S(2)}, u32[]{:S(2)}) collective-permute-start(f32[22,768]{1,0:T(8,128)} %get-tuple-element.1011), channel_id=1, source_target_pairs={{0,16},{2,18},{4,20},{6,22},{8,24},{10,26},{12,28},{14,30},{16,0},... | collective-permute-start | bytes 202760 | tf_op jit(solution)/shard_map/ppermute | solution.py:801
  343.8 14.6 %collective-permute-start.40 = (f32[22,768]{1,0:T(8,128)}, f32[22,768]{1,0:T(8,128)S(1)}, u32[]{:S(2)}, u32[]{:S(2)}) collective-permute-start(f32[22,768]{1,0:T(8,128)} %get-tuple-element.1011), channel_id=1, source_target_pairs={{0,24},{2,26},{4,28},{6,30},{8,16},{10,18},{12,20},{14,22},{16,8},... | collective-permute-start | bytes 202760 | tf_op jit(solution)/shard_map/ppermute | solution.py:801
  348.0 17.9 %all-to-all-start.6 = ((bf16[4,2,2,48,384]{4,3,2,1,0:T(8,128)(2,1)}), bf16[4,2,2,48,384]{4,3,2,1,0:T(8,128)(2,1)S(1)}, u32[]{:S(2)}, u32[]{:S(2)}) async-start(bf16[4,2,2,48,384]{4,3,2,1,0:T(8,128)(2,1)} %get-tuple-element.1013), calls=%async_computation.6 | async-start | bytes 1179648 | tf_op jit(solution)/shard_map/all_to_all | solution.py:882
  (65 other events, 619.1 us)

commit v5 on v4

--- a/solution.py
+++ b/solution.py
@@ -518,13 +518,17 @@
     )(x, own, got, vec)
 
 
-def ffn_kernel(first, count, piece, groups, c_ref, plan0_ref, plan1_ref, *refs):
+def ffn_kernel(first, count, piece, groups, near, c_ref, plan0_ref, plan1_ref, *refs):
     xs_ref, dys_ref, ub_ref, *rest = refs
+    if near:
+        pos_refs, rest = rest[:2], rest[2:]
     if not first:
         zin_ref, din_ref, *rest = rest
     w_refs = [rest[2 * c : 2 * c + 2] for c in range(count)]
     rest = rest[2 * count :]
     z_ref, da_ref, *rest = rest
+    if near:
+        near_refs, rest = rest[:2], rest[2:]
     g_refs = [rest[2 * c : 2 * c + 2] for c in range(count)]
     gub_ref, wu_s, wd_s, gu_s, gd_s, x_s, dy_s, z_s, da_s, sems, in_sems, out_sems = rest[2 * count :]
     experts = wu_s.shape[0]
@@ -620,6 +624,13 @@
         for c in writes(i):
             c.start()
 
+    if near:
+        rows = da_s[per:].reshape(per * TILE, da_s.shape[2])
+        for pos_ref, out_ref in zip(pos_refs, near_refs):
+            slot = lax.broadcasted_iota(jnp.int32, (per * TILE, out_ref.shape[0]), 0)
+            pick = (slot == pos_ref[...]).astype(f32).astype(bf16)
+            out_ref[...] = tn_dot(pick, rows).astype(bf16)
+
     for c in range(count):
         lanes = pl.ds(c * hc, hc)
         for ry, rz, rx in spots:
@@ -634,7 +645,7 @@
             c.wait()
 
 
-def ffn(coords, plans, xs, dys, up_b, weights, carry):
+def ffn(coords, plans, xs, dys, up_b, weights, carry, places=()):
     slots, width = xs.shape
     tiles = slots // TILE
     groups = len(plans)
@@ -644,10 +655,11 @@
     experts, piece, hc = gshape[3:]
     hid = hc * count
     out = pl.pallas_call(
-        functools.partial(ffn_kernel, first, count, piece, groups),
+        functools.partial(ffn_kernel, first, count, piece, groups, bool(places)),
         out_shape=[
             jax.ShapeDtypeStruct((slots, width), bf16),
             jax.ShapeDtypeStruct((slots, width), bf16),
+            *[jax.ShapeDtypeStruct((p.shape[1], width), bf16) for p in places],
             *[jax.ShapeDtypeStruct(gshape, bf16)] * (2 * count),
             jax.ShapeDtypeStruct((experts, 1, hid), f32),
         ],
@@ -655,10 +667,13 @@
             num_scalar_prefetch=3,
             grid=(1,),
             in_specs=[
-                ANY, ANY, full_spec((experts, 1, hid)), *([] if first else [ANY, ANY]),
-                *[ANY] * (2 * count),
+                ANY, ANY, full_spec((experts, 1, hid)), *[full_spec(p.shape) for p in places],
+                *([] if first else [ANY, ANY]), *[ANY] * (2 * count),
             ],
-            out_specs=[ANY, ANY, *[full_spec(gshape)] * (2 * count), full_spec((experts, 1, hid))],
+            out_specs=[
+                ANY, ANY, *[full_spec((p.shape[1], width)) for p in places], *[full_spec(gshape)] * (2 * count),
+                full_spec((experts, 1, hid)),
+            ],
             scratch_shapes=[
                 *[pltpu.VMEM((experts, width, hid), bf16)] * 2,
                 *[pltpu.VMEM((experts, width, hid), f32)] * 2,
@@ -671,8 +686,11 @@
         compiler_params=params(1),
         cost_estimate=cost(12 * slots * width * hid * 1.5, 4e7, 2 * slots * hid),
         name="ffn",
-    )(coords, plans[0], plans[-1], xs, dys, up_b, *carry, *[w for pair in weights for w in pair])
+    )(coords, plans[0], plans[-1], xs, dys, up_b, *places, *carry, *[w for pair in weights for w in pair])
     zs, das, *rest = out
+    rows, rest = rest[: len(places)], rest[len(places) :]
+    if places:
+        return zs, das, [rest[2 * c : 2 * c + 2] for c in range(count)], rest[2 * count], rows
     return zs, das, [rest[2 * c : 2 * c + 2] for c in range(count)], rest[2 * count]
 
 
@@ -995,11 +1013,14 @@
         take = lambda k: lax.dynamic_slice_in_dim(v, k * mine_tokens, mine_tokens, 0)
         return take(part).reshape(1, mine_tokens), take(1 - part).reshape(1, mine_tokens)
 
-    def finish(x2, z_sum, mods):
+    def bias_rows(mods):
         kinds = lax.dynamic_slice_in_dim(mods, part * mine_tokens, mine_tokens, 0)[:, None]
         bias_of = jnp.zeros((mine_tokens, width), f32)
         for e in range(experts):
             bias_of = jnp.where(kinds == e, down_bias[e][None], bias_of)
+        return bias_of
+
+    def finish(x2, z_sum, bias_of):
         return (x2 + (z_sum + bias_of)).astype(bf16)
 
     def small_rows(sums1, sums2, bsum, g_upb, g_down_bias):
@@ -1024,11 +1045,11 @@
         hc = half // CHUNKS
         up_b = lax.dynamic_slice_in_dim(up_bias, hid_start, half, 1)
 
-        def call_experts(k, xs, dys, weights, carry):
+        def call_experts(k, xs, dys, weights, carry, places=()):
             call = CALLS[k]
             ub = up_b[:, None, call[0] * hc : (call[-1] + 1) * hc]
             return ffn(
-                coords, (plan_own, plan), xs, dys, ub, [weights[c] for c in call], carry
+                coords, (plan_own, plan), xs, dys, ub, [weights[c] for c in call], carry, places
             )
 
         def begin():
@@ -1043,9 +1064,10 @@
             pieces[0] = four_times(pieces[0])
             ab = gather_z(w_qkv[:2], jnp.stack([w_qkv[2], w_out]), size)
             mods, pos, plan_own = token_plan(segments, modality, experts)
-            return pieces, ab, mods, pos, plan_own, flip(plan_own, 1, size), small_inputs()
-
-        pieces, ab, mods, pos, plan_own, plan, smalls = phase(pred, begin)
+            plan = flip(plan_own, 1, size)
+            return pieces, ab, mods, pos, plan_own, plan, bias_rows(mods), small_inputs()
+
+        pieces, ab, mods, pos, plan_own, plan, bias_of, smalls = phase(pred, begin)
         x_mine, dy_mine, proj_bias, seg_row, windows, vec, ln1 = smalls
 
         def weights_in():
@@ -1101,8 +1123,11 @@
 
         def second():
             def inside():
-                zs, das, more, gub = call_experts(1, xs, dys, weights, (zs0, das0))
-                return zs, das, more, gub, both_cores(pos_near, das, 1)
+                zs, das, more, gub, (mine, other) = call_experts(
+                    1, xs, dys, weights, (zs0, das0), pos_near
+                )
+                near = (mine.astype(f32) + swap(other).astype(f32)).astype(bf16)
+                return zs, das, more, gub, near
 
             return phase(inner, inside), sums_y(coords, grads[0], size)
 
@@ -1139,7 +1164,7 @@
             def out_rows():
                 mine, other = unsort_tokens(pos_here, zs, 0, 2)
                 z_sum = mine.astype(f32) + swap(other).astype(f32) + z_near.astype(f32)
-                out = finish(x2, z_sum, mods)
+                out = finish(x2, z_sum, bias_of)
                 return out, swap(out), swap(grad)
 
             rows_all = phase(inner, lambda: small_rows(sums1, sums2, bsum, g_upb, g_down_bias))
@@ -1162,21 +1187,23 @@
         g2 = add_z(coords, v2[0], got2)
         near = flip(jnp.concatenate([v[1] for v in (g0, g1, g2)], axis=-1), 1, size)
         total = phase(inner, lambda: small + flip(small, 2, size))
-        rows_z = jnp.stack([total] + [flip(total, 4 * rz, size) for rz in (1, 2, 3)])
-        pick = lambda z: lax.dynamic_index_in_dim(rows_z, coords[0] ^ z, 0, False)
-        small = pick(0) + pick(1) + pick(2) + pick(3)
+        rows_z = [flip(total, 4 * rz, size) for rz in (1, 2, 3)]
         layer_output, grad_input = whole(
             rows_kernel, "rows", [((parts,) + v.shape, v.dtype) for v in (out, grad)],
             out, out_other, grad, grad_other, prefetch=(coords,),
         )
+        g_qkv, g_out = whole(
+            qkv_grad_kernel, "qkv_grad", [(w_qkv.shape, f32), (w_out.shape, f32)], own, got,
+            prefetch=(after(coords, layer_output),),
+        )
+        last = after(coords, g_out)
         g_up, g_down = whole(
             expert_grad_kernel, "expert_grad", [(w_up.shape, f32)] * 2,
-            g0[0], g1[0], g2[0], near, prefetch=(coords,),
+            g0[0], g1[0], g2[0], near, prefetch=(last,),
         )
-        g_qkv, g_out = whole(
-            qkv_grad_kernel, "qkv_grad", [(w_qkv.shape, f32), (w_out.shape, f32)], own, got,
-            prefetch=(coords,),
-        )
+        rows_z = jnp.stack([after(total, g_up)] + rows_z)
+        pick = lambda z: lax.dynamic_index_in_dim(rows_z, last[0] ^ z, 0, False)
+        small = pick(0) + pick(1) + pick(2) + pick(3)
     else:
         coords = jnp.stack([0, 0, 0, part]).astype(jnp.int32)
         x_mine, dy_mine, proj_bias, seg_row, windows, vec, ln1 = small_inputs()
@@ -1213,7 +1240,7 @@
         g_qk, g_vo = scatter_plain((ga0, ga1), (gb0, gb1))
         g_qkv, g_out = jnp.concatenate([g_qk, g_vo[:1]]), g_vo[1]
         own = deal(unsort_tokens([pos_row], zs, 0, 1)[0].reshape(by_core))
-        layer_output = share(finish(x2, jnp.sum(own.astype(f32), axis=0), mods))
+        layer_output = share(finish(x2, jnp.sum(own.astype(f32), axis=0), bias_rows(mods)))
         grad_input = share(grad_mine)
         small = lax.psum(small_rows(sums1, sums2, bsum, g_upb, g_down_bias), ("dp", "mp"))
 

time: 374 us -> 367 us (0.981)
  Pallas kernels: 175 us -> 171 us
    pallas_call x4 -> x3, Pallas kernels: 20.9 us -> 15.7 us  [unsort_tokens(): pl.pallas_call(functools.partial(unsort_kernel, len(places)), out_shape=[...]
    cond x61 -> x54, local copies, waits for them, and re-layouts: 10.5 us -> 6.42 us
  transfers between devices with their start and end apart: 49 -> 49, of which waited for: 22 -> 22; matrix products, arithmetic and copies ran while one was open for 12% -> 11% of each run, Pallas kernels for 45% -> 45%
where the time goes in v5:
time: 367 us; the launch traced here: 364 us
  Pallas kernels  171 us (47%)
  starting transfers between devices  85.8 us (23%)
  waiting for transfers between devices  46.9 us (13%)
  local copies, waits for them, and re-layouts  35.2 us (10%)
  other arithmetic  21.4 us (6%)
    pallas_call x2, Pallas kernels, ffn(): pl.pallas_call(functools.partial(ffn_kernel, first, count, piece, groups,...  50.8 us
    all_to_all x7, starting transfers between devices, deal_z(): return lax.all_to_all(v, 'dp', 0, 0, axis_index_groups=groups, tiled=True)  45.8 us
    ppermute x29, starting transfers between devices, flip(): return lax.ppermute(x, 'dp', [(i, i ^ mask) for i in range(size)])  38 us
    pallas_call x11, Pallas kernels, whole(): pl.pallas_call(kernel, out_shape=[jax.ShapeDtypeStruct(s, d) for s, d in...  34.6 us
    pallas_call x1, Pallas kernels, attn_bwd(): pl.pallas_call(functools.partial(attn_bwd_kernel, heads, piece), out_shap...  24.1 us
    ppermute x29, waiting for transfers between devices, flip(): return lax.ppermute(x, 'dp', [(i, i ^ mask) for i in range(size)])  22.4 us
    ppermute x13, waiting for transfers between devices, swap(): return lax.ppermute(v, 'mp', [(0, 1), (1, 0)])  21.7 us
    pallas_call x4, Pallas kernels, sort_tokens(): pl.pallas_call(functools.partial(sort_kernel, len(sources)), out_shape=ja...  19.3 us
  transfers between devices with their start and end apart: 49, of which 22 were waited for; matrix products, arithmetic and copies ran while one was open for 11% of the time, Pallas kernels for 45%

profile of v5, /device:TPU:0, one launch (start us, length us, event | category | flops | bytes accessed | tf_op | source)
XLA Modules:
  0.0 363.5 jit_solution(7868228711303006765)
XLA Ops:
  1.4 26.8 %conditional.21 = (bf16[4,2,2,3,48,256]{5,4,3,2,1,0:T(8,128)(2,1)}, bf16[2,2,3,48,256]{4,3,2,1,0:T(8,128)(2,1)S(1)}, bf16[2,2,3,48,256]{4,3,2,1,0:T(8,128)(2,1)}...) conditional(s32[]{:T(128)} %convert_element_type.89, () %tuple.182, ...), branch_computations={%region_0.1_spmd, %region_1.9_spmd} | conditional | flops 11818124 | bytes 19933624 | solution.py:893
  29.3 32.5 %conditional.22 = (bf16[4,2,2,3,48,256]{5,4,3,2,1,0:T(8,128)(2,1)}, bf16[2,4,2,48,384]{4,3,2,1,0:T(8,128)(2,1)}, bf16[2,4,2,48,384]{4,3,2,1,0:T(8,128)(2,1)}, bf...) conditional(s32[]{:T(128)} %convert_element_type.89, () %tuple.181, ...), branch_computations={%region_9.10_spmd, %region_10.13_spmd} | conditional | flops 2421230592 | bytes 33819932 | solution.py:893
  34.5 25.3 %conditional = (bf16[2,4,2,48,384]{4,3,2,1,0:T(8,128)(2,1)}, bf16[2,4,2,48,384]{4,3,2,1,0:T(8,128)(2,1)}, bf16[2,4,2,48,384]{4,3,2,1,0:T(8,128)(2,1)}, bf16[2,4,...) conditional(s32[]{:T(128)} %convert_element_type.53, () %tuple.104, ...), branch_computations={%region_11.11_spmd, %region_12.12_spmd} | conditional | flops 2421230592 | bytes 23989290 | solution.py:893
  61.8 32.5 %conditional.23 = (bf16[2,3,3,512,128]{4,3,2,1,0:T(8,128)(2,1)}, bf16[2,3,128,512]{3,2,1,0:T(8,128)(2,1)}, bf16[2,512,384]{2,1,0:T(8,128)(2,1)}, bf16[2,3,128,51...) conditional(s32[]{:T(128)} %convert_element_type.89, () %tuple.187, ...), branch_computations={%region_13.14_spmd, %region_14.17_spmd} | conditional | flops 20010000384 | bytes 38994812 | solution.py:893
  69.3 22.5 %conditional.1 = (bf16[2,3,3,512,128]{4,3,2,1,0:T(8,128)(2,1)}, bf16[2,3,128,512]{3,2,1,0:T(8,128)(2,1)}, bf16[2,512,384]{2,1,0:T(8,128)(2,1)}, bf16[2,3,128,512...) conditional(s32[]{:T(128)} %convert_element_type.54, () %tuple.110, ...), branch_computations={%region_15.15_spmd, %region_16.16_spmd} | conditional | flops 20010000384 | bytes 21299772 | solution.py:893
  69.9 15.7 %attn_fwd.1 = (bf16[512,768]{1,0:T(8,128)(2,1)}, bf16[512,768]{1,0:T(8,128)(2,1)}, bf16[2,3,3,512,128]{4,3,2,1,0:T(8,128)(2,1)}, bf16[2,3,128,512]{3,2,1,0:T(8,1...) custom-call(s32[4]{0:T(128)S(1)} %get-tuple-element.527.c_ref, ...), custom_call_target="tpu_custom_call" | custom-call | flops 20000000000 | bytes 10000000 | tf_op jit(solution)/shard_map/cond/branch_1_fun/cond/branch_1_fun/attn_fwd/pallas_call | solution.py:235
  94.3 32.7 %conditional.24 = (bf16[3072,768]{1,0:T(8,128)(2,1)}, bf16[3072,768]{1,0:T(8,128)(2,1)}, bf16[4,2,2,3,48,256]{5,4,3,2,1,0:T(8,128)(2,1)}, bf16[4,2,2,3,48,256]{5,4,3,2,1,0:T(8,128)(2,1)}) conditional(s32[]{:T(128)} %convert_element_type.89, () %tuple.186, (pred[]{:T(512)}, bf16[512,768]{1,0:T(8,128)(2,1)}, bf16[512,768]{1,0:T(8,128)(2,1)}, ...), branch_computations={%region_17.18_spmd, %region_18.23_spmd} | conditional | flops 7247757312 | bytes 60278096 | solution.py:893
  102.0 14.8 %conditional.2 = (bf16[3072,768]{1,0:T(8,128)(2,1)}, bf16[3072,768]{1,0:T(8,128)(2,1)}) conditional(s32[]{:T(128)} %convert_element_type.55, () %tuple.117, (bf16[512,768]{1,0:T(8,128)(2,1)}, s32[1,512]{1,0:T(1,128)}, s32[1,512]{1,0:T(1,128)}, bf16[3072,768]{1,0:T(8,128)(2,1)}, bf16[512,768]{1,0:T(8,128)(2,1)}, /*index=5*/s32[1,512]{1,0:T(1,128)}, ...), branch_computations={%region_19.19_spmd, %region_20.20_spmd} | conditional | flops 4831838208 | bytes 32583064 | solution.py:893
  118.9 8.1 %conditional.3 = (bf16[3072,768]{1,0:T(8,128)(2,1)}) conditional(s32[]{:T(128)} %convert_element_type.55, () %tuple.116, (bf16[512,768]{1,0:T(8,128)(2,1)S(1)}, s32[1,512]{1,0:T(1,128)}, s32[1,512]{1,0:T(1,128)}, bf16[3072,768]{1,0:T(8,128)(2,1)}) %tuple.120), branch_computations={%region_21.21_spmd, %region_22.22_spmd} | conditional | flops 2415919104 | bytes 16291532 | solution.py:893
  127.1 30.2 %conditional.25 = (bf16[3072,768]{1,0:T(8,128)(2,1)}, bf16[3072,768]{1,0:T(8,128)(2,1)}, bf16[4,2,2,3,48,256]{5,4,3,2,1,0:T(8,128)(2,1)S(1)}, bf16[4,2,2,3,48,25...) conditional(s32[]{:T(128)} %convert_element_type.89, () %tuple.190, ...), branch_computations={%region_23.24_spmd, %region_24.25_spmd} | conditional | flops 21743271936 | bytes 44743272 | solution.py:893
  129.2 28.1 %ffn.2 = (bf16[3072,768]{1,0:T(8,128)(2,1)}, bf16[3072,768]{1,0:T(8,128)(2,1)}, bf16[4,2,2,3,48,256]{5,4,3,2,1,0:T(8,128)(2,1)S(1)}, bf16[4,2,2,3,48,256]{5,4,3,...) custom-call(s32[4]{0:T(128)S(1)} %get-tuple-element.595.c_ref, ...), custom_call_target="tpu_custom_call" | custom-call | flops 21743271936 | bytes 40000000 | tf_op jit(solution)/shard_map/cond/branch_1_fun/ffn/pallas_call | solution.py:657
  157.3 32.0 %conditional.26 = (bf16[3072,768]{1,0:T(8,128)(2,1)}, bf16[3072,768]{1,0:T(8,128)(2,1)}, bf16[4,2,2,3,48,256]{5,4,3,2,1,0:T(8,128)(2,1)}, bf16[4,2,2,3,48,256]{5...) conditional(s32[]{:T(128)} %convert_element_type.89, () %tuple.185, ...), branch_computations={%region_25.26_spmd, %region_26.29_spmd} | conditional | flops 10874209280 | bytes 54236196 | solution.py:893
  158.0 28.0 %conditional.4 = (bf16[3072,768]{1,0:T(8,128)(2,1)}, bf16[3072,768]{1,0:T(8,128)(2,1)}, bf16[4,2,2,3,48,256]{5,4,3,2,1,0:T(8,128)(2,1)}, bf16[4,2,2,3,48,256]{5,...) conditional(s32[]{:T(128)} %convert_element_type.63, () %tuple.127, ...), branch_computations={%region_27.27_spmd, %region_28.28_spmd} | conditional | flops 10873208832 | bytes 45517400 | solution.py:893
  158.6 22.6 %ffn.3 = (bf16[3072,768]{1,0:T(8,128)(2,1)}, bf16[3072,768]{1,0:T(8,128)(2,1)}, bf16[512,768]{1,0:T(8,128)(2,1)}, bf16[512,768]{1,0:T(8,128)(2,1)}, bf16[4,2,2,3...) custom-call(s32[4]{0:T(128)S(1)} %get-tuple-element.613.c_ref, ...), custom_call_target="tpu_custom_call" | custom-call | flops 10871635968 | bytes 40000000 | tf_op jit(solution)/shard_map/cond/branch_1_fun/cond/branch_1_fun/ffn/pallas_call | solution.py:657
  190.0 50.4 %conditional.27 = (f32[512,768]{1,0:T(8,128)}, bf16[512,768]{1,0:T(8,128)(2,1)}, bf16[512,768]{1,0:T(8,128)(2,1)}, f32[8,768]{1,0:T(8,128)}, bf16[512,768]{1,0:T...) conditional(s32[]{:T(128)} %convert_element_type.89, () %tuple.194, ...), branch_computations={%region_29.30_spmd, %region_30.35_spmd} | conditional | flops 4855410688 | bytes 67070724 | solution.py:893
  190.0 14.9 %all-to-all-start.3 = ((bf16[4,2,2,3,48,256]{5,4,3,2,1,0:T(8,128)(2,1)}), bf16[4,2,2,3,48,256]{5,4,3,2,1,0:T(8,128)(2,1)S(1)}, u32[]{:S(2)}, u32[]{:S(2)}) async-start(bf16[4,2,2,3,48,256]{5,4,3,2,1,0:T(8,128)(2,1)} %get-tuple-element.694), calls=%async_computation.3 | async-start | bytes 2359296 | tf_op jit(solution)/shard_map/cond/branch_1_fun/all_to_all | solution.py:900
  207.9 13.3 %conditional.5 = (bf16[512,768]{1,0:T(8,128)(2,1)S(1)}, bf16[512,768]{1,0:T(8,128)(2,1)}, bf16[512,768]{1,0:T(8,128)(2,1)}) conditional(s32[]{:T(128)} %convert_element_type.80, () %tuple.136, (s32[1,512]{1,0:T(1,128)}, s32[1,512]{1,0:T(1,128)}, bf16[3072,768]{1,0:T(8,128)(2,1)}, s32[1,512]{1,0:T(1,128)}, s32[1,512]{1,0:T(1,128)}, ...), branch_computations={%region_31.31_spmd, %region_32.32_spmd} | conditional | flops 4833411072 | bytes 31796612 | solution.py:893
  226.0 7.3 %conditional.6 = (f32[512,768]{1,0:T(8,128)}, bf16[512,768]{1,0:T(8,128)(2,1)}, bf16[512,768]{1,0:T(8,128)(2,1)}, f32[8,768]{1,0:T(8,128)}) conditional(s32[]{:T(128)} %convert_element_type.80, () %tuple.135, (f32[2,768]{1,0:T(2,128)S(1)}, bf16[512,768]{1,0:T(8,128)(2,1)S(1)}, bf16[512,768]{1,0:T(8,128)(2,1)}, bf16[512,768]{1,0:T(8,128)(2,1)}, ...), branch_computations={%region_33.33_spmd, %region_34.34_spmd} | conditional | flops 20000000 | bytes 11151944 | solution.py:893
  240.4 45.8 %conditional.28 = (f32[512,768]{1,0:T(8,128)}, f32[8,768]{1,0:T(8,128)}, bf16[2,4,2,48,384]{4,3,2,1,0:T(8,128)(2,1)}, bf16[2,4,2,48,384]{4,3,2,1,0:T(8,128)(2,1)...) conditional(s32[]{:T(128)} %convert_element_type.89, () %tuple.193, ...), branch_computations={%region_35.36_spmd, %region_36.39_spmd} | conditional | flops 40021999616 | bytes 53709544 | solution.py:893
  248.2 31.8 %conditional.7 = (f32[512,768]{1,0:T(8,128)}, f32[8,768]{1,0:T(8,128)}, bf16[2,4,2,48,384]{4,3,2,1,0:T(8,128)(2,1)}, bf16[2,4,2,48,384]{4,3,2,1,0:T(8,128)(2,1)}...) conditional(s32[]{:T(128)} %convert_element_type.81, () %tuple.143, ...), branch_computations={%region_37.37_spmd, %region_38.38_spmd} | conditional | flops 40020000768 | bytes 34305916 | solution.py:893
  248.8 24.1 %attn_bwd.1 = (bf16[512,768]{1,0:T(8,128)(2,1)}, bf16[512,768]{1,0:T(8,128)(2,1)}, bf16[2,4,2,48,384]{4,3,2,1,0:T(8,128)(2,1)}, bf16[2,4,2,48,384]{4,3,2,1,0:T(8...) custom-call(s32[4]{0:T(128)S(1)} %get-tuple-element.701.c_ref, ...), custom_call_target="tpu_custom_call" | custom-call | flops 40000000000 | bytes 20000000 | tf_op jit(solution)/shard_map/cond/branch_1_fun/cond/branch_1_fun/attn_bwd/pallas_call | solution.py:386
  286.3 42.0 %conditional.29 = (f32[2,2,48,384]{3,2,1,0:T(8,128)S(1)}, bf16[4,2,2,48,384]{4,3,2,1,0:T(8,128)(2,1)}, bf16[4,2,2,3,48,256]{5,4,3,2,1,0:T(8,128)(2,1)}, bf16[512...) conditional(s32[]{:T(128)} %convert_element_type.89, () %tuple.180, ...), branch_computations={%region_39.40_spmd, %region_40.47_spmd} | conditional | flops 2421101824 | bytes 51153768 | solution.py:893
  286.3 6.6 %all-to-all-start.4 = ((bf16[4,2,2,3,48,256]{5,4,3,2,1,0:T(8,128)(2,1)}), bf16[4,2,2,3,48,256]{5,4,3,2,1,0:T(8,128)(2,1)}, u32[]{:S(2)}, u32[]{:S(2)}) async-start(bf16[4,2,2,3,48,256]{5,4,3,2,1,0:T(8,128)(2,1)} %get-tuple-element.804), calls=%async_computation.4 | async-start | bytes 2359296 | tf_op jit(solution)/shard_map/cond/branch_1_fun/all_to_all | solution.py:900
  293.7 14.5 %conditional.8 = (bf16[512,768]{1,0:T(8,128)(2,1)}, bf16[512,768]{1,0:T(8,128)(2,1)}, f32[512,768]{1,0:T(8,128)}) conditional(s32[]{:T(128)} %convert_element_type.86, () %tuple.149, (s32[1,512]{1,0:T(1,128)}, s32[1,512]{1,0:T(1,128)}, bf16[3072,768]{1,0:T(8,128)(2,1)}, bf16[512,768]{1,0:T(8,128)(2,1)}, f32[512,768]{1,0:T(8,128)S(1)}, ...), branch_computations={%region_41.41_spmd, %region_42.42_spmd} | conditional | flops 2419064832 | bytes 28874512 | solution.py:893
  (284 shorter events, 265.1 us)
Async XLA Ops:
  3.1 17.5 %collective-permute-start.30 = (bf16[2,2,48,384]{3,2,1,0:T(8,128)(2,1)S(1)}, bf16[2,2,48,384]{3,2,1,0:T(8,128)(2,1)}, u32[]{:S(2)}, u32[]{:S(2)}) collective-permute-start(bf16[2,2,48,384]{3,2,1,0:T(8,128)(2,1)S(1)} %pad_maximum_fusion.8), channel_id=1, source_target_pairs={{0,8},{2,10},{4,12},{6,14},{8,0},{10,2},{12,4},{14,6},{16,24},{18,... | collective-permute-start | bytes 442376 | tf_op jit(solution)/shard_map/cond/branch_1_fun/ppermute | solution.py:819
  6.2 15.4 %collective-permute-start.31 = (bf16[2,2,48,384]{3,2,1,0:T(8,128)(2,1)S(1)}, bf16[2,2,48,384]{3,2,1,0:T(8,128)(2,1)}, u32[]{:S(2)}, u32[]{:S(2)}) collective-permute-start(bf16[2,2,48,384]{3,2,1,0:T(8,128)(2,1)S(1)} %pad_maximum_fusion.8), channel_id=1, source_target_pairs={{0,16},{2,18},{4,20},{6,22},{8,24},{10,26},{12,28},{14,30},{16,0},... | collective-permute-start | bytes 442376 | tf_op jit(solution)/shard_map/cond/branch_1_fun/ppermute | solution.py:819
  29.3 32.5 %all-to-all-start.5 = ((bf16[4,2,2,3,48,256]{5,4,3,2,1,0:T(8,128)(2,1)}), bf16[4,2,2,3,48,256]{5,4,3,2,1,0:T(8,128)(2,1)}, u32[]{:S(2)}, u32[]{:S(2)}) async-start(bf16[4,2,2,3,48,256]{5,4,3,2,1,0:T(8,128)(2,1)} %get-tuple-element.504), calls=%async_computation.5 | async-start | bytes 2359296 | tf_op jit(solution)/shard_map/cond/branch_1_fun/all_to_all | solution.py:900
  61.8 32.5 %all-to-all-start = ((bf16[4,2,2,3,48,256]{5,4,3,2,1,0:T(8,128)(2,1)}), bf16[4,2,2,3,48,256]{5,4,3,2,1,0:T(8,128)(2,1)}, u32[]{:S(2)}, u32[]{:S(2)}) async-start(bf16[4,2,2,3,48,256]{5,4,3,2,1,0:T(8,128)(2,1)} %get-tuple-element.569), calls=%async_computation | async-start | bytes 2359296 | tf_op jit(solution)/shard_map/cond/branch_1_fun/all_to_all | solution.py:900
  66.2 27.3 %collective-permute-start.1 = (bf16[4,2,2,3,48,256]{5,4,3,2,1,0:T(8,128)(2,1)}, bf16[4,2,2,3,48,256]{5,4,3,2,1,0:T(8,128)(2,1)}, u32[]{:S(2)}, u32[]{:S(2)}) collective-permute-start(bf16[4,2,2,3,48,256]{5,4,3,2,1,0:T(8,128)(2,1)} %get-tuple-element.568), channel_id=1, source_target_pairs={{0,4},{2,6},{4,0},{6,2},{8,12},{10,14},{12,8},{14,10},{16,20},{18,... | collective-permute-start | bytes 3538952 | tf_op jit(solution)/shard_map/cond/branch_1_fun/ppermute | solution.py:819
  67.8 24.0 %collective-permute-start.2 = (bf16[512,768]{1,0:T(8,128)(2,1)S(1)}, bf16[512,768]{1,0:T(8,128)(2,1)}, u32[]{:S(2)}, u32[]{:S(2)}) collective-permute-start(bf16[512,768]{1,0:T(8,128)(2,1)S(1)} %get-tuple-element.570), channel_id=1, source_target_pairs={{0,2},{2,0},{4,6},{6,4},{8,10},{10,8},{12,14},{14,12},{16,18},{18,... | collective-permute-start | bytes 2359304 | tf_op jit(solution)/shard_map/cond/branch_1_fun/ppermute | solution.py:819
  94.3 32.7 %all-to-all-start.1 = ((bf16[4,2,2,3,48,256]{5,4,3,2,1,0:T(8,128)(2,1)}), bf16[4,2,2,3,48,256]{5,4,3,2,1,0:T(8,128)(2,1)}, u32[]{:S(2)}, u32[]{:S(2)}) async-start(bf16[4,2,2,3,48,256]{5,4,3,2,1,0:T(8,128)(2,1)} %get-tuple-element.594), calls=%async_computation.1 | async-start | bytes 2359296 | tf_op jit(solution)/shard_map/cond/branch_1_fun/all_to_all | solution.py:900
  98.9 28.2 %collective-permute-start.7 = (bf16[4,2,2,3,48,256]{5,4,3,2,1,0:T(8,128)(2,1)}, bf16[4,2,2,3,48,256]{5,4,3,2,1,0:T(8,128)(2,1)}, u32[]{:S(2)}, u32[]{:S(2)}) collective-permute-start(bf16[4,2,2,3,48,256]{5,4,3,2,1,0:T(8,128)(2,1)} %get-tuple-element.593), channel_id=1, source_target_pairs={{0,4},{2,6},{4,0},{6,2},{8,12},{10,14},{12,8},{14,10},{16,20},{18,... | collective-permute-start | bytes 3538952 | tf_op jit(solution)/shard_map/cond/branch_1_fun/ppermute | solution.py:819
  100.5 18.4 %collective-permute-start.6 = (bf16[512,768]{1,0:T(8,128)(2,1)}, bf16[512,768]{1,0:T(8,128)(2,1)S(1)}, u32[]{:S(2)}, u32[]{:S(2)}) collective-permute-start(bf16[512,768]{1,0:T(8,128)(2,1)} %get-tuple-element.583), channel_id=1, source_target_pairs={{0,2},{2,0},{4,6},{6,4},{8,10},{10,8},{12,14},{14,12},{16,18},{18,... | collective-permute-start | bytes 2359304 | tf_op jit(solution)/shard_map/cond/branch_1_fun/ppermute | solution.py:819
  127.1 30.2 %collective-permute-start.8 = (bf16[4,2,2,3,48,256]{5,4,3,2,1,0:T(8,128)(2,1)}, bf16[4,2,2,3,48,256]{5,4,3,2,1,0:T(8,128)(2,1)}, u32[]{:S(2)}, u32[]{:S(2)}) collective-permute-start(bf16[4,2,2,3,48,256]{5,4,3,2,1,0:T(8,128)(2,1)} %get-tuple-element.612), channel_id=1, source_target_pairs={{0,4},{2,6},{4,0},{6,2},{8,12},{10,14},{12,8},{14,10},{16,20},{18,... | collective-permute-start | bytes 3538952 | tf_op jit(solution)/shard_map/cond/branch_1_fun/ppermute | solution.py:819
  157.3 28.7 %collective-permute-start.17 = (bf16[4,2,2,3,48,256]{5,4,3,2,1,0:T(8,128)(2,1)}, bf16[4,2,2,3,48,256]{5,4,3,2,1,0:T(8,128)(2,1)}, u32[]{:S(2)}, u32[]{:S(2)}) collective-permute-start(bf16[4,2,2,3,48,256]{5,4,3,2,1,0:T(8,128)(2,1)} %get-tuple-element.652), channel_id=1, source_target_pairs={{0,4},{2,6},{4,0},{6,2},{8,12},{10,14},{12,8},{14,10},{16,20},{18,... | collective-permute-start | bytes 3538952 | tf_op jit(solution)/shard_map/cond/branch_1_fun/ppermute | solution.py:819
  190.0 46.5 %all-to-all-start.3 = ((bf16[4,2,2,3,48,256]{5,4,3,2,1,0:T(8,128)(2,1)}), bf16[4,2,2,3,48,256]{5,4,3,2,1,0:T(8,128)(2,1)S(1)}, u32[]{:S(2)}, u32[]{:S(2)}) async-start(bf16[4,2,2,3,48,256]{5,4,3,2,1,0:T(8,128)(2,1)} %get-tuple-element.694), calls=%async_computation.3 | async-start | bytes 2359296 | tf_op jit(solution)/shard_map/cond/branch_1_fun/all_to_all | solution.py:900
  204.9 28.4 %collective-permute-start.21 = (bf16[4,2,2,3,48,256]{5,4,3,2,1,0:T(8,128)(2,1)}, bf16[4,2,2,3,48,256]{5,4,3,2,1,0:T(8,128)(2,1)}, u32[]{:S(2)}, u32[]{:S(2)}) collective-permute-start(bf16[4,2,2,3,48,256]{5,4,3,2,1,0:T(8,128)(2,1)} %get-tuple-element.698), channel_id=1, source_target_pairs={{0,4},{2,6},{4,0},{6,2},{8,12},{10,14},{12,8},{14,10},{16,20},{18,... | collective-permute-start | bytes 3538952 | tf_op jit(solution)/shard_map/cond/branch_1_fun/ppermute | solution.py:819
  206.4 19.6 %collective-permute-start.20 = (bf16[512,768]{1,0:T(8,128)(2,1)}, bf16[512,768]{1,0:T(8,128)(2,1)}, u32[]{:S(2)}, u32[]{:S(2)}) collective-permute-start(bf16[512,768]{1,0:T(8,128)(2,1)} %get-tuple-element.684), channel_id=1, source_target_pairs={{0,2},{2,0},{4,6},{6,4},{8,10},{10,8},{12,14},{14,12},{16,18},{18,... | collective-permute-start | bytes 2359304 | tf_op jit(solution)/shard_map/cond/branch_1_fun/ppermute | solution.py:819
  240.4 43.1 %all-to-all-start.2 = ((bf16[4,2,2,3,48,256]{5,4,3,2,1,0:T(8,128)(2,1)}), bf16[4,2,2,3,48,256]{5,4,3,2,1,0:T(8,128)(2,1)}, u32[]{:S(2)}, u32[]{:S(2)}) async-start(bf16[4,2,2,3,48,256]{5,4,3,2,1,0:T(8,128)(2,1)} %get-tuple-element.758), calls=%async_computation.2 | async-start | bytes 2359296 | tf_op jit(solution)/shard_map/cond/branch_1_fun/all_to_all | solution.py:900
  245.3 34.7 %collective-permute-start.12 = (bf16[4,2,2,3,48,256]{5,4,3,2,1,0:T(8,128)(2,1)}, bf16[4,2,2,3,48,256]{5,4,3,2,1,0:T(8,128)(2,1)}, u32[]{:S(2)}, u32[]{:S(2)}) collective-permute-start(bf16[4,2,2,3,48,256]{5,4,3,2,1,0:T(8,128)(2,1)} %get-tuple-element.762), channel_id=1, source_target_pairs={{0,4},{2,6},{4,0},{6,2},{8,12},{10,14},{12,8},{14,10},{16,20},{18,... | collective-permute-start | bytes 3538952 | tf_op jit(solution)/shard_map/cond/branch_1_fun/ppermute | solution.py:819
  246.7 39.6 %collective-permute-start.11 = (bf16[512,768]{1,0:T(8,128)(2,1)}, bf16[512,768]{1,0:T(8,128)(2,1)}, u32[]{:S(2)}, u32[]{:S(2)}) collective-permute-start(bf16[512,768]{1,0:T(8,128)(2,1)} %get-tuple-element.756), channel_id=1, source_target_pairs={{0,2},{2,0},{4,6},{6,4},{8,10},{10,8},{12,14},{14,12},{16,18},{18,... | collective-permute-start | bytes 2359304 | tf_op jit(solution)/shard_map/cond/branch_1_fun/ppermute | solution.py:819
  286.3 42.0 %all-to-all-start.4 = ((bf16[4,2,2,3,48,256]{5,4,3,2,1,0:T(8,128)(2,1)}), bf16[4,2,2,3,48,256]{5,4,3,2,1,0:T(8,128)(2,1)}, u32[]{:S(2)}, u32[]{:S(2)}) async-start(bf16[4,2,2,3,48,256]{5,4,3,2,1,0:T(8,128)(2,1)} %get-tuple-element.804), calls=%async_computation.4 | async-start | bytes 2359296 | tf_op jit(solution)/shard_map/cond/branch_1_fun/all_to_all | solution.py:900
  292.9 15.5 %collective-permute-start.25 = (bf16[2,4,2,48,384]{4,3,2,1,0:T(8,128)(2,1)}, bf16[2,4,2,48,384]{4,3,2,1,0:T(8,128)(2,1)}, u32[]{:S(2)}, u32[]{:S(2)}) collective-permute-start(bf16[2,4,2,48,384]{4,3,2,1,0:T(8,128)(2,1)} %get-tuple-element.795), channel_id=1, source_target_pairs={{0,4},{2,6},{4,0},{6,2},{8,12},{10,14},{12,8},{14,10},{16,20},{18,... | collective-permute-start | bytes 1769480 | tf_op jit(solution)/shard_map/cond/branch_1_fun/ppermute | solution.py:819
  293.7 15.1 %collective-permute-start.26 = (bf16[2,4,2,48,384]{4,3,2,1,0:T(8,128)(2,1)}, bf16[2,4,2,48,384]{4,3,2,1,0:T(8,128)(2,1)}, u32[]{:S(2)}, u32[]{:S(2)}) collective-permute-start(bf16[2,4,2,48,384]{4,3,2,1,0:T(8,128)(2,1)} %get-tuple-element.797), channel_id=1, source_target_pairs={{0,2},{2,0},{4,6},{6,4},{8,10},{10,8},{12,14},{14,12},{16,18},{18,... | collective-permute-start | bytes 1769480 | tf_op jit(solution)/shard_map/cond/branch_1_fun/ppermute | solution.py:819
  328.3 24.7 %all-to-all-start.6 = ((bf16[4,2,2,48,384]{4,3,2,1,0:T(8,128)(2,1)}), bf16[4,2,2,48,384]{4,3,2,1,0:T(8,128)(2,1)S(1)}, u32[]{:S(2)}, u32[]{:S(2)}) async-start(bf16[4,2,2,48,384]{4,3,2,1,0:T(8,128)(2,1)} %get-tuple-element.1007), calls=%async_computation.6 | async-start | bytes 1179648 | tf_op jit(solution)/shard_map/all_to_all | solution.py:900
  337.1 19.3 %collective-permute-start.38 = (bf16[2,3,48,768]{3,2,1,0:T(8,128)(2,1)S(1)}, bf16[2,3,48,768]{3,2,1,0:T(8,128)(2,1)S(1)}, u32[]{:S(2)}, u32[]{:S(2)}) collective-permute-start(bf16[2,3,48,768]{3,2,1,0:T(8,128)(2,1)S(1)} %pad_maximum_fusion.12), channel_id=1, source_target_pairs={{0,2},{2,0},{4,6},{6,4},{8,10},{10,8},{12,14},{14,12},{16,18},{18,... | collective-permute-start | bytes 1327112 | tf_op jit(solution)/shard_map/ppermute | solution.py:819
  343.2 17.0 %collective-permute-start.39 = (f32[22,768]{1,0:T(8,128)S(1)}, f32[22,768]{1,0:T(8,128)S(1)}, u32[]{:S(2)}, u32[]{:S(2)}) collective-permute-start(f32[22,768]{1,0:T(8,128)S(1)} %get-tuple-element.1504), channel_id=1, source_target_pairs={{0,8},{2,10},{4,12},{6,14},{8,0},{10,2},{12,4},{14,6},{16,24},{18,... | collective-permute-start | bytes 202760 | tf_op jit(solution)/shard_map/ppermute | solution.py:819
  345.2 14.9 %collective-permute-start.40 = (f32[22,768]{1,0:T(8,128)S(1)}, f32[22,768]{1,0:T(8,128)S(1)}, u32[]{:S(2)}, u32[]{:S(2)}) collective-permute-start(f32[22,768]{1,0:T(8,128)S(1)} %get-tuple-element.1504), channel_id=1, source_target_pairs={{0,16},{2,18},{4,20},{6,22},{8,24},{10,26},{12,28},{14,30},{16,0},... | collective-permute-start | bytes 202760 | tf_op jit(solution)/shard_map/ppermute | solution.py:819
  (62 other events, 573.7 us)

commit v6 on v5

--- a/solution.py
+++ b/solution.py
@@ -14,7 +14,7 @@
 CHUNKS = 3
 SCALE = 1.0
 CALLS = ((0, 1), (2,))
-VMEM = 58 * 1024 * 1024
+MIB = 1024 * 1024
 LOG2E = math.log2(math.e)
 f32 = jnp.float32
 bf16 = jnp.bfloat16
@@ -38,9 +38,9 @@
     return lax.dot_general(a, b, (((0,), (0,)), ((), ())), preferred_element_type=f32)
 
 
-def params(grid_rank):
+def params(grid_rank, mib=20):
     return pltpu.CompilerParams(
-        dimension_semantics=("arbitrary",) * grid_rank, vmem_limit_bytes=VMEM
+        dimension_semantics=("arbitrary",) * grid_rank, vmem_limit_bytes=mib * MIB
     )
 
 
@@ -255,7 +255,7 @@
                 pltpu.SemaphoreType.DMA((64,)),
             ],
         ),
-        compiler_params=params(1),
+        compiler_params=params(1, 26),
         cost_estimate=cost(2e10, 1e7, 3e6),
         name="attn_fwd",
     )(coords, windows, x, seg_row, ln, proj_bias, *pa, *pb)
@@ -264,7 +264,7 @@
 def attn_bwd_kernel(
     heads, piece, c_ref, win_ref, dxr_ref, dxr2_ref, x_ref, srow_ref, ln_ref, qkv_ref, kt_ref, o_ref, ot_ref, lse_ref, a0, a1_, b0, b1_,
     da1_ref, da1_other_ref, ga0_ref, ga1_ref, gb0_ref, gb1_ref, bsum_ref,
-    w_s, wo_s, bias_s, dp_s, gw_s, go_s, do_s, row_s, dk_s, dv_s, dqt_s, a1t_s, sems,
+    w_s, wo_s, bias_s, dp_s, gw_s, go_s, do_s, row_s, dk_s, dv_s, dqt_s, a1_s, dxr_s, o_s, sems,
 ):
     cols = heads * HD
     pairs = cols // 128
@@ -289,12 +289,12 @@
     def _():
         for c in copies:
             c.start()
-        gw_s[...] = jnp.zeros_like(gw_s)
-        go_s[...] = jnp.zeros_like(go_s)
         bsum_ref[...] = jnp.zeros_like(bsum_ref)
 
     xhat1, _ = norm_parts(x_ref[0].astype(f32))
-    a1t_s[...] = (xhat1 * ln_ref[0:1] + ln_ref[1:2]).astype(bf16).T
+    here = pl.ds(pl.multiple_of(step * seq, 128), seq)
+    a1_s[here, :] = (xhat1 * ln_ref[0:1] + ln_ref[1:2]).astype(bf16)
+    o_s[here, :] = o_ref[0]
     fill_bias(srow_ref, bias_s)
 
     @pl.when(step == 0)
@@ -304,7 +304,7 @@
 
     dxr = jnp.where(step == c_ref[3], dxr_ref[...], dxr2_ref[...])
     do = nn_dot(dxr, wo_s[...]).astype(bf16)
-    go_s[...] += nn_dot(dxr.T, o_ref[0])
+    dxr_s[here, :] = dxr
     scale = HD ** (-0.5)
     scale2 = scale * LOG2E
     do_s[...] = do
@@ -339,11 +339,11 @@
     each_window(win_ref, step, seq // 128, block)
 
     for p in range(pairs):
-        dp_s[:, p * 128 : (p + 1) * 128] = dqt_s[p].T
-        dp_s[:, cols + p * 128 : cols + (p + 1) * 128] = (dk_s[p] * scale).astype(bf16)
-        dp_s[:, 2 * cols + p * 128 : 2 * cols + (p + 1) * 128] = dv_s[p].astype(bf16)
-
-    dproj = dp_s[...]
+        dp_s[here, p * 128 : (p + 1) * 128] = dqt_s[p].T
+        dp_s[here, cols + p * 128 : cols + (p + 1) * 128] = (dk_s[p] * scale).astype(bf16)
+        dp_s[here, 2 * cols + p * 128 : 2 * cols + (p + 1) * 128] = dv_s[p].astype(bf16)
+
+    dproj = dp_s[here, :]
     da1 = nt_dot(dproj, w_s[...]).astype(bf16)
 
     @pl.when(step == c_ref[3])
@@ -355,20 +355,21 @@
         da1_other_ref[...] = da1
 
     bsum_ref[...] += jnp.sum(dproj.astype(f32), axis=0, keepdims=True)
-    gw_s[...] += nn_dot(a1t_s[...], dproj)
 
     @pl.when(step == pl.num_programs(0) - 1)
     def _():
+        gw_s[...] = tn_dot(a1_s[...], dp_s[...]).astype(bf16)
+        go_s[...] = tn_dot(dxr_s[...], o_s[...]).astype(bf16)
         for outer in range(2):
             for inner in range(2):
                 for rz in range(4):
                     ra = pl.ds(pl.multiple_of(place(c_ref, "a", outer, inner, rz) * piece, 16), piece)
                     rb = pl.ds(pl.multiple_of(place(c_ref, "b", outer, inner, rz) * piece, 16), piece)
                     ga, gb = ((ga0_ref, gb0_ref), (ga1_ref, gb1_ref))[outer]
-                    ga[inner, rz, 0] = gw_s[ra, :cols].astype(bf16)
-                    ga[inner, rz, 1] = gw_s[ra, cols : 2 * cols].astype(bf16)
-                    gb[inner, rz, 0] = gw_s[rb, 2 * cols :].astype(bf16)
-                    gb[inner, rz, 1] = go_s[rb, :].astype(bf16)
+                    ga[inner, rz, 0] = gw_s[ra, :cols]
+                    ga[inner, rz, 1] = gw_s[ra, cols : 2 * cols]
+                    gb[inner, rz, 0] = gw_s[rb, 2 * cols :]
+                    gb[inner, rz, 1] = go_s[rb, :]
 
 
 def attn_bwd(coords, windows, dxr, dxr2, x, seg_row, ln, saved, pa, pb):
@@ -413,19 +414,21 @@
                 pltpu.VMEM((width, 3 * cols), bf16),
                 pltpu.VMEM((width, cols), bf16),
                 pltpu.VMEM((seq, seq), f32),
-                pltpu.VMEM((seq, 3 * cols), bf16),
-                pltpu.VMEM((width, 3 * cols), f32),
-                pltpu.VMEM((width, cols), f32),
+                pltpu.VMEM((rows * seq, 3 * cols), bf16),
+                pltpu.VMEM((width, 3 * cols), bf16),
+                pltpu.VMEM((width, cols), bf16),
                 pltpu.VMEM((seq, cols), bf16),
                 pltpu.VMEM((pairs, 2, seq), f32),
                 pltpu.VMEM((pairs, seq, 128), f32),
                 pltpu.VMEM((pairs, seq, 128), f32),
                 pltpu.VMEM((pairs, 128, seq), bf16),
-                pltpu.VMEM((width, seq), bf16),
+                pltpu.VMEM((rows * seq, width), bf16),
+                pltpu.VMEM((rows * seq, width), bf16),
+                pltpu.VMEM((rows * seq, cols), bf16),
                 pltpu.SemaphoreType.DMA((64,)),
             ],
         ),
-        compiler_params=params(1),
+        compiler_params=params(1, 34),
         cost_estimate=cost(4e10, 2e7, 3e6),
         name="attn_bwd",
     )(coords, windows, dxr, dxr2, x, seg_row, ln, qkv, kt, o, ot, lse, *pa, *pb)
@@ -683,7 +686,7 @@
                 pltpu.SemaphoreType.DMA((2, tiles)),
             ],
         ),
-        compiler_params=params(1),
+        compiler_params=params(1, 46 if groups == 2 else 60),
         cost_estimate=cost(12 * slots * width * hid * 1.5, 4e7, 2 * slots * hid),
         name="ffn",
     )(coords, plans[0], plans[-1], xs, dys, up_b, *places, *carry, *[w for pair in weights for w in pair])

time: 367 us -> 345 us (0.940)
  local copies, waits for them, and re-layouts: 35.2 us -> 20.2 us
  Pallas kernels: 171 us -> 156 us
  waiting for transfers between devices: 46.9 us -> 56.8 us
    ppermute x29, waiting for transfers between devices: 22.4 us -> 31.9 us  [flip(): return lax.ppermute(x, 'dp', [(i, i ^ mask) for i in range(size)])]
    pallas_call x11, Pallas kernels: 34.6 us -> 26.9 us  [whole(): pl.pallas_call(kernel, out_shape=[jax.ShapeDtypeStruct(s, d) for s, d in...]
    cond x54 -> x34, local copies, waits for them, and re-layouts: 6.42 us -> 0.09 us
  transfers between devices with their start and end apart: 49 -> 49, of which waited for: 22 -> 27; matrix products, arithmetic and copies ran while one was open for 11% -> 9% of each run, Pallas kernels for 45% -> 44%
where the time goes in v6:
time: 345 us; the launch traced here: 341 us
  Pallas kernels  156 us (45%)
  starting transfers between devices  85.4 us (25%)
  waiting for transfers between devices  56.8 us (16%)
  local copies, waits for them, and re-layouts  20.2 us (6%)
  other arithmetic  19.2 us (6%)
    pallas_call x2, Pallas kernels, ffn(): pl.pallas_call(functools.partial(ffn_kernel, first, count, piece, groups,...  50 us
    all_to_all x7, starting transfers between devices, deal_z(): return lax.all_to_all(v, 'dp', 0, 0, axis_index_groups=groups, tiled=True)  43.5 us
    ppermute x29, starting transfers between devices, flip(): return lax.ppermute(x, 'dp', [(i, i ^ mask) for i in range(size)])  39.6 us
    ppermute x29, waiting for transfers between devices, flip(): return lax.ppermute(x, 'dp', [(i, i ^ mask) for i in range(size)])  31.9 us
    pallas_call x11, Pallas kernels, whole(): pl.pallas_call(kernel, out_shape=[jax.ShapeDtypeStruct(s, d) for s, d in...  26.9 us
    pallas_call x1, Pallas kernels, attn_bwd(): pl.pallas_call(functools.partial(attn_bwd_kernel, heads, piece), out_shap...  23.7 us
    ppermute x13, waiting for transfers between devices, swap(): return lax.ppermute(v, 'mp', [(0, 1), (1, 0)])  20.5 us
    pallas_call x4, Pallas kernels, sort_tokens(): pl.pallas_call(functools.partial(sort_kernel, len(sources)), out_shape=ja...  18.3 us
  transfers between devices with their start and end apart: 49, of which 27 were waited for; matrix products, arithmetic and copies ran while one was open for 9% of the time, Pallas kernels for 44%

profile of v6, /device:TPU:0, one launch (start us, length us, event | category | flops | bytes accessed | tf_op | source)
XLA Modules:
  0.0 341.4 jit_solution(3429814612568327779)
XLA Ops:
  1.4 23.7 %conditional.21 = (bf16[4,2,2,3,48,256]{5,4,3,2,1,0:T(8,128)(2,1)}, bf16[2,2,3,48,256]{4,3,2,1,0:T(8,128)(2,1)S(1)}, bf16[2,2,3,48,256]{4,3,2,1,0:T(8,128)(2,1)S...) conditional(s32[]{:T(128)} %convert_element_type.89, () %tuple.182, ...), branch_computations={%region_0.1_spmd, %region_1.9_spmd} | conditional | flops 11818124 | bytes 18735460 | solution.py:896
  26.2 31.7 %conditional.22 = (bf16[4,2,2,3,48,256]{5,4,3,2,1,0:T(8,128)(2,1)}, bf16[2,4,2,48,384]{4,3,2,1,0:T(8,128)(2,1)}, bf16[2,4,2,48,384]{4,3,2,1,0:T(8,128)(2,1)}, bf...) conditional(s32[]{:T(128)} %convert_element_type.89, () %tuple.181, ...), branch_computations={%region_9.10_spmd, %region_10.13_spmd} | conditional | flops 2421230592 | bytes 33819932 | solution.py:896
  31.2 24.0 %conditional = (bf16[2,4,2,48,384]{4,3,2,1,0:T(8,128)(2,1)}, bf16[2,4,2,48,384]{4,3,2,1,0:T(8,128)(2,1)}, bf16[2,4,2,48,384]{4,3,2,1,0:T(8,128)(2,1)}, bf16[2,4,...) conditional(s32[]{:T(128)} %convert_element_type.53, () %tuple.104, ...), branch_computations={%region_11.11_spmd, %region_12.12_spmd} | conditional | flops 2421230592 | bytes 23989290 | solution.py:896
  58.0 32.5 %conditional.23 = (bf16[2,3,3,512,128]{4,3,2,1,0:T(8,128)(2,1)}, bf16[2,3,128,512]{3,2,1,0:T(8,128)(2,1)}, bf16[2,512,384]{2,1,0:T(8,128)(2,1)}, bf16[2,3,128,51...) conditional(s32[]{:T(128)} %convert_element_type.89, () %tuple.187, ...), branch_computations={%region_13.14_spmd, %region_14.17_spmd} | conditional | flops 20010000384 | bytes 35849056 | solution.py:896
  65.5 19.3 %conditional.1 = (bf16[2,3,3,512,128]{4,3,2,1,0:T(8,128)(2,1)}, bf16[2,3,128,512]{3,2,1,0:T(8,128)(2,1)}, bf16[2,512,384]{2,1,0:T(8,128)(2,1)}, bf16[2,3,128,512...) conditional(s32[]{:T(128)} %convert_element_type.54, () %tuple.110, ...), branch_computations={%region_15.15_spmd, %region_16.16_spmd} | conditional | flops 20010000384 | bytes 18154016 | solution.py:896
  65.5 15.2 %attn_fwd.1 = (bf16[512,768]{1,0:T(8,128)(2,1)S(1)}, bf16[512,768]{1,0:T(8,128)(2,1)S(1)}, bf16[2,3,3,512,128]{4,3,2,1,0:T(8,128)(2,1)}, bf16[2,3,128,512]{3,2,1...) custom-call(s32[4]{0:T(128)S(1)} %get-tuple-element.527.c_ref, ...), custom_call_target="tpu_custom_call" | custom-call | flops 20000000000 | bytes 10000000 | tf_op jit(solution)/shard_map/cond/branch_1_fun/cond/branch_1_fun/attn_fwd/pallas_call | solution.py:235
  90.5 32.6 %conditional.24 = (bf16[3072,768]{1,0:T(8,128)(2,1)}, bf16[3072,768]{1,0:T(8,128)(2,1)}, bf16[4,2,2,3,48,256]{5,4,3,2,1,0:T(8,128)(2,1)}, bf16[4,2,2,3,48,256]{5,4,3,2,1,0:T(8,128)(2,1)}) conditional(s32[]{:T(128)} %convert_element_type.89, () %tuple.186, (pred[]{:T(512)}, bf16[512,768]{1,0:T(8,128)(2,1)}, bf16[512,768]{1,0:T(8,128)(2,1)}, ...), branch_computations={%region_17.18_spmd, %region_18.23_spmd} | conditional | flops 7247757312 | bytes 50840828 | solution.py:896
  98.2 12.4 %conditional.2 = (bf16[3072,768]{1,0:T(8,128)(2,1)}, bf16[3072,768]{1,0:T(8,128)(2,1)}) conditional(s32[]{:T(128)} %convert_element_type.55, () %tuple.117, (bf16[512,768]{1,0:T(8,128)(2,1)}, s32[1,512]{1,0:T(1,128)}, s32[1,512]{1,0:T(1,128)}, bf16[3072,768]{1,0:T(8,128)(2,1)}, bf16[512,768]{1,0:T(8,128)(2,1)}, /*index=5*/s32[1,512]{1,0:T(1,128)}, ...), branch_computations={%region_19.19_spmd, %region_20.20_spmd} | conditional | flops 4831838208 | bytes 26291552 | solution.py:896
  115.1 6.9 %conditional.3 = (bf16[3072,768]{1,0:T(8,128)(2,1)}) conditional(s32[]{:T(128)} %convert_element_type.55, () %tuple.116, (bf16[512,768]{1,0:T(8,128)(2,1)S(1)}, s32[1,512]{1,0:T(1,128)}, s32[1,512]{1,0:T(1,128)}, bf16[3072,768]{1,0:T(8,128)(2,1)}) %tuple.120), branch_computations={%region_21.21_spmd, %region_22.22_spmd} | conditional | flops 2415919104 | bytes 13145776 | solution.py:896
  123.2 29.5 %conditional.25 = (bf16[3072,768]{1,0:T(8,128)(2,1)}, bf16[3072,768]{1,0:T(8,128)(2,1)}, bf16[4,2,2,3,48,256]{5,4,3,2,1,0:T(8,128)(2,1)S(1)}, bf16[4,2,2,3,48,25...) conditional(s32[]{:T(128)} %convert_element_type.89, () %tuple.190, ...), branch_computations={%region_23.24_spmd, %region_24.25_spmd} | conditional | flops 21743271936 | bytes 44743272 | solution.py:896
  124.8 27.9 %ffn.2 = (bf16[3072,768]{1,0:T(8,128)(2,1)}, bf16[3072,768]{1,0:T(8,128)(2,1)}, bf16[4,2,2,3,48,256]{5,4,3,2,1,0:T(8,128)(2,1)S(1)}, bf16[4,2,2,3,48,256]{5,4,3,...) custom-call(s32[4]{0:T(128)S(1)} %get-tuple-element.595.c_ref, ...), custom_call_target="tpu_custom_call" | custom-call | flops 21743271936 | bytes 40000000 | tf_op jit(solution)/shard_map/cond/branch_1_fun/ffn/pallas_call | solution.py:660
  152.7 28.9 %conditional.26 = (bf16[3072,768]{1,0:T(8,128)(2,1)}, bf16[3072,768]{1,0:T(8,128)(2,1)}, bf16[4,2,2,3,48,256]{5,4,3,2,1,0:T(8,128)(2,1)}, bf16[4,2,2,3,48,256]{5...) conditional(s32[]{:T(128)} %convert_element_type.89, () %tuple.185, ...), branch_computations={%region_25.26_spmd, %region_26.29_spmd} | conditional | flops 10874209280 | bytes 54236196 | solution.py:896
  153.3 25.5 %conditional.4 = (bf16[3072,768]{1,0:T(8,128)(2,1)}, bf16[3072,768]{1,0:T(8,128)(2,1)}, bf16[4,2,2,3,48,256]{5,4,3,2,1,0:T(8,128)(2,1)}, bf16[4,2,2,3,48,256]{5,...) conditional(s32[]{:T(128)} %convert_element_type.63, () %tuple.127, ...), branch_computations={%region_27.27_spmd, %region_28.28_spmd} | conditional | flops 10873208832 | bytes 45517400 | solution.py:896
  153.3 22.1 %ffn.3 = (bf16[3072,768]{1,0:T(8,128)(2,1)}, bf16[3072,768]{1,0:T(8,128)(2,1)}, bf16[512,768]{1,0:T(8,128)(2,1)S(1)}, bf16[512,768]{1,0:T(8,128)(2,1)S(1)}, bf16...) custom-call(s32[4]{0:T(128)S(1)} %get-tuple-element.613.c_ref, ...), custom_call_target="tpu_custom_call" | custom-call | flops 10871635968 | bytes 40000000 | tf_op jit(solution)/shard_map/cond/branch_1_fun/cond/branch_1_fun/ffn/pallas_call | solution.py:660
  182.9 48.0 %conditional.27 = (f32[512,768]{1,0:T(8,128)}, bf16[512,768]{1,0:T(8,128)(2,1)}, bf16[512,768]{1,0:T(8,128)(2,1)}, f32[8,768]{1,0:T(8,128)}, bf16[512,768]{1,0:T...) conditional(s32[]{:T(128)} %convert_element_type.89, () %tuple.194, ...), branch_computations={%region_29.30_spmd, %region_30.35_spmd} | conditional | flops 4855410688 | bytes 59206348 | solution.py:896
  182.9 14.8 %all-to-all-start.3 = ((bf16[4,2,2,3,48,256]{5,4,3,2,1,0:T(8,128)(2,1)}), bf16[4,2,2,3,48,256]{5,4,3,2,1,0:T(8,128)(2,1)S(1)}, u32[]{:S(2)}, u32[]{:S(2)}) async-start(bf16[4,2,2,3,48,256]{5,4,3,2,1,0:T(8,128)(2,1)} %get-tuple-element.694), calls=%async_computation.3 | async-start | bytes 2359296 | tf_op jit(solution)/shard_map/cond/branch_1_fun/all_to_all | solution.py:903
  200.7 11.3 %conditional.5 = (bf16[512,768]{1,0:T(8,128)(2,1)S(1)}, bf16[512,768]{1,0:T(8,128)(2,1)}, bf16[512,768]{1,0:T(8,128)(2,1)}) conditional(s32[]{:T(128)} %convert_element_type.80, () %tuple.136, (s32[1,512]{1,0:T(1,128)}, s32[1,512]{1,0:T(1,128)}, bf16[3072,768]{1,0:T(8,128)(2,1)}, s32[1,512]{1,0:T(1,128)}, s32[1,512]{1,0:T(1,128)}, ...), branch_computations={%region_31.31_spmd, %region_32.32_spmd} | conditional | flops 4833411072 | bytes 28650856 | solution.py:896
  218.2 6.7 %conditional.6 = (f32[512,768]{1,0:T(8,128)}, bf16[512,768]{1,0:T(8,128)(2,1)}, bf16[512,768]{1,0:T(8,128)(2,1)}, f32[8,768]{1,0:T(8,128)}) conditional(s32[]{:T(128)} %convert_element_type.80, () %tuple.135, (f32[2,768]{1,0:T(2,128)S(1)}, bf16[512,768]{1,0:T(8,128)(2,1)S(1)}, bf16[512,768]{1,0:T(8,128)(2,1)}, bf16[512,768]{1,0:T(8,128)(2,1)}, ...), branch_computations={%region_33.33_spmd, %region_34.34_spmd} | conditional | flops 20000000 | bytes 11151944 | solution.py:896
  231.0 42.6 %conditional.28 = (f32[512,768]{1,0:T(8,128)}, f32[8,768]{1,0:T(8,128)}, bf16[2,4,2,48,384]{4,3,2,1,0:T(8,128)(2,1)}, bf16[2,4,2,48,384]{4,3,2,1,0:T(8,128)(2,1)...) conditional(s32[]{:T(128)} %convert_element_type.89, () %tuple.193, ...), branch_computations={%region_35.36_spmd, %region_36.39_spmd} | conditional | flops 40021999616 | bytes 50563788 | solution.py:896
  238.5 29.5 %conditional.7 = (f32[512,768]{1,0:T(8,128)}, f32[8,768]{1,0:T(8,128)}, bf16[2,4,2,48,384]{4,3,2,1,0:T(8,128)(2,1)}, bf16[2,4,2,48,384]{4,3,2,1,0:T(8,128)(2,1)}...) conditional(s32[]{:T(128)} %convert_element_type.81, () %tuple.143, ...), branch_computations={%region_37.37_spmd, %region_38.38_spmd} | conditional | flops 40020000768 | bytes 31160160 | solution.py:896
  238.5 23.7 %attn_bwd.1 = (bf16[512,768]{1,0:T(8,128)(2,1)S(1)}, bf16[512,768]{1,0:T(8,128)(2,1)S(1)}, bf16[2,4,2,48,384]{4,3,2,1,0:T(8,128)(2,1)}, bf16[2,4,2,48,384]{4,3,2...) custom-call(s32[4]{0:T(128)S(1)} %get-tuple-element.701.c_ref, ...), custom_call_target="tpu_custom_call" | custom-call | flops 40000000000 | bytes 20000000 | tf_op jit(solution)/shard_map/cond/branch_1_fun/cond/branch_1_fun/attn_bwd/pallas_call | solution.py:387
  273.6 35.9 %conditional.29 = (f32[2,2,48,384]{3,2,1,0:T(8,128)S(1)}, bf16[4,2,2,48,384]{4,3,2,1,0:T(8,128)(2,1)}, bf16[4,2,2,3,48,256]{5,4,3,2,1,0:T(8,128)(2,1)}, bf16[512...) conditional(s32[]{:T(128)} %convert_element_type.89, () %tuple.180, ...), branch_computations={%region_39.40_spmd, %region_40.47_spmd} | conditional | flops 2421101824 | bytes 55122792 | solution.py:896
  280.1 12.7 %conditional.8 = (bf16[512,768]{1,0:T(8,128)(2,1)}, bf16[512,768]{1,0:T(8,128)(2,1)}, f32[512,768]{1,0:T(8,128)}) conditional(s32[]{:T(128)} %convert_element_type.86, () %tuple.149, (s32[1,512]{1,0:T(1,128)}, s32[1,512]{1,0:T(1,128)}, bf16[3072,768]{1,0:T(8,128)(2,1)}, bf16[512,768]{1,0:T(8,128)(2,1)}, f32[512,768]{1,0:T(8,128)}, ...), branch_computations={%region_41.41_spmd, %region_42.42_spmd} | conditional | flops 2419064832 | bytes 35165996 | solution.py:896
  301.5 6.4 %conditional.10 = (f32[22,768]{1,0:T(8,128)}) conditional(s32[]{:T(128)} %convert_element_type.86, () %tuple.152, f32[22,768]{1,0:T(8,128)S(1)} %get-tuple-element.1502), branch_computations={%region_45.45_spmd, %region_46.46_spmd} | conditional | flops 33792 | bytes 946264 | solution.py:896
  (254 shorter events, 245.0 us)
Async XLA Ops:
  3.1 17.7 %collective-permute-start.30 = (bf16[2,2,48,384]{3,2,1,0:T(8,128)(2,1)S(1)}, bf16[2,2,48,384]{3,2,1,0:T(8,128)(2,1)S(1)}, u32[]{:S(2)}, u32[]{:S(2)}) collective-permute-start(bf16[2,2,48,384]{3,2,1,0:T(8,128)(2,1)S(1)} %pad_maximum_fusion.8), channel_id=1, source_target_pairs={{0,8},{2,10},{4,12},{6,14},{8,0},{10,2},{12,4},{14,6},{16,24},{18,... | collective-permute-start | bytes 442376 | tf_op jit(solution)/shard_map/cond/branch_1_fun/ppermute | solution.py:822
  6.2 14.6 %collective-permute-start.31 = (bf16[2,2,48,384]{3,2,1,0:T(8,128)(2,1)S(1)}, bf16[2,2,48,384]{3,2,1,0:T(8,128)(2,1)S(1)}, u32[]{:S(2)}, u32[]{:S(2)}) collective-permute-start(bf16[2,2,48,384]{3,2,1,0:T(8,128)(2,1)S(1)} %pad_maximum_fusion.8), channel_id=1, source_target_pairs={{0,16},{2,18},{4,20},{6,22},{8,24},{10,26},{12,28},{14,30},{16,0},... | collective-permute-start | bytes 442376 | tf_op jit(solution)/shard_map/cond/branch_1_fun/ppermute | solution.py:822
  26.2 31.7 %all-to-all-start.5 = ((bf16[4,2,2,3,48,256]{5,4,3,2,1,0:T(8,128)(2,1)}), bf16[4,2,2,3,48,256]{5,4,3,2,1,0:T(8,128)(2,1)}, u32[]{:S(2)}, u32[]{:S(2)}) async-start(bf16[4,2,2,3,48,256]{5,4,3,2,1,0:T(8,128)(2,1)} %get-tuple-element.504), calls=%async_computation.5 | async-start | bytes 2359296 | tf_op jit(solution)/shard_map/cond/branch_1_fun/all_to_all | solution.py:903
  39.9 12.5 %collective-permute-start.35 = (bf16[2,4,2,48,384]{4,3,2,1,0:T(8,128)(2,1)}, bf16[2,4,2,48,384]{4,3,2,1,0:T(8,128)(2,1)}, u32[]{:S(2)}, u32[]{:S(2)}) collective-permute-start(bf16[2,4,2,48,384]{4,3,2,1,0:T(8,128)(2,1)} %pad_maximum_fusion), channel_id=1, source_target_pairs={{0,4},{2,6},{4,0},{6,2},{8,12},{10,14},{12,8},{14,10},{16,20},{18,... | collective-permute-start | bytes 1769480 | tf_op jit(solution)/shard_map/cond/branch_1_fun/cond/branch_1_fun/ppermute | solution.py:822
  58.0 32.5 %all-to-all-start = ((bf16[4,2,2,3,48,256]{5,4,3,2,1,0:T(8,128)(2,1)}), bf16[4,2,2,3,48,256]{5,4,3,2,1,0:T(8,128)(2,1)}, u32[]{:S(2)}, u32[]{:S(2)}) async-start(bf16[4,2,2,3,48,256]{5,4,3,2,1,0:T(8,128)(2,1)} %get-tuple-element.569), calls=%async_computation | async-start | bytes 2359296 | tf_op jit(solution)/shard_map/cond/branch_1_fun/all_to_all | solution.py:903
  62.4 27.3 %collective-permute-start.1 = (bf16[4,2,2,3,48,256]{5,4,3,2,1,0:T(8,128)(2,1)}, bf16[4,2,2,3,48,256]{5,4,3,2,1,0:T(8,128)(2,1)}, u32[]{:S(2)}, u32[]{:S(2)}) collective-permute-start(bf16[4,2,2,3,48,256]{5,4,3,2,1,0:T(8,128)(2,1)} %get-tuple-element.568), channel_id=1, source_target_pairs={{0,4},{2,6},{4,0},{6,2},{8,12},{10,14},{12,8},{14,10},{16,20},{18,... | collective-permute-start | bytes 3538952 | tf_op jit(solution)/shard_map/cond/branch_1_fun/ppermute | solution.py:822
  64.0 20.8 %collective-permute-start.2 = (bf16[512,768]{1,0:T(8,128)(2,1)}, bf16[512,768]{1,0:T(8,128)(2,1)}, u32[]{:S(2)}, u32[]{:S(2)}) collective-permute-start(bf16[512,768]{1,0:T(8,128)(2,1)} %get-tuple-element.570), channel_id=1, source_target_pairs={{0,2},{2,0},{4,6},{6,4},{8,10},{10,8},{12,14},{14,12},{16,18},{18,... | collective-permute-start | bytes 2359304 | tf_op jit(solution)/shard_map/cond/branch_1_fun/ppermute | solution.py:822
  90.5 32.6 %all-to-all-start.1 = ((bf16[4,2,2,3,48,256]{5,4,3,2,1,0:T(8,128)(2,1)}), bf16[4,2,2,3,48,256]{5,4,3,2,1,0:T(8,128)(2,1)}, u32[]{:S(2)}, u32[]{:S(2)}) async-start(bf16[4,2,2,3,48,256]{5,4,3,2,1,0:T(8,128)(2,1)} %get-tuple-element.594), calls=%async_computation.1 | async-start | bytes 2359296 | tf_op jit(solution)/shard_map/cond/branch_1_fun/all_to_all | solution.py:903
  95.1 27.3 %collective-permute-start.7 = (bf16[4,2,2,3,48,256]{5,4,3,2,1,0:T(8,128)(2,1)}, bf16[4,2,2,3,48,256]{5,4,3,2,1,0:T(8,128)(2,1)}, u32[]{:S(2)}, u32[]{:S(2)}) collective-permute-start(bf16[4,2,2,3,48,256]{5,4,3,2,1,0:T(8,128)(2,1)} %get-tuple-element.593), channel_id=1, source_target_pairs={{0,4},{2,6},{4,0},{6,2},{8,12},{10,14},{12,8},{14,10},{16,20},{18,... | collective-permute-start | bytes 3538952 | tf_op jit(solution)/shard_map/cond/branch_1_fun/ppermute | solution.py:822
  96.7 18.4 %collective-permute-start.6 = (bf16[512,768]{1,0:T(8,128)(2,1)}, bf16[512,768]{1,0:T(8,128)(2,1)S(1)}, u32[]{:S(2)}, u32[]{:S(2)}) collective-permute-start(bf16[512,768]{1,0:T(8,128)(2,1)} %get-tuple-element.583), channel_id=1, source_target_pairs={{0,2},{2,0},{4,6},{6,4},{8,10},{10,8},{12,14},{14,12},{16,18},{18,... | collective-permute-start | bytes 2359304 | tf_op jit(solution)/shard_map/cond/branch_1_fun/ppermute | solution.py:822
  123.2 29.5 %collective-permute-start.8 = (bf16[4,2,2,3,48,256]{5,4,3,2,1,0:T(8,128)(2,1)}, bf16[4,2,2,3,48,256]{5,4,3,2,1,0:T(8,128)(2,1)}, u32[]{:S(2)}, u32[]{:S(2)}) collective-permute-start(bf16[4,2,2,3,48,256]{5,4,3,2,1,0:T(8,128)(2,1)} %get-tuple-element.612), channel_id=1, source_target_pairs={{0,4},{2,6},{4,0},{6,2},{8,12},{10,14},{12,8},{14,10},{16,20},{18,... | collective-permute-start | bytes 3538952 | tf_op jit(solution)/shard_map/cond/branch_1_fun/ppermute | solution.py:822
  152.7 26.9 %collective-permute-start.17 = (bf16[4,2,2,3,48,256]{5,4,3,2,1,0:T(8,128)(2,1)}, bf16[4,2,2,3,48,256]{5,4,3,2,1,0:T(8,128)(2,1)S(1)}, u32[]{:S(2)}, u32[]{:S(2)}) collective-permute-start(bf16[4,2,2,3,48,256]{5,4,3,2,1,0:T(8,128)(2,1)} %get-tuple-element.652), channel_id=1, source_target_pairs={{0,4},{2,6},{4,0},{6,2},{8,12},{10,14},{12,8},{14,10},{16,20},{18,... | collective-permute-start | bytes 3538952 | tf_op jit(solution)/shard_map/cond/branch_1_fun/ppermute | solution.py:822
  182.9 45.6 %all-to-all-start.3 = ((bf16[4,2,2,3,48,256]{5,4,3,2,1,0:T(8,128)(2,1)}), bf16[4,2,2,3,48,256]{5,4,3,2,1,0:T(8,128)(2,1)S(1)}, u32[]{:S(2)}, u32[]{:S(2)}) async-start(bf16[4,2,2,3,48,256]{5,4,3,2,1,0:T(8,128)(2,1)} %get-tuple-element.694), calls=%async_computation.3 | async-start | bytes 2359296 | tf_op jit(solution)/shard_map/cond/branch_1_fun/all_to_all | solution.py:903
  197.7 27.5 %collective-permute-start.21 = (bf16[4,2,2,3,48,256]{5,4,3,2,1,0:T(8,128)(2,1)}, bf16[4,2,2,3,48,256]{5,4,3,2,1,0:T(8,128)(2,1)S(1)}, u32[]{:S(2)}, u32[]{:S(2)}) collective-permute-start(bf16[4,2,2,3,48,256]{5,4,3,2,1,0:T(8,128)(2,1)} %get-tuple-element.698), channel_id=1, source_target_pairs={{0,4},{2,6},{4,0},{6,2},{8,12},{10,14},{12,8},{14,10},{16,20},{18,... | collective-permute-start | bytes 3538952 | tf_op jit(solution)/shard_map/cond/branch_1_fun/ppermute | solution.py:822
  199.2 18.9 %collective-permute-start.20 = (bf16[512,768]{1,0:T(8,128)(2,1)}, bf16[512,768]{1,0:T(8,128)(2,1)}, u32[]{:S(2)}, u32[]{:S(2)}) collective-permute-start(bf16[512,768]{1,0:T(8,128)(2,1)} %get-tuple-element.684), channel_id=1, source_target_pairs={{0,2},{2,0},{4,6},{6,4},{8,10},{10,8},{12,14},{14,12},{16,18},{18,... | collective-permute-start | bytes 2359304 | tf_op jit(solution)/shard_map/cond/branch_1_fun/ppermute | solution.py:822
  231.0 40.3 %all-to-all-start.2 = ((bf16[4,2,2,3,48,256]{5,4,3,2,1,0:T(8,128)(2,1)}), bf16[4,2,2,3,48,256]{5,4,3,2,1,0:T(8,128)(2,1)S(1)}, u32[]{:S(2)}, u32[]{:S(2)}) async-start(bf16[4,2,2,3,48,256]{5,4,3,2,1,0:T(8,128)(2,1)} %get-tuple-element.758), calls=%async_computation.2 | async-start | bytes 2359296 | tf_op jit(solution)/shard_map/cond/branch_1_fun/all_to_all | solution.py:903
  235.5 32.4 %collective-permute-start.12 = (bf16[4,2,2,3,48,256]{5,4,3,2,1,0:T(8,128)(2,1)}, bf16[4,2,2,3,48,256]{5,4,3,2,1,0:T(8,128)(2,1)S(1)}, u32[]{:S(2)}, u32[]{:S(2)}) collective-permute-start(bf16[4,2,2,3,48,256]{5,4,3,2,1,0:T(8,128)(2,1)} %get-tuple-element.762), channel_id=1, source_target_pairs={{0,4},{2,6},{4,0},{6,2},{8,12},{10,14},{12,8},{14,10},{16,20},{18,... | collective-permute-start | bytes 3538952 | tf_op jit(solution)/shard_map/cond/branch_1_fun/ppermute | solution.py:822
  237.0 36.5 %collective-permute-start.11 = (bf16[512,768]{1,0:T(8,128)(2,1)}, bf16[512,768]{1,0:T(8,128)(2,1)}, u32[]{:S(2)}, u32[]{:S(2)}) collective-permute-start(bf16[512,768]{1,0:T(8,128)(2,1)} %get-tuple-element.756), channel_id=1, source_target_pairs={{0,2},{2,0},{4,6},{6,4},{8,10},{10,8},{12,14},{14,12},{16,18},{18,... | collective-permute-start | bytes 2359304 | tf_op jit(solution)/shard_map/cond/branch_1_fun/ppermute | solution.py:822
  273.6 35.8 %all-to-all-start.4 = ((bf16[4,2,2,3,48,256]{5,4,3,2,1,0:T(8,128)(2,1)}), bf16[4,2,2,3,48,256]{5,4,3,2,1,0:T(8,128)(2,1)}, u32[]{:S(2)}, u32[]{:S(2)}) async-start(bf16[4,2,2,3,48,256]{5,4,3,2,1,0:T(8,128)(2,1)} %get-tuple-element.804), calls=%async_computation.4 | async-start | bytes 2359296 | tf_op jit(solution)/shard_map/cond/branch_1_fun/all_to_all | solution.py:903
  278.9 15.4 %collective-permute-start.25 = (bf16[2,4,2,48,384]{4,3,2,1,0:T(8,128)(2,1)}, bf16[2,4,2,48,384]{4,3,2,1,0:T(8,128)(2,1)S(1)}, u32[]{:S(2)}, u32[]{:S(2)}) collective-permute-start(bf16[2,4,2,48,384]{4,3,2,1,0:T(8,128)(2,1)} %get-tuple-element.795), channel_id=1, source_target_pairs={{0,4},{2,6},{4,0},{6,2},{8,12},{10,14},{12,8},{14,10},{16,20},{18,... | collective-permute-start | bytes 1769480 | tf_op jit(solution)/shard_map/cond/branch_1_fun/ppermute | solution.py:822
  279.5 15.0 %collective-permute-start.26 = (bf16[2,4,2,48,384]{4,3,2,1,0:T(8,128)(2,1)}, bf16[2,4,2,48,384]{4,3,2,1,0:T(8,128)(2,1)S(1)}, u32[]{:S(2)}, u32[]{:S(2)}) collective-permute-start(bf16[2,4,2,48,384]{4,3,2,1,0:T(8,128)(2,1)} %get-tuple-element.797), channel_id=1, source_target_pairs={{0,2},{2,0},{4,6},{6,4},{8,10},{10,8},{12,14},{14,12},{16,18},{18,... | collective-permute-start | bytes 1769480 | tf_op jit(solution)/shard_map/cond/branch_1_fun/ppermute | solution.py:822
  309.4 25.1 %all-to-all-start.6 = ((bf16[4,2,2,48,384]{4,3,2,1,0:T(8,128)(2,1)}), bf16[4,2,2,48,384]{4,3,2,1,0:T(8,128)(2,1)S(1)}, u32[]{:S(2)}, u32[]{:S(2)}) async-start(bf16[4,2,2,48,384]{4,3,2,1,0:T(8,128)(2,1)} %get-tuple-element.1007), calls=%async_computation.6 | async-start | bytes 1179648 | tf_op jit(solution)/shard_map/all_to_all | solution.py:903
  317.5 18.6 %collective-permute-start.38 = (bf16[2,3,48,768]{3,2,1,0:T(8,128)(2,1)S(1)}, bf16[2,3,48,768]{3,2,1,0:T(8,128)(2,1)S(1)}, u32[]{:S(2)}, u32[]{:S(2)}) collective-permute-start(bf16[2,3,48,768]{3,2,1,0:T(8,128)(2,1)S(1)} %pad_maximum_fusion.12), channel_id=1, source_target_pairs={{0,2},{2,0},{4,6},{6,4},{8,10},{10,8},{12,14},{14,12},{16,18},{18,... | collective-permute-start | bytes 1327112 | tf_op jit(solution)/shard_map/ppermute | solution.py:822
  324.7 13.2 %collective-permute-start.39 = (f32[22,768]{1,0:T(8,128)S(1)}, f32[22,768]{1,0:T(8,128)S(1)}, u32[]{:S(2)}, u32[]{:S(2)}) collective-permute-start(f32[22,768]{1,0:T(8,128)S(1)} %get-tuple-element.1504), channel_id=1, source_target_pairs={{0,8},{2,10},{4,12},{6,14},{8,0},{10,2},{12,4},{14,6},{16,24},{18,... | collective-permute-start | bytes 202760 | tf_op jit(solution)/shard_map/ppermute | solution.py:822
  (47 other events, 431.1 us)

commit v7 on v6

--- a/solution.py
+++ b/solution.py
@@ -38,7 +38,7 @@
     return lax.dot_general(a, b, (((0,), (0,)), ((), ())), preferred_element_type=f32)
 
 
-def params(grid_rank, mib=20):
+def params(grid_rank, mib=14):
     return pltpu.CompilerParams(
         dimension_semantics=("arbitrary",) * grid_rank, vmem_limit_bytes=mib * MIB
     )
@@ -255,7 +255,7 @@
                 pltpu.SemaphoreType.DMA((64,)),
             ],
         ),
-        compiler_params=params(1, 26),
+        compiler_params=params(1, 22),
         cost_estimate=cost(2e10, 1e7, 3e6),
         name="attn_fwd",
     )(coords, windows, x, seg_row, ln, proj_bias, *pa, *pb)
@@ -428,7 +428,7 @@
                 pltpu.SemaphoreType.DMA((64,)),
             ],
         ),
-        compiler_params=params(1, 34),
+        compiler_params=params(1, 30),
         cost_estimate=cost(4e10, 2e7, 3e6),
         name="attn_bwd",
     )(coords, windows, dxr, dxr2, x, seg_row, ln, qkv, kt, o, ot, lse, *pa, *pb)
@@ -686,7 +686,7 @@
                 pltpu.SemaphoreType.DMA((2, tiles)),
             ],
         ),
-        compiler_params=params(1, 46 if groups == 2 else 60),
+        compiler_params=params(1, 42 if groups == 2 else 60),
         cost_estimate=cost(12 * slots * width * hid * 1.5, 4e7, 2 * slots * hid),
         name="ffn",
     )(coords, plans[0], plans[-1], xs, dys, up_b, *places, *carry, *[w for pair in weights for w in pair])

time: 345 us -> 345 us (level)
  no operation moved by 1% of the time
where the time goes in v7:
time: 345 us; the launch traced here: 341 us
  Pallas kernels  156 us (45%)
  starting transfers between devices  83.9 us (24%)
  waiting for transfers between devices  58 us (17%)
  local copies, waits for them, and re-layouts  20.2 us (6%)
  other arithmetic  19.2 us (6%)
    pallas_call x2, Pallas kernels, ffn(): pl.pallas_call(functools.partial(ffn_kernel, first, count, piece, groups,...  50 us
    all_to_all x7, starting transfers between devices, deal_z(): return lax.all_to_all(v, 'dp', 0, 0, axis_index_groups=groups, tiled=True)  42.9 us
    ppermute x29, starting transfers between devices, flip(): return lax.ppermute(x, 'dp', [(i, i ^ mask) for i in range(size)])  38.7 us
    ppermute x29, waiting for transfers between devices, flip(): return lax.ppermute(x, 'dp', [(i, i ^ mask) for i in range(size)])  33.1 us
    pallas_call x11, Pallas kernels, whole(): pl.pallas_call(kernel, out_shape=[jax.ShapeDtypeStruct(s, d) for s, d in...  26.9 us
    pallas_call x1, Pallas kernels, attn_bwd(): pl.pallas_call(functools.partial(attn_bwd_kernel, heads, piece), out_shap...  23.7 us
    ppermute x13, waiting for transfers between devices, swap(): return lax.ppermute(v, 'mp', [(0, 1), (1, 0)])  20.5 us
    pallas_call x4, Pallas kernels, sort_tokens(): pl.pallas_call(functools.partial(sort_kernel, len(sources)), out_shape=ja...  18.3 us
  transfers between devices with their start and end apart: 49, of which 27 were waited for; matrix products, arithmetic and copies ran while one was open for 9% of the time, Pallas kernels for 44%

profile of v7, /device:TPU:0, one launch (start us, length us, event | category | flops | bytes accessed | tf_op | source)
XLA Modules:
  0.0 341.1 jit_solution(9217914271347883882)
XLA Ops:
  1.4 23.7 %conditional.21 = (bf16[4,2,2,3,48,256]{5,4,3,2,1,0:T(8,128)(2,1)}, bf16[2,2,3,48,256]{4,3,2,1,0:T(8,128)(2,1)S(1)}, bf16[2,2,3,48,256]{4,3,2,1,0:T(8,128)(2,1)S...) conditional(s32[]{:T(128)} %convert_element_type.89, () %tuple.182, ...), branch_computations={%region_0.1_spmd, %region_1.9_spmd} | conditional | flops 11818124 | bytes 18735460 | solution.py:896
  26.2 31.7 %conditional.22 = (bf16[4,2,2,3,48,256]{5,4,3,2,1,0:T(8,128)(2,1)}, bf16[2,4,2,48,384]{4,3,2,1,0:T(8,128)(2,1)}, bf16[2,4,2,48,384]{4,3,2,1,0:T(8,128)(2,1)}, bf...) conditional(s32[]{:T(128)} %convert_element_type.89, () %tuple.181, ...), branch_computations={%region_9.10_spmd, %region_10.13_spmd} | conditional | flops 2421230592 | bytes 33819932 | solution.py:896
  31.2 24.0 %conditional = (bf16[2,4,2,48,384]{4,3,2,1,0:T(8,128)(2,1)}, bf16[2,4,2,48,384]{4,3,2,1,0:T(8,128)(2,1)}, bf16[2,4,2,48,384]{4,3,2,1,0:T(8,128)(2,1)}, bf16[2,4,...) conditional(s32[]{:T(128)} %convert_element_type.53, () %tuple.104, ...), branch_computations={%region_11.11_spmd, %region_12.12_spmd} | conditional | flops 2421230592 | bytes 23989290 | solution.py:896
  58.0 32.5 %conditional.23 = (bf16[2,3,3,512,128]{4,3,2,1,0:T(8,128)(2,1)}, bf16[2,3,128,512]{3,2,1,0:T(8,128)(2,1)}, bf16[2,512,384]{2,1,0:T(8,128)(2,1)}, bf16[2,3,128,51...) conditional(s32[]{:T(128)} %convert_element_type.89, () %tuple.187, ...), branch_computations={%region_13.14_spmd, %region_14.17_spmd} | conditional | flops 20010000384 | bytes 35849056 | solution.py:896
  65.5 19.3 %conditional.1 = (bf16[2,3,3,512,128]{4,3,2,1,0:T(8,128)(2,1)}, bf16[2,3,128,512]{3,2,1,0:T(8,128)(2,1)}, bf16[2,512,384]{2,1,0:T(8,128)(2,1)}, bf16[2,3,128,512...) conditional(s32[]{:T(128)} %convert_element_type.54, () %tuple.110, ...), branch_computations={%region_15.15_spmd, %region_16.16_spmd} | conditional | flops 20010000384 | bytes 18154016 | solution.py:896
  65.5 15.2 %attn_fwd.1 = (bf16[512,768]{1,0:T(8,128)(2,1)S(1)}, bf16[512,768]{1,0:T(8,128)(2,1)S(1)}, bf16[2,3,3,512,128]{4,3,2,1,0:T(8,128)(2,1)}, bf16[2,3,128,512]{3,2,1...) custom-call(s32[4]{0:T(128)S(1)} %get-tuple-element.527.c_ref, ...), custom_call_target="tpu_custom_call" | custom-call | flops 20000000000 | bytes 10000000 | tf_op jit(solution)/shard_map/cond/branch_1_fun/cond/branch_1_fun/attn_fwd/pallas_call | solution.py:235
  90.5 32.6 %conditional.24 = (bf16[3072,768]{1,0:T(8,128)(2,1)}, bf16[3072,768]{1,0:T(8,128)(2,1)}, bf16[4,2,2,3,48,256]{5,4,3,2,1,0:T(8,128)(2,1)}, bf16[4,2,2,3,48,256]{5,4,3,2,1,0:T(8,128)(2,1)}) conditional(s32[]{:T(128)} %convert_element_type.89, () %tuple.186, (pred[]{:T(512)}, bf16[512,768]{1,0:T(8,128)(2,1)}, bf16[512,768]{1,0:T(8,128)(2,1)}, ...), branch_computations={%region_17.18_spmd, %region_18.23_spmd} | conditional | flops 7247757312 | bytes 50840828 | solution.py:896
  98.2 12.4 %conditional.2 = (bf16[3072,768]{1,0:T(8,128)(2,1)}, bf16[3072,768]{1,0:T(8,128)(2,1)}) conditional(s32[]{:T(128)} %convert_element_type.55, () %tuple.117, (bf16[512,768]{1,0:T(8,128)(2,1)}, s32[1,512]{1,0:T(1,128)}, s32[1,512]{1,0:T(1,128)}, bf16[3072,768]{1,0:T(8,128)(2,1)}, bf16[512,768]{1,0:T(8,128)(2,1)}, /*index=5*/s32[1,512]{1,0:T(1,128)}, ...), branch_computations={%region_19.19_spmd, %region_20.20_spmd} | conditional | flops 4831838208 | bytes 26291552 | solution.py:896
  115.1 6.9 %conditional.3 = (bf16[3072,768]{1,0:T(8,128)(2,1)}) conditional(s32[]{:T(128)} %convert_element_type.55, () %tuple.116, (bf16[512,768]{1,0:T(8,128)(2,1)S(1)}, s32[1,512]{1,0:T(1,128)}, s32[1,512]{1,0:T(1,128)}, bf16[3072,768]{1,0:T(8,128)(2,1)}) %tuple.120), branch_computations={%region_21.21_spmd, %region_22.22_spmd} | conditional | flops 2415919104 | bytes 13145776 | solution.py:896
  123.2 29.5 %conditional.25 = (bf16[3072,768]{1,0:T(8,128)(2,1)}, bf16[3072,768]{1,0:T(8,128)(2,1)}, bf16[4,2,2,3,48,256]{5,4,3,2,1,0:T(8,128)(2,1)S(1)}, bf16[4,2,2,3,48,25...) conditional(s32[]{:T(128)} %convert_element_type.89, () %tuple.190, ...), branch_computations={%region_23.24_spmd, %region_24.25_spmd} | conditional | flops 21743271936 | bytes 44743272 | solution.py:896
  124.8 27.9 %ffn.2 = (bf16[3072,768]{1,0:T(8,128)(2,1)}, bf16[3072,768]{1,0:T(8,128)(2,1)}, bf16[4,2,2,3,48,256]{5,4,3,2,1,0:T(8,128)(2,1)S(1)}, bf16[4,2,2,3,48,256]{5,4,3,...) custom-call(s32[4]{0:T(128)S(1)} %get-tuple-element.595.c_ref, ...), custom_call_target="tpu_custom_call" | custom-call | flops 21743271936 | bytes 40000000 | tf_op jit(solution)/shard_map/cond/branch_1_fun/ffn/pallas_call | solution.py:660
  152.7 29.0 %conditional.26 = (bf16[3072,768]{1,0:T(8,128)(2,1)}, bf16[3072,768]{1,0:T(8,128)(2,1)}, bf16[4,2,2,3,48,256]{5,4,3,2,1,0:T(8,128)(2,1)}, bf16[4,2,2,3,48,256]{5...) conditional(s32[]{:T(128)} %convert_element_type.89, () %tuple.185, ...), branch_computations={%region_25.26_spmd, %region_26.29_spmd} | conditional | flops 10874209280 | bytes 54236196 | solution.py:896
  152.8 25.6 %conditional.4 = (bf16[3072,768]{1,0:T(8,128)(2,1)}, bf16[3072,768]{1,0:T(8,128)(2,1)}, bf16[4,2,2,3,48,256]{5,4,3,2,1,0:T(8,128)(2,1)}, bf16[4,2,2,3,48,256]{5,...) conditional(s32[]{:T(128)} %convert_element_type.63, () %tuple.127, ...), branch_computations={%region_27.27_spmd, %region_28.28_spmd} | conditional | flops 10873208832 | bytes 45517400 | solution.py:896
  152.8 22.1 %ffn.3 = (bf16[3072,768]{1,0:T(8,128)(2,1)}, bf16[3072,768]{1,0:T(8,128)(2,1)}, bf16[512,768]{1,0:T(8,128)(2,1)S(1)}, bf16[512,768]{1,0:T(8,128)(2,1)S(1)}, bf16...) custom-call(s32[4]{0:T(128)S(1)} %get-tuple-element.613.c_ref, ...), custom_call_target="tpu_custom_call" | custom-call | flops 10871635968 | bytes 40000000 | tf_op jit(solution)/shard_map/cond/branch_1_fun/cond/branch_1_fun/ffn/pallas_call | solution.py:660
  183.0 48.0 %conditional.27 = (f32[512,768]{1,0:T(8,128)}, bf16[512,768]{1,0:T(8,128)(2,1)}, bf16[512,768]{1,0:T(8,128)(2,1)}, f32[8,768]{1,0:T(8,128)}, bf16[512,768]{1,0:T...) conditional(s32[]{:T(128)} %convert_element_type.89, () %tuple.194, ...), branch_computations={%region_29.30_spmd, %region_30.35_spmd} | conditional | flops 4855410688 | bytes 59206348 | solution.py:896
  183.0 14.8 %all-to-all-start.3 = ((bf16[4,2,2,3,48,256]{5,4,3,2,1,0:T(8,128)(2,1)}), bf16[4,2,2,3,48,256]{5,4,3,2,1,0:T(8,128)(2,1)S(1)}, u32[]{:S(2)}, u32[]{:S(2)}) async-start(bf16[4,2,2,3,48,256]{5,4,3,2,1,0:T(8,128)(2,1)} %get-tuple-element.694), calls=%async_computation.3 | async-start | bytes 2359296 | tf_op jit(solution)/shard_map/cond/branch_1_fun/all_to_all | solution.py:903
  200.7 11.3 %conditional.5 = (bf16[512,768]{1,0:T(8,128)(2,1)S(1)}, bf16[512,768]{1,0:T(8,128)(2,1)}, bf16[512,768]{1,0:T(8,128)(2,1)}) conditional(s32[]{:T(128)} %convert_element_type.80, () %tuple.136, (s32[1,512]{1,0:T(1,128)}, s32[1,512]{1,0:T(1,128)}, bf16[3072,768]{1,0:T(8,128)(2,1)}, s32[1,512]{1,0:T(1,128)}, s32[1,512]{1,0:T(1,128)}, ...), branch_computations={%region_31.31_spmd, %region_32.32_spmd} | conditional | flops 4833411072 | bytes 28650856 | solution.py:896
  218.1 6.7 %conditional.6 = (f32[512,768]{1,0:T(8,128)}, bf16[512,768]{1,0:T(8,128)(2,1)}, bf16[512,768]{1,0:T(8,128)(2,1)}, f32[8,768]{1,0:T(8,128)}) conditional(s32[]{:T(128)} %convert_element_type.80, () %tuple.135, (f32[2,768]{1,0:T(2,128)S(1)}, bf16[512,768]{1,0:T(8,128)(2,1)S(1)}, bf16[512,768]{1,0:T(8,128)(2,1)}, bf16[512,768]{1,0:T(8,128)(2,1)}, ...), branch_computations={%region_33.33_spmd, %region_34.34_spmd} | conditional | flops 20000000 | bytes 11151944 | solution.py:896
  230.9 42.9 %conditional.28 = (f32[512,768]{1,0:T(8,128)}, f32[8,768]{1,0:T(8,128)}, bf16[2,4,2,48,384]{4,3,2,1,0:T(8,128)(2,1)}, bf16[2,4,2,48,384]{4,3,2,1,0:T(8,128)(2,1)...) conditional(s32[]{:T(128)} %convert_element_type.89, () %tuple.193, ...), branch_computations={%region_35.36_spmd, %region_36.39_spmd} | conditional | flops 40021999616 | bytes 50563788 | solution.py:896
  238.8 29.4 %conditional.7 = (f32[512,768]{1,0:T(8,128)}, f32[8,768]{1,0:T(8,128)}, bf16[2,4,2,48,384]{4,3,2,1,0:T(8,128)(2,1)}, bf16[2,4,2,48,384]{4,3,2,1,0:T(8,128)(2,1)}...) conditional(s32[]{:T(128)} %convert_element_type.81, () %tuple.143, ...), branch_computations={%region_37.37_spmd, %region_38.38_spmd} | conditional | flops 40020000768 | bytes 31160160 | solution.py:896
  238.8 23.7 %attn_bwd.1 = (bf16[512,768]{1,0:T(8,128)(2,1)S(1)}, bf16[512,768]{1,0:T(8,128)(2,1)S(1)}, bf16[2,4,2,48,384]{4,3,2,1,0:T(8,128)(2,1)}, bf16[2,4,2,48,384]{4,3,2...) custom-call(s32[4]{0:T(128)S(1)} %get-tuple-element.701.c_ref, ...), custom_call_target="tpu_custom_call" | custom-call | flops 40000000000 | bytes 20000000 | tf_op jit(solution)/shard_map/cond/branch_1_fun/cond/branch_1_fun/attn_bwd/pallas_call | solution.py:387
  273.9 36.1 %conditional.29 = (f32[2,2,48,384]{3,2,1,0:T(8,128)S(1)}, bf16[4,2,2,48,384]{4,3,2,1,0:T(8,128)(2,1)}, bf16[4,2,2,3,48,256]{5,4,3,2,1,0:T(8,128)(2,1)}, bf16[512...) conditional(s32[]{:T(128)} %convert_element_type.89, () %tuple.180, ...), branch_computations={%region_39.40_spmd, %region_40.47_spmd} | conditional | flops 2421101824 | bytes 55122792 | solution.py:896
  279.9 12.7 %conditional.8 = (bf16[512,768]{1,0:T(8,128)(2,1)}, bf16[512,768]{1,0:T(8,128)(2,1)}, f32[512,768]{1,0:T(8,128)}) conditional(s32[]{:T(128)} %convert_element_type.86, () %tuple.149, (s32[1,512]{1,0:T(1,128)}, s32[1,512]{1,0:T(1,128)}, bf16[3072,768]{1,0:T(8,128)(2,1)}, bf16[512,768]{1,0:T(8,128)(2,1)}, f32[512,768]{1,0:T(8,128)}, ...), branch_computations={%region_41.41_spmd, %region_42.42_spmd} | conditional | flops 2419064832 | bytes 35165996 | solution.py:896
  302.1 6.4 %conditional.10 = (f32[22,768]{1,0:T(8,128)}) conditional(s32[]{:T(128)} %convert_element_type.86, () %tuple.152, f32[22,768]{1,0:T(8,128)S(1)} %get-tuple-element.1502), branch_computations={%region_45.45_spmd, %region_46.46_spmd} | conditional | flops 33792 | bytes 946264 | solution.py:896
  (254 shorter events, 244.6 us)
Async XLA Ops:
  3.1 17.7 %collective-permute-start.30 = (bf16[2,2,48,384]{3,2,1,0:T(8,128)(2,1)S(1)}, bf16[2,2,48,384]{3,2,1,0:T(8,128)(2,1)S(1)}, u32[]{:S(2)}, u32[]{:S(2)}) collective-permute-start(bf16[2,2,48,384]{3,2,1,0:T(8,128)(2,1)S(1)} %pad_maximum_fusion.8), channel_id=1, source_target_pairs={{0,8},{2,10},{4,12},{6,14},{8,0},{10,2},{12,4},{14,6},{16,24},{18,... | collective-permute-start | bytes 442376 | tf_op jit(solution)/shard_map/cond/branch_1_fun/ppermute | solution.py:822
  6.2 14.6 %collective-permute-start.31 = (bf16[2,2,48,384]{3,2,1,0:T(8,128)(2,1)S(1)}, bf16[2,2,48,384]{3,2,1,0:T(8,128)(2,1)S(1)}, u32[]{:S(2)}, u32[]{:S(2)}) collective-permute-start(bf16[2,2,48,384]{3,2,1,0:T(8,128)(2,1)S(1)} %pad_maximum_fusion.8), channel_id=1, source_target_pairs={{0,16},{2,18},{4,20},{6,22},{8,24},{10,26},{12,28},{14,30},{16,0},... | collective-permute-start | bytes 442376 | tf_op jit(solution)/shard_map/cond/branch_1_fun/ppermute | solution.py:822
  26.2 31.7 %all-to-all-start.5 = ((bf16[4,2,2,3,48,256]{5,4,3,2,1,0:T(8,128)(2,1)}), bf16[4,2,2,3,48,256]{5,4,3,2,1,0:T(8,128)(2,1)}, u32[]{:S(2)}, u32[]{:S(2)}) async-start(bf16[4,2,2,3,48,256]{5,4,3,2,1,0:T(8,128)(2,1)} %get-tuple-element.504), calls=%async_computation.5 | async-start | bytes 2359296 | tf_op jit(solution)/shard_map/cond/branch_1_fun/all_to_all | solution.py:903
  39.9 12.5 %collective-permute-start.35 = (bf16[2,4,2,48,384]{4,3,2,1,0:T(8,128)(2,1)}, bf16[2,4,2,48,384]{4,3,2,1,0:T(8,128)(2,1)}, u32[]{:S(2)}, u32[]{:S(2)}) collective-permute-start(bf16[2,4,2,48,384]{4,3,2,1,0:T(8,128)(2,1)} %pad_maximum_fusion), channel_id=1, source_target_pairs={{0,4},{2,6},{4,0},{6,2},{8,12},{10,14},{12,8},{14,10},{16,20},{18,... | collective-permute-start | bytes 1769480 | tf_op jit(solution)/shard_map/cond/branch_1_fun/cond/branch_1_fun/ppermute | solution.py:822
  58.0 32.5 %all-to-all-start = ((bf16[4,2,2,3,48,256]{5,4,3,2,1,0:T(8,128)(2,1)}), bf16[4,2,2,3,48,256]{5,4,3,2,1,0:T(8,128)(2,1)}, u32[]{:S(2)}, u32[]{:S(2)}) async-start(bf16[4,2,2,3,48,256]{5,4,3,2,1,0:T(8,128)(2,1)} %get-tuple-element.569), calls=%async_computation | async-start | bytes 2359296 | tf_op jit(solution)/shard_map/cond/branch_1_fun/all_to_all | solution.py:903
  62.4 27.3 %collective-permute-start.1 = (bf16[4,2,2,3,48,256]{5,4,3,2,1,0:T(8,128)(2,1)}, bf16[4,2,2,3,48,256]{5,4,3,2,1,0:T(8,128)(2,1)}, u32[]{:S(2)}, u32[]{:S(2)}) collective-permute-start(bf16[4,2,2,3,48,256]{5,4,3,2,1,0:T(8,128)(2,1)} %get-tuple-element.568), channel_id=1, source_target_pairs={{0,4},{2,6},{4,0},{6,2},{8,12},{10,14},{12,8},{14,10},{16,20},{18,... | collective-permute-start | bytes 3538952 | tf_op jit(solution)/shard_map/cond/branch_1_fun/ppermute | solution.py:822
  64.0 20.8 %collective-permute-start.2 = (bf16[512,768]{1,0:T(8,128)(2,1)}, bf16[512,768]{1,0:T(8,128)(2,1)}, u32[]{:S(2)}, u32[]{:S(2)}) collective-permute-start(bf16[512,768]{1,0:T(8,128)(2,1)} %get-tuple-element.570), channel_id=1, source_target_pairs={{0,2},{2,0},{4,6},{6,4},{8,10},{10,8},{12,14},{14,12},{16,18},{18,... | collective-permute-start | bytes 2359304 | tf_op jit(solution)/shard_map/cond/branch_1_fun/ppermute | solution.py:822
  90.5 32.6 %all-to-all-start.1 = ((bf16[4,2,2,3,48,256]{5,4,3,2,1,0:T(8,128)(2,1)}), bf16[4,2,2,3,48,256]{5,4,3,2,1,0:T(8,128)(2,1)}, u32[]{:S(2)}, u32[]{:S(2)}) async-start(bf16[4,2,2,3,48,256]{5,4,3,2,1,0:T(8,128)(2,1)} %get-tuple-element.594), calls=%async_computation.1 | async-start | bytes 2359296 | tf_op jit(solution)/shard_map/cond/branch_1_fun/all_to_all | solution.py:903
  95.1 27.3 %collective-permute-start.7 = (bf16[4,2,2,3,48,256]{5,4,3,2,1,0:T(8,128)(2,1)}, bf16[4,2,2,3,48,256]{5,4,3,2,1,0:T(8,128)(2,1)}, u32[]{:S(2)}, u32[]{:S(2)}) collective-permute-start(bf16[4,2,2,3,48,256]{5,4,3,2,1,0:T(8,128)(2,1)} %get-tuple-element.593), channel_id=1, source_target_pairs={{0,4},{2,6},{4,0},{6,2},{8,12},{10,14},{12,8},{14,10},{16,20},{18,... | collective-permute-start | bytes 3538952 | tf_op jit(solution)/shard_map/cond/branch_1_fun/ppermute | solution.py:822
  96.7 18.4 %collective-permute-start.6 = (bf16[512,768]{1,0:T(8,128)(2,1)}, bf16[512,768]{1,0:T(8,128)(2,1)S(1)}, u32[]{:S(2)}, u32[]{:S(2)}) collective-permute-start(bf16[512,768]{1,0:T(8,128)(2,1)} %get-tuple-element.583), channel_id=1, source_target_pairs={{0,2},{2,0},{4,6},{6,4},{8,10},{10,8},{12,14},{14,12},{16,18},{18,... | collective-permute-start | bytes 2359304 | tf_op jit(solution)/shard_map/cond/branch_1_fun/ppermute | solution.py:822
  123.2 29.5 %collective-permute-start.8 = (bf16[4,2,2,3,48,256]{5,4,3,2,1,0:T(8,128)(2,1)}, bf16[4,2,2,3,48,256]{5,4,3,2,1,0:T(8,128)(2,1)}, u32[]{:S(2)}, u32[]{:S(2)}) collective-permute-start(bf16[4,2,2,3,48,256]{5,4,3,2,1,0:T(8,128)(2,1)} %get-tuple-element.612), channel_id=1, source_target_pairs={{0,4},{2,6},{4,0},{6,2},{8,12},{10,14},{12,8},{14,10},{16,20},{18,... | collective-permute-start | bytes 3538952 | tf_op jit(solution)/shard_map/cond/branch_1_fun/ppermute | solution.py:822
  152.7 26.9 %collective-permute-start.17 = (bf16[4,2,2,3,48,256]{5,4,3,2,1,0:T(8,128)(2,1)}, bf16[4,2,2,3,48,256]{5,4,3,2,1,0:T(8,128)(2,1)S(1)}, u32[]{:S(2)}, u32[]{:S(2)}) collective-permute-start(bf16[4,2,2,3,48,256]{5,4,3,2,1,0:T(8,128)(2,1)} %get-tuple-element.652), channel_id=1, source_target_pairs={{0,4},{2,6},{4,0},{6,2},{8,12},{10,14},{12,8},{14,10},{16,20},{18,... | collective-permute-start | bytes 3538952 | tf_op jit(solution)/shard_map/cond/branch_1_fun/ppermute | solution.py:822
  183.0 45.5 %all-to-all-start.3 = ((bf16[4,2,2,3,48,256]{5,4,3,2,1,0:T(8,128)(2,1)}), bf16[4,2,2,3,48,256]{5,4,3,2,1,0:T(8,128)(2,1)S(1)}, u32[]{:S(2)}, u32[]{:S(2)}) async-start(bf16[4,2,2,3,48,256]{5,4,3,2,1,0:T(8,128)(2,1)} %get-tuple-element.694), calls=%async_computation.3 | async-start | bytes 2359296 | tf_op jit(solution)/shard_map/cond/branch_1_fun/all_to_all | solution.py:903
  197.8 27.5 %collective-permute-start.21 = (bf16[4,2,2,3,48,256]{5,4,3,2,1,0:T(8,128)(2,1)}, bf16[4,2,2,3,48,256]{5,4,3,2,1,0:T(8,128)(2,1)S(1)}, u32[]{:S(2)}, u32[]{:S(2)}) collective-permute-start(bf16[4,2,2,3,48,256]{5,4,3,2,1,0:T(8,128)(2,1)} %get-tuple-element.698), channel_id=1, source_target_pairs={{0,4},{2,6},{4,0},{6,2},{8,12},{10,14},{12,8},{14,10},{16,20},{18,... | collective-permute-start | bytes 3538952 | tf_op jit(solution)/shard_map/cond/branch_1_fun/ppermute | solution.py:822
  199.2 18.9 %collective-permute-start.20 = (bf16[512,768]{1,0:T(8,128)(2,1)}, bf16[512,768]{1,0:T(8,128)(2,1)}, u32[]{:S(2)}, u32[]{:S(2)}) collective-permute-start(bf16[512,768]{1,0:T(8,128)(2,1)} %get-tuple-element.684), channel_id=1, source_target_pairs={{0,2},{2,0},{4,6},{6,4},{8,10},{10,8},{12,14},{14,12},{16,18},{18,... | collective-permute-start | bytes 2359304 | tf_op jit(solution)/shard_map/cond/branch_1_fun/ppermute | solution.py:822
  230.9 40.6 %all-to-all-start.2 = ((bf16[4,2,2,3,48,256]{5,4,3,2,1,0:T(8,128)(2,1)}), bf16[4,2,2,3,48,256]{5,4,3,2,1,0:T(8,128)(2,1)S(1)}, u32[]{:S(2)}, u32[]{:S(2)}) async-start(bf16[4,2,2,3,48,256]{5,4,3,2,1,0:T(8,128)(2,1)} %get-tuple-element.758), calls=%async_computation.2 | async-start | bytes 2359296 | tf_op jit(solution)/shard_map/cond/branch_1_fun/all_to_all | solution.py:903
  235.8 32.5 %collective-permute-start.12 = (bf16[4,2,2,3,48,256]{5,4,3,2,1,0:T(8,128)(2,1)}, bf16[4,2,2,3,48,256]{5,4,3,2,1,0:T(8,128)(2,1)S(1)}, u32[]{:S(2)}, u32[]{:S(2)}) collective-permute-start(bf16[4,2,2,3,48,256]{5,4,3,2,1,0:T(8,128)(2,1)} %get-tuple-element.762), channel_id=1, source_target_pairs={{0,4},{2,6},{4,0},{6,2},{8,12},{10,14},{12,8},{14,10},{16,20},{18,... | collective-permute-start | bytes 3538952 | tf_op jit(solution)/shard_map/cond/branch_1_fun/ppermute | solution.py:822
  237.3 36.6 %collective-permute-start.11 = (bf16[512,768]{1,0:T(8,128)(2,1)}, bf16[512,768]{1,0:T(8,128)(2,1)}, u32[]{:S(2)}, u32[]{:S(2)}) collective-permute-start(bf16[512,768]{1,0:T(8,128)(2,1)} %get-tuple-element.756), channel_id=1, source_target_pairs={{0,2},{2,0},{4,6},{6,4},{8,10},{10,8},{12,14},{14,12},{16,18},{18,... | collective-permute-start | bytes 2359304 | tf_op jit(solution)/shard_map/cond/branch_1_fun/ppermute | solution.py:822
  273.9 36.1 %all-to-all-start.4 = ((bf16[4,2,2,3,48,256]{5,4,3,2,1,0:T(8,128)(2,1)}), bf16[4,2,2,3,48,256]{5,4,3,2,1,0:T(8,128)(2,1)}, u32[]{:S(2)}, u32[]{:S(2)}) async-start(bf16[4,2,2,3,48,256]{5,4,3,2,1,0:T(8,128)(2,1)} %get-tuple-element.804), calls=%async_computation.4 | async-start | bytes 2359296 | tf_op jit(solution)/shard_map/cond/branch_1_fun/all_to_all | solution.py:903
  278.4 15.6 %collective-permute-start.25 = (bf16[2,4,2,48,384]{4,3,2,1,0:T(8,128)(2,1)}, bf16[2,4,2,48,384]{4,3,2,1,0:T(8,128)(2,1)S(1)}, u32[]{:S(2)}, u32[]{:S(2)}) collective-permute-start(bf16[2,4,2,48,384]{4,3,2,1,0:T(8,128)(2,1)} %get-tuple-element.795), channel_id=1, source_target_pairs={{0,4},{2,6},{4,0},{6,2},{8,12},{10,14},{12,8},{14,10},{16,20},{18,... | collective-permute-start | bytes 1769480 | tf_op jit(solution)/shard_map/cond/branch_1_fun/ppermute | solution.py:822
  279.8 15.0 %collective-permute-start.26 = (bf16[2,4,2,48,384]{4,3,2,1,0:T(8,128)(2,1)}, bf16[2,4,2,48,384]{4,3,2,1,0:T(8,128)(2,1)S(1)}, u32[]{:S(2)}, u32[]{:S(2)}) collective-permute-start(bf16[2,4,2,48,384]{4,3,2,1,0:T(8,128)(2,1)} %get-tuple-element.797), channel_id=1, source_target_pairs={{0,2},{2,0},{4,6},{6,4},{8,10},{10,8},{12,14},{14,12},{16,18},{18,... | collective-permute-start | bytes 1769480 | tf_op jit(solution)/shard_map/cond/branch_1_fun/ppermute | solution.py:822
  309.9 24.3 %all-to-all-start.6 = ((bf16[4,2,2,48,384]{4,3,2,1,0:T(8,128)(2,1)}), bf16[4,2,2,48,384]{4,3,2,1,0:T(8,128)(2,1)S(1)}, u32[]{:S(2)}, u32[]{:S(2)}) async-start(bf16[4,2,2,48,384]{4,3,2,1,0:T(8,128)(2,1)} %get-tuple-element.1007), calls=%async_computation.6 | async-start | bytes 1179648 | tf_op jit(solution)/shard_map/all_to_all | solution.py:903
  318.0 17.8 %collective-permute-start.38 = (bf16[2,3,48,768]{3,2,1,0:T(8,128)(2,1)S(1)}, bf16[2,3,48,768]{3,2,1,0:T(8,128)(2,1)S(1)}, u32[]{:S(2)}, u32[]{:S(2)}) collective-permute-start(bf16[2,3,48,768]{3,2,1,0:T(8,128)(2,1)S(1)} %pad_maximum_fusion.12), channel_id=1, source_target_pairs={{0,2},{2,0},{4,6},{6,4},{8,10},{10,8},{12,14},{14,12},{16,18},{18,... | collective-permute-start | bytes 1327112 | tf_op jit(solution)/shard_map/ppermute | solution.py:822
  324.4 13.2 %collective-permute-start.39 = (f32[22,768]{1,0:T(8,128)S(1)}, f32[22,768]{1,0:T(8,128)S(1)}, u32[]{:S(2)}, u32[]{:S(2)}) collective-permute-start(f32[22,768]{1,0:T(8,128)S(1)} %get-tuple-element.1504), channel_id=1, source_target_pairs={{0,8},{2,10},{4,12},{6,14},{8,0},{10,2},{12,4},{14,6},{16,24},{18,... | collective-permute-start | bytes 202760 | tf_op jit(solution)/shard_map/ppermute | solution.py:822
  (47 other events, 432.6 us)
